TPU v7x, 32 devices: a whole 2x2x4 slice. The times are simulated.
32 devices in a mesh: rep: 8 (over z, x), dp: 4 (over y, core).
Axes of the slice: x: 2, y: 2, z: 4, core: 2. Of those that a mesh axis runs over, the one named last changes fastest.
Arguments:
- residual_flow: bfloat16 [1536, 1024], P('dp'), may hold values from -6 to 6
- rooted_input_matrix: bfloat16 [8, 1024, 2048], P('rep', None, 'dp'), may hold values from -6 to 6
- chain_normal_draws: bfloat16 [8, 1024, 2048], P('rep', None, 'dp'), may hold values from -6 to 6
- output_matrix: bfloat16 [2048, 1024], P('dp'), may hold values from -0.125 to 0.125
- chain_heat: float32 [8], P('rep'), may hold values from 0.05 to 1
- matched_chain: int32 [8], P('rep'), may hold values from 0 to 7, as said below
- swap_mask: int32 [8], P('rep'), may hold values from 0 to 1, as said below
Outputs:
- swapped: bfloat16 [8, 1024, 2048], P('rep', None, 'dp')
- chain_gaps: float32 [8, 2, 2048], P('rep', None, 'dp')
Inputs may be any that keep to these rules, and one draw needn't show every extreme that they name: Replicas form aligned blocks of four; in each block one of these holds: 4b with 4b + 1 and 4b + 2 with 4b + 3 are mates; only 4b + 1 with 4b + 2; only 4b with 4b + 1; only 4b + 2 with 4b + 3. matched_chain[r] is r's mate, or r where r has none. `swap_mask`: mates carry the same flag; a replica without a mate carries 0; every matched pair of the first block carries 1.
All inputs are finite; a program needn't handle non-finite values.
Results may differ from a plain program's by a relative error of at most 0.014.
Values may be sent and summed in bfloat16 or wider, within the bound.
No kernel may reach another device: no remote copies, remote signals or barrier semaphores. Data moves between devices by JAX's collectives and lax.ppermute only.
A program may use at most 64 MiB of HBM per device.

v0:
```python
import math

import jax
import jax.numpy as jnp
from jax import lax
from jax.sharding import PartitionSpec as P

drift_stride = 0.5


def shifted(value, axis, steps):
    count = lax.axis_size(axis)
    pairs = [(source, (source + steps) % count) for source in range(count)]
    return lax.ppermute(value, axis, pairs)


def normalize(residual_flow):
    values = residual_flow.astype(jnp.float32)
    center = values - jnp.mean(values, axis=1, keepdims=True)
    spread = jnp.mean(center * center, axis=1, keepdims=True)
    return (center * lax.rsqrt(spread + 1e-05)).astype(jnp.bfloat16)


def gelu_value(values):
    inner = math.sqrt(2.0 / math.pi) * (values + 0.044715 * values * values * values)
    return 0.5 * values * (1.0 + jnp.tanh(inner))


def gelu_slope(values):
    coeff = math.sqrt(2.0 / math.pi)
    inner = coeff * (values + 0.044715 * values * values * values)
    tangent = jnp.tanh(inner)
    return 0.5 * (1.0 + tangent) + 0.5 * values * (1.0 - tangent * tangent) * coeff * (
        1.0 + 3.0 * 0.044715 * values * values
    )


def next_errors(output, residual_flow):
    width = residual_flow.shape[1]
    ahead = output[:-1] - residual_flow[1:].astype(jnp.float32)
    return jnp.concatenate([ahead, jnp.zeros((1, width), jnp.float32)], axis=0).astype(jnp.bfloat16)


def against_rows(errors, weight):
    return lax.dot_general(
        errors, weight, (((1,), (1,)), ((), ())), preferred_element_type=jnp.float32
    )


def body(
    residual_flow,
    rooted_input_matrix,
    chain_normal_draws,
    output_matrix,
    chain_heat,
    matched_chain,
    swap_mask,
):
    width = rooted_input_matrix.shape[1]
    factor = width ** (-0.5)
    normed = normalize(residual_flow)
    params = rooted_input_matrix[0]
    preact = (
        jnp.dot(
            normed,
            lax.all_gather(params, "dp", axis=1, tiled=True),
            preferred_element_type=jnp.float32,
        )
        * factor
    )
    down_full = lax.all_gather(output_matrix, "dp", axis=0, tiled=True)
    hidden = gelu_value(preact).astype(jnp.bfloat16)
    output = residual_flow.astype(jnp.float32) + jnp.dot(
        hidden, down_full, preferred_element_type=jnp.float32
    )
    errors = next_errors(output, residual_flow)
    hidden_grad = against_rows(errors, down_full)
    preact_grad = (hidden_grad * gelu_slope(preact)).astype(jnp.bfloat16)
    partial_value = (
        lax.dot_general(
            normed, preact_grad, (((0,), (0,)), ((), ())), preferred_element_type=jnp.float32
        )
        * factor
    )
    gradient = lax.psum_scatter(
        partial_value.astype(jnp.bfloat16), "dp", scatter_dimension=1, tiled=True
    ).astype(jnp.float32)
    current = params.astype(jnp.float32)
    moved = (
        current
        - drift_stride * (gradient + current)
        + jnp.sqrt(2.0 * drift_stride * chain_heat[0]) * chain_normal_draws[0].astype(jnp.float32)
    )
    refreshed_input_matrix = moved.astype(jnp.bfloat16)
    own_rank = lax.axis_index("rep")
    mate = matched_chain[0]
    taken = swap_mask[0] == 1
    below = shifted(refreshed_input_matrix, "rep", 1)
    above = shifted(refreshed_input_matrix, "rep", -1)
    result = jnp.where(
        taken & (mate == own_rank - 1),
        below,
        jnp.where(taken & (mate == own_rank + 1), above, refreshed_input_matrix),
    )
    own_values = refreshed_input_matrix.astype(jnp.float32)
    lower_diff = own_values - below.astype(jnp.float32)
    upper_diff = own_values - above.astype(jnp.float32)
    chain_gaps = jnp.stack(
        [jnp.mean(lower_diff * lower_diff, axis=0), jnp.mean(upper_diff * upper_diff, axis=0)],
        axis=0,
    )
    return (result[None], chain_gaps[None])


def solution(mesh):
    placed = (
        P("dp", None),
        P("rep", None, "dp"),
        P("rep", None, "dp"),
        P("dp", None),
        P("rep"),
        P("rep"),
        P("rep"),
    )
    return jax.shard_map(
        body,
        mesh=mesh,
        in_specs=placed,
        out_specs=(P("rep", None, "dp"), P("rep", None, "dp")),
        check_vma=False,
    )
```

profile of v0, /device:TPU:0, one launch (start us, length us, event | category | flops | bytes accessed | tf_op | source)
XLA Modules:
  0.0 201.8 jit_solution(6651590608696738037)
XLA Ops:
  7.2 0.0 copy-start
  7.2 0.0 all-gather.6.cloned.1.call-start
  7.2 0.7 all-gather.6.cloned.1.call-update
  7.9 0.0 all-gather.4.cloned.1.call-start
  8.0 0.7 all-gather.4.cloned.1.call-update
  8.7 0.0 reduce-scatter.2.cloned.1.call-start
  8.7 1.3 convert_element_type.43
  10.0 0.0 copy-done
  10.0 0.2 convert_reduce_fusion
  10.2 0.4 multiply_reduce_fusion
  10.6 36.2 %all-gather.6.cloned.1.call-done = bf16[1,1024,2048]{2,1,0:T(8,128)(2,1)} async-done(((bf16[1,1024,512]{2,1,0:T(8,128)(2,1)}), bf16[1,1024,2048]{2,1,0:T(8,128)(2,1)}) %all-gather.6.cloned.1.call-update) | async-done | bytes 4194320 | tf_op jit(solution)/shard_map/all_gather | solution.py:66
  46.8 5.8 %fusion = f32[384,2048]{1,0:T(8,128)} fusion(bf16[1,1024,2048]{2,1,0:T(8,128)(2,1)} %all-gather.6.cloned.1.call-done, bf16[384,1024]{1,0:T(8,128)(2,1)S(1)} %copy-done, f32[384]{0:T(512)S(1)} %add_rsqrt_fusion, f32[384]{0:T(512)S(1)} %broadcast_multiply_fusion.2), kind=kOutput, calls=%fused_computation.2 | convolution fusion | flops 1612185600 | bytes 8129536 | tf_op jit(solution)/shard_map/dot_general | solution.py:64
  52.6 30.2 %all-gather.4.cloned.1.call-done = bf16[2048,1024]{1,0:T(8,128)(2,1)} async-done(((bf16[512,1024]{1,0:T(8,128)(2,1)}), bf16[2048,1024]{1,0:T(8,128)(2,1)}) %all-gather.4.cloned.1.call-update) | async-done | bytes 4194320 | tf_op jit(solution)/shard_map/all_gather | solution.py:71
  82.9 5.3 %fusion.12 = f32[384,1024]{1,0:T(8,128)S(1)} fusion(bf16[2048,1024]{1,0:T(8,128)(2,1)} %all-gather.4.cloned.1.call-done, f32[384,2048]{1,0:T(8,128)} %fusion), kind=kOutput, calls=%fused_computation.20 | convolution fusion | flops 1618477056 | bytes 8912896 | tf_op jit(solution)/shard_map/dot_general | solution.py:73
  88.1 0.5 fusion.14
  88.6 9.2 %multiply_convert_fusion = bf16[1024,2048]{1,0:T(8,128)(2,1)} fusion(f32[384,2048]{1,0:T(8,128)} %fusion, bf16[2048,1024]{1,0:T(8,128)(2,1)} %all-gather.4.cloned.1.call-done, bf16[383,1024]{1,0:T(8,128)(2,1)S(1)} %fusion.14, bf16[384,1024]{1,0:T(8,128)(2,1)S(1)} %copy-done, f32[384]{0:T(512)S(1)} %add_rsqrt_fusion, f32[384]{0:T(512)S(1)} %broadcast_multiply_fusion.2), kind=kOutput, calls=%fused_computation | convolution fusion | flops 3242721280 | bytes 13108224 | tf_op jit(solution)/shard_map/dot_general | solution.py:80
  97.8 0.0 copy-start.1
  97.8 0.0 copy-start.2
  97.8 0.0 reduce-scatter.2.cloned.1.call-update
  98.7 43.8 %reduce-scatter.2.cloned.1.call-done = bf16[1024,512]{1,0:T(8,128)(2,1)} async-done(((bf16[1024,2048]{1,0:T(8,128)(2,1)}), bf16[1024,512]{1,0:T(8,128)(2,1)}) %reduce-scatter.2.cloned.1.call-update) | async-done | bytes 1048592 | tf_op jit(solution)/shard_map/reduce_scatter | solution.py:85
  142.5 0.0 copy-done.1
  142.5 0.0 copy-done.2
  142.5 1.8 fusion.11
  144.3 1.5 collective-permute-start
  145.9 3.3 %collective-permute-start.1 = (bf16[1024,512]{1,0:T(8,128)(2,1)S(1)}, bf16[1024,512]{1,0:T(8,128)(2,1)S(1)}, u32[]{:S(2)}, u32[]{:S(2)}) collective-permute-start(bf16[1024,512]{1,0:T(8,128)(2,1)S(1)} %fusion.11), channel_id=1, source_target_pairs={{0,28},{4,0},{8,4},{12,8},{16,12},{20,16},{24,20},{28,24},{1,29},{... | collective-permute-start | bytes 3145736 | tf_op jit(solution)/shard_map/ppermute | solution.py:14
  150.4 40.3 %collective-permute-done = bf16[1024,512]{1,0:T(8,128)(2,1)S(1)} collective-permute-done((bf16[1024,512]{1,0:T(8,128)(2,1)S(1)}, bf16[1024,512]{1,0:T(8,128)(2,1)S(1)}, u32[]{:S(2)}, u32[]{:S(2)}) %collective-permute-start) | collective-permute-done | bytes 1048608 | tf_op jit(solution)/shard_map/ppermute | solution.py:14
  190.8 2.2 %collective-permute-done.1 = bf16[1024,512]{1,0:T(8,128)(2,1)S(1)} collective-permute-done((bf16[1024,512]{1,0:T(8,128)(2,1)S(1)}, bf16[1024,512]{1,0:T(8,128)(2,1)S(1)}, u32[]{:S(2)}, u32[]{:S(2)}) %collective-permute-start.1) | collective-permute-done | bytes 1048608 | tf_op jit(solution)/shard_map/ppermute | solution.py:14
  193.0 0.6 fusion.6
  193.6 0.6 maximum_bitcast_fusion
  194.2 1.1 select_bitcast_fusion
  (3 shorter events, 0.0 us)
Async XLA Ops:
  7.2 2.8 %copy-start = (bf16[384,1024]{1,0:T(8,128)(2,1)S(1)}, bf16[384,1024]{1,0:T(8,128)(2,1)}, u32[]{:S(2)}) copy-start(bf16[384,1024]{1,0:T(8,128)(2,1)} %param.7) | copy-start | bytes 2359300
  7.2 39.6 %all-gather.6.cloned.1.call-start = ((), (), s32[]{:S(2)}) async-start(), calls=%async_computation.3 | async-start | bytes 5242880 | tf_op jit(solution)/shard_map/all_gather | solution.py:66
  7.9 75.0 %all-gather.4.cloned.1.call-start = ((), (), s32[]{:S(2)}) async-start(), calls=%async_computation.1 | async-start | bytes 5242880 | tf_op jit(solution)/shard_map/all_gather | solution.py:71
  8.7 133.9 %reduce-scatter.2.cloned.1.call-start = ((), (), s32[]{:S(2)}) async-start(), calls=%async_computation.2 | async-start | bytes 5242880 | tf_op jit(solution)/shard_map/reduce_scatter | solution.py:85
  97.8 44.7 %copy-start.1 = (bf16[1,1024,512]{2,1,0:T(8,128)(2,1)S(1)}, bf16[1,1024,512]{2,1,0:T(8,128)(2,1)}, u32[]{:S(2)}) copy-start(bf16[1,1024,512]{2,1,0:T(8,128)(2,1)} %param.8) | copy-start | bytes 3145732
  97.8 44.7 %copy-start.2 = (bf16[1,1024,512]{2,1,0:T(8,128)(2,1)S(1)}, bf16[1,1024,512]{2,1,0:T(8,128)(2,1)}, u32[]{:S(2)}) copy-start(bf16[1,1024,512]{2,1,0:T(8,128)(2,1)} %param.9) | copy-start | bytes 3145732
  144.3 46.4 %collective-permute-start = (bf16[1024,512]{1,0:T(8,128)(2,1)S(1)}, bf16[1024,512]{1,0:T(8,128)(2,1)S(1)}, u32[]{:S(2)}, u32[]{:S(2)}) collective-permute-start(bf16[1024,512]{1,0:T(8,128)(2,1)S(1)} %fusion.11), channel_id=1, source_target_pairs={{0,4},{4,8},{8,12},{12,16},{16,20},{20,24},{24,28},{28,0},{1,5},{5... | collective-permute-start | bytes 3145736 | tf_op jit(solution)/shard_map/ppermute | solution.py:14
  145.9 47.1 %collective-permute-start.1 = (bf16[1024,512]{1,0:T(8,128)(2,1)S(1)}, bf16[1024,512]{1,0:T(8,128)(2,1)S(1)}, u32[]{:S(2)}, u32[]{:S(2)}) collective-permute-start(bf16[1024,512]{1,0:T(8,128)(2,1)S(1)} %fusion.11), channel_id=1, source_target_pairs={{0,28},{4,0},{8,4},{12,8},{16,12},{20,16},{24,20},{28,24},{1,29},{... | collective-permute-start | bytes 3145736 | tf_op jit(solution)/shard_map/ppermute | solution.py:14
Sparse Core Ops, SparseCore 0:
  9.6 37.1 all-gather.5
  48.3 34.4 all-gather.3
  98.0 44.4 reduce-scatter.1
where the time goes:
time: 202 us
  waiting for transfers between devices  154 us (76%)
  matrix products  20.4 us (10%)
  between operations  15.9 us (8%)
  other arithmetic  6.44 us (3%)
  starting transfers between devices  4.89 us (2%)
    reduce_scatter x1, waiting for transfers between devices, body(): lax.psum_scatter(partial_value.astype(jnp.bfloat16), 'dp', scatter_dimens...  43.8 us
    ppermute x2, waiting for transfers between devices, shifted(): return lax.ppermute(value, axis, pairs)  42.5 us
    all_gather x1, waiting for transfers between devices, body(): lax.all_gather(params, 'dp', axis=1, tiled=True)  36.2 us
    all_gather x1, waiting for transfers between devices, body(): down_full = lax.all_gather(output_matrix, 'dp', axis=0, tiled=True)  30.2 us
    dot_general x1, matrix products, body(): lax.dot_general(normed, preact_grad, (((0,), (0,)), ((), ())), preferred_...  9.25 us
    dot_general x1, matrix products, body(): jnp.dot(normed, lax.all_gather(params, 'dp', axis=1, tiled=True), preferr...  5.84 us
    dot_general x1, matrix products, body(): jnp.dot(hidden, down_full, preferred_element_type=jnp.float32)  5.27 us
    ppermute x2, starting transfers between devices, shifted(): return lax.ppermute(value, axis, pairs)  4.78 us
  transfers between devices with their start and end apart: 5, of which 5 were waited for; matrix products, arithmetic and copies ran while one was open for 4% of the time, Pallas kernels for 0%

commit v1 on v0

v1 whole, which is shorter than its diff:
```python
import functools
import math

import jax
import jax.numpy as jnp
from jax import lax
from jax.experimental import pallas as pl
from jax.experimental.pallas import tpu as pltpu
from jax.sharding import PartitionSpec as P

drift_stride = 0.5
lanes = 128
f32 = jnp.float32
bf16 = jnp.bfloat16
limit = pltpu.CompilerParams(vmem_limit_bytes=40 * 1024 * 1024)
smem = pl.BlockSpec(memory_space=pltpu.SMEM)


def matmul(left, right):
    return jnp.dot(left, right, preferred_element_type=f32)


def against_rows(left, right):
    return lax.dot_general(left, right, (((1,), (1,)), ((), ())), preferred_element_type=f32)


def cost(macs, nbytes):
    return pl.CostEstimate(flops=2 * macs, bytes_accessed=nbytes, transcendentals=0)


def whole(array):
    rank = array.ndim
    return pl.BlockSpec(array.shape, lambda *_: (0,) * rank)


def shape(dims, dtype=bf16):
    return jax.ShapeDtypeStruct(dims, dtype)


def assemble_kernel(place_ref, own, across, behind, upper, lower, out):
    rows = own.shape[0]
    half = rows // 2
    for place in range(4):

        @pl.when(place_ref[0] == place)
        def _():
            out[place * rows : (place + 1) * rows] = own[...]
            out[(place ^ 1) * rows : ((place ^ 1) + 1) * rows] = across[...]
            out[(place ^ 2) * rows : ((place ^ 2) + 1) * rows] = behind[...]
            out[(place ^ 3) * rows : (place ^ 3) * rows + half] = upper[...]
            out[(place ^ 3) * rows + half : ((place ^ 3) + 1) * rows] = lower[...]


def assemble(place, pieces):
    rows, width = pieces[0].shape
    return pl.pallas_call(
        assemble_kernel,
        grid=(1,),
        out_shape=shape((4 * rows, width)),
        in_specs=[smem] + [whole(piece) for piece in pieces],
        out_specs=pl.BlockSpec((4 * rows, width), lambda *_: (0, 0)),
        compiler_params=limit,
        cost_estimate=cost(0, 16 * rows * width),
    )(place, *pieces)


def forward_kernel(tokens, own_in, mate_in, own_out, mate_out, normed_t, slope, first, second, normed, total):
    step = pl.program_id(0)
    steps = pl.num_programs(0)
    width = tokens.shape[1]

    @pl.when(step == 0)
    def _():
        values = tokens[...].astype(f32)
        center = values - jnp.mean(values, axis=1, keepdims=True)
        spread = jnp.mean(center * center, axis=1, keepdims=True)
        scaled = (center * lax.rsqrt(spread + 1e-05)).astype(bf16)
        normed[...] = scaled
        total[...] = jnp.zeros_like(total)

    def part(weight_in, weight_out):
        values = matmul(normed[...], weight_in[...]) * (width**-0.5)
        coeff = math.sqrt(2.0 / math.pi)
        square = values * values
        gate = 0.5 + 0.5 * jnp.tanh(coeff * values * (1.0 + 0.044715 * square))
        hidden = values * gate
        slope[0] = (
            gate + hidden * (1.0 - gate) * (2.0 * coeff + 6.0 * 0.044715 * coeff * square)
        ).astype(bf16)
        total[...] += matmul(hidden.astype(bf16), weight_out[...])

    @pl.when(step < steps // 2)
    def _():
        part(own_in, own_out)

    @pl.when(step >= steps // 2)
    def _():
        part(mate_in, mate_out)

    @pl.when(step == steps - 1)
    def _():
        half = first.shape[0]
        first[...] = total[:half].astype(bf16)
        second[...] = total[half:].astype(bf16)
        normed_t[...] = normed[...].T


def forward(tokens, own_in, mate_in, own_out, mate_out):
    count, width = tokens.shape
    block = own_in.shape[1]
    tile = block // 2
    per = block // tile
    early = lambda step: jnp.minimum(step, per - 1)
    late = lambda step: jnp.maximum(step - per, 0)
    return pl.pallas_call(
        forward_kernel,
        grid=(2 * per,),
        out_shape=(
            shape((width, count)),
            shape((2, count, block)),
            shape((count // 2, width)),
            shape((count // 2, width)),
        ),
        in_specs=[
            whole(tokens),
            pl.BlockSpec((width, tile), lambda step: (0, early(step))),
            pl.BlockSpec((width, tile), lambda step: (0, late(step))),
            pl.BlockSpec((tile, width), lambda step: (early(step), 0)),
            pl.BlockSpec((tile, width), lambda step: (late(step), 0)),
        ],
        out_specs=(
            pl.BlockSpec((width, count), lambda step: (0, 0)),
            pl.BlockSpec((1, count, tile), lambda step: (step // per, 0, step % per)),
            pl.BlockSpec((count // 2, width), lambda step: (0, 0)),
            pl.BlockSpec((count // 2, width), lambda step: (0, 0)),
        ),
        scratch_shapes=[pltpu.VMEM((count, width), bf16), pltpu.VMEM((count, width), f32)],
        compiler_params=limit,
        cost_estimate=cost(4 * count * width * block, 8 * width * block),
    )(tokens, own_in, mate_in, own_out, mate_out)


def errors_kernel(last, tokens, own_part, sent_part, weight, weight_mate, errors, grads):
    count = errors.shape[0]
    base = tokens.shape[0] - count if last else 0
    span = count if last else count + 16
    values = tokens[base : base + span].astype(f32)
    ahead = pltpu.roll(values, span - 1, 0)[:count]
    result = values[:count] + own_part[...].astype(f32) + sent_part[...].astype(f32) - ahead
    if last:
        rank = lax.broadcasted_iota(jnp.int32, result.shape, 0)
        result = jnp.where(rank == count - 1, 0.0, result)
    result = result.astype(bf16)
    errors[...] = result
    grads[:, :lanes] = against_rows(result, weight[...]).astype(bf16)
    grads[:, lanes:] = against_rows(result, weight_mate[...]).astype(bf16)


def errors_of(last, tokens, own_part, sent_part, weight, weight_mate):
    count, width = own_part.shape
    rows = pl.BlockSpec((lanes, width), lambda *_: (0, 0))
    return pl.pallas_call(
        functools.partial(errors_kernel, last),
        grid=(1,),
        out_shape=(shape((count, width)), shape((count, 2 * lanes))),
        in_specs=[whole(tokens), whole(own_part), whole(sent_part), rows, rows],
        out_specs=(
            pl.BlockSpec((count, width), lambda *_: (0, 0)),
            pl.BlockSpec((count, 2 * lanes), lambda *_: (0, 0)),
        ),
        compiler_params=limit,
        cost_estimate=cost(2 * count * width * lanes, 10 * count * width),
    )(tokens, own_part, sent_part, weight, weight_mate)


def away_kernel(first, second, weight, weight_mate, grads):
    half = first.shape[0]
    for at, errors in ((0, first), (half, second)):
        grads[at : at + half, :lanes] = against_rows(errors[...], weight[...]).astype(bf16)
        grads[at : at + half, lanes:] = against_rows(errors[...], weight_mate[...]).astype(bf16)


def away(chunk, first, second, weight, weight_mate):
    half, width = first.shape
    rows = pl.BlockSpec((lanes, width), lambda *_: (chunk, 0))
    return pl.pallas_call(
        away_kernel,
        grid=(1,),
        out_shape=shape((2 * half, 2 * lanes)),
        in_specs=[whole(first), whole(second), rows, rows],
        out_specs=pl.BlockSpec((2 * half, 2 * lanes), lambda *_: (0, 0)),
        compiler_params=limit,
        cost_estimate=cost(4 * half * width * lanes, 8 * half * width),
    )(first, second, weight, weight_mate)


def home_kernel(first, second, weight, weight_mate, slope, grads):
    half = first.shape[0]
    for at, errors in ((0, first), (half, second)):
        for side, rows in ((0, weight), (1, weight_mate)):
            product = against_rows(errors[...], rows[...]) * slope[side, at : at + half].astype(f32)
            grads[0, at : at + half, side * lanes : (side + 1) * lanes] = product.astype(bf16)


def home(first, second, weight, weight_mate, slope):
    half, width = first.shape
    chunks = weight.shape[0] // lanes
    rows = pl.BlockSpec((lanes, width), lambda chunk: (chunk, 0))
    return pl.pallas_call(
        home_kernel,
        grid=(chunks,),
        out_shape=shape((chunks, 2 * half, 2 * lanes)),
        in_specs=[
            whole(first),
            whole(second),
            rows,
            rows,
            pl.BlockSpec((2, 2 * half, lanes), lambda chunk: (0, 0, chunk)),
        ],
        out_specs=pl.BlockSpec((1, 2 * half, 2 * lanes), lambda chunk: (chunk, 0, 0)),
        compiler_params=limit,
        cost_estimate=cost(4 * chunks * half * width * lanes, 10 * half * width),
    )(first, second, weight, weight_mate, slope)


def gradient_kernel(parts, *refs):
    arrived = refs[:parts]
    slope, near, normed_a, normed_b, keep, send, mixed = refs[parts:]
    factor = normed_a.shape[0] ** -0.5
    count = arrived[0].shape[0]
    for part in range(parts):
        rows = slice(part * count, (part + 1) * count)
        for side in range(2):
            cols = slice(side * lanes, (side + 1) * lanes)
            mixed[rows, cols] = (
                arrived[part][:, cols].astype(f32) * slope[side, rows].astype(f32)
            ).astype(bf16)
    total = (matmul(normed_a[...], mixed[...]) + matmul(normed_b[...], near[0])) * factor
    keep[...] = total[:, :lanes]
    send[...] = total[:, lanes:].astype(bf16)


def gradient(chunk, arrived, slope, near, normed_a, normed_b):
    width, count = normed_a.shape
    return pl.pallas_call(
        functools.partial(gradient_kernel, len(arrived)),
        grid=(1,),
        out_shape=(shape((width, lanes), f32), shape((width, lanes))),
        in_specs=[whole(piece) for piece in arrived]
        + [
            pl.BlockSpec((2, count, lanes), lambda *_: (0, 0, chunk)),
            pl.BlockSpec((1, count, 2 * lanes), lambda *_: (chunk, 0, 0)),
            whole(normed_a),
            whole(normed_b),
        ],
        out_specs=(
            pl.BlockSpec((width, lanes), lambda *_: (0, 0)),
            pl.BlockSpec((width, lanes), lambda *_: (0, 0)),
        ),
        scratch_shapes=[pltpu.VMEM((count, 2 * lanes), bf16)],
        compiler_params=limit,
        cost_estimate=cost(4 * width * count * lanes, 4 * width * count),
    )(*arrived, slope, near, normed_a, normed_b)


def update_kernel(heat, keep, sent, params, noise, out):
    current = params[0].astype(f32)
    slope = keep[...] + sent[...].astype(f32)
    moved = current - drift_stride * (slope + current) + heat[0] * noise[0].astype(f32)
    out[...] = moved.astype(bf16)


def update(chunk, heat, keep, sent, params, noise):
    width = keep.shape[0]
    cols = pl.BlockSpec((1, width, lanes), lambda *_: (0, 0, chunk))
    return pl.pallas_call(
        update_kernel,
        grid=(1,),
        out_shape=shape((width, lanes)),
        in_specs=[smem, whole(keep), whole(sent), cols, cols],
        out_specs=pl.BlockSpec((width, lanes), lambda *_: (0, 0)),
        compiler_params=limit,
        cost_estimate=cost(0, 12 * width * lanes),
    )(heat, keep, sent, params, noise)


def finish_kernel(count, start, *refs):
    taken = refs[0]
    own, across, beyond = (refs[1 + i * count : 1 + (i + 1) * count] for i in range(3))
    result, gaps = refs[-2], refs[-1]
    odd = taken[0] == 1
    for at in range(count):
        cols = slice(at * lanes, (at + 1) * lanes)
        mine = own[at][...]
        near = across[at][...]
        far = beyond[at][...]
        result[0, :, cols] = jnp.where(taken[1] == 1, near, jnp.where(taken[2] == 1, far, mine))
        mine = mine.astype(f32)
        near = near.astype(f32) - mine
        far = far.astype(f32) - mine
        near = jnp.mean(near * near, axis=0, keepdims=True)
        far = jnp.mean(far * far, axis=0, keepdims=True)
        gaps[0, 0:1, cols] = jnp.where(odd, near, far)
        gaps[0, 1:2, cols] = jnp.where(odd, far, near)


def finish(start, chunks, block, flags, own, across, beyond, so_far):
    count = len(own)
    width = own[0].shape[0]
    anywhere = pl.BlockSpec(memory_space=pl.ANY)
    given = list(so_far) if so_far is not None else []
    extra = len(given)
    step = start // count

    def kernel(*refs):
        data = refs[: 1 + 3 * count]
        finish_kernel(count, start, *data, refs[-2], refs[-1])

    return pl.pallas_call(
        kernel,
        grid=(1,),
        out_shape=(shape((1, width, block)), shape((1, 2, block), f32)),
        in_specs=[smem]
        + [whole(piece) for piece in (*own, *across, *beyond)]
        + [anywhere] * extra,
        out_specs=(
            pl.BlockSpec((1, width, count * lanes), lambda *_: (0, 0, step)),
            pl.BlockSpec((1, 2, count * lanes), lambda *_: (0, 0, step)),
        ),
        input_output_aliases={1 + 3 * count + i: i for i in range(extra)},
        compiler_params=limit,
        cost_estimate=cost(0, 8 * width * lanes * count),
    )(flags, *own, *across, *beyond, *given)


def body(
    residual_flow,
    rooted_input_matrix,
    chain_normal_draws,
    output_matrix,
    chain_heat,
    matched_chain,
    swap_mask,
):
    replicas = lax.axis_size("rep")
    rank = lax.axis_index("rep")
    place = rank % 4
    params = rooted_input_matrix[0]
    block = params.shape[1]
    count = residual_flow.shape[0]

    def to_core(value):
        return lax.ppermute(value, "dp", [(i, i ^ 1) for i in range(4)])

    def to_chip(value):
        return lax.ppermute(value, "dp", [(i, i ^ 2) for i in range(4)])

    def to_mate(value):
        return lax.ppermute(value, "rep", [(i, i ^ 1) for i in range(replicas)])

    def to_pair(value):
        return lax.ppermute(value, "rep", [(i, i ^ 2) for i in range(replicas)])

    def to_next(value):
        pairs = [(i, (i + (2 if i % 2 == 0 else -2)) % replicas) for i in range(replicas)]
        return lax.ppermute(value, "rep", pairs)

    def spread(value):
        rows = value.shape[0] // 4
        own = to_chip(lax.dynamic_slice_in_dim(value, place * rows, rows, 0))
        across = to_mate(own)
        behind = to_pair(own)
        upper = to_mate(behind[: rows // 2])
        lower = to_pair(across[rows // 2 :])
        return assemble(place.astype(jnp.int32)[None], (own, across, behind, upper, lower))

    mate_in = to_core(params)
    mate_out = to_core(output_matrix)
    far_tokens = spread(residual_flow)
    far_out = spread(output_matrix)
    far_out_mate = to_core(far_out)

    normed_a, slope_a, *sent_a = forward(residual_flow, params, mate_in, output_matrix, mate_out)
    first_sum = to_chip(sent_a[0])
    second_sum = to_chip(sent_a[1])
    normed_b, slope_b, *part_b = forward(far_tokens, params, mate_in, output_matrix, mate_out)

    first_errors, first_grads = errors_of(
        False, far_tokens, part_b[0], first_sum, far_out, far_out_mate
    )
    first_grads = to_chip(first_grads)
    second_errors, second_grads = errors_of(
        True, far_tokens, part_b[1], second_sum, far_out, far_out_mate
    )
    second_grads = to_chip(second_grads)
    arrived = [(first_grads, second_grads)]
    chunks = block // lanes
    for chunk in range(1, chunks):
        arrived.append((to_chip(away(chunk, first_errors, second_errors, far_out, far_out_mate)),))
    near = home(first_errors, second_errors, output_matrix, mate_out, slope_b)

    heat = jnp.sqrt(2.0 * drift_stride * chain_heat)
    taken = swap_mask[0] == 1
    across_rank = rank ^ 1
    odd = rank % 2
    beyond_rank = jnp.where(odd == 1, rank + 1, rank - 1)
    flags = jnp.stack(
        [odd, taken & (matched_chain[0] == across_rank), taken & (matched_chain[0] == beyond_rank)]
    ).astype(jnp.int32)

    own, across, beyond = [], [], []
    for chunk in range(chunks):
        keep, send = gradient(chunk, arrived[chunk], slope_a, near, normed_a, normed_b)
        fresh = update(chunk, heat, keep, to_core(send), rooted_input_matrix, chain_normal_draws)
        own.append(fresh)
        across.append(to_mate(fresh))
        beyond.append(to_next(across[-1]))
    done = None
    for start, stop in ((0, 2), (2, 3), (3, 4)):
        done = finish(
            start, chunks, block, flags, own[start:stop], across[start:stop], beyond[start:stop], done
        )
    return done


def solution(mesh):
    placed = (
        P("dp", None),
        P("rep", None, "dp"),
        P("rep", None, "dp"),
        P("dp", None),
        P("rep"),
        P("rep"),
        P("rep"),
    )
    return jax.shard_map(
        body,
        mesh=mesh,
        in_specs=placed,
        out_specs=(P("rep", None, "dp"), P("rep", None, "dp")),
        check_vma=False,
    )
```

time: 202 us -> 121 us (0.60)
  waiting for transfers between devices: 154 us -> 48.1 us
  starting transfers between devices: 4.89 us -> 36.1 us
  Pallas kernels: 0 us -> 29.4 us
  matrix products: 20.4 us -> 0 us
  between operations: 15.9 us -> 2.94 us
  other arithmetic: 6.44 us -> 0.08 us
  local copies, waits for them, and re-layouts: 0.01 us -> 4.41 us
    all_gather x2 -> x0, waiting for transfers between devices: 66.5 us -> none  [the longest x1 36.2 us: body(): lax.all_gather(params, 'dp', axis=1, tiled=True)]
    reduce_scatter x1 -> x0, waiting for transfers between devices: 43.8 us -> none  [body(): lax.psum_scatter(partial_value.astype(jnp.bfloat16), 'dp', scatter_dimens...]
    ppermute x2 -> x32, starting transfers between devices: 4.78 us -> 36.1 us  [the longest x9 12.7 us: to_chip(): return lax.ppermute(value, 'dp', [(i, i ^ 2) for i in range(4)])]
    pallas_call x0 -> x21, Pallas kernels: none -> 29.4 us  [the longest x2 13.8 us: forward(): pl.pallas_call(forward_kernel, grid=(2 * per,), out_shape=(shape((width,...]
    dot_general x3 -> x0, matrix products: 20.4 us -> none  [the longest x1 9.25 us: body(): lax.dot_general(normed, preact_grad, (((0,), (0,)), ((), ())), preferred_...]
    ppermute x2 -> x32, waiting for transfers between devices: 42.5 us -> 48.1 us  [the longest x8 19.1 us: to_mate(): return lax.ppermute(value, 'rep', [(i, i ^ 1) for i in range(replicas)])]
    convert_element_type x2 -> x0, other arithmetic: 3.1 us -> none  [the longest x1 1.81 us: body(): refreshed_input_matrix = moved.astype(jnp.bfloat16)]
    unnamed x6 -> x10, local copies, waits for them, and re-layouts: 0.01 us -> 2.37 us
  transfers between devices with their start and end apart: 5 -> 32, of which waited for: 5 -> 15; matrix products, arithmetic and copies ran while one was open for 4% -> 1% of each run, Pallas kernels for 0% -> 22%
where the time goes in v1:
time: 121 us
  waiting for transfers between devices  48.1 us (40%)
  starting transfers between devices  36.1 us (30%)
  Pallas kernels  29.4 us (24%)
  local copies, waits for them, and re-layouts  4.41 us (4%)
  between operations  2.94 us (2%)
    ppermute x8, waiting for transfers between devices, to_mate(): return lax.ppermute(value, 'rep', [(i, i ^ 1) for i in range(replicas)])  19.1 us
    ppermute x9, waiting for transfers between devices, to_chip(): return lax.ppermute(value, 'dp', [(i, i ^ 2) for i in range(4)])  18.6 us
    pallas_call x2, Pallas kernels, forward(): pl.pallas_call(forward_kernel, grid=(2 * per,), out_shape=(shape((width,...  13.8 us
    ppermute x9, starting transfers between devices, to_chip(): return lax.ppermute(value, 'dp', [(i, i ^ 2) for i in range(4)])  12.7 us
    ppermute x8, starting transfers between devices, to_mate(): return lax.ppermute(value, 'rep', [(i, i ^ 1) for i in range(replicas)])  10.5 us
    ppermute x4, waiting for transfers between devices, to_pair(): return lax.ppermute(value, 'rep', [(i, i ^ 2) for i in range(replicas)])  7.26 us
    ppermute x4, starting transfers between devices, to_next(): return lax.ppermute(value, 'rep', pairs)  6.65 us
    pallas_call x3, Pallas kernels, finish(): pl.pallas_call(kernel, grid=(1,), out_shape=(shape((1, width, block)), sh...  4.57 us
  transfers between devices with their start and end apart: 32, of which 15 were waited for; matrix products, arithmetic and copies ran while one was open for 1% of the time, Pallas kernels for 22%

profile of v1, /device:TPU:0, one launch (start us, length us, event | category | flops | bytes accessed | tf_op | source)
XLA Modules:
  0.0 121.1 jit_solution(5745866112113276728)
XLA Ops:
  1.6 3.0 %collective-permute-start.8 = (bf16[128,1024]{1,0:T(8,128)(2,1)S(1)}, bf16[128,1024]{1,0:T(8,128)(2,1)S(1)}, u32[]{:S(2)}, u32[]{:S(2)}) collective-permute-start(bf16[128,1024]{1,0:T(8,128)(2,1)S(1)} %constant_dynamic-slice_fusion), channel_id=1, source_target_pairs={{0,2},{1,3},{2,0},{3,1},{4,6},{5,7},{6,4},{7,5},{8,10},{9,11},{10,... | collective-permute-start | bytes 786440 | tf_op jit(solution)/shard_map/ppermute | solution.py:356
  5.2 5.8 %collective-permute-done.8.own = bf16[128,1024]{1,0:T(8,128)(2,1)S(1)} collective-permute-done((bf16[128,1024]{1,0:T(8,128)(2,1)S(1)}, bf16[128,1024]{1,0:T(8,128)(2,1)S(1)}, u32[]{:S(2)}, u32[]{:S(2)}) %collective-permute-start.8) | collective-permute-done | bytes 262176 | tf_op jit(solution)/shard_map/ppermute | solution.py:356
  11.0 1.8 %collective-permute-start.10 = (bf16[128,1024]{1,0:T(8,128)(2,1)S(1)}, bf16[128,1024]{1,0:T(8,128)(2,1)S(1)}, u32[]{:S(2)}, u32[]{:S(2)}) collective-permute-start(bf16[128,1024]{1,0:T(8,128)(2,1)S(1)} %collective-permute-done.8.own), channel_id=1, source_target_pairs={{0,8},{4,12},{8,0},{12,4},{16,24},{20,28},{24,16},{28,20},{1,9},{5... | collective-permute-start | bytes 786440 | tf_op jit(solution)/shard_map/ppermute | solution.py:362
  14.2 4.2 %collective-permute-done.10.behind = bf16[128,1024]{1,0:T(8,128)(2,1)S(1)} collective-permute-done((bf16[128,1024]{1,0:T(8,128)(2,1)S(1)}, bf16[128,1024]{1,0:T(8,128)(2,1)S(1)}, u32[]{:S(2)}, u32[]{:S(2)}) %collective-permute-start.10) | collective-permute-done | bytes 262176 | tf_op jit(solution)/shard_map/ppermute | solution.py:362
  19.9 1.6 %collective-permute-start.12 = (bf16[64,1024]{1,0:T(8,128)(2,1)S(1)}, bf16[64,1024]{1,0:T(8,128)(2,1)S(1)}, u32[]{:S(2)}, u32[]{:S(2)}) collective-permute-start(bf16[64,1024]{1,0:T(8,128)(2,1)S(1)} %slice.19), channel_id=1, source_target_pairs={{0,8},{4,12},{8,0},{12,4},{16,24},{20,28},{24,16},{28,20},{1,9},{5... | collective-permute-start | bytes 393224 | tf_op jit(solution)/shard_map/ppermute | solution.py:362
  21.6 1.9 %collective-permute-done.11.upper = bf16[64,1024]{1,0:T(8,128)(2,1)S(1)} collective-permute-done((bf16[64,1024]{1,0:T(8,128)(2,1)S(1)}, bf16[64,1024]{1,0:T(8,128)(2,1)S(1)}, u32[]{:S(2)}, u32[]{:S(2)}) %collective-permute-start.11) | collective-permute-done | bytes 131104 | tf_op jit(solution)/shard_map/ppermute | solution.py:359
  26.2 1.9 %collective-permute-start = (bf16[96,1024]{1,0:T(8,128)(2,1)S(1)}, bf16[96,1024]{1,0:T(8,128)(2,1)S(1)}, u32[]{:S(2)}, u32[]{:S(2)}) collective-permute-start(bf16[96,1024]{1,0:T(8,128)(2,1)S(1)} %constant_dynamic-slice_fusion.1), channel_id=1, source_target_pairs={{0,2},{1,3},{2,0},{3,1},{4,6},{5,7},{6,4},{7,5},{8,10},{9,11},{10,... | collective-permute-start | bytes 589832 | tf_op jit(solution)/shard_map/ppermute | solution.py:356
  28.1 5.4 %collective-permute-done.own = bf16[96,1024]{1,0:T(8,128)(2,1)S(1)} collective-permute-done((bf16[96,1024]{1,0:T(8,128)(2,1)S(1)}, bf16[96,1024]{1,0:T(8,128)(2,1)S(1)}, u32[]{:S(2)}, u32[]{:S(2)}) %collective-permute-start) | collective-permute-done | bytes 196640 | tf_op jit(solution)/shard_map/ppermute | solution.py:356
  33.5 1.7 %collective-permute-start.1 = (bf16[96,1024]{1,0:T(8,128)(2,1)S(1)}, bf16[96,1024]{1,0:T(8,128)(2,1)S(1)}, u32[]{:S(2)}, u32[]{:S(2)}) collective-permute-start(bf16[96,1024]{1,0:T(8,128)(2,1)S(1)} %collective-permute-done.own), channel_id=1, source_target_pairs={{0,4},{4,0},{8,12},{12,8},{16,20},{20,16},{24,28},{28,24},{1,5},{5... | collective-permute-start | bytes 589832 | tf_op jit(solution)/shard_map/ppermute | solution.py:359
  37.9 6.9 %shard_map.88 = (bf16[1024,384]{1,0:T(8,128)(2,1)S(1)}, bf16[2,384,512]{2,1,0:T(8,128)(2,1)S(1)}, bf16[192,1024]{1,0:T(8,128)(2,1)S(1)}, bf16[192,1024]{1,0:T(8,128)(2,1)S(1)}) custom-call(bf16[384,1024]{1,0:T(8,128)(2,1)S(1)} %copy-done.4, bf16[1024,512]{1,0:T(8,128)(2,1)S(1)} %bitcast.10, bf16[1024,512]{1,0:T(8,128)(2,1)} %collective-permute-done.5.mate_in, ...), custom_call_target="tpu_custom_call" | custom-call | flops 1610612736 | bytes 4194304 | tf_op jit(solution)/shard_map/pallas_call | solution.py:115
  44.8 1.6 %collective-permute-start.7 = (bf16[192,1024]{1,0:T(8,128)(2,1)S(1)}, bf16[192,1024]{1,0:T(8,128)(2,1)S(1)}, u32[]{:S(2)}, u32[]{:S(2)}) collective-permute-start(bf16[192,1024]{1,0:T(8,128)(2,1)S(1)} %get-tuple-element.27), channel_id=1, source_target_pairs={{0,2},{1,3},{2,0},{3,1},{4,6},{5,7},{6,4},{7,5},{8,10},{9,11},{10,... | collective-permute-start | bytes 1179656 | tf_op jit(solution)/shard_map/ppermute | solution.py:356
  46.9 1.6 %collective-permute-start.3 = (bf16[48,1024]{1,0:T(8,128)(2,1)S(1)}, bf16[48,1024]{1,0:T(8,128)(2,1)S(1)}, u32[]{:S(2)}, u32[]{:S(2)}) collective-permute-start(bf16[48,1024]{1,0:T(8,128)(2,1)S(1)} %slice.16), channel_id=1, source_target_pairs={{0,4},{4,0},{8,12},{12,8},{16,20},{20,16},{24,28},{28,24},{1,5},{5... | collective-permute-start | bytes 294920 | tf_op jit(solution)/shard_map/ppermute | solution.py:359
  49.0 2.6 %collective-permute-done.3.upper = bf16[48,1024]{1,0:T(8,128)(2,1)S(1)} collective-permute-done((bf16[48,1024]{1,0:T(8,128)(2,1)S(1)}, bf16[48,1024]{1,0:T(8,128)(2,1)S(1)}, u32[]{:S(2)}, u32[]{:S(2)}) %collective-permute-start.3) | collective-permute-done | bytes 98336 | tf_op jit(solution)/shard_map/ppermute | solution.py:359
  51.6 1.6 %collective-permute-done.4.lower = bf16[48,1024]{1,0:T(8,128)(2,1)S(1)} collective-permute-done((bf16[48,1024]{1,0:T(8,128)(2,1)S(1)}, bf16[48,1024]{1,0:T(8,128)(2,1)S(1)}, u32[]{:S(2)}, u32[]{:S(2)}) %collective-permute-start.4) | collective-permute-done | bytes 98336 | tf_op jit(solution)/shard_map/ppermute | solution.py:362
  53.4 6.9 %shard_map.87 = (bf16[1024,384]{1,0:T(8,128)(2,1)S(1)}, bf16[2,384,512]{2,1,0:T(8,128)(2,1)S(1)}, bf16[192,1024]{1,0:T(8,128)(2,1)S(1)}, bf16[192,1024]{1,0:T(8,128)(2,1)S(1)}) custom-call(bf16[384,1024]{1,0:T(8,128)(2,1)S(1)} %shard_map.86.tokens, bf16[1024,512]{1,0:T(8,128)(2,1)S(1)} %bitcast.11, bf16[1024,512]{1,0:T(8,128)(2,1)} %collective-permute-done.5.mate_in, ...), custom_call_target="tpu_custom_call" | custom-call | flops 1610612736 | bytes 4194304 | tf_op jit(solution)/shard_map/pallas_call | solution.py:115
  60.8 2.5 %collective-permute-done.14.sent_part = bf16[192,1024]{1,0:T(8,128)(2,1)S(1)} collective-permute-done((bf16[192,1024]{1,0:T(8,128)(2,1)S(1)}, bf16[192,1024]{1,0:T(8,128)(2,1)S(1)}, u32[]{:S(2)}, u32[]{:S(2)}) %collective-permute-start.14) | collective-permute-done | bytes 393248 | tf_op jit(solution)/shard_map/ppermute | solution.py:356
  64.3 1.6 %collective-permute-start.19 = (bf16[384,256]{1,0:T(8,128)(2,1)S(1)}, bf16[384,256]{1,0:T(8,128)(2,1)S(1)}, u32[]{:S(2)}, u32[]{:S(2)}) collective-permute-start(bf16[384,256]{1,0:T(8,128)(2,1)S(1)} %shard_map.96), channel_id=1, source_target_pairs={{0,2},{1,3},{2,0},{3,1},{4,6},{5,7},{6,4},{7,5},{8,10},{9,11},{10,... | collective-permute-start | bytes 589832 | tf_op jit(solution)/shard_map/ppermute | solution.py:356
  69.6 1.6 %collective-permute-start.15 = (bf16[384,256]{1,0:T(8,128)(2,1)S(1)}, bf16[384,256]{1,0:T(8,128)(2,1)S(1)}, u32[]{:S(2)}, u32[]{:S(2)}) collective-permute-start(bf16[384,256]{1,0:T(8,128)(2,1)S(1)} %shard_map.92), channel_id=1, source_target_pairs={{0,2},{1,3},{2,0},{3,1},{4,6},{5,7},{6,4},{7,5},{8,10},{9,11},{10,... | collective-permute-start | bytes 589832 | tf_op jit(solution)/shard_map/ppermute | solution.py:356
  71.2 3.7 %shard_map.93.refs_2_.refs_3_ = bf16[4,384,256]{2,1,0:T(8,128)(2,1)S(1)} custom-call(bf16[192,1024]{1,0:T(8,128)(2,1)S(1)} %get-tuple-element.28.first, bf16[192,1024]{1,0:T(8,128)(2,1)S(1)} %get-tuple-element.31.second, bf16[512,1024]{1,0:T(8,128)(2,1)S(1)} %copy-done.3, bf16[512,1024]{1,0:T(8,128)(2,1)} %collective-permute-done.6.mate_out.weight_mate, ...), custom_call_target="tpu_custom_call" | custom-call | flops 805306368 | bytes 1966080 | tf_op jit(solution)/shard_map/pallas_call | solution.py:209
  74.9 3.6 %collective-permute-done.23.refs_0_ = bf16[192,256]{1,0:T(8,128)(2,1)S(1)} collective-permute-done((bf16[192,256]{1,0:T(8,128)(2,1)S(1)}, bf16[192,256]{1,0:T(8,128)(2,1)S(1)}, u32[]{:S(2)}, u32[]{:S(2)}) %collective-permute-start.23) | collective-permute-done | bytes 98336 | tf_op jit(solution)/shard_map/ppermute | solution.py:356
  85.1 1.6 %collective-permute-start.28 = (bf16[1024,128]{1,0:T(8,128)(2,1)S(1)}, bf16[1024,128]{1,0:T(8,128)(2,1)S(1)}, u32[]{:S(2)}, u32[]{:S(2)}) collective-permute-start(bf16[1024,128]{1,0:T(8,128)(2,1)S(1)} %shard_map.100.refs_1_), channel_id=1, source_target_pairs={{0,4},{4,0},{8,12},{12,8},{16,20},{20,16},{24,28},{28,24},{1,5},{5... | collective-permute-start | bytes 786440 | tf_op jit(solution)/shard_map/ppermute | solution.py:359
  88.1 1.6 %collective-permute-start.21 = (bf16[1024,128]{1,0:T(8,128)(2,1)S(1)}, bf16[1024,128]{1,0:T(8,128)(2,1)S(1)}, u32[]{:S(2)}, u32[]{:S(2)}) collective-permute-start(bf16[1024,128]{1,0:T(8,128)(2,1)S(1)} %shard_map.98.refs_1_), channel_id=1, source_target_pairs={{0,4},{4,0},{8,12},{12,8},{16,20},{20,16},{24,28},{28,24},{1,5},{5... | collective-permute-start | bytes 786440 | tf_op jit(solution)/shard_map/ppermute | solution.py:359
  90.7 3.7 %collective-permute-done.28.refs_3_ = bf16[1024,128]{1,0:T(8,128)(2,1)S(1)} collective-permute-done((bf16[1024,128]{1,0:T(8,128)(2,1)S(1)}, bf16[1024,128]{1,0:T(8,128)(2,1)S(1)}, u32[]{:S(2)}, u32[]{:S(2)}) %collective-permute-start.28) | collective-permute-done | bytes 262176 | tf_op jit(solution)/shard_map/ppermute | solution.py:359
  94.4 1.7 %collective-permute-start.30 = (bf16[1024,128]{1,0:T(8,128)(2,1)S(1)}, bf16[1024,128]{1,0:T(8,128)(2,1)S(1)}, u32[]{:S(2)}, u32[]{:S(2)}) collective-permute-start(bf16[1024,128]{1,0:T(8,128)(2,1)S(1)} %collective-permute-done.28.refs_3_), channel_id=1, source_target_pairs={{0,8},{4,28},{8,16},{12,4},{16,24},{20,12},{24,0},{28,20},{1,9},{5... | collective-permute-start | bytes 786440 | tf_op jit(solution)/shard_map/ppermute | solution.py:366
  96.0 4.0 %collective-permute-done.29.refs_4_ = bf16[1024,128]{1,0:T(8,128)(2,1)S(1)} collective-permute-done((bf16[1024,128]{1,0:T(8,128)(2,1)S(1)}, bf16[1024,128]{1,0:T(8,128)(2,1)S(1)}, u32[]{:S(2)}, u32[]{:S(2)}) %collective-permute-start.29) | collective-permute-done | bytes 262176 | tf_op jit(solution)/shard_map/ppermute | solution.py:359
  100.0 1.7 %collective-permute-start.31 = (bf16[1024,128]{1,0:T(8,128)(2,1)S(1)}, bf16[1024,128]{1,0:T(8,128)(2,1)S(1)}, u32[]{:S(2)}, u32[]{:S(2)}) collective-permute-start(bf16[1024,128]{1,0:T(8,128)(2,1)S(1)} %collective-permute-done.29.refs_4_), channel_id=1, source_target_pairs={{0,8},{4,28},{8,16},{12,4},{16,24},{20,12},{24,0},{28,20},{1,9},{5... | collective-permute-start | bytes 786440 | tf_op jit(solution)/shard_map/ppermute | solution.py:366
  101.7 4.0 %collective-permute-done.21.refs_2_ = bf16[1024,128]{1,0:T(8,128)(2,1)S(1)} collective-permute-done((bf16[1024,128]{1,0:T(8,128)(2,1)S(1)}, bf16[1024,128]{1,0:T(8,128)(2,1)S(1)}, u32[]{:S(2)}, u32[]{:S(2)}) %collective-permute-start.21) | collective-permute-done | bytes 262176 | tf_op jit(solution)/shard_map/ppermute | solution.py:359
  105.6 1.7 %collective-permute-start.22 = (bf16[1024,128]{1,0:T(8,128)(2,1)S(1)}, bf16[1024,128]{1,0:T(8,128)(2,1)S(1)}, u32[]{:S(2)}, u32[]{:S(2)}) collective-permute-start(bf16[1024,128]{1,0:T(8,128)(2,1)S(1)} %collective-permute-done.21.refs_2_), channel_id=1, source_target_pairs={{0,8},{4,28},{8,16},{12,4},{16,24},{20,12},{24,0},{28,20},{1,9},{5... | collective-permute-start | bytes 786440 | tf_op jit(solution)/shard_map/ppermute | solution.py:366
  107.3 3.0 %collective-permute-done.17.refs_2_ = bf16[1024,128]{1,0:T(8,128)(2,1)S(1)} collective-permute-done((bf16[1024,128]{1,0:T(8,128)(2,1)S(1)}, bf16[1024,128]{1,0:T(8,128)(2,1)S(1)}, u32[]{:S(2)}, u32[]{:S(2)}) %collective-permute-start.17) | collective-permute-done | bytes 262176 | tf_op jit(solution)/shard_map/ppermute | solution.py:359
  110.3 1.7 %collective-permute-start.18 = (bf16[1024,128]{1,0:T(8,128)(2,1)S(1)}, bf16[1024,128]{1,0:T(8,128)(2,1)S(1)}, u32[]{:S(2)}, u32[]{:S(2)}) collective-permute-start(bf16[1024,128]{1,0:T(8,128)(2,1)S(1)} %collective-permute-done.17.refs_2_), channel_id=1, source_target_pairs={{0,8},{4,28},{8,16},{12,4},{16,24},{20,12},{24,0},{28,20},{1,9},{5... | collective-permute-start | bytes 786440 | tf_op jit(solution)/shard_map/ppermute | solution.py:366
  113.4 1.7 %shard_map.104 = (bf16[1,1024,512]{2,1,0:T(8,128)(2,1)}, f32[1,2,512]{2,1,0:T(2,128)}) custom-call(s32[3]{0:T(128)S(1)} %pad_add_fusion.refs_0_, bf16[1024,128]{1,0:T(8,128)(2,1)S(1)} %shard_map.100.refs_1_, bf16[1024,128]{1,0:T(8,128)(2,1)S(1)} %shard_map.103.refs_2_, bf16[1024,128]{1,0:T(8,128)(2,1)S(1)} %collective-permute-done.28.refs_3_, ...), custom_call_target="tpu_custom_call" | custom-call | bytes 2097152 | tf_op jit(solution)/shard_map/pallas_call | solution.py:319
  116.5 3.1 %collective-permute-done.18.refs_3_ = bf16[1024,128]{1,0:T(8,128)(2,1)S(1)} collective-permute-done((bf16[1024,128]{1,0:T(8,128)(2,1)S(1)}, bf16[1024,128]{1,0:T(8,128)(2,1)S(1)}, u32[]{:S(2)}, u32[]{:S(2)}) %collective-permute-start.18) | collective-permute-done | bytes 262176 | tf_op jit(solution)/shard_map/ppermute | solution.py:366
  (70 shorter events, 27.5 us)
Async XLA Ops:
  1.6 9.3 %collective-permute-start.8 = (bf16[128,1024]{1,0:T(8,128)(2,1)S(1)}, bf16[128,1024]{1,0:T(8,128)(2,1)S(1)}, u32[]{:S(2)}, u32[]{:S(2)}) collective-permute-start(bf16[128,1024]{1,0:T(8,128)(2,1)S(1)} %constant_dynamic-slice_fusion), channel_id=1, source_target_pairs={{0,2},{1,3},{2,0},{3,1},{4,6},{5,7},{6,4},{7,5},{8,10},{9,11},{10,... | collective-permute-start | bytes 786440 | tf_op jit(solution)/shard_map/ppermute | solution.py:356
  4.7 30.9 %collective-permute-start.5 = (bf16[1024,512]{1,0:T(8,128)(2,1)}, bf16[1024,512]{1,0:T(8,128)(2,1)}, u32[]{:S(2)}, u32[]{:S(2)}) collective-permute-start(bf16[1024,512]{1,0:T(8,128)(2,1)} %bitcast.9), channel_id=1, source_target_pairs={{0,1},{1,0},{2,3},{3,2},{4,5},{5,4},{6,7},{7,6},{8,9},{9,8},{10,11... | collective-permute-start | bytes 3145736 | tf_op jit(solution)/shard_map/ppermute | solution.py:353
  4.7 30.9 %collective-permute-start.6 = (bf16[512,1024]{1,0:T(8,128)(2,1)}, bf16[512,1024]{1,0:T(8,128)(2,1)}, u32[]{:S(2)}, u32[]{:S(2)}) collective-permute-start(bf16[512,1024]{1,0:T(8,128)(2,1)} %weight.1), channel_id=1, source_target_pairs={{0,1},{1,0},{2,3},{3,2},{4,5},{5,4},{6,7},{7,6},{8,9},{9,8},{10,11... | collective-permute-start | bytes 3145736 | tf_op jit(solution)/shard_map/ppermute | solution.py:353
  11.0 7.5 %collective-permute-start.10 = (bf16[128,1024]{1,0:T(8,128)(2,1)S(1)}, bf16[128,1024]{1,0:T(8,128)(2,1)S(1)}, u32[]{:S(2)}, u32[]{:S(2)}) collective-permute-start(bf16[128,1024]{1,0:T(8,128)(2,1)S(1)} %collective-permute-done.8.own), channel_id=1, source_target_pairs={{0,8},{4,12},{8,0},{12,4},{16,24},{20,28},{24,16},{28,20},{1,9},{5... | collective-permute-start | bytes 786440 | tf_op jit(solution)/shard_map/ppermute | solution.py:362
  12.8 7.2 %collective-permute-start.9 = (bf16[128,1024]{1,0:T(8,128)(2,1)S(1)}, bf16[128,1024]{1,0:T(8,128)(2,1)S(1)}, u32[]{:S(2)}, u32[]{:S(2)}) collective-permute-start(bf16[128,1024]{1,0:T(8,128)(2,1)S(1)} %collective-permute-done.8.own), channel_id=1, source_target_pairs={{0,4},{4,0},{8,12},{12,8},{16,20},{20,16},{24,28},{28,24},{1,5},{5... | collective-permute-start | bytes 786440 | tf_op jit(solution)/shard_map/ppermute | solution.py:359
  18.5 5.0 %collective-permute-start.11 = (bf16[64,1024]{1,0:T(8,128)(2,1)S(1)}, bf16[64,1024]{1,0:T(8,128)(2,1)S(1)}, u32[]{:S(2)}, u32[]{:S(2)}) collective-permute-start(bf16[64,1024]{1,0:T(8,128)(2,1)S(1)} %slice.18), channel_id=1, source_target_pairs={{0,4},{4,0},{8,12},{12,8},{16,20},{20,16},{24,28},{28,24},{1,5},{5... | collective-permute-start | bytes 393224 | tf_op jit(solution)/shard_map/ppermute | solution.py:359
  19.9 5.0 %collective-permute-start.12 = (bf16[64,1024]{1,0:T(8,128)(2,1)S(1)}, bf16[64,1024]{1,0:T(8,128)(2,1)S(1)}, u32[]{:S(2)}, u32[]{:S(2)}) collective-permute-start(bf16[64,1024]{1,0:T(8,128)(2,1)S(1)} %slice.19), channel_id=1, source_target_pairs={{0,8},{4,12},{8,0},{12,4},{16,24},{20,28},{24,16},{28,20},{1,9},{5... | collective-permute-start | bytes 393224 | tf_op jit(solution)/shard_map/ppermute | solution.py:362
  25.1 35.3 %collective-permute-start.13 = (bf16[512,1024]{1,0:T(8,128)(2,1)S(1)}, bf16[512,1024]{1,0:T(8,128)(2,1)S(1)}, u32[]{:S(2)}, u32[]{:S(2)}) collective-permute-start(bf16[512,1024]{1,0:T(8,128)(2,1)S(1)} %shard_map.89.weight), channel_id=1, source_target_pairs={{0,1},{1,0},{2,3},{3,2},{4,5},{5,4},{6,7},{7,6},{8,9},{9,8},{10,11... | collective-permute-start | bytes 3145736 | tf_op jit(solution)/shard_map/ppermute | solution.py:353
  26.2 7.3 %collective-permute-start = (bf16[96,1024]{1,0:T(8,128)(2,1)S(1)}, bf16[96,1024]{1,0:T(8,128)(2,1)S(1)}, u32[]{:S(2)}, u32[]{:S(2)}) collective-permute-start(bf16[96,1024]{1,0:T(8,128)(2,1)S(1)} %constant_dynamic-slice_fusion.1), channel_id=1, source_target_pairs={{0,2},{1,3},{2,0},{3,1},{4,6},{5,7},{6,4},{7,5},{8,10},{9,11},{10,... | collective-permute-start | bytes 589832 | tf_op jit(solution)/shard_map/ppermute | solution.py:356
  33.5 15.0 %collective-permute-start.1 = (bf16[96,1024]{1,0:T(8,128)(2,1)S(1)}, bf16[96,1024]{1,0:T(8,128)(2,1)S(1)}, u32[]{:S(2)}, u32[]{:S(2)}) collective-permute-start(bf16[96,1024]{1,0:T(8,128)(2,1)S(1)} %collective-permute-done.own), channel_id=1, source_target_pairs={{0,4},{4,0},{8,12},{12,8},{16,20},{20,16},{24,28},{28,24},{1,5},{5... | collective-permute-start | bytes 589832 | tf_op jit(solution)/shard_map/ppermute | solution.py:359
  35.2 11.7 %collective-permute-start.2 = (bf16[96,1024]{1,0:T(8,128)(2,1)S(1)}, bf16[96,1024]{1,0:T(8,128)(2,1)S(1)}, u32[]{:S(2)}, u32[]{:S(2)}) collective-permute-start(bf16[96,1024]{1,0:T(8,128)(2,1)S(1)} %collective-permute-done.own), channel_id=1, source_target_pairs={{0,8},{4,12},{8,0},{12,4},{16,24},{20,28},{24,16},{28,20},{1,9},{5... | collective-permute-start | bytes 589832 | tf_op jit(solution)/shard_map/ppermute | solution.py:362
  44.8 15.5 %collective-permute-start.7 = (bf16[192,1024]{1,0:T(8,128)(2,1)S(1)}, bf16[192,1024]{1,0:T(8,128)(2,1)S(1)}, u32[]{:S(2)}, u32[]{:S(2)}) collective-permute-start(bf16[192,1024]{1,0:T(8,128)(2,1)S(1)} %get-tuple-element.27), channel_id=1, source_target_pairs={{0,2},{1,3},{2,0},{3,1},{4,6},{5,7},{6,4},{7,5},{8,10},{9,11},{10,... | collective-permute-start | bytes 1179656 | tf_op jit(solution)/shard_map/ppermute | solution.py:356
  46.4 16.9 %collective-permute-start.14 = (bf16[192,1024]{1,0:T(8,128)(2,1)S(1)}, bf16[192,1024]{1,0:T(8,128)(2,1)S(1)}, u32[]{:S(2)}, u32[]{:S(2)}) collective-permute-start(bf16[192,1024]{1,0:T(8,128)(2,1)S(1)} %get-tuple-element.30), channel_id=1, source_target_pairs={{0,2},{1,3},{2,0},{3,1},{4,6},{5,7},{6,4},{7,5},{8,10},{9,11},{10,... | collective-permute-start | bytes 1179656 | tf_op jit(solution)/shard_map/ppermute | solution.py:356
  46.9 4.7 %collective-permute-start.3 = (bf16[48,1024]{1,0:T(8,128)(2,1)S(1)}, bf16[48,1024]{1,0:T(8,128)(2,1)S(1)}, u32[]{:S(2)}, u32[]{:S(2)}) collective-permute-start(bf16[48,1024]{1,0:T(8,128)(2,1)S(1)} %slice.16), channel_id=1, source_target_pairs={{0,4},{4,0},{8,12},{12,8},{16,20},{20,16},{24,28},{28,24},{1,5},{5... | collective-permute-start | bytes 294920 | tf_op jit(solution)/shard_map/ppermute | solution.py:359
  48.5 4.7 %collective-permute-start.4 = (bf16[48,1024]{1,0:T(8,128)(2,1)S(1)}, bf16[48,1024]{1,0:T(8,128)(2,1)S(1)}, u32[]{:S(2)}, u32[]{:S(2)}) collective-permute-start(bf16[48,1024]{1,0:T(8,128)(2,1)S(1)} %slice.17), channel_id=1, source_target_pairs={{0,8},{4,12},{8,0},{12,4},{16,24},{20,28},{24,16},{28,20},{1,9},{5... | collective-permute-start | bytes 294920 | tf_op jit(solution)/shard_map/ppermute | solution.py:362
  64.3 16.3 %collective-permute-start.19 = (bf16[384,256]{1,0:T(8,128)(2,1)S(1)}, bf16[384,256]{1,0:T(8,128)(2,1)S(1)}, u32[]{:S(2)}, u32[]{:S(2)}) collective-permute-start(bf16[384,256]{1,0:T(8,128)(2,1)S(1)} %shard_map.96), channel_id=1, source_target_pairs={{0,2},{1,3},{2,0},{3,1},{4,6},{5,7},{6,4},{7,5},{8,10},{9,11},{10,... | collective-permute-start | bytes 589832 | tf_op jit(solution)/shard_map/ppermute | solution.py:356
  66.5 15.4 %collective-permute-start.26 = (bf16[384,256]{1,0:T(8,128)(2,1)S(1)}, bf16[384,256]{1,0:T(8,128)(2,1)S(1)}, u32[]{:S(2)}, u32[]{:S(2)}) collective-permute-start(bf16[384,256]{1,0:T(8,128)(2,1)S(1)} %shard_map.101), channel_id=1, source_target_pairs={{0,2},{1,3},{2,0},{3,1},{4,6},{5,7},{6,4},{7,5},{8,10},{9,11},{10,... | collective-permute-start | bytes 589832 | tf_op jit(solution)/shard_map/ppermute | solution.py:356
  67.0 11.5 %collective-permute-start.23 = (bf16[192,256]{1,0:T(8,128)(2,1)S(1)}, bf16[192,256]{1,0:T(8,128)(2,1)S(1)}, u32[]{:S(2)}, u32[]{:S(2)}) collective-permute-start(bf16[192,256]{1,0:T(8,128)(2,1)S(1)} %get-tuple-element.40), channel_id=1, source_target_pairs={{0,2},{1,3},{2,0},{3,1},{4,6},{5,7},{6,4},{7,5},{8,10},{9,11},{10,... | collective-permute-start | bytes 294920 | tf_op jit(solution)/shard_map/ppermute | solution.py:356
  68.6 11.2 %collective-permute-start.24 = (bf16[192,256]{1,0:T(8,128)(2,1)S(1)}, bf16[192,256]{1,0:T(8,128)(2,1)S(1)}, u32[]{:S(2)}, u32[]{:S(2)}) collective-permute-start(bf16[192,256]{1,0:T(8,128)(2,1)S(1)} %get-tuple-element.41), channel_id=1, source_target_pairs={{0,2},{1,3},{2,0},{3,1},{4,6},{5,7},{6,4},{7,5},{8,10},{9,11},{10,... | collective-permute-start | bytes 294920 | tf_op jit(solution)/shard_map/ppermute | solution.py:356
  69.6 13.1 %collective-permute-start.15 = (bf16[384,256]{1,0:T(8,128)(2,1)S(1)}, bf16[384,256]{1,0:T(8,128)(2,1)S(1)}, u32[]{:S(2)}, u32[]{:S(2)}) collective-permute-start(bf16[384,256]{1,0:T(8,128)(2,1)S(1)} %shard_map.92), channel_id=1, source_target_pairs={{0,2},{1,3},{2,0},{3,1},{4,6},{5,7},{6,4},{7,5},{8,10},{9,11},{10,... | collective-permute-start | bytes 589832 | tf_op jit(solution)/shard_map/ppermute | solution.py:356
  80.5 4.2 %collective-permute-start.25 = (bf16[1024,128]{1,0:T(8,128)(2,1)S(1)}, bf16[1024,128]{1,0:T(8,128)(2,1)S(1)}, u32[]{:S(2)}, u32[]{:S(2)}) collective-permute-start(bf16[1024,128]{1,0:T(8,128)(2,1)S(1)} %get-tuple-element.43), channel_id=1, source_target_pairs={{0,1},{1,0},{2,3},{3,2},{4,5},{5,4},{6,7},{7,6},{8,9},{9,8},{10,11... | collective-permute-start | bytes 786440 | tf_op jit(solution)/shard_map/ppermute | solution.py:353
  81.3 6.4 %collective-permute-start.20 = (bf16[1024,128]{1,0:T(8,128)(2,1)S(1)}, bf16[1024,128]{1,0:T(8,128)(2,1)S(1)}, u32[]{:S(2)}, u32[]{:S(2)}) collective-permute-start(bf16[1024,128]{1,0:T(8,128)(2,1)S(1)} %get-tuple-element.39), channel_id=1, source_target_pairs={{0,1},{1,0},{2,3},{3,2},{4,5},{5,4},{6,7},{7,6},{8,9},{9,8},{10,11... | collective-permute-start | bytes 786440 | tf_op jit(solution)/shard_map/ppermute | solution.py:353
  82.6 4.1 %collective-permute-start.27 = (bf16[1024,128]{1,0:T(8,128)(2,1)S(1)}, bf16[1024,128]{1,0:T(8,128)(2,1)S(1)}, u32[]{:S(2)}, u32[]{:S(2)}) collective-permute-start(bf16[1024,128]{1,0:T(8,128)(2,1)S(1)} %get-tuple-element.45), channel_id=1, source_target_pairs={{0,1},{1,0},{2,3},{3,2},{4,5},{5,4},{6,7},{7,6},{8,9},{9,8},{10,11... | collective-permute-start | bytes 786440 | tf_op jit(solution)/shard_map/ppermute | solution.py:353
  83.5 6.2 %collective-permute-start.16 = (bf16[1024,128]{1,0:T(8,128)(2,1)S(1)}, bf16[1024,128]{1,0:T(8,128)(2,1)S(1)}, u32[]{:S(2)}, u32[]{:S(2)}) collective-permute-start(bf16[1024,128]{1,0:T(8,128)(2,1)S(1)} %get-tuple-element.37), channel_id=1, source_target_pairs={{0,1},{1,0},{2,3},{3,2},{4,5},{5,4},{6,7},{7,6},{8,9},{9,8},{10,11... | collective-permute-start | bytes 786440 | tf_op jit(solution)/shard_map/ppermute | solution.py:353
  85.1 9.2 %collective-permute-start.28 = (bf16[1024,128]{1,0:T(8,128)(2,1)S(1)}, bf16[1024,128]{1,0:T(8,128)(2,1)S(1)}, u32[]{:S(2)}, u32[]{:S(2)}) collective-permute-start(bf16[1024,128]{1,0:T(8,128)(2,1)S(1)} %shard_map.100.refs_1_), channel_id=1, source_target_pairs={{0,4},{4,0},{8,12},{12,8},{16,20},{20,16},{24,28},{28,24},{1,5},{5... | collective-permute-start | bytes 786440 | tf_op jit(solution)/shard_map/ppermute | solution.py:359
  87.1 12.9 %collective-permute-start.29 = (bf16[1024,128]{1,0:T(8,128)(2,1)S(1)}, bf16[1024,128]{1,0:T(8,128)(2,1)S(1)}, u32[]{:S(2)}, u32[]{:S(2)}) collective-permute-start(bf16[1024,128]{1,0:T(8,128)(2,1)S(1)} %shard_map.103.refs_2_), channel_id=1, source_target_pairs={{0,4},{4,0},{8,12},{12,8},{16,20},{20,16},{24,28},{28,24},{1,5},{5... | collective-permute-start | bytes 786440 | tf_op jit(solution)/shard_map/ppermute | solution.py:359
  88.1 17.5 %collective-permute-start.21 = (bf16[1024,128]{1,0:T(8,128)(2,1)S(1)}, bf16[1024,128]{1,0:T(8,128)(2,1)S(1)}, u32[]{:S(2)}, u32[]{:S(2)}) collective-permute-start(bf16[1024,128]{1,0:T(8,128)(2,1)S(1)} %shard_map.98.refs_1_), channel_id=1, source_target_pairs={{0,4},{4,0},{8,12},{12,8},{16,20},{20,16},{24,28},{28,24},{1,5},{5... | collective-permute-start | bytes 786440 | tf_op jit(solution)/shard_map/ppermute | solution.py:359
  90.1 20.2 %collective-permute-start.17 = (bf16[1024,128]{1,0:T(8,128)(2,1)S(1)}, bf16[1024,128]{1,0:T(8,128)(2,1)S(1)}, u32[]{:S(2)}, u32[]{:S(2)}) collective-permute-start(bf16[1024,128]{1,0:T(8,128)(2,1)S(1)} %shard_map.95.refs_1_), channel_id=1, source_target_pairs={{0,4},{4,0},{8,12},{12,8},{16,20},{20,16},{24,28},{28,24},{1,5},{5... | collective-permute-start | bytes 786440 | tf_op jit(solution)/shard_map/ppermute | solution.py:359
  94.4 19.0 %collective-permute-start.30 = (bf16[1024,128]{1,0:T(8,128)(2,1)S(1)}, bf16[1024,128]{1,0:T(8,128)(2,1)S(1)}, u32[]{:S(2)}, u32[]{:S(2)}) collective-permute-start(bf16[1024,128]{1,0:T(8,128)(2,1)S(1)} %collective-permute-done.28.refs_3_), channel_id=1, source_target_pairs={{0,8},{4,28},{8,16},{12,4},{16,24},{20,12},{24,0},{28,20},{1,9},{5... | collective-permute-start | bytes 786440 | tf_op jit(solution)/shard_map/ppermute | solution.py:366
  100.0 13.4 %collective-permute-start.31 = (bf16[1024,128]{1,0:T(8,128)(2,1)S(1)}, bf16[1024,128]{1,0:T(8,128)(2,1)S(1)}, u32[]{:S(2)}, u32[]{:S(2)}) collective-permute-start(bf16[1024,128]{1,0:T(8,128)(2,1)S(1)} %collective-permute-done.29.refs_4_), channel_id=1, source_target_pairs={{0,8},{4,28},{8,16},{12,4},{16,24},{20,12},{24,0},{28,20},{1,9},{5... | collective-permute-start | bytes 786440 | tf_op jit(solution)/shard_map/ppermute | solution.py:366
  105.6 9.5 %collective-permute-start.22 = (bf16[1024,128]{1,0:T(8,128)(2,1)S(1)}, bf16[1024,128]{1,0:T(8,128)(2,1)S(1)}, u32[]{:S(2)}, u32[]{:S(2)}) collective-permute-start(bf16[1024,128]{1,0:T(8,128)(2,1)S(1)} %collective-permute-done.21.refs_2_), channel_id=1, source_target_pairs={{0,8},{4,28},{8,16},{12,4},{16,24},{20,12},{24,0},{28,20},{1,9},{5... | collective-permute-start | bytes 786440 | tf_op jit(solution)/shard_map/ppermute | solution.py:366
  110.3 9.3 %collective-permute-start.18 = (bf16[1024,128]{1,0:T(8,128)(2,1)S(1)}, bf16[1024,128]{1,0:T(8,128)(2,1)S(1)}, u32[]{:S(2)}, u32[]{:S(2)}) collective-permute-start(bf16[1024,128]{1,0:T(8,128)(2,1)S(1)} %collective-permute-done.17.refs_2_), channel_id=1, source_target_pairs={{0,8},{4,28},{8,16},{12,4},{16,24},{20,12},{24,0},{28,20},{1,9},{5... | collective-permute-start | bytes 786440 | tf_op jit(solution)/shard_map/ppermute | solution.py:366
  (5 other events, 23.7 us)

commit v2 on v0

v2 whole, which is shorter than its diff:
```python
import functools
import math

import jax
import jax.numpy as jnp
from jax import lax
from jax.experimental import pallas as pl
from jax.experimental.pallas import tpu as pltpu
from jax.sharding import PartitionSpec as P

drift_stride = 0.5
lanes = 128
f32 = jnp.float32
bf16 = jnp.bfloat16
smem = pl.BlockSpec(memory_space=pltpu.SMEM)


def matmul(left, right):
    return jnp.dot(left, right, preferred_element_type=f32)


def against_rows(left, right):
    return lax.dot_general(left, right, (((1,), (1,)), ((), ())), preferred_element_type=f32)


def limit(mebibytes):
    return pltpu.CompilerParams(vmem_limit_bytes=mebibytes * 1024 * 1024)


def cost(macs, nbytes):
    return pl.CostEstimate(flops=2 * macs, bytes_accessed=nbytes, transcendentals=0)


def whole(array):
    rank = array.ndim
    return pl.BlockSpec(array.shape, lambda *_: (0,) * rank)


def shape(dims, dtype=bf16):
    return jax.ShapeDtypeStruct(dims, dtype)


def after(value, *earlier):
    anywhere = pl.BlockSpec(memory_space=pl.ANY)
    return pl.pallas_call(
        lambda *refs: None,
        out_shape=shape(value.shape, value.dtype),
        in_specs=[anywhere] * (1 + len(earlier)),
        out_specs=anywhere,
        input_output_aliases={0: 0},
        compiler_params=limit(1),
    )(value, *earlier)


def shares_kernel(place, tokens, weight, token_share, weight_share):
    token_share[...] = tokens[...]
    weight_share[...] = weight[...]


def shares(place, tokens, weight):
    sizes = [(value.shape[0] // 4, value.shape[1]) for value in (tokens, weight)]
    return pl.pallas_call(
        shares_kernel,
        out_shape=[shape(size) for size in sizes],
        grid_spec=pltpu.PrefetchScalarGridSpec(
            num_scalar_prefetch=1,
            grid=(1,),
            in_specs=[pl.BlockSpec(size, lambda _, place: (place[0], 0)) for size in sizes],
            out_specs=[pl.BlockSpec(size, lambda *_: (0, 0)) for size in sizes],
        ),
        compiler_params=limit(3),
        cost_estimate=cost(0, 4 * sizes[0][0] * sizes[0][1]),
    )(place, tokens, weight)


def assemble_kernel(place_ref, own, across, behind, upper, lower, out):
    rows = own.shape[0]
    half = rows // 2
    for place in range(4):

        @pl.when(place_ref[0] == place)
        def _():
            out[place * rows : (place + 1) * rows] = own[...]
            out[(place ^ 1) * rows : ((place ^ 1) + 1) * rows] = across[...]
            out[(place ^ 2) * rows : ((place ^ 2) + 1) * rows] = behind[...]
            out[(place ^ 3) * rows : (place ^ 3) * rows + half] = upper[...]
            out[(place ^ 3) * rows + half : ((place ^ 3) + 1) * rows] = lower[...]


def assemble(place, pieces):
    rows, width = pieces[0].shape
    return pl.pallas_call(
        assemble_kernel,
        grid=(1,),
        out_shape=shape((4 * rows, width)),
        in_specs=[smem] + [whole(piece) for piece in pieces],
        out_specs=pl.BlockSpec((4 * rows, width), lambda *_: (0, 0)),
        compiler_params=limit(6),
        cost_estimate=cost(0, 16 * rows * width),
    )(place, *pieces)


def normalized(tokens):
    values = tokens.astype(f32)
    center = values - jnp.mean(values, axis=1, keepdims=True)
    spread = jnp.mean(center * center, axis=1, keepdims=True)
    return (center * lax.rsqrt(spread + 1e-05)).astype(bf16)


def gelu_both(values):
    coeff = math.sqrt(2.0 / math.pi)
    square = values * values
    gate = 0.5 + 0.5 * jnp.tanh(coeff * values * (1.0 + 0.044715 * square))
    hidden = values * gate
    slope = gate + hidden * (1.0 - gate) * (2.0 * coeff + 6.0 * 0.044715 * coeff * square)
    return hidden.astype(bf16), slope.astype(bf16)


def forward_core(tokens, weights_in, weights_out, normed_t, slopes, total):
    count, width = tokens.shape
    block = weights_in[0].shape[1]
    tile = min(256, block)
    normed = normalized(tokens)
    normed_t[...] = normed.T
    for side in range(2):
        for at in range(0, block, tile):
            values = matmul(normed, weights_in[side][:, at : at + tile]) * (width**-0.5)
            hidden, slopes[side][:, at : at + tile] = gelu_both(values)
            term = matmul(hidden, weights_out[side][at : at + tile])
            if side + at == 0:
                total[...] = term
            else:
                total[...] += term


def forward_kernel(tokens, own_in, mate_in, own_out, mate_out, normed_t, slope, slope_mate, out, total):
    weights = (own_in, mate_in), (own_out, mate_out)
    forward_core(tokens[...], *weights, normed_t, (slope, slope_mate), total)
    out[...] = total[...].astype(bf16)


def forward_far_kernel(place, *refs):
    pieces = refs[:5]
    own_in, mate_in, own_out, mate_out, normed_t, slope, slope_mate, out, total, tokens = refs[5:]
    assemble_kernel(place, *pieces, tokens)
    weights = (own_in, mate_in), (own_out, mate_out)
    forward_core(tokens[...], *weights, normed_t, (slope, slope_mate), total)
    count = tokens.shape[0]
    values = tokens[...].astype(f32)
    ahead = pltpu.roll(values, count - 1, 0)
    rank = lax.broadcasted_iota(jnp.int32, values.shape, 0)
    base = total[...] + values - ahead
    out[...] = jnp.where(rank == count - 1, 0.0, base)


def forward(given, count, weights, far):
    width, block = weights[0].shape
    outs = (
        shape((width, count)),
        shape((count, block)),
        shape((count, block)),
        shape((count, width), f32 if far else bf16),
    )
    scratch = [pltpu.VMEM((count, width), f32)]
    if far:
        scratch.append(pltpu.VMEM((count, width), bf16))
    return pl.pallas_call(
        forward_far_kernel if far else forward_kernel,
        grid=(1,),
        out_shape=outs,
        in_specs=[smem if value.ndim == 1 else whole(value) for value in (*given, *weights)],
        out_specs=[whole(out) for out in outs],
        scratch_shapes=scratch,
        compiler_params=limit(20),
        cost_estimate=cost(4 * count * width * block, 8 * width * block),
    )(*given, *weights)


def errors_kernel(base, sent, far, errors):
    count = errors.shape[0]
    result = base[...] + sent[...].astype(f32)
    rank = lax.broadcasted_iota(jnp.int32, result.shape, 0)
    errors[...] = jnp.where(rank == count - 1, 0.0, result).astype(bf16)


def errors_of(base, sent, far):
    return pl.pallas_call(
        errors_kernel,
        grid=(1,),
        out_shape=shape(base.shape),
        in_specs=[whole(base), whole(sent), pl.BlockSpec(memory_space=pl.ANY)],
        out_specs=whole(base),
        compiler_params=limit(8),
        cost_estimate=cost(0, 10 * base.size),
    )(base, sent, far)


def away_kernel(start, errors, errors_mate, far, *grads):
    count = errors.shape[0]
    for at, out in enumerate(grads):
        rows = slice((start + at) * lanes, (start + at + 1) * lanes)
        out[:count] = against_rows(errors[...], far[rows]).astype(bf16)
        out[count:] = against_rows(errors_mate[...], far[rows]).astype(bf16)


def away(start, stop, errors, errors_mate, far):
    count, width = errors.shape
    given = (errors, errors_mate, far)
    outs = [shape((2 * count, lanes))] * (stop - start)
    return pl.pallas_call(
        functools.partial(away_kernel, start),
        grid=(1,),
        out_shape=outs,
        in_specs=[whole(value) for value in given],
        out_specs=[whole(out) for out in outs],
        compiler_params=limit(8),
        cost_estimate=cost(2 * len(outs) * count * width * lanes, 4 * count * width),
    )(*given)


def near_kernel(errors, errors_mate, weight, slope, slope_mate, near):
    count = errors.shape[0]
    for chunk in range(near.shape[0]):
        rows = slice(chunk * lanes, (chunk + 1) * lanes)
        for at, source, factor in ((0, errors, slope), (count, errors_mate, slope_mate)):
            product = against_rows(source[...], weight[rows]) * factor[:, rows].astype(f32)
            near[chunk, at : at + count] = product.astype(bf16)


def near_of(errors, errors_mate, weight, slope, slope_mate):
    count, width = errors.shape
    chunks = weight.shape[0] // lanes
    given = (errors, errors_mate, weight, slope, slope_mate)
    out = shape((chunks, 2 * count, lanes))
    return pl.pallas_call(
        near_kernel,
        grid=(1,),
        out_shape=out,
        in_specs=[whole(value) for value in given],
        out_specs=whole(out),
        compiler_params=limit(10),
        cost_estimate=cost(2 * chunks * count * width * lanes, 10 * count * width),
    )(*given)


def update_kernel(
    heat, arrived, near, slope, slope_mate, normed, normed_mate, far, far_mate, params, noise, *rest
):
    out = rest[-1]
    width, count = normed.shape
    total = matmul(far[...], near[0, :count]) + matmul(far_mate[...], near[0, count:])
    mixed = (arrived[:count].astype(f32) * slope[...].astype(f32)).astype(bf16)
    total += matmul(normed[...], mixed)
    mixed = (arrived[count:].astype(f32) * slope_mate[...].astype(f32)).astype(bf16)
    total += matmul(normed_mate[...], mixed)
    current = params[0].astype(f32)
    moved = (
        current
        - drift_stride * (total * width**-0.5 + current)
        + heat[0] * noise[0].astype(f32)
    )
    out[...] = moved.astype(bf16)


def update(chunk, heat, arrived, near, slopes, normed, params, noise, *earlier):
    width, count = normed[0].shape
    columns = pl.BlockSpec((count, lanes), lambda *_: (0, chunk))
    block = pl.BlockSpec((1, width, lanes), lambda *_: (0, 0, chunk))
    out = shape((width, lanes))
    return pl.pallas_call(
        update_kernel,
        grid=(1,),
        out_shape=out,
        in_specs=[
            smem,
            whole(arrived),
            pl.BlockSpec((1, 2 * count, lanes), lambda *_: (chunk, 0, 0)),
            columns,
            columns,
        ]
        + [whole(value) for value in normed]
        + [block, block]
        + [pl.BlockSpec(memory_space=pl.ANY)] * len(earlier),
        out_specs=whole(out),
        compiler_params=limit(12),
        cost_estimate=cost(4 * width * count * lanes, 8 * width * count),
    )(heat, arrived, near, *slopes, *normed, params, noise, *earlier)


def finish_kernel(count, start, *refs):
    taken = refs[0]
    own, across, beyond = (refs[1 + i * count : 1 + (i + 1) * count] for i in range(3))
    result, gaps = refs[-2], refs[-1]
    odd = taken[0] == 1
    for at in range(count):
        cols = slice(at * lanes, (at + 1) * lanes)
        mine = own[at][...]
        near = across[at][...]
        far = beyond[at][...]
        result[0, :, cols] = jnp.where(taken[1] == 1, near, jnp.where(taken[2] == 1, far, mine))
        mine = mine.astype(f32)
        near = near.astype(f32) - mine
        far = far.astype(f32) - mine
        near = jnp.mean(near * near, axis=0, keepdims=True)
        far = jnp.mean(far * far, axis=0, keepdims=True)
        gaps[0, 0:1, cols] = jnp.where(odd, near, far)
        gaps[0, 1:2, cols] = jnp.where(odd, far, near)


def finish(start, chunks, block, flags, own, across, beyond, so_far):
    count = len(own)
    width = own[0].shape[0]
    anywhere = pl.BlockSpec(memory_space=pl.ANY)
    given = list(so_far) if so_far is not None else []
    extra = len(given)
    step = start // count

    def kernel(*refs):
        data = refs[: 1 + 3 * count]
        finish_kernel(count, start, *data, refs[-2], refs[-1])

    return pl.pallas_call(
        kernel,
        grid=(1,),
        out_shape=(shape((1, width, block)), shape((1, 2, block), f32)),
        in_specs=[smem]
        + [whole(piece) for piece in (*own, *across, *beyond)]
        + [anywhere] * extra,
        out_specs=(
            pl.BlockSpec((1, width, count * lanes), lambda *_: (0, 0, step)),
            pl.BlockSpec((1, 2, count * lanes), lambda *_: (0, 0, step)),
        ),
        input_output_aliases={1 + 3 * count + i: i for i in range(extra)},
        compiler_params=limit(8),
        cost_estimate=cost(0, 8 * width * lanes * count),
    )(flags, *own, *across, *beyond, *given)


def body(
    residual_flow,
    rooted_input_matrix,
    chain_normal_draws,
    output_matrix,
    chain_heat,
    matched_chain,
    swap_mask,
):
    replicas = lax.axis_size("rep")
    rank = lax.axis_index("rep")
    place = rank % 4
    params = rooted_input_matrix[0]
    block = params.shape[1]
    count = residual_flow.shape[0]

    def to_core(value):
        return lax.ppermute(value, "dp", [(i, i ^ 1) for i in range(4)])

    def to_chip(value):
        return lax.ppermute(value, "dp", [(i, i ^ 2) for i in range(4)])

    def to_mate(value):
        return lax.ppermute(value, "rep", [(i, i ^ 1) for i in range(replicas)])

    def to_pair(value):
        return lax.ppermute(value, "rep", [(i, i ^ 2) for i in range(replicas)])

    def to_next(value):
        pairs = [(i, (i + (2 if i % 2 == 0 else -2)) % replicas) for i in range(replicas)]
        return lax.ppermute(value, "rep", pairs)

    def step_one(own):
        return to_mate(own), to_pair(own)

    def step_two(own, across, behind):
        half = own.shape[0] // 2
        return own, across, behind, to_mate(behind[:half]), to_pair(across[half:])

    spot = place.astype(jnp.int32)[None]
    mate_in = to_core(params)
    mate_out = to_core(output_matrix)
    token_share, weight_share = shares(spot, residual_flow, output_matrix)
    token_own = to_chip(token_share)
    weight_own = to_chip(weight_share)
    weights = (params, mate_in, output_matrix, mate_out)
    normed, slope, slope_send, part = forward((residual_flow,), count, weights, False)
    token_own_early = token_own
    token_own = after(token_own, part)
    sent = to_chip(after(part, token_own_early))
    normed_mate = to_core(normed)
    slope_mate = to_core(slope_send)
    token_across, token_behind = step_one(token_own)
    token_pieces = step_two(token_own, token_across, token_behind)
    weight_across, weight_behind = step_one(weight_own)
    far, far_slope, far_slope_send, base = forward((spot, *token_pieces), count, weights, True)
    far_mate = to_core(far)
    far_slope_mate = to_core(far_slope_send)
    weight_across = after(weight_across, base)
    weight_pieces = step_two(weight_own, weight_across, weight_behind)
    far_out = assemble(spot, weight_pieces)

    errors = errors_of(base, sent, far_out)
    errors_mate = to_core(errors)
    chunks = block // lanes
    grads = away(0, 1, errors, errors_mate, far_out)
    grads += away(1, chunks, errors, errors_mate, far_out)
    arrived = [to_chip(value) for value in grads]
    near = near_of(errors, errors_mate, output_matrix, far_slope, far_slope_mate)

    heat = jnp.sqrt(2.0 * drift_stride * chain_heat)
    taken = swap_mask[0] == 1
    across_rank = rank ^ 1
    odd = rank % 2
    beyond_rank = jnp.where(odd == 1, rank + 1, rank - 1)
    flags = jnp.stack(
        [odd, taken & (matched_chain[0] == across_rank), taken & (matched_chain[0] == beyond_rank)]
    ).astype(jnp.int32)

    own, across, beyond = [], [], []
    for chunk in range(chunks):
        earlier = across[chunk - 2 : chunk - 1] if chunk >= 2 else own[:chunk]
        fresh = update(
            chunk,
            heat,
            arrived[chunk],
            near,
            (slope, slope_mate),
            (normed, normed_mate, far, far_mate),
            rooted_input_matrix,
            chain_normal_draws,
            *earlier,
        )
        own.append(fresh)
        across.append(to_mate(fresh))
        beyond.append(to_next(across[-1]))
    done = None
    for start, stop in ((0, 2), (2, 3), (3, 4)):
        done = finish(
            start, chunks, block, flags, own[start:stop], across[start:stop], beyond[start:stop], done
        )
    return done


def solution(mesh):
    placed = (
        P("dp", None),
        P("rep", None, "dp"),
        P("rep", None, "dp"),
        P("dp", None),
        P("rep"),
        P("rep"),
        P("rep"),
    )
    return jax.shard_map(
        body,
        mesh=mesh,
        in_specs=placed,
        out_specs=(P("rep", None, "dp"), P("rep", None, "dp")),
        check_vma=False,
    )
```

time: 202 us -> 94.1 us (0.47)
  waiting for transfers between devices: 154 us -> 38 us
  starting transfers between devices: 4.89 us -> 30.2 us
  matrix products: 20.4 us -> 0 us
  Pallas kernels: 0 us -> 19 us
  between operations: 15.9 us -> 2.87 us
  other arithmetic: 6.44 us -> 0.08 us
  local copies, waits for them, and re-layouts: 0.01 us -> 3.68 us
    all_gather x2 -> x0, waiting for transfers between devices: 66.5 us -> none  [the longest x1 36.2 us: body(): lax.all_gather(params, 'dp', axis=1, tiled=True)]
    reduce_scatter x1 -> x0, waiting for transfers between devices: 43.8 us -> none  [body(): lax.psum_scatter(partial_value.astype(jnp.bfloat16), 'dp', scatter_dimens...]
    ppermute x2 -> x30, starting transfers between devices: 4.78 us -> 30.2 us  [the longest x8 9.9 us: to_mate(): return lax.ppermute(value, 'rep', [(i, i ^ 1) for i in range(replicas)])]
    dot_general x3 -> x0, matrix products: 20.4 us -> none  [the longest x1 9.25 us: body(): lax.dot_general(normed, preact_grad, (((0,), (0,)), ((), ())), preferred_...]
    pallas_call x0 -> x18, Pallas kernels: none -> 19 us  [the longest x2 5.83 us: forward(): pl.pallas_call(forward_far_kernel if far else forward_kernel, grid=(1,),...]
    ppermute x2 -> x30, waiting for transfers between devices: 42.5 us -> 38 us  [the longest x4 11.2 us: to_next(): return lax.ppermute(value, 'rep', pairs)]
    unnamed x6 -> x15, local copies, waits for them, and re-layouts: 0.01 us -> 3.65 us
    convert_element_type x2 -> x0, other arithmetic: 3.1 us -> none  [the longest x1 1.81 us: body(): refreshed_input_matrix = moved.astype(jnp.bfloat16)]
  transfers between devices with their start and end apart: 5 -> 30, of which waited for: 5 -> 18; matrix products, arithmetic and copies ran while one was open for 4% -> 0% of each run, Pallas kernels for 0% -> 19%
where the time goes in v2:
time: 94.1 us; the launch traced here: 93.9 us
  waiting for transfers between devices  38 us (40%)
  starting transfers between devices  30.2 us (32%)
  Pallas kernels  19 us (20%)
  local copies, waits for them, and re-layouts  3.68 us (4%)
  between operations  2.87 us (3%)
    ppermute x4, waiting for transfers between devices, to_next(): return lax.ppermute(value, 'rep', pairs)  11.2 us
    ppermute x7, waiting for transfers between devices, to_chip(): return lax.ppermute(value, 'dp', [(i, i ^ 2) for i in range(4)])  10.6 us
    ppermute x8, starting transfers between devices, to_mate(): return lax.ppermute(value, 'rep', [(i, i ^ 1) for i in range(replicas)])  9.9 us
    ppermute x7, starting transfers between devices, to_chip(): return lax.ppermute(value, 'dp', [(i, i ^ 2) for i in range(4)])  9.17 us
    ppermute x4, waiting for transfers between devices, to_pair(): return lax.ppermute(value, 'rep', [(i, i ^ 2) for i in range(replicas)])  7.43 us
    ppermute x8, waiting for transfers between devices, to_mate(): return lax.ppermute(value, 'rep', [(i, i ^ 1) for i in range(replicas)])  7.42 us
    pallas_call x2, Pallas kernels, forward(): pl.pallas_call(forward_far_kernel if far else forward_kernel, grid=(1,),...  5.83 us
    ppermute x4, starting transfers between devices, to_pair(): return lax.ppermute(value, 'rep', [(i, i ^ 2) for i in range(replicas)])  5.51 us
  transfers between devices with their start and end apart: 30, of which 18 were waited for; matrix products, arithmetic and copies ran while one was open for 0% of the time, Pallas kernels for 19%

profile of v2, /device:TPU:0, one launch (start us, length us, event | category | flops | bytes accessed | tf_op | source)
XLA Modules:
  0.0 93.9 jit_solution(5825196242075196801)
XLA Ops:
  1.2 1.2 %copy-done.2 = bf16[512,1024]{1,0:T(8,128)(2,1)S(1)} copy-done((bf16[512,1024]{1,0:T(8,128)(2,1)S(1)}, bf16[512,1024]{1,0:T(8,128)(2,1)}, u32[]{:S(2)}) %copy-start.2) | copy-done | bytes 1048600
  3.6 3.0 %collective-permute-start = (bf16[96,1024]{1,0:T(8,128)(2,1)S(1)}, bf16[96,1024]{1,0:T(8,128)(2,1)S(1)}, u32[]{:S(2)}, u32[]{:S(2)}) collective-permute-start(bf16[96,1024]{1,0:T(8,128)(2,1)S(1)} %get-tuple-element.19), channel_id=1, source_target_pairs={{0,2},{1,3},{2,0},{3,1},{4,6},{5,7},{6,4},{7,5},{8,10},{9,11},{10,... | collective-permute-start | bytes 589832 | tf_op jit(solution)/shard_map/ppermute | solution.py:359
  8.0 2.9 %shard_map.87 = (bf16[1024,384]{1,0:T(8,128)(2,1)S(1)}, bf16[384,512]{1,0:T(8,128)(2,1)S(1)}, bf16[384,512]{1,0:T(8,128)(2,1)S(1)}, bf16[384,1024]{1,0:T(8,128)(2,1)S(1)}) custom-call(bf16[384,1024]{1,0:T(8,128)(2,1)S(1)} %copy-done.6, bf16[1024,512]{1,0:T(8,128)(2,1)S(1)} %bitcast.10, bf16[1024,512]{1,0:T(8,128)(2,1)S(1)} %collective-permute-done.1.mate_in.refs_6_, ...), custom_call_target="tpu_custom_call" | custom-call | flops 1610612736 | bytes 4194304 | tf_op jit(solution)/shard_map/pallas_call | solution.py:167
  11.0 1.4 %collective-permute-done.refs_0_.refs_1_ = bf16[96,1024]{1,0:T(8,128)(2,1)S(1)} collective-permute-done((bf16[96,1024]{1,0:T(8,128)(2,1)S(1)}, bf16[96,1024]{1,0:T(8,128)(2,1)S(1)}, u32[]{:S(2)}, u32[]{:S(2)}) %collective-permute-start) | collective-permute-done | bytes 196640 | tf_op jit(solution)/shard_map/ppermute | solution.py:359
  12.3 2.1 %collective-permute-start.7 = (bf16[384,1024]{1,0:T(8,128)(2,1)S(1)}, bf16[384,1024]{1,0:T(8,128)(2,1)S(1)}, u32[]{:S(2)}, u32[]{:S(2)}) collective-permute-start(bf16[384,1024]{1,0:T(8,128)(2,1)S(1)} %shard_map.90), channel_id=1, source_target_pairs={{0,2},{1,3},{2,0},{3,1},{4,6},{5,7},{6,4},{7,5},{8,10},{9,11},{10,... | collective-permute-start | bytes 2359304 | tf_op jit(solution)/shard_map/ppermute | solution.py:359
  14.4 1.6 %collective-permute-start.4 = (bf16[96,1024]{1,0:T(8,128)(2,1)S(1)}, bf16[96,1024]{1,0:T(8,128)(2,1)S(1)}, u32[]{:S(2)}, u32[]{:S(2)}) collective-permute-start(bf16[96,1024]{1,0:T(8,128)(2,1)S(1)} %shard_map.88.refs_0_), channel_id=1, source_target_pairs={{0,8},{4,12},{8,0},{12,4},{16,24},{20,28},{24,16},{28,20},{1,9},{5... | collective-permute-start | bytes 589832 | tf_op jit(solution)/shard_map/ppermute | solution.py:365
  16.0 1.5 %collective-permute-start.3 = (bf16[96,1024]{1,0:T(8,128)(2,1)S(1)}, bf16[96,1024]{1,0:T(8,128)(2,1)S(1)}, u32[]{:S(2)}, u32[]{:S(2)}) collective-permute-start(bf16[96,1024]{1,0:T(8,128)(2,1)S(1)} %shard_map.88.refs_0_), channel_id=1, source_target_pairs={{0,4},{4,0},{8,12},{12,8},{16,20},{20,16},{24,28},{28,24},{1,5},{5... | collective-permute-start | bytes 589832 | tf_op jit(solution)/shard_map/ppermute | solution.py:362
  18.0 2.1 %collective-permute-start.10 = (bf16[128,1024]{1,0:T(8,128)(2,1)S(1)}, bf16[128,1024]{1,0:T(8,128)(2,1)S(1)}, u32[]{:S(2)}, u32[]{:S(2)}) collective-permute-start(bf16[128,1024]{1,0:T(8,128)(2,1)S(1)} %collective-permute-done.8.own), channel_id=1, source_target_pairs={{0,8},{4,12},{8,0},{12,4},{16,24},{20,28},{24,16},{28,20},{1,9},{5... | collective-permute-start | bytes 786440 | tf_op jit(solution)/shard_map/ppermute | solution.py:365
  20.1 1.5 %collective-permute-start.9 = (bf16[128,1024]{1,0:T(8,128)(2,1)S(1)}, bf16[128,1024]{1,0:T(8,128)(2,1)S(1)}, u32[]{:S(2)}, u32[]{:S(2)}) collective-permute-start(bf16[128,1024]{1,0:T(8,128)(2,1)S(1)} %collective-permute-done.8.own), channel_id=1, source_target_pairs={{0,4},{4,0},{8,12},{12,8},{16,20},{20,16},{24,28},{28,24},{1,5},{5... | collective-permute-start | bytes 786440 | tf_op jit(solution)/shard_map/ppermute | solution.py:362
  22.5 1.3 %collective-permute-start.6 = (bf16[48,1024]{1,0:T(8,128)(2,1)S(1)}, bf16[48,1024]{1,0:T(8,128)(2,1)S(1)}, u32[]{:S(2)}, u32[]{:S(2)}) collective-permute-start(bf16[48,1024]{1,0:T(8,128)(2,1)S(1)} %slice.17), channel_id=1, source_target_pairs={{0,8},{4,12},{8,0},{12,4},{16,24},{20,28},{24,16},{28,20},{1,9},{5... | collective-permute-start | bytes 294920 | tf_op jit(solution)/shard_map/ppermute | solution.py:365
  23.8 2.9 %collective-permute-done.10.behind = bf16[128,1024]{1,0:T(8,128)(2,1)S(1)} collective-permute-done((bf16[128,1024]{1,0:T(8,128)(2,1)S(1)}, bf16[128,1024]{1,0:T(8,128)(2,1)S(1)}, u32[]{:S(2)}, u32[]{:S(2)}) %collective-permute-start.10) | collective-permute-done | bytes 262176 | tf_op jit(solution)/shard_map/ppermute | solution.py:365
  26.8 1.6 %collective-permute-start.11 = (bf16[64,1024]{1,0:T(8,128)(2,1)S(1)}, bf16[64,1024]{1,0:T(8,128)(2,1)S(1)}, u32[]{:S(2)}, u32[]{:S(2)}) collective-permute-start(bf16[64,1024]{1,0:T(8,128)(2,1)S(1)} %slice.18), channel_id=1, source_target_pairs={{0,4},{4,0},{8,12},{12,8},{16,20},{20,16},{24,28},{28,24},{1,5},{5... | collective-permute-start | bytes 393224 | tf_op jit(solution)/shard_map/ppermute | solution.py:362
  28.3 2.5 %collective-permute-done.5.refs_3_ = bf16[48,1024]{1,0:T(8,128)(2,1)S(1)} collective-permute-done((bf16[48,1024]{1,0:T(8,128)(2,1)S(1)}, bf16[48,1024]{1,0:T(8,128)(2,1)S(1)}, u32[]{:S(2)}, u32[]{:S(2)}) %collective-permute-start.5) | collective-permute-done | bytes 98336 | tf_op jit(solution)/shard_map/ppermute | solution.py:362
  30.8 2.9 %shard_map.89 = (bf16[1024,384]{1,0:T(8,128)(2,1)S(1)}, bf16[384,512]{1,0:T(8,128)(2,1)S(1)}, bf16[384,512]{1,0:T(8,128)(2,1)S(1)}, f32[384,1024]{1,0:T(8,128)S(1)}) custom-call(s32[1]{0:T(128)} %bitcast.5.place.place_ref, bf16[96,1024]{1,0:T(8,128)(2,1)S(1)} %shard_map.88.refs_0_, bf16[96,1024]{1,0:T(8,128)(2,1)S(1)} %collective-permute-done.3.refs_1_, ...), custom_call_target="tpu_custom_call" | custom-call | flops 1610612736 | bytes 4194304 | tf_op jit(solution)/shard_map/pallas_call | solution.py:167
  34.3 4.5 %collective-permute-done.12.lower = bf16[64,1024]{1,0:T(8,128)(2,1)S(1)} collective-permute-done((bf16[64,1024]{1,0:T(8,128)(2,1)S(1)}, bf16[64,1024]{1,0:T(8,128)(2,1)S(1)}, u32[]{:S(2)}, u32[]{:S(2)}) %collective-permute-start.12) | collective-permute-done | bytes 131104 | tf_op jit(solution)/shard_map/ppermute | solution.py:365
  42.8 1.4 %shard_map.94 = (bf16[768,128]{1,0:T(8,128)(2,1)S(1)}, bf16[768,128]{1,0:T(8,128)(2,1)S(1)}, bf16[768,128]{1,0:T(8,128)(2,1)S(1)}) custom-call(bf16[384,1024]{1,0:T(8,128)(2,1)S(1)} %shard_map.93.errors, bf16[384,1024]{1,0:T(8,128)(2,1)S(1)} %collective-permute-done.13.errors_mate, bf16[512,1024]{1,0:T(8,128)(2,1)S(1)} %shard_map.92.far), custom_call_target="tpu_custom_call" | custom-call | flops 603979776 | bytes 1572864 | tf_op jit(solution)/shard_map/pallas_call | solution.py:210
  44.4 1.3 %collective-permute-start.19 = (bf16[768,128]{1,0:T(8,128)(2,1)S(1)}, bf16[768,128]{1,0:T(8,128)(2,1)S(1)}, u32[]{:S(2)}, u32[]{:S(2)}) collective-permute-start(bf16[768,128]{1,0:T(8,128)(2,1)S(1)} %get-tuple-element.30), channel_id=1, source_target_pairs={{0,2},{1,3},{2,0},{3,1},{4,6},{5,7},{6,4},{7,5},{8,10},{9,11},{10,... | collective-permute-start | bytes 589832 | tf_op jit(solution)/shard_map/ppermute | solution.py:359
  46.4 1.8 %shard_map.95.near = bf16[4,768,128]{2,1,0:T(8,128)(2,1)S(1)} custom-call(bf16[384,1024]{1,0:T(8,128)(2,1)S(1)} %shard_map.93.errors, bf16[384,1024]{1,0:T(8,128)(2,1)S(1)} %collective-permute-done.13.errors_mate, bf16[512,1024]{1,0:T(8,128)(2,1)S(1)} %copy-done.4, bf16[384,512]{1,0:T(8,128)(2,1)S(1)} %get-tuple-element.24.slope, ...), custom_call_target="tpu_custom_call" | custom-call | flops 805306368 | bytes 3932160 | tf_op jit(solution)/shard_map/pallas_call | solution.py:235
  48.2 1.7 %collective-permute-done.20.arrived = bf16[768,128]{1,0:T(8,128)(2,1)S(1)} collective-permute-done((bf16[768,128]{1,0:T(8,128)(2,1)S(1)}, bf16[768,128]{1,0:T(8,128)(2,1)S(1)}, u32[]{:S(2)}, u32[]{:S(2)}) %collective-permute-start.20) | collective-permute-done | bytes 196640 | tf_op jit(solution)/shard_map/ppermute | solution.py:359
  51.1 1.5 %collective-permute-start.25 = (bf16[1024,128]{1,0:T(8,128)(2,1)S(1)}, bf16[1024,128]{1,0:T(8,128)(2,1)S(1)}, u32[]{:S(2)}, u32[]{:S(2)}) collective-permute-start(bf16[1024,128]{1,0:T(8,128)(2,1)S(1)} %shard_map.97.rest_0_.refs_1_), channel_id=1, source_target_pairs={{0,4},{4,0},{8,12},{12,8},{16,20},{20,16},{24,28},{28,24},{1,5},{5... | collective-permute-start | bytes 786440 | tf_op jit(solution)/shard_map/ppermute | solution.py:362
  54.5 1.5 %collective-permute-start.21 = (bf16[1024,128]{1,0:T(8,128)(2,1)S(1)}, bf16[1024,128]{1,0:T(8,128)(2,1)S(1)}, u32[]{:S(2)}, u32[]{:S(2)}) collective-permute-start(bf16[1024,128]{1,0:T(8,128)(2,1)S(1)} %shard_map.98.refs_2_), channel_id=1, source_target_pairs={{0,4},{4,0},{8,12},{12,8},{16,20},{20,16},{24,28},{28,24},{1,5},{5... | collective-permute-start | bytes 786440 | tf_op jit(solution)/shard_map/ppermute | solution.py:362
  56.6 1.4 %collective-permute-start.14 = (bf16[768,128]{1,0:T(8,128)(2,1)S(1)}, bf16[768,128]{1,0:T(8,128)(2,1)S(1)}, u32[]{:S(2)}, u32[]{:S(2)}) collective-permute-start(bf16[768,128]{1,0:T(8,128)(2,1)S(1)} %get-tuple-element.23), channel_id=1, source_target_pairs={{0,2},{1,3},{2,0},{3,1},{4,6},{5,7},{6,4},{7,5},{8,10},{9,11},{10,... | collective-permute-start | bytes 589832 | tf_op jit(solution)/shard_map/ppermute | solution.py:359
  58.0 5.8 %collective-permute-done.24.arrived = bf16[768,128]{1,0:T(8,128)(2,1)S(1)} collective-permute-done((bf16[768,128]{1,0:T(8,128)(2,1)S(1)}, bf16[768,128]{1,0:T(8,128)(2,1)S(1)}, u32[]{:S(2)}, u32[]{:S(2)}) %collective-permute-start.24) | collective-permute-done | bytes 196640 | tf_op jit(solution)/shard_map/ppermute | solution.py:359
  68.7 2.7 %collective-permute-start.29 = (bf16[1024,128]{1,0:T(8,128)(2,1)S(1)}, bf16[1024,128]{1,0:T(8,128)(2,1)S(1)}, u32[]{:S(2)}, u32[]{:S(2)}) collective-permute-start(bf16[1024,128]{1,0:T(8,128)(2,1)S(1)} %collective-permute-done.21.rest_0_.refs_4_), channel_id=1, source_target_pairs={{0,8},{4,28},{8,16},{12,4},{16,24},{20,12},{24,0},{28,20},{1,9},{5... | collective-permute-start | bytes 786440 | tf_op jit(solution)/shard_map/ppermute | solution.py:369
  71.4 2.2 %collective-permute-done.26.refs_2_ = bf16[1024,128]{1,0:T(8,128)(2,1)S(1)} collective-permute-done((bf16[1024,128]{1,0:T(8,128)(2,1)S(1)}, bf16[1024,128]{1,0:T(8,128)(2,1)S(1)}, u32[]{:S(2)}, u32[]{:S(2)}) %collective-permute-start.26) | collective-permute-done | bytes 262176 | tf_op jit(solution)/shard_map/ppermute | solution.py:362
  74.0 2.4 %collective-permute-done.22.refs_2_ = bf16[1024,128]{1,0:T(8,128)(2,1)S(1)} collective-permute-done((bf16[1024,128]{1,0:T(8,128)(2,1)S(1)}, bf16[1024,128]{1,0:T(8,128)(2,1)S(1)}, u32[]{:S(2)}, u32[]{:S(2)}) %collective-permute-start.22) | collective-permute-done | bytes 262176 | tf_op jit(solution)/shard_map/ppermute | solution.py:362
  79.3 5.6 %collective-permute-done.29.refs_6_ = bf16[1024,128]{1,0:T(8,128)(2,1)S(1)} collective-permute-done((bf16[1024,128]{1,0:T(8,128)(2,1)S(1)}, bf16[1024,128]{1,0:T(8,128)(2,1)S(1)}, u32[]{:S(2)}, u32[]{:S(2)}) %collective-permute-start.29) | collective-permute-done | bytes 262176 | tf_op jit(solution)/shard_map/ppermute | solution.py:369
  84.9 1.7 %shard_map.101 = (bf16[1,1024,512]{2,1,0:T(8,128)(2,1)}, f32[1,2,512]{2,1,0:T(2,128)}) custom-call(s32[3]{0:T(128)S(1)} %pad_add_fusion.refs_0_, bf16[1024,128]{1,0:T(8,128)(2,1)S(1)} %shard_map.97.rest_0_.refs_1_, bf16[1024,128]{1,0:T(8,128)(2,1)S(1)} %shard_map.98.refs_2_, bf16[1024,128]{1,0:T(8,128)(2,1)S(1)} %collective-permute-done.25.rest_0_.refs_3_, ...), custom_call_target="tpu_custom_call" | custom-call | bytes 2097152 | tf_op jit(solution)/shard_map/pallas_call | solution.py:322
  86.6 3.0 %collective-permute-done.27.refs_3_ = bf16[1024,128]{1,0:T(8,128)(2,1)S(1)} collective-permute-done((bf16[1024,128]{1,0:T(8,128)(2,1)S(1)}, bf16[1024,128]{1,0:T(8,128)(2,1)S(1)}, u32[]{:S(2)}, u32[]{:S(2)}) %collective-permute-start.27) | collective-permute-done | bytes 262176 | tf_op jit(solution)/shard_map/ppermute | solution.py:369
  89.7 1.4 %shard_map.102 = (bf16[1,1024,512]{2,1,0:T(8,128)(2,1)}, f32[1,2,512]{2,1,0:T(2,128)}) custom-call(s32[3]{0:T(128)S(1)} %pad_add_fusion.refs_0_, bf16[1024,128]{1,0:T(8,128)(2,1)S(1)} %shard_map.100.refs_1_, bf16[1024,128]{1,0:T(8,128)(2,1)S(1)} %collective-permute-done.26.refs_2_, ...), custom_call_target="tpu_custom_call", output_to_operand_aliasing={{0}: (4, {}), {1}: (5, {})} | custom-call | bytes 1048576 | tf_op jit(solution)/shard_map/pallas_call | solution.py:322
  91.1 1.4 %collective-permute-done.23.refs_3_ = bf16[1024,128]{1,0:T(8,128)(2,1)S(1)} collective-permute-done((bf16[1024,128]{1,0:T(8,128)(2,1)S(1)}, bf16[1024,128]{1,0:T(8,128)(2,1)S(1)}, u32[]{:S(2)}, u32[]{:S(2)}) %collective-permute-start.23) | collective-permute-done | bytes 262176 | tf_op jit(solution)/shard_map/ppermute | solution.py:369
  92.5 1.4 %shard_map.103 = (bf16[1,1024,512]{2,1,0:T(8,128)(2,1)}, f32[1,2,512]{2,1,0:T(2,128)}) custom-call(s32[3]{0:T(128)S(1)} %pad_add_fusion.refs_0_, bf16[1024,128]{1,0:T(8,128)(2,1)S(1)} %shard_map.99.refs_1_, bf16[1024,128]{1,0:T(8,128)(2,1)S(1)} %collective-permute-done.22.refs_2_, ...), custom_call_target="tpu_custom_call", output_to_operand_aliasing={{0}: (4, {}), {1}: (5, {})} | custom-call | bytes 1048576 | tf_op jit(solution)/shard_map/pallas_call | solution.py:322
  (66 shorter events, 19.6 us)
Async XLA Ops:
  0.6 6.1 %copy-start = (bf16[1,1024,512]{2,1,0:T(8,128)(2,1)S(1)}, bf16[1,1024,512]{2,1,0:T(8,128)(2,1)}, u32[]{:S(2)}) copy-start(bf16[1,1024,512]{2,1,0:T(8,128)(2,1)} %params.7) | copy-start | bytes 3145732
  0.6 6.1 %collective-permute-start.1 = (bf16[1024,512]{1,0:T(8,128)(2,1)}, bf16[1024,512]{1,0:T(8,128)(2,1)S(1)}, u32[]{:S(2)}, u32[]{:S(2)}) collective-permute-start(bf16[1024,512]{1,0:T(8,128)(2,1)} %bitcast.9), channel_id=1, source_target_pairs={{0,1},{1,0},{2,3},{3,2},{4,5},{5,4},{6,7},{7,6},{8,9},{9,8},{10,11... | collective-permute-start | bytes 3145736 | tf_op jit(solution)/shard_map/ppermute | solution.py:356
  1.2 5.6 %collective-permute-start.2 = (bf16[512,1024]{1,0:T(8,128)(2,1)}, bf16[512,1024]{1,0:T(8,128)(2,1)S(1)}, u32[]{:S(2)}, u32[]{:S(2)}) collective-permute-start(bf16[512,1024]{1,0:T(8,128)(2,1)} %weight.3), channel_id=1, source_target_pairs={{0,1},{1,0},{2,3},{3,2},{4,5},{5,4},{6,7},{7,6},{8,9},{9,8},{10,11... | collective-permute-start | bytes 3145736 | tf_op jit(solution)/shard_map/ppermute | solution.py:356
  3.6 8.7 %collective-permute-start = (bf16[96,1024]{1,0:T(8,128)(2,1)S(1)}, bf16[96,1024]{1,0:T(8,128)(2,1)S(1)}, u32[]{:S(2)}, u32[]{:S(2)}) collective-permute-start(bf16[96,1024]{1,0:T(8,128)(2,1)S(1)} %get-tuple-element.19), channel_id=1, source_target_pairs={{0,2},{1,3},{2,0},{3,1},{4,6},{5,7},{6,4},{7,5},{8,10},{9,11},{10,... | collective-permute-start | bytes 589832 | tf_op jit(solution)/shard_map/ppermute | solution.py:359
  6.6 11.3 %collective-permute-start.8 = (bf16[128,1024]{1,0:T(8,128)(2,1)S(1)}, bf16[128,1024]{1,0:T(8,128)(2,1)S(1)}, u32[]{:S(2)}, u32[]{:S(2)}) collective-permute-start(bf16[128,1024]{1,0:T(8,128)(2,1)S(1)} %get-tuple-element.22), channel_id=1, source_target_pairs={{0,2},{1,3},{2,0},{3,1},{4,6},{5,7},{6,4},{7,5},{8,10},{9,11},{10,... | collective-permute-start | bytes 786440 | tf_op jit(solution)/shard_map/ppermute | solution.py:359
  10.9 19.8 %copy-start.4 = (bf16[512,1024]{1,0:T(8,128)(2,1)S(1)}, bf16[512,1024]{1,0:T(8,128)(2,1)}, u32[]{:S(2)}) copy-start(bf16[512,1024]{1,0:T(8,128)(2,1)} %weight.3) | copy-start | bytes 3145732
  12.3 26.7 %collective-permute-start.7 = (bf16[384,1024]{1,0:T(8,128)(2,1)S(1)}, bf16[384,1024]{1,0:T(8,128)(2,1)S(1)}, u32[]{:S(2)}, u32[]{:S(2)}) collective-permute-start(bf16[384,1024]{1,0:T(8,128)(2,1)S(1)} %shard_map.90), channel_id=1, source_target_pairs={{0,2},{1,3},{2,0},{3,1},{4,6},{5,7},{6,4},{7,5},{8,10},{9,11},{10,... | collective-permute-start | bytes 2359304 | tf_op jit(solution)/shard_map/ppermute | solution.py:359
  14.4 7.2 %collective-permute-start.4 = (bf16[96,1024]{1,0:T(8,128)(2,1)S(1)}, bf16[96,1024]{1,0:T(8,128)(2,1)S(1)}, u32[]{:S(2)}, u32[]{:S(2)}) collective-permute-start(bf16[96,1024]{1,0:T(8,128)(2,1)S(1)} %shard_map.88.refs_0_), channel_id=1, source_target_pairs={{0,8},{4,12},{8,0},{12,4},{16,24},{20,28},{24,16},{28,20},{1,9},{5... | collective-permute-start | bytes 589832 | tf_op jit(solution)/shard_map/ppermute | solution.py:365
  16.0 6.5 %collective-permute-start.3 = (bf16[96,1024]{1,0:T(8,128)(2,1)S(1)}, bf16[96,1024]{1,0:T(8,128)(2,1)S(1)}, u32[]{:S(2)}, u32[]{:S(2)}) collective-permute-start(bf16[96,1024]{1,0:T(8,128)(2,1)S(1)} %shard_map.88.refs_0_), channel_id=1, source_target_pairs={{0,4},{4,0},{8,12},{12,8},{16,20},{20,16},{24,28},{28,24},{1,5},{5... | collective-permute-start | bytes 589832 | tf_op jit(solution)/shard_map/ppermute | solution.py:362
  18.0 8.8 %collective-permute-start.10 = (bf16[128,1024]{1,0:T(8,128)(2,1)S(1)}, bf16[128,1024]{1,0:T(8,128)(2,1)S(1)}, u32[]{:S(2)}, u32[]{:S(2)}) collective-permute-start(bf16[128,1024]{1,0:T(8,128)(2,1)S(1)} %collective-permute-done.8.own), channel_id=1, source_target_pairs={{0,8},{4,12},{8,0},{12,4},{16,24},{20,28},{24,16},{28,20},{1,9},{5... | collective-permute-start | bytes 786440 | tf_op jit(solution)/shard_map/ppermute | solution.py:365
  20.1 13.6 %collective-permute-start.9 = (bf16[128,1024]{1,0:T(8,128)(2,1)S(1)}, bf16[128,1024]{1,0:T(8,128)(2,1)S(1)}, u32[]{:S(2)}, u32[]{:S(2)}) collective-permute-start(bf16[128,1024]{1,0:T(8,128)(2,1)S(1)} %collective-permute-done.8.own), channel_id=1, source_target_pairs={{0,4},{4,0},{8,12},{12,8},{16,20},{20,16},{24,28},{28,24},{1,5},{5... | collective-permute-start | bytes 786440 | tf_op jit(solution)/shard_map/ppermute | solution.py:362
  21.6 9.2 %collective-permute-start.5 = (bf16[48,1024]{1,0:T(8,128)(2,1)S(1)}, bf16[48,1024]{1,0:T(8,128)(2,1)S(1)}, u32[]{:S(2)}, u32[]{:S(2)}) collective-permute-start(bf16[48,1024]{1,0:T(8,128)(2,1)S(1)} %slice.16), channel_id=1, source_target_pairs={{0,4},{4,0},{8,12},{12,8},{16,20},{20,16},{24,28},{28,24},{1,5},{5... | collective-permute-start | bytes 294920 | tf_op jit(solution)/shard_map/ppermute | solution.py:362
  22.5 8.3 %collective-permute-start.6 = (bf16[48,1024]{1,0:T(8,128)(2,1)S(1)}, bf16[48,1024]{1,0:T(8,128)(2,1)S(1)}, u32[]{:S(2)}, u32[]{:S(2)}) collective-permute-start(bf16[48,1024]{1,0:T(8,128)(2,1)S(1)} %slice.17), channel_id=1, source_target_pairs={{0,8},{4,12},{8,0},{12,4},{16,24},{20,28},{24,16},{28,20},{1,9},{5... | collective-permute-start | bytes 294920 | tf_op jit(solution)/shard_map/ppermute | solution.py:365
  26.8 7.5 %collective-permute-start.11 = (bf16[64,1024]{1,0:T(8,128)(2,1)S(1)}, bf16[64,1024]{1,0:T(8,128)(2,1)S(1)}, u32[]{:S(2)}, u32[]{:S(2)}) collective-permute-start(bf16[64,1024]{1,0:T(8,128)(2,1)S(1)} %slice.18), channel_id=1, source_target_pairs={{0,4},{4,0},{8,12},{12,8},{16,20},{20,16},{24,28},{28,24},{1,5},{5... | collective-permute-start | bytes 393224 | tf_op jit(solution)/shard_map/ppermute | solution.py:362
  33.8 5.0 %collective-permute-start.12 = (bf16[64,1024]{1,0:T(8,128)(2,1)S(1)}, bf16[64,1024]{1,0:T(8,128)(2,1)S(1)}, u32[]{:S(2)}, u32[]{:S(2)}) collective-permute-start(bf16[64,1024]{1,0:T(8,128)(2,1)S(1)} %slice.19), channel_id=1, source_target_pairs={{0,8},{4,12},{8,0},{12,4},{16,24},{20,28},{24,16},{28,20},{1,9},{5... | collective-permute-start | bytes 393224 | tf_op jit(solution)/shard_map/ppermute | solution.py:365
  39.2 2.4 %collective-permute-start.13 = (bf16[384,1024]{1,0:T(8,128)(2,1)S(1)}, bf16[384,1024]{1,0:T(8,128)(2,1)S(1)}, u32[]{:S(2)}, u32[]{:S(2)}) collective-permute-start(bf16[384,1024]{1,0:T(8,128)(2,1)S(1)} %shard_map.93.errors), channel_id=1, source_target_pairs={{0,1},{1,0},{2,3},{3,2},{4,5},{5,4},{6,7},{7,6},{8,9},{9,8},{10,11... | collective-permute-start | bytes 2359304 | tf_op jit(solution)/shard_map/ppermute | solution.py:356
  39.3 8.9 %collective-permute-start.17 = (bf16[1024,384]{1,0:T(8,128)(2,1)S(1)}, bf16[1024,384]{1,0:T(8,128)(2,1)S(1)}, u32[]{:S(2)}, u32[]{:S(2)}) collective-permute-start(bf16[1024,384]{1,0:T(8,128)(2,1)S(1)} %get-tuple-element.28.normed), channel_id=1, source_target_pairs={{0,1},{1,0},{2,3},{3,2},{4,5},{5,4},{6,7},{7,6},{8,9},{9,8},{10,11... | collective-permute-start | bytes 2359304 | tf_op jit(solution)/shard_map/ppermute | solution.py:356
  39.8 8.4 %collective-permute-start.18 = (bf16[1024,384]{1,0:T(8,128)(2,1)S(1)}, bf16[1024,384]{1,0:T(8,128)(2,1)S(1)}, u32[]{:S(2)}, u32[]{:S(2)}) collective-permute-start(bf16[1024,384]{1,0:T(8,128)(2,1)S(1)} %get-tuple-element.29.far), channel_id=1, source_target_pairs={{0,1},{1,0},{2,3},{3,2},{4,5},{5,4},{6,7},{7,6},{8,9},{9,8},{10,11... | collective-permute-start | bytes 2359304 | tf_op jit(solution)/shard_map/ppermute | solution.py:356
  39.9 4.5 %collective-permute-start.15 = (bf16[384,512]{1,0:T(8,128)(2,1)S(1)}, bf16[384,512]{1,0:T(8,128)(2,1)S(1)}, u32[]{:S(2)}, u32[]{:S(2)}) collective-permute-start(bf16[384,512]{1,0:T(8,128)(2,1)S(1)} %get-tuple-element.25), channel_id=1, source_target_pairs={{0,1},{1,0},{2,3},{3,2},{4,5},{5,4},{6,7},{7,6},{8,9},{9,8},{10,11... | collective-permute-start | bytes 1179656 | tf_op jit(solution)/shard_map/ppermute | solution.py:356
  40.3 7.9 %collective-permute-start.16 = (bf16[384,512]{1,0:T(8,128)(2,1)S(1)}, bf16[384,512]{1,0:T(8,128)(2,1)S(1)}, u32[]{:S(2)}, u32[]{:S(2)}) collective-permute-start(bf16[384,512]{1,0:T(8,128)(2,1)S(1)} %get-tuple-element.27), channel_id=1, source_target_pairs={{0,1},{1,0},{2,3},{3,2},{4,5},{5,4},{6,7},{7,6},{8,9},{9,8},{10,11... | collective-permute-start | bytes 1179656 | tf_op jit(solution)/shard_map/ppermute | solution.py:356
  42.1 7.8 %collective-permute-start.20 = (bf16[768,128]{1,0:T(8,128)(2,1)S(1)}, bf16[768,128]{1,0:T(8,128)(2,1)S(1)}, u32[]{:S(2)}, u32[]{:S(2)}) collective-permute-start(bf16[768,128]{1,0:T(8,128)(2,1)S(1)} %shard_map.96), channel_id=1, source_target_pairs={{0,2},{1,3},{2,0},{3,1},{4,6},{5,7},{6,4},{7,5},{8,10},{9,11},{10,... | collective-permute-start | bytes 589832 | tf_op jit(solution)/shard_map/ppermute | solution.py:359
  44.4 9.0 %collective-permute-start.19 = (bf16[768,128]{1,0:T(8,128)(2,1)S(1)}, bf16[768,128]{1,0:T(8,128)(2,1)S(1)}, u32[]{:S(2)}, u32[]{:S(2)}) collective-permute-start(bf16[768,128]{1,0:T(8,128)(2,1)S(1)} %get-tuple-element.30), channel_id=1, source_target_pairs={{0,2},{1,3},{2,0},{3,1},{4,6},{5,7},{6,4},{7,5},{8,10},{9,11},{10,... | collective-permute-start | bytes 589832 | tf_op jit(solution)/shard_map/ppermute | solution.py:359
  51.1 12.8 %collective-permute-start.25 = (bf16[1024,128]{1,0:T(8,128)(2,1)S(1)}, bf16[1024,128]{1,0:T(8,128)(2,1)S(1)}, u32[]{:S(2)}, u32[]{:S(2)}) collective-permute-start(bf16[1024,128]{1,0:T(8,128)(2,1)S(1)} %shard_map.97.rest_0_.refs_1_), channel_id=1, source_target_pairs={{0,4},{4,0},{8,12},{12,8},{16,20},{20,16},{24,28},{28,24},{1,5},{5... | collective-permute-start | bytes 786440 | tf_op jit(solution)/shard_map/ppermute | solution.py:362
  54.5 11.6 %collective-permute-start.21 = (bf16[1024,128]{1,0:T(8,128)(2,1)S(1)}, bf16[1024,128]{1,0:T(8,128)(2,1)S(1)}, u32[]{:S(2)}, u32[]{:S(2)}) collective-permute-start(bf16[1024,128]{1,0:T(8,128)(2,1)S(1)} %shard_map.98.refs_2_), channel_id=1, source_target_pairs={{0,4},{4,0},{8,12},{12,8},{16,20},{20,16},{24,28},{28,24},{1,5},{5... | collective-permute-start | bytes 786440 | tf_op jit(solution)/shard_map/ppermute | solution.py:362
  56.0 7.8 %collective-permute-start.24 = (bf16[768,128]{1,0:T(8,128)(2,1)S(1)}, bf16[768,128]{1,0:T(8,128)(2,1)S(1)}, u32[]{:S(2)}, u32[]{:S(2)}) collective-permute-start(bf16[768,128]{1,0:T(8,128)(2,1)S(1)} %get-tuple-element.31), channel_id=1, source_target_pairs={{0,2},{1,3},{2,0},{3,1},{4,6},{5,7},{6,4},{7,5},{8,10},{9,11},{10,... | collective-permute-start | bytes 589832 | tf_op jit(solution)/shard_map/ppermute | solution.py:359
  56.6 9.4 %collective-permute-start.14 = (bf16[768,128]{1,0:T(8,128)(2,1)S(1)}, bf16[768,128]{1,0:T(8,128)(2,1)S(1)}, u32[]{:S(2)}, u32[]{:S(2)}) collective-permute-start(bf16[768,128]{1,0:T(8,128)(2,1)S(1)} %get-tuple-element.23), channel_id=1, source_target_pairs={{0,2},{1,3},{2,0},{3,1},{4,6},{5,7},{6,4},{7,5},{8,10},{9,11},{10,... | collective-permute-start | bytes 589832 | tf_op jit(solution)/shard_map/ppermute | solution.py:359
  65.0 8.6 %collective-permute-start.26 = (bf16[1024,128]{1,0:T(8,128)(2,1)S(1)}, bf16[1024,128]{1,0:T(8,128)(2,1)S(1)}, u32[]{:S(2)}, u32[]{:S(2)}) collective-permute-start(bf16[1024,128]{1,0:T(8,128)(2,1)S(1)} %shard_map.100.refs_1_), channel_id=1, source_target_pairs={{0,4},{4,0},{8,12},{12,8},{16,20},{20,16},{24,28},{28,24},{1,5},{5... | collective-permute-start | bytes 786440 | tf_op jit(solution)/shard_map/ppermute | solution.py:362
  67.2 9.2 %collective-permute-start.22 = (bf16[1024,128]{1,0:T(8,128)(2,1)S(1)}, bf16[1024,128]{1,0:T(8,128)(2,1)S(1)}, u32[]{:S(2)}, u32[]{:S(2)}) collective-permute-start(bf16[1024,128]{1,0:T(8,128)(2,1)S(1)} %shard_map.99.refs_1_), channel_id=1, source_target_pairs={{0,4},{4,0},{8,12},{12,8},{16,20},{20,16},{24,28},{28,24},{1,5},{5... | collective-permute-start | bytes 786440 | tf_op jit(solution)/shard_map/ppermute | solution.py:362
  68.3 11.0 %collective-permute-start.28 = (bf16[1024,128]{1,0:T(8,128)(2,1)S(1)}, bf16[1024,128]{1,0:T(8,128)(2,1)S(1)}, u32[]{:S(2)}, u32[]{:S(2)}) collective-permute-start(bf16[1024,128]{1,0:T(8,128)(2,1)S(1)} %collective-permute-done.25.rest_0_.refs_3_), channel_id=1, source_target_pairs={{0,8},{4,28},{8,16},{12,4},{16,24},{20,12},{24,0},{28,20},{1,9},{5... | collective-permute-start | bytes 786440 | tf_op jit(solution)/shard_map/ppermute | solution.py:369
  68.7 16.2 %collective-permute-start.29 = (bf16[1024,128]{1,0:T(8,128)(2,1)S(1)}, bf16[1024,128]{1,0:T(8,128)(2,1)S(1)}, u32[]{:S(2)}, u32[]{:S(2)}) collective-permute-start(bf16[1024,128]{1,0:T(8,128)(2,1)S(1)} %collective-permute-done.21.rest_0_.refs_4_), channel_id=1, source_target_pairs={{0,8},{4,28},{8,16},{12,4},{16,24},{20,12},{24,0},{28,20},{1,9},{5... | collective-permute-start | bytes 786440 | tf_op jit(solution)/shard_map/ppermute | solution.py:369
  73.6 16.1 %collective-permute-start.27 = (bf16[1024,128]{1,0:T(8,128)(2,1)S(1)}, bf16[1024,128]{1,0:T(8,128)(2,1)S(1)}, u32[]{:S(2)}, u32[]{:S(2)}) collective-permute-start(bf16[1024,128]{1,0:T(8,128)(2,1)S(1)} %collective-permute-done.26.refs_2_), channel_id=1, source_target_pairs={{0,8},{4,28},{8,16},{12,4},{16,24},{20,12},{24,0},{28,20},{1,9},{5... | collective-permute-start | bytes 786440 | tf_op jit(solution)/shard_map/ppermute | solution.py:369
  76.4 16.1 %collective-permute-start.23 = (bf16[1024,128]{1,0:T(8,128)(2,1)S(1)}, bf16[1024,128]{1,0:T(8,128)(2,1)S(1)}, u32[]{:S(2)}, u32[]{:S(2)}) collective-permute-start(bf16[1024,128]{1,0:T(8,128)(2,1)S(1)} %collective-permute-done.22.refs_2_), channel_id=1, source_target_pairs={{0,8},{4,28},{8,16},{12,4},{16,24},{20,12},{24,0},{28,20},{1,9},{5... | collective-permute-start | bytes 786440 | tf_op jit(solution)/shard_map/ppermute | solution.py:369
  (5 other events, 10.3 us)

commit v3 on v2

v3 whole, which is shorter than its diff:
```python
import functools
import math

import jax
import jax.numpy as jnp
from jax import lax
from jax.experimental import pallas as pl
from jax.experimental.pallas import tpu as pltpu
from jax.sharding import PartitionSpec as P

drift_stride = 0.5
f32 = jnp.float32
bf16 = jnp.bfloat16
smem = pl.BlockSpec(memory_space=pltpu.SMEM)


def matmul(left, right):
    return jnp.dot(left, right, preferred_element_type=f32)


def against_rows(left, right):
    return lax.dot_general(left, right, (((1,), (1,)), ((), ())), preferred_element_type=f32)


def limit(mebibytes):
    return pltpu.CompilerParams(vmem_limit_bytes=mebibytes * 1024 * 1024)


def cost(macs, nbytes):
    return pl.CostEstimate(flops=2 * macs, bytes_accessed=nbytes, transcendentals=0)


vmem = pl.BlockSpec(memory_space=pltpu.VMEM)
anywhere = pl.BlockSpec(memory_space=pl.ANY)


def shape(dims, dtype=bf16):
    return jax.ShapeDtypeStruct(dims, dtype)


def after(value, *earlier):
    return pl.pallas_call(
        lambda *refs: None,
        out_shape=shape(value.shape, value.dtype),
        in_specs=[anywhere] * (1 + len(earlier)),
        out_specs=anywhere,
        input_output_aliases={0: 0},
        compiler_params=limit(1),
    )(value, *earlier)


def share_kernel(value, out):
    rows = out.shape[0]
    place = lax.axis_index("rep") & 3
    out[...] = value[pl.ds(pl.multiple_of(place * rows, rows), rows)]


def share(value):
    return pl.pallas_call(
        share_kernel,
        out_shape=shape((value.shape[0] // 4, value.shape[1])),
        in_specs=[vmem],
        out_specs=vmem,
        compiler_params=limit(1),
        cost_estimate=cost(3 * 10**9, value.size),
    )(value)


def assemble_kernel(own, across, behind, upper, lower, out):
    rows = own.shape[0]
    half = rows // 2
    for place in range(4):

        @pl.when((lax.axis_index("rep") & 3) == place)
        def _():
            out[place * rows : (place + 1) * rows] = own[...]
            out[(place ^ 1) * rows : ((place ^ 1) + 1) * rows] = across[...]
            out[(place ^ 2) * rows : ((place ^ 2) + 1) * rows] = behind[...]
            out[(place ^ 3) * rows : (place ^ 3) * rows + half] = upper[...]
            out[(place ^ 3) * rows + half : ((place ^ 3) + 1) * rows] = lower[...]


def normalized(tokens):
    values = tokens.astype(f32)
    center = values - jnp.mean(values, axis=1, keepdims=True)
    spread = jnp.mean(center * center, axis=1, keepdims=True)
    return (center * lax.rsqrt(spread + 1e-05)).astype(bf16)


def gelu_both(values):
    coeff = math.sqrt(2.0 / math.pi)
    square = values * values
    gate = 0.5 + 0.5 * jnp.tanh(coeff * values * (1.0 + 0.044715 * square))
    hidden = values * gate
    slope = gate + hidden * (1.0 - gate) * (2.0 * coeff + 6.0 * 0.044715 * coeff * square)
    return hidden.astype(bf16), slope.astype(bf16)


def forward_core(tokens, weights_in, weights_out, normed_t, slopes, total, ready=None):
    count, width = tokens.shape
    block = weights_in[0].shape[1]
    tile = min(256, block)
    normed = normalized(tokens[...])
    normed_t[...] = normed.T
    for side in range(2):
        for at in range(0, block, tile):
            if ready is not None and side + at == 0:
                ready[0].wait()
            values = matmul(normed, weights_in[side][:, at : at + tile]) * (width**-0.5)
            hidden, slopes[side][:, at : at + tile] = gelu_both(values)
            if ready is not None and side + at == 0:
                ready[1].wait()
            term = matmul(hidden, weights_out[side][at : at + tile])
            if side + at == 0:
                total[...] = term
            else:
                total[...] += term


def forward_kernel(
    tokens_from, in_from, mate_in, out_from, mate_out, normed_t, slope, slope_mate, out, *scratch
):
    total, tokens, own_in, own_out, done = scratch
    copies = [
        pltpu.make_async_copy(source, target, done.at[at])
        for at, (source, target) in enumerate(
            ((tokens_from, tokens), (in_from, own_in), (out_from, own_out))
        )
    ]
    for copy in copies:
        copy.start()
    copies[0].wait()
    weights = (own_in, mate_in), (own_out, mate_out)
    forward_core(tokens, *weights, normed_t, (slope, slope_mate), total, copies[1:])
    out[...] = total[...].astype(bf16)


def forward_far_kernel(*refs):
    pieces = refs[:5]
    own_in, mate_in, own_out, mate_out, normed_t, slope, slope_mate = refs[5:12]
    out, total, tokens = refs[12:]
    assemble_kernel(*pieces, tokens)
    weights = (own_in, mate_in), (own_out, mate_out)
    forward_core(tokens, *weights, normed_t, (slope, slope_mate), total)
    count = tokens.shape[0]
    values = tokens[...].astype(f32)
    ahead = pltpu.roll(values, count - 1, 0)
    rank = lax.broadcasted_iota(jnp.int32, values.shape, 0)
    base = total[...] + values - ahead
    out[...] = jnp.where(rank == count - 1, 0.0, base)


def forward(given, count, weights, far):
    width, block = weights[0].shape
    outs = (
        shape((width, count)),
        shape((count, block)),
        shape((count, block)),
        shape((count, width), f32 if far else bf16),
    )
    scratch = [pltpu.VMEM((count, width), f32), pltpu.VMEM((count, width), bf16)]
    specs = [vmem] * (len(given) + len(weights))
    if not far:
        specs = [anywhere, anywhere, vmem, anywhere, vmem]
        scratch += [pltpu.VMEM(value.shape, bf16) for value in (weights[0], weights[2])]
        scratch.append(pltpu.SemaphoreType.DMA((3,)))
    return pl.pallas_call(
        forward_far_kernel if far else forward_kernel,
        out_shape=outs,
        in_specs=specs,
        out_specs=[vmem for out in outs],
        scratch_shapes=scratch,
        compiler_params=limit(20),
        cost_estimate=cost(4 * count * width * block, 8 * width * block),
    )(*given, *weights)


def errors_kernel(base, sent, *refs):
    errors = refs[-1]
    result = base[...] + sent[...].astype(f32)
    rank = lax.broadcasted_iota(jnp.int32, result.shape, 0)
    errors[...] = jnp.where(rank == result.shape[0] - 1, 0.0, result).astype(bf16)


def errors_of(base, sent, *earlier):
    return pl.pallas_call(
        errors_kernel,
        out_shape=shape(base.shape),
        in_specs=[vmem, vmem] + [anywhere] * len(earlier),
        out_specs=vmem,
        compiler_params=limit(8),
        cost_estimate=cost(0, 8 * base.size),
    )(base, sent, *earlier)


def hidden_kernel(errors, weight, slope, *refs):
    out = refs[-1]
    tile = min(256, weight.shape[0])
    for at in range(0, weight.shape[0], tile):
        cols = slice(at, at + tile)
        product = against_rows(errors[...], weight[cols]) * slope[:, cols].astype(f32)
        out[:, cols] = product.astype(bf16)


def hidden_of(errors, weight, slope, *earlier):
    count, width = errors.shape
    block = weight.shape[0]
    return pl.pallas_call(
        hidden_kernel,
        out_shape=shape((count, block)),
        in_specs=[vmem] * 3 + [anywhere] * len(earlier),
        out_specs=vmem,
        compiler_params=limit(8),
        cost_estimate=cost(count * width * block, 2 * width * block),
    )(errors, weight, slope, *earlier)


def update_kernel(start, heat, *refs):
    grads, normed = refs[:4], refs[4:8]
    params, noise = refs[8:10]
    out = refs[-1]
    here = slice(start, start + out.shape[0])
    total = 0.0
    for values, grad in zip(normed, grads):
        total += matmul(values[here], grad[...])
    current = params[0, here].astype(f32)
    strength = jnp.sqrt(jnp.full((1, out.shape[1]), 2.0 * drift_stride * heat[0], f32))
    slope = total * params.shape[1] ** -0.5
    moved = current - drift_stride * (slope + current) + strength * noise[0, here].astype(f32)
    out[...] = moved.astype(bf16)


def update(start, rows, heat, grads, normed, params, noise, *earlier):
    width, count = normed[0].shape
    block = grads[0].shape[1]
    return pl.pallas_call(
        functools.partial(update_kernel, start),
        out_shape=shape((rows, block)),
        in_specs=[smem] + [vmem] * 10 + [anywhere] * len(earlier),
        out_specs=vmem,
        compiler_params=limit(4),
        cost_estimate=cost(4 * rows * count * block, 8 * rows * count),
    )(heat, *grads, *normed, params, noise, *earlier)


def role(mate, swapped):
    rank = lax.axis_index("rep")
    odd = rank & 1
    taken = swapped[0] == 1
    return odd, taken & (mate[0] == rank + 1 - 2 * odd), taken & (mate[0] == rank - 1 + 2 * odd)


def finish_kernel(start, stop, count, mate, swapped, *refs):
    own, across, beyond = (refs[i * count : (i + 1) * count] for i in range(3))
    result, gaps, out, done = refs[-4:]
    odd, near_taken, far_taken = role(mate, swapped)
    near_sum = far_sum = 0.0
    at = 0
    for part in range(count):
        mine, near, far = (pieces[part][...] for pieces in (own, across, beyond))
        out[at : at + mine.shape[0]] = jnp.where(near_taken, near, jnp.where(far_taken, far, mine))
        at += mine.shape[0]
        mine = mine.astype(f32)
        near = near.astype(f32) - mine
        far = far.astype(f32) - mine
        near_sum += jnp.sum(near * near, axis=0, keepdims=True)
        far_sum += jnp.sum(far * far, axis=0, keepdims=True)
    copy = pltpu.make_async_copy(out, result.at[0, pl.ds(start, stop - start)], done)
    copy.start()
    if start > 0:
        so_far = refs[3 * count]
        near_sum += so_far[0, 0:1]
        far_sum += so_far[0, 1:2]
    if stop == result.shape[1]:
        near_sum *= 1.0 / result.shape[1]
        far_sum *= 1.0 / result.shape[1]
        near_sum, far_sum = (
            jnp.where(odd == 1, near_sum, far_sum),
            jnp.where(odd == 1, far_sum, near_sum),
        )
    gaps[0, 0:1] = near_sum
    gaps[0, 1:2] = far_sum
    copy.wait()


def finish(width, start, pairing, own, across, beyond, so_far):
    count = len(own)
    block = own[0].shape[1]
    stop = start + sum(value.shape[0] for value in own)
    given = [*own, *across, *beyond]
    specs = [vmem] * len(given)
    aliases = {}
    if start > 0:
        given += [so_far[1], so_far[0]]
        specs += [vmem, anywhere]
        aliases = {1 + len(given): 0}
    return pl.pallas_call(
        functools.partial(finish_kernel, start, stop, count),
        out_shape=(shape((1, width, block)), shape((1, 2, block), f32)),
        in_specs=[smem, smem] + specs,
        out_specs=(anywhere, vmem),
        scratch_shapes=[pltpu.VMEM((stop - start, block), bf16), pltpu.SemaphoreType.DMA],
        input_output_aliases=aliases,
        compiler_params=limit(4),
        cost_estimate=cost(0, 8 * (stop - start) * block),
    )(*pairing, *given)


def body(
    residual_flow,
    rooted_input_matrix,
    chain_normal_draws,
    output_matrix,
    chain_heat,
    matched_chain,
    swap_mask,
):
    replicas = lax.axis_size("rep")
    params = rooted_input_matrix[0]
    block = params.shape[1]
    count = residual_flow.shape[0]

    def to_core(value):
        return lax.ppermute(value, "dp", [(i, i ^ 1) for i in range(4)])

    def to_chip(value):
        return lax.ppermute(value, "dp", [(i, i ^ 2) for i in range(4)])

    def to_mate(value):
        return lax.ppermute(value, "rep", [(i, i ^ 1) for i in range(replicas)])

    def to_pair(value):
        return lax.ppermute(value, "rep", [(i, i ^ 2) for i in range(replicas)])

    def to_next(value):
        pairs = [(i, (i + (2 if i % 2 == 0 else -2)) % replicas) for i in range(replicas)]
        return lax.ppermute(value, "rep", pairs)

    def step_one(own):
        return to_mate(own), to_pair(own)

    def step_two(own, across, behind):
        half = own.shape[0] // 2
        return own, across, behind, to_mate(behind[:half]), to_pair(across[half:])

    mate_in = to_core(params)
    mate_out = to_core(output_matrix)
    token_own = to_chip(share(residual_flow))
    weights = (params, mate_in, output_matrix, mate_out)
    normed, slope, slope_send, part = forward((residual_flow,), count, weights, False)
    sent = to_chip(after(part, token_own))
    token_own = after(token_own, part)
    token_across, token_behind = step_one(token_own)
    token_pieces = step_two(token_own, token_across, token_behind)
    normed_mate = to_core(normed)
    slope_mate = to_core(slope_send)
    far, far_slope, far_slope_send, base = forward(token_pieces, count, weights, True)
    far_mate = to_core(far)
    far_slope_mate = to_core(far_slope_send)

    errors = errors_of(base, sent, normed_mate, slope_mate)
    back = to_chip(errors)
    far_grads = [
        hidden_of(errors, output_matrix, far_slope),
        hidden_of(to_core(errors), output_matrix, far_slope_mate),
    ]
    back = after(back, *far_grads, far_mate)
    near_grads = [
        hidden_of(back, output_matrix, slope),
        hidden_of(to_core(back), output_matrix, slope_mate),
    ]
    grads = near_grads + far_grads

    pairing = (matched_chain, swap_mask)
    width = params.shape[0]
    sizes = [width * part // 8 for part in (1, 2, 2, 2, 1)]
    starts = [sum(sizes[:chunk]) for chunk in range(len(sizes))]
    own, across, beyond = [], [], []
    for chunk, (start, rows) in enumerate(zip(starts, sizes)):
        fresh = update(
            start,
            rows,
            chain_heat,
            grads,
            (normed, normed_mate, far, far_mate),
            rooted_input_matrix,
            chain_normal_draws,
            *own[-1:],
        )
        if chunk >= 2:
            fresh = after(fresh, across[chunk - 2])
        own.append(fresh)
        across.append(to_mate(fresh))
    done = None
    cut = len(sizes) - 1
    for first, stop in ((0, cut), (cut, cut + 1)):
        for chunk in range(first, stop):
            if chunk >= 2:
                across[chunk] = after(across[chunk], beyond[chunk - 2])
            beyond.append(to_next(across[chunk]))
        given = (pieces[first:stop] for pieces in (own, across, beyond))
        done = finish(width, starts[first], pairing, *given, done)
    return done


def solution(mesh):
    placed = (
        P("dp", None),
        P("rep", None, "dp"),
        P("rep", None, "dp"),
        P("dp", None),
        P("rep"),
        P("rep"),
        P("rep"),
    )
    return jax.shard_map(
        body,
        mesh=mesh,
        in_specs=placed,
        out_specs=(P("rep", None, "dp"), P("rep", None, "dp")),
        check_vma=False,
    )
```

time: 94.1 us -> 91.3 us (0.970)
  Pallas kernels: 19 us -> 15.2 us
  waiting for transfers between devices: 38 us -> 41 us
  local copies, waits for them, and re-layouts: 3.68 us -> 1.25 us
    ppermute x7 -> x3, waiting for transfers between devices: 10.6 us -> 18.6 us  [to_chip(): return lax.ppermute(value, 'dp', [(i, i ^ 2) for i in range(4)])]
    pallas_call x15, Pallas kernels: 19 us -> 15.2 us  [the longest x2 6.55 us: forward(): pl.pallas_call(forward_far_kernel if far else forward_kernel, out_shape=o...]
    ppermute x4 -> x5, waiting for transfers between devices: 11.2 us -> 7.46 us  [to_next(): return lax.ppermute(value, 'rep', pairs)]
    ppermute x4 -> x5, starting transfers between devices: 3.89 us -> 7.01 us  [to_next(): return lax.ppermute(value, 'rep', pairs)]
    ppermute x8 -> x7, starting transfers between devices: 9.9 us -> 12.8 us  [to_mate(): return lax.ppermute(value, 'rep', [(i, i ^ 1) for i in range(replicas)])]
    ppermute x7 -> x3, starting transfers between devices: 9.17 us -> 6.5 us  [to_chip(): return lax.ppermute(value, 'dp', [(i, i ^ 2) for i in range(4)])]
    unnamed x15 -> x11, local copies, waits for them, and re-layouts: 3.65 us -> 1.24 us
    ppermute x4 -> x2, waiting for transfers between devices: 7.43 us -> 5.08 us  [to_pair(): return lax.ppermute(value, 'rep', [(i, i ^ 2) for i in range(replicas)])]
  transfers between devices with their start and end apart: 30 -> 25, of which waited for: 18 -> 16; matrix products, arithmetic and copies ran while one was open for 0% -> 0% of each run, Pallas kernels for 19% -> 14%
where the time goes in v3:
time: 91.3 us; the launch traced here: 91.1 us
  waiting for transfers between devices  41 us (45%)
  starting transfers between devices  30.8 us (34%)
  Pallas kernels  15.2 us (17%)
  between operations  2.8 us (3%)
  local copies, waits for them, and re-layouts  1.25 us (1%)
    ppermute x3, waiting for transfers between devices, to_chip(): return lax.ppermute(value, 'dp', [(i, i ^ 2) for i in range(4)])  18.6 us
    ppermute x7, starting transfers between devices, to_mate(): return lax.ppermute(value, 'rep', [(i, i ^ 1) for i in range(replicas)])  12.8 us
    ppermute x7, waiting for transfers between devices, to_mate(): return lax.ppermute(value, 'rep', [(i, i ^ 1) for i in range(replicas)])  7.72 us
    ppermute x5, waiting for transfers between devices, to_next(): return lax.ppermute(value, 'rep', pairs)  7.46 us
    ppermute x5, starting transfers between devices, to_next(): return lax.ppermute(value, 'rep', pairs)  7.01 us
    pallas_call x2, Pallas kernels, forward(): pl.pallas_call(forward_far_kernel if far else forward_kernel, out_shape=o...  6.55 us
    ppermute x3, starting transfers between devices, to_chip(): return lax.ppermute(value, 'dp', [(i, i ^ 2) for i in range(4)])  6.5 us
    ppermute x2, waiting for transfers between devices, to_pair(): return lax.ppermute(value, 'rep', [(i, i ^ 2) for i in range(replicas)])  5.08 us
  transfers between devices with their start and end apart: 25, of which 16 were waited for; matrix products, arithmetic and copies ran while one was open for 0% of the time, Pallas kernels for 14%

profile of v3, /device:TPU:0, one launch (start us, length us, event | category | flops | bytes accessed | tf_op | source)
XLA Modules:
  0.0 91.1 jit_solution(3053048256670925426)
XLA Ops:
  1.2 1.2 %copy-done.3 = bf16[384,1024]{1,0:T(8,128)(2,1)S(1)} copy-done((bf16[384,1024]{1,0:T(8,128)(2,1)S(1)}, bf16[384,1024]{1,0:T(8,128)(2,1)}, u32[]{:S(2)}) %copy-start.3) | copy-done | bytes 786456
  2.4 3.0 %collective-permute-start = (bf16[96,1024]{1,0:T(8,128)(2,1)S(1)}, bf16[96,1024]{1,0:T(8,128)(2,1)S(1)}, u32[]{:S(2)}, u32[]{:S(2)}) collective-permute-start(bf16[96,1024]{1,0:T(8,128)(2,1)S(1)} %shard_map.86), channel_id=1, source_target_pairs={{0,2},{1,3},{2,0},{3,1},{4,6},{5,7},{6,4},{7,5},{8,10},{9,11},{10,... | collective-permute-start | bytes 589832 | tf_op jit(solution)/shard_map/ppermute | solution.py:327
  5.5 3.6 %shard_map.87 = (bf16[1024,384]{1,0:T(8,128)(2,1)S(1)}, bf16[384,512]{1,0:T(8,128)(2,1)S(1)}, bf16[384,512]{1,0:T(8,128)(2,1)S(1)}, bf16[384,1024]{1,0:T(8,128)(2,1)S(1)}) custom-call(bf16[384,1024]{1,0:T(8,128)(2,1)S(1)} %copy-done.4, bf16[1024,512]{1,0:T(8,128)(2,1)S(1)} %bitcast.2, bf16[1024,512]{1,0:T(8,128)(2,1)S(1)} %collective-permute-done.1.mate_in.refs_6_, ...), custom_call_target="tpu_custom_call" | custom-call | flops 1610612736 | bytes 4194304 | tf_op jit(solution)/shard_map/pallas_call | solution.py:167
  9.3 1.2 %collective-permute-done.refs_0_.refs_1_ = bf16[96,1024]{1,0:T(8,128)(2,1)S(1)} collective-permute-done((bf16[96,1024]{1,0:T(8,128)(2,1)S(1)}, bf16[96,1024]{1,0:T(8,128)(2,1)S(1)}, u32[]{:S(2)}, u32[]{:S(2)}) %collective-permute-start) | collective-permute-done | bytes 196640 | tf_op jit(solution)/shard_map/ppermute | solution.py:327
  10.6 1.7 %collective-permute-start.7 = (bf16[384,1024]{1,0:T(8,128)(2,1)S(1)}, bf16[384,1024]{1,0:T(8,128)(2,1)S(1)}, u32[]{:S(2)}, u32[]{:S(2)}) collective-permute-start(bf16[384,1024]{1,0:T(8,128)(2,1)S(1)} %shard_map.90), channel_id=1, source_target_pairs={{0,2},{1,3},{2,0},{3,1},{4,6},{5,7},{6,4},{7,5},{8,10},{9,11},{10,... | collective-permute-start | bytes 2359304 | tf_op jit(solution)/shard_map/ppermute | solution.py:327
  12.3 1.6 %collective-permute-start.4 = (bf16[96,1024]{1,0:T(8,128)(2,1)S(1)}, bf16[96,1024]{1,0:T(8,128)(2,1)S(1)}, u32[]{:S(2)}, u32[]{:S(2)}) collective-permute-start(bf16[96,1024]{1,0:T(8,128)(2,1)S(1)} %shard_map.88.refs_0_), channel_id=1, source_target_pairs={{0,8},{4,12},{8,0},{12,4},{16,24},{20,28},{24,16},{28,20},{1,9},{5... | collective-permute-start | bytes 589832 | tf_op jit(solution)/shard_map/ppermute | solution.py:333
  13.9 1.5 %collective-permute-start.3 = (bf16[96,1024]{1,0:T(8,128)(2,1)S(1)}, bf16[96,1024]{1,0:T(8,128)(2,1)S(1)}, u32[]{:S(2)}, u32[]{:S(2)}) collective-permute-start(bf16[96,1024]{1,0:T(8,128)(2,1)S(1)} %shard_map.88.refs_0_), channel_id=1, source_target_pairs={{0,4},{4,0},{8,12},{12,8},{16,20},{20,16},{24,28},{28,24},{1,5},{5... | collective-permute-start | bytes 589832 | tf_op jit(solution)/shard_map/ppermute | solution.py:330
  15.4 3.5 %collective-permute-done.4.refs_2_ = bf16[96,1024]{1,0:T(8,128)(2,1)S(1)} collective-permute-done((bf16[96,1024]{1,0:T(8,128)(2,1)S(1)}, bf16[96,1024]{1,0:T(8,128)(2,1)S(1)}, u32[]{:S(2)}, u32[]{:S(2)}) %collective-permute-start.4) | collective-permute-done | bytes 196640 | tf_op jit(solution)/shard_map/ppermute | solution.py:333
  18.9 1.6 %collective-permute-start.5 = (bf16[48,1024]{1,0:T(8,128)(2,1)S(1)}, bf16[48,1024]{1,0:T(8,128)(2,1)S(1)}, u32[]{:S(2)}, u32[]{:S(2)}) collective-permute-start(bf16[48,1024]{1,0:T(8,128)(2,1)S(1)} %slice.8), channel_id=1, source_target_pairs={{0,4},{4,0},{8,12},{12,8},{16,20},{20,16},{24,28},{28,24},{1,5},{5... | collective-permute-start | bytes 294920 | tf_op jit(solution)/shard_map/ppermute | solution.py:330
  20.5 1.6 %collective-permute-start.6 = (bf16[48,1024]{1,0:T(8,128)(2,1)S(1)}, bf16[48,1024]{1,0:T(8,128)(2,1)S(1)}, u32[]{:S(2)}, u32[]{:S(2)}) collective-permute-start(bf16[48,1024]{1,0:T(8,128)(2,1)S(1)} %slice.9), channel_id=1, source_target_pairs={{0,8},{4,12},{8,0},{12,4},{16,24},{20,28},{24,16},{28,20},{1,9},{5... | collective-permute-start | bytes 294920 | tf_op jit(solution)/shard_map/ppermute | solution.py:333
  22.1 1.5 %collective-permute-done.5.refs_3_ = bf16[48,1024]{1,0:T(8,128)(2,1)S(1)} collective-permute-done((bf16[48,1024]{1,0:T(8,128)(2,1)S(1)}, bf16[48,1024]{1,0:T(8,128)(2,1)S(1)}, u32[]{:S(2)}, u32[]{:S(2)}) %collective-permute-start.5) | collective-permute-done | bytes 98336 | tf_op jit(solution)/shard_map/ppermute | solution.py:330
  23.6 1.6 %collective-permute-done.6.refs_4_ = bf16[48,1024]{1,0:T(8,128)(2,1)S(1)} collective-permute-done((bf16[48,1024]{1,0:T(8,128)(2,1)S(1)}, bf16[48,1024]{1,0:T(8,128)(2,1)S(1)}, u32[]{:S(2)}, u32[]{:S(2)}) %collective-permute-start.6) | collective-permute-done | bytes 98336 | tf_op jit(solution)/shard_map/ppermute | solution.py:333
  25.1 2.9 %shard_map.89 = (bf16[1024,384]{1,0:T(8,128)(2,1)S(1)}, bf16[384,512]{1,0:T(8,128)(2,1)S(1)}, bf16[384,512]{1,0:T(8,128)(2,1)S(1)}, f32[384,1024]{1,0:T(8,128)S(1)}) custom-call(bf16[96,1024]{1,0:T(8,128)(2,1)S(1)} %shard_map.88.refs_0_, bf16[96,1024]{1,0:T(8,128)(2,1)S(1)} %collective-permute-done.3.refs_1_, ...), custom_call_target="tpu_custom_call" | custom-call | flops 1610612736 | bytes 4194304 | tf_op jit(solution)/shard_map/pallas_call | solution.py:167
  28.1 2.0 %collective-permute-done.7.sent = bf16[384,1024]{1,0:T(8,128)(2,1)S(1)} collective-permute-done((bf16[384,1024]{1,0:T(8,128)(2,1)S(1)}, bf16[384,1024]{1,0:T(8,128)(2,1)S(1)}, u32[]{:S(2)}, u32[]{:S(2)}) %collective-permute-start.7) | collective-permute-done | bytes 786464 | tf_op jit(solution)/shard_map/ppermute | solution.py:327
  30.8 1.7 %collective-permute-start.10 = (bf16[384,1024]{1,0:T(8,128)(2,1)S(1)}, bf16[384,1024]{1,0:T(8,128)(2,1)S(1)}, u32[]{:S(2)}, u32[]{:S(2)}) collective-permute-start(bf16[384,1024]{1,0:T(8,128)(2,1)S(1)} %shard_map.91.errors), channel_id=1, source_target_pairs={{0,2},{1,3},{2,0},{3,1},{4,6},{5,7},{6,4},{7,5},{8,10},{9,11},{10,... | collective-permute-start | bytes 2359304 | tf_op jit(solution)/shard_map/ppermute | solution.py:327
  33.1 1.1 %collective-permute-done.12.slope = bf16[384,512]{1,0:T(8,128)(2,1)S(1)} collective-permute-done((bf16[384,512]{1,0:T(8,128)(2,1)S(1)}, bf16[384,512]{1,0:T(8,128)(2,1)S(1)}, u32[]{:S(2)}, u32[]{:S(2)}) %collective-permute-start.12) | collective-permute-done | bytes 393248 | tf_op jit(solution)/shard_map/ppermute | solution.py:324
  34.9 15.4 %collective-permute-done.10.refs_0_ = bf16[384,1024]{1,0:T(8,128)(2,1)S(1)} collective-permute-done((bf16[384,1024]{1,0:T(8,128)(2,1)S(1)}, bf16[384,1024]{1,0:T(8,128)(2,1)S(1)}, u32[]{:S(2)}, u32[]{:S(2)}) %collective-permute-start.10) | collective-permute-done | bytes 786464 | tf_op jit(solution)/shard_map/ppermute | solution.py:327
  53.7 1.8 %collective-permute-start.15 = (bf16[128,512]{1,0:T(8,128)(2,1)S(1)}, bf16[128,512]{1,0:T(8,128)(2,1)S(1)}, u32[]{:S(2)}, u32[]{:S(2)}) collective-permute-start(bf16[128,512]{1,0:T(8,128)(2,1)S(1)} %shard_map.97.refs_10_.refs_0_), channel_id=1, source_target_pairs={{0,4},{4,0},{8,12},{12,8},{16,20},{20,16},{24,28},{28,24},{1,5},{5... | collective-permute-start | bytes 393224 | tf_op jit(solution)/shard_map/ppermute | solution.py:330
  57.4 2.4 %collective-permute-done.15.refs_1_.refs_4_ = bf16[128,512]{1,0:T(8,128)(2,1)S(1)} collective-permute-done((bf16[128,512]{1,0:T(8,128)(2,1)S(1)}, bf16[128,512]{1,0:T(8,128)(2,1)S(1)}, u32[]{:S(2)}, u32[]{:S(2)}) %collective-permute-start.15) | collective-permute-done | bytes 131104 | tf_op jit(solution)/shard_map/ppermute | solution.py:330
  59.8 2.0 %collective-permute-start.17 = (bf16[256,512]{1,0:T(8,128)(2,1)S(1)}, bf16[256,512]{1,0:T(8,128)(2,1)S(1)}, u32[]{:S(2)}, u32[]{:S(2)}) collective-permute-start(bf16[256,512]{1,0:T(8,128)(2,1)S(1)} %shard_map.100.refs_10_.refs_2_), channel_id=1, source_target_pairs={{0,4},{4,0},{8,12},{12,8},{16,20},{20,16},{24,28},{28,24},{1,5},{5... | collective-permute-start | bytes 786440 | tf_op jit(solution)/shard_map/ppermute | solution.py:330
  61.8 1.6 %collective-permute-start.19 = (bf16[128,512]{1,0:T(8,128)(2,1)S(1)}, bf16[128,512]{1,0:T(8,128)(2,1)S(1)}, u32[]{:S(2)}, u32[]{:S(2)}) collective-permute-start(bf16[128,512]{1,0:T(8,128)(2,1)S(1)} %collective-permute-done.15.refs_1_.refs_4_), channel_id=1, source_target_pairs={{0,8},{4,28},{8,16},{12,4},{16,24},{20,12},{24,0},{28,20},{1,9},{5... | collective-permute-start | bytes 393224 | tf_op jit(solution)/shard_map/ppermute | solution.py:337
  64.2 1.3 %collective-permute-done.16.refs_1_.refs_5_ = bf16[256,512]{1,0:T(8,128)(2,1)S(1)} collective-permute-done((bf16[256,512]{1,0:T(8,128)(2,1)S(1)}, bf16[256,512]{1,0:T(8,128)(2,1)S(1)}, u32[]{:S(2)}, u32[]{:S(2)}) %collective-permute-start.16) | collective-permute-done | bytes 262176 | tf_op jit(solution)/shard_map/ppermute | solution.py:330
  65.5 1.9 %collective-permute-start.22 = (bf16[256,512]{1,0:T(8,128)(2,1)S(1)}, bf16[256,512]{1,0:T(8,128)(2,1)S(1)}, u32[]{:S(2)}, u32[]{:S(2)}) collective-permute-start(bf16[256,512]{1,0:T(8,128)(2,1)S(1)} %shard_map.102.refs_10_.refs_3_), channel_id=1, source_target_pairs={{0,4},{4,0},{8,12},{12,8},{16,20},{20,16},{24,28},{28,24},{1,5},{5... | collective-permute-start | bytes 786440 | tf_op jit(solution)/shard_map/ppermute | solution.py:330
  67.4 1.6 %collective-permute-start.23 = (bf16[256,512]{1,0:T(8,128)(2,1)S(1)}, bf16[256,512]{1,0:T(8,128)(2,1)S(1)}, u32[]{:S(2)}, u32[]{:S(2)}) collective-permute-start(bf16[256,512]{1,0:T(8,128)(2,1)S(1)} %collective-permute-done.16.refs_1_.refs_5_), channel_id=1, source_target_pairs={{0,8},{4,28},{8,16},{12,4},{16,24},{20,12},{24,0},{28,20},{1,9},{5... | collective-permute-start | bytes 786440 | tf_op jit(solution)/shard_map/ppermute | solution.py:337
  69.5 1.6 %collective-permute-done.17.refs_1_.refs_0_ = bf16[256,512]{1,0:T(8,128)(2,1)S(1)} collective-permute-done((bf16[256,512]{1,0:T(8,128)(2,1)S(1)}, bf16[256,512]{1,0:T(8,128)(2,1)S(1)}, u32[]{:S(2)}, u32[]{:S(2)}) %collective-permute-start.17) | collective-permute-done | bytes 262176 | tf_op jit(solution)/shard_map/ppermute | solution.py:330
  71.1 1.9 %collective-permute-start.20 = (bf16[256,512]{1,0:T(8,128)(2,1)S(1)}, bf16[256,512]{1,0:T(8,128)(2,1)S(1)}, u32[]{:S(2)}, u32[]{:S(2)}) collective-permute-start(bf16[256,512]{1,0:T(8,128)(2,1)S(1)} %shard_map.105.refs_6_), channel_id=1, source_target_pairs={{0,8},{4,28},{8,16},{12,4},{16,24},{20,12},{24,0},{28,20},{1,9},{5... | collective-permute-start | bytes 786440 | tf_op jit(solution)/shard_map/ppermute | solution.py:337
  73.1 3.6 %collective-permute-start.18 = (bf16[128,512]{1,0:T(8,128)(2,1)S(1)}, bf16[128,512]{1,0:T(8,128)(2,1)S(1)}, u32[]{:S(2)}, u32[]{:S(2)}) collective-permute-start(bf16[128,512]{1,0:T(8,128)(2,1)S(1)} %shard_map.104.refs_0_), channel_id=1, source_target_pairs={{0,4},{4,0},{8,12},{12,8},{16,20},{20,16},{24,28},{28,24},{1,5},{5... | collective-permute-start | bytes 393224 | tf_op jit(solution)/shard_map/ppermute | solution.py:330
  76.8 1.9 %collective-permute-start.24 = (bf16[256,512]{1,0:T(8,128)(2,1)S(1)}, bf16[256,512]{1,0:T(8,128)(2,1)S(1)}, u32[]{:S(2)}, u32[]{:S(2)}) collective-permute-start(bf16[256,512]{1,0:T(8,128)(2,1)S(1)} %shard_map.107.refs_7_), channel_id=1, source_target_pairs={{0,8},{4,28},{8,16},{12,4},{16,24},{20,12},{24,0},{28,20},{1,9},{5... | collective-permute-start | bytes 786440 | tf_op jit(solution)/shard_map/ppermute | solution.py:337
  79.6 2.8 %collective-permute-done.20.refs_1_.refs_10_ = bf16[256,512]{1,0:T(8,128)(2,1)S(1)} collective-permute-done((bf16[256,512]{1,0:T(8,128)(2,1)S(1)}, bf16[256,512]{1,0:T(8,128)(2,1)S(1)}, u32[]{:S(2)}, u32[]{:S(2)}) %collective-permute-start.20) | collective-permute-done | bytes 262176 | tf_op jit(solution)/shard_map/ppermute | solution.py:337
  83.7 4.3 %collective-permute-done.24.refs_11_ = bf16[256,512]{1,0:T(8,128)(2,1)S(1)} collective-permute-done((bf16[256,512]{1,0:T(8,128)(2,1)S(1)}, bf16[256,512]{1,0:T(8,128)(2,1)S(1)}, u32[]{:S(2)}, u32[]{:S(2)}) %collective-permute-start.24) | collective-permute-done | bytes 262176 | tf_op jit(solution)/shard_map/ppermute | solution.py:337
  88.0 1.5 %shard_map.108 = (bf16[1,1024,512]{2,1,0:T(8,128)(2,1)}, f32[1,2,512]{2,1,0:T(2,128)S(1)}) custom-call(s32[1]{0:T(128)S(6)} %copy.30.mate, s32[1]{0:T(128)S(6)} %copy.31.swapped, bf16[128,512]{1,0:T(8,128)(2,1)S(1)} %shard_map.97.refs_10_.refs_0_, bf16[256,512]{1,0:T(8,128)(2,1)S(1)} %shard_map.98.refs_10_.refs_1_, ...), custom_call_target="tpu_custom_call" | custom-call | bytes 3670016 | tf_op jit(solution)/shard_map/pallas_call | solution.py:297
  89.8 1.3 %shard_map.109 = (bf16[1,1024,512]{2,1,0:T(8,128)(2,1)}, f32[1,2,512]{2,1,0:T(2,128)}) custom-call(s32[1]{0:T(128)S(6)} %copy.30.mate, s32[1]{0:T(128)S(6)} %copy.31.swapped, bf16[128,512]{1,0:T(8,128)(2,1)S(1)} %shard_map.104.refs_0_, bf16[128,512]{1,0:T(8,128)(2,1)S(1)} %shard_map.106.refs_1_, ...), custom_call_target="tpu_custom_call", output_to_operand_aliasing={{0}: (6, {})} | custom-call | bytes 524288 | tf_op jit(solution)/shard_map/pallas_call | solution.py:297
  (55 shorter events, 9.9 us)
Async XLA Ops:
  0.6 4.8 %copy-start = (bf16[1,1024,512]{2,1,0:T(8,128)(2,1)S(1)}, bf16[1,1024,512]{2,1,0:T(8,128)(2,1)}, u32[]{:S(2)}) copy-start(bf16[1,1024,512]{2,1,0:T(8,128)(2,1)} %refs_8_.9) | copy-start | bytes 3145732
  0.6 4.8 %copy-start.2 = (bf16[512,1024]{1,0:T(8,128)(2,1)S(1)}, bf16[512,1024]{1,0:T(8,128)(2,1)}, u32[]{:S(2)}) copy-start(bf16[512,1024]{1,0:T(8,128)(2,1)} %weight.7) | copy-start | bytes 3145732
  0.6 4.8 %collective-permute-start.1 = (bf16[1024,512]{1,0:T(8,128)(2,1)}, bf16[1024,512]{1,0:T(8,128)(2,1)S(1)}, u32[]{:S(2)}, u32[]{:S(2)}) collective-permute-start(bf16[1024,512]{1,0:T(8,128)(2,1)} %bitcast.1), channel_id=1, source_target_pairs={{0,1},{1,0},{2,3},{3,2},{4,5},{5,4},{6,7},{7,6},{8,9},{9,8},{10,11... | collective-permute-start | bytes 3145736 | tf_op jit(solution)/shard_map/ppermute | solution.py:324
  1.2 4.3 %collective-permute-start.2 = (bf16[512,1024]{1,0:T(8,128)(2,1)}, bf16[512,1024]{1,0:T(8,128)(2,1)S(1)}, u32[]{:S(2)}, u32[]{:S(2)}) collective-permute-start(bf16[512,1024]{1,0:T(8,128)(2,1)} %weight.7), channel_id=1, source_target_pairs={{0,1},{1,0},{2,3},{3,2},{4,5},{5,4},{6,7},{7,6},{8,9},{9,8},{10,11... | collective-permute-start | bytes 3145736 | tf_op jit(solution)/shard_map/ppermute | solution.py:324
  1.2 1.2 %copy-start.3 = (bf16[384,1024]{1,0:T(8,128)(2,1)S(1)}, bf16[384,1024]{1,0:T(8,128)(2,1)}, u32[]{:S(2)}) copy-start(bf16[384,1024]{1,0:T(8,128)(2,1)} %tokens_from.1) | copy-start | bytes 2359300
  2.4 3.1 %copy-start.4 = (bf16[384,1024]{1,0:T(8,128)(2,1)S(1)}, bf16[384,1024]{1,0:T(8,128)(2,1)}, u32[]{:S(2)}) copy-start(bf16[384,1024]{1,0:T(8,128)(2,1)} %tokens_from.1) | copy-start | bytes 2359300
  2.4 8.1 %collective-permute-start = (bf16[96,1024]{1,0:T(8,128)(2,1)S(1)}, bf16[96,1024]{1,0:T(8,128)(2,1)S(1)}, u32[]{:S(2)}, u32[]{:S(2)}) collective-permute-start(bf16[96,1024]{1,0:T(8,128)(2,1)S(1)} %shard_map.86), channel_id=1, source_target_pairs={{0,2},{1,3},{2,0},{3,1},{4,6},{5,7},{6,4},{7,5},{8,10},{9,11},{10,... | collective-permute-start | bytes 589832 | tf_op jit(solution)/shard_map/ppermute | solution.py:327
  9.2 18.9 %collective-permute-start.8 = (bf16[1024,384]{1,0:T(8,128)(2,1)S(1)}, bf16[1024,384]{1,0:T(8,128)(2,1)S(1)}, u32[]{:S(2)}, u32[]{:S(2)}) collective-permute-start(bf16[1024,384]{1,0:T(8,128)(2,1)S(1)} %get-tuple-element.14.refs_4_), channel_id=1, source_target_pairs={{0,1},{1,0},{2,3},{3,2},{4,5},{5,4},{6,7},{7,6},{8,9},{9,8},{10,11... | collective-permute-start | bytes 2359304 | tf_op jit(solution)/shard_map/ppermute | solution.py:324
  10.6 19.5 %collective-permute-start.7 = (bf16[384,1024]{1,0:T(8,128)(2,1)S(1)}, bf16[384,1024]{1,0:T(8,128)(2,1)S(1)}, u32[]{:S(2)}, u32[]{:S(2)}) collective-permute-start(bf16[384,1024]{1,0:T(8,128)(2,1)S(1)} %shard_map.90), channel_id=1, source_target_pairs={{0,2},{1,3},{2,0},{3,1},{4,6},{5,7},{6,4},{7,5},{8,10},{9,11},{10,... | collective-permute-start | bytes 2359304 | tf_op jit(solution)/shard_map/ppermute | solution.py:327
  12.3 6.6 %collective-permute-start.4 = (bf16[96,1024]{1,0:T(8,128)(2,1)S(1)}, bf16[96,1024]{1,0:T(8,128)(2,1)S(1)}, u32[]{:S(2)}, u32[]{:S(2)}) collective-permute-start(bf16[96,1024]{1,0:T(8,128)(2,1)S(1)} %shard_map.88.refs_0_), channel_id=1, source_target_pairs={{0,8},{4,12},{8,0},{12,4},{16,24},{20,28},{24,16},{28,20},{1,9},{5... | collective-permute-start | bytes 589832 | tf_op jit(solution)/shard_map/ppermute | solution.py:333
  13.9 6.6 %collective-permute-start.3 = (bf16[96,1024]{1,0:T(8,128)(2,1)S(1)}, bf16[96,1024]{1,0:T(8,128)(2,1)S(1)}, u32[]{:S(2)}, u32[]{:S(2)}) collective-permute-start(bf16[96,1024]{1,0:T(8,128)(2,1)S(1)} %shard_map.88.refs_0_), channel_id=1, source_target_pairs={{0,4},{4,0},{8,12},{12,8},{16,20},{20,16},{24,28},{28,24},{1,5},{5... | collective-permute-start | bytes 589832 | tf_op jit(solution)/shard_map/ppermute | solution.py:330
  15.4 12.7 %collective-permute-start.9 = (bf16[384,512]{1,0:T(8,128)(2,1)S(1)}, bf16[384,512]{1,0:T(8,128)(2,1)S(1)}, u32[]{:S(2)}, u32[]{:S(2)}) collective-permute-start(bf16[384,512]{1,0:T(8,128)(2,1)S(1)} %get-tuple-element.15), channel_id=1, source_target_pairs={{0,1},{1,0},{2,3},{3,2},{4,5},{5,4},{6,7},{7,6},{8,9},{9,8},{10,11... | collective-permute-start | bytes 1179656 | tf_op jit(solution)/shard_map/ppermute | solution.py:324
  18.9 4.7 %collective-permute-start.5 = (bf16[48,1024]{1,0:T(8,128)(2,1)S(1)}, bf16[48,1024]{1,0:T(8,128)(2,1)S(1)}, u32[]{:S(2)}, u32[]{:S(2)}) collective-permute-start(bf16[48,1024]{1,0:T(8,128)(2,1)S(1)} %slice.8), channel_id=1, source_target_pairs={{0,4},{4,0},{8,12},{12,8},{16,20},{20,16},{24,28},{28,24},{1,5},{5... | collective-permute-start | bytes 294920 | tf_op jit(solution)/shard_map/ppermute | solution.py:330
  20.5 4.7 %collective-permute-start.6 = (bf16[48,1024]{1,0:T(8,128)(2,1)S(1)}, bf16[48,1024]{1,0:T(8,128)(2,1)S(1)}, u32[]{:S(2)}, u32[]{:S(2)}) collective-permute-start(bf16[48,1024]{1,0:T(8,128)(2,1)S(1)} %slice.9), channel_id=1, source_target_pairs={{0,8},{4,12},{8,0},{12,4},{16,24},{20,28},{24,16},{28,20},{1,9},{5... | collective-permute-start | bytes 294920 | tf_op jit(solution)/shard_map/ppermute | solution.py:333
  30.2 4.0 %collective-permute-start.11 = (bf16[384,1024]{1,0:T(8,128)(2,1)S(1)}, bf16[384,1024]{1,0:T(8,128)(2,1)S(1)}, u32[]{:S(2)}, u32[]{:S(2)}) collective-permute-start(bf16[384,1024]{1,0:T(8,128)(2,1)S(1)} %shard_map.91.errors), channel_id=1, source_target_pairs={{0,1},{1,0},{2,3},{3,2},{4,5},{5,4},{6,7},{7,6},{8,9},{9,8},{10,11... | collective-permute-start | bytes 2359304 | tf_op jit(solution)/shard_map/ppermute | solution.py:324
  30.3 4.6 %collective-permute-start.13 = (bf16[1024,384]{1,0:T(8,128)(2,1)S(1)}, bf16[1024,384]{1,0:T(8,128)(2,1)S(1)}, u32[]{:S(2)}, u32[]{:S(2)}) collective-permute-start(bf16[1024,384]{1,0:T(8,128)(2,1)S(1)} %get-tuple-element.18.refs_6_), channel_id=1, source_target_pairs={{0,1},{1,0},{2,3},{3,2},{4,5},{5,4},{6,7},{7,6},{8,9},{9,8},{10,11... | collective-permute-start | bytes 2359304 | tf_op jit(solution)/shard_map/ppermute | solution.py:324
  30.8 19.5 %collective-permute-start.10 = (bf16[384,1024]{1,0:T(8,128)(2,1)S(1)}, bf16[384,1024]{1,0:T(8,128)(2,1)S(1)}, u32[]{:S(2)}, u32[]{:S(2)}) collective-permute-start(bf16[384,1024]{1,0:T(8,128)(2,1)S(1)} %shard_map.91.errors), channel_id=1, source_target_pairs={{0,2},{1,3},{2,0},{3,1},{4,6},{5,7},{6,4},{7,5},{8,10},{9,11},{10,... | collective-permute-start | bytes 2359304 | tf_op jit(solution)/shard_map/ppermute | solution.py:327
  32.5 1.7 %collective-permute-start.12 = (bf16[384,512]{1,0:T(8,128)(2,1)S(1)}, bf16[384,512]{1,0:T(8,128)(2,1)S(1)}, u32[]{:S(2)}, u32[]{:S(2)}) collective-permute-start(bf16[384,512]{1,0:T(8,128)(2,1)S(1)} %get-tuple-element.17), channel_id=1, source_target_pairs={{0,1},{1,0},{2,3},{3,2},{4,5},{5,4},{6,7},{7,6},{8,9},{9,8},{10,11... | collective-permute-start | bytes 1179656 | tf_op jit(solution)/shard_map/ppermute | solution.py:324
  50.3 2.3 %collective-permute-start.14 = (bf16[384,1024]{1,0:T(8,128)(2,1)S(1)}, bf16[384,1024]{1,0:T(8,128)(2,1)S(1)}, u32[]{:S(2)}, u32[]{:S(2)}) collective-permute-start(bf16[384,1024]{1,0:T(8,128)(2,1)S(1)} %shard_map.94.errors), channel_id=1, source_target_pairs={{0,1},{1,0},{2,3},{3,2},{4,5},{5,4},{6,7},{7,6},{8,9},{9,8},{10,11... | collective-permute-start | bytes 2359304 | tf_op jit(solution)/shard_map/ppermute | solution.py:324
  51.6 1.6 %copy-start.1 = (bf16[1,1024,512]{2,1,0:T(8,128)(2,1)S(1)}, bf16[1,1024,512]{2,1,0:T(8,128)(2,1)}, u32[]{:S(2)}) copy-start(bf16[1,1024,512]{2,1,0:T(8,128)(2,1)} %refs_9_.9) | copy-start | bytes 3145732
  53.7 6.1 %collective-permute-start.15 = (bf16[128,512]{1,0:T(8,128)(2,1)S(1)}, bf16[128,512]{1,0:T(8,128)(2,1)S(1)}, u32[]{:S(2)}, u32[]{:S(2)}) collective-permute-start(bf16[128,512]{1,0:T(8,128)(2,1)S(1)} %shard_map.97.refs_10_.refs_0_), channel_id=1, source_target_pairs={{0,4},{4,0},{8,12},{12,8},{16,20},{20,16},{24,28},{28,24},{1,5},{5... | collective-permute-start | bytes 393224 | tf_op jit(solution)/shard_map/ppermute | solution.py:330
  56.2 9.3 %collective-permute-start.16 = (bf16[256,512]{1,0:T(8,128)(2,1)S(1)}, bf16[256,512]{1,0:T(8,128)(2,1)S(1)}, u32[]{:S(2)}, u32[]{:S(2)}) collective-permute-start(bf16[256,512]{1,0:T(8,128)(2,1)S(1)} %shard_map.98.refs_10_.refs_1_), channel_id=1, source_target_pairs={{0,4},{4,0},{8,12},{12,8},{16,20},{20,16},{24,28},{28,24},{1,5},{5... | collective-permute-start | bytes 786440 | tf_op jit(solution)/shard_map/ppermute | solution.py:330
  59.8 11.3 %collective-permute-start.17 = (bf16[256,512]{1,0:T(8,128)(2,1)S(1)}, bf16[256,512]{1,0:T(8,128)(2,1)S(1)}, u32[]{:S(2)}, u32[]{:S(2)}) collective-permute-start(bf16[256,512]{1,0:T(8,128)(2,1)S(1)} %shard_map.100.refs_10_.refs_2_), channel_id=1, source_target_pairs={{0,4},{4,0},{8,12},{12,8},{16,20},{20,16},{24,28},{28,24},{1,5},{5... | collective-permute-start | bytes 786440 | tf_op jit(solution)/shard_map/ppermute | solution.py:330
  61.8 9.3 %collective-permute-start.19 = (bf16[128,512]{1,0:T(8,128)(2,1)S(1)}, bf16[128,512]{1,0:T(8,128)(2,1)S(1)}, u32[]{:S(2)}, u32[]{:S(2)}) collective-permute-start(bf16[128,512]{1,0:T(8,128)(2,1)S(1)} %collective-permute-done.15.refs_1_.refs_4_), channel_id=1, source_target_pairs={{0,8},{4,28},{8,16},{12,4},{16,24},{20,12},{24,0},{28,20},{1,9},{5... | collective-permute-start | bytes 393224 | tf_op jit(solution)/shard_map/ppermute | solution.py:337
  65.5 11.2 %collective-permute-start.22 = (bf16[256,512]{1,0:T(8,128)(2,1)S(1)}, bf16[256,512]{1,0:T(8,128)(2,1)S(1)}, u32[]{:S(2)}, u32[]{:S(2)}) collective-permute-start(bf16[256,512]{1,0:T(8,128)(2,1)S(1)} %shard_map.102.refs_10_.refs_3_), channel_id=1, source_target_pairs={{0,4},{4,0},{8,12},{12,8},{16,20},{20,16},{24,28},{28,24},{1,5},{5... | collective-permute-start | bytes 786440 | tf_op jit(solution)/shard_map/ppermute | solution.py:330
  67.4 9.4 %collective-permute-start.23 = (bf16[256,512]{1,0:T(8,128)(2,1)S(1)}, bf16[256,512]{1,0:T(8,128)(2,1)S(1)}, u32[]{:S(2)}, u32[]{:S(2)}) collective-permute-start(bf16[256,512]{1,0:T(8,128)(2,1)S(1)} %collective-permute-done.16.refs_1_.refs_5_), channel_id=1, source_target_pairs={{0,8},{4,28},{8,16},{12,4},{16,24},{20,12},{24,0},{28,20},{1,9},{5... | collective-permute-start | bytes 786440 | tf_op jit(solution)/shard_map/ppermute | solution.py:337
  71.1 11.3 %collective-permute-start.20 = (bf16[256,512]{1,0:T(8,128)(2,1)S(1)}, bf16[256,512]{1,0:T(8,128)(2,1)S(1)}, u32[]{:S(2)}, u32[]{:S(2)}) collective-permute-start(bf16[256,512]{1,0:T(8,128)(2,1)S(1)} %shard_map.105.refs_6_), channel_id=1, source_target_pairs={{0,8},{4,28},{8,16},{12,4},{16,24},{20,12},{24,0},{28,20},{1,9},{5... | collective-permute-start | bytes 786440 | tf_op jit(solution)/shard_map/ppermute | solution.py:337
  73.1 6.5 %collective-permute-start.18 = (bf16[128,512]{1,0:T(8,128)(2,1)S(1)}, bf16[128,512]{1,0:T(8,128)(2,1)S(1)}, u32[]{:S(2)}, u32[]{:S(2)}) collective-permute-start(bf16[128,512]{1,0:T(8,128)(2,1)S(1)} %shard_map.104.refs_0_), channel_id=1, source_target_pairs={{0,4},{4,0},{8,12},{12,8},{16,20},{20,16},{24,28},{28,24},{1,5},{5... | collective-permute-start | bytes 393224 | tf_op jit(solution)/shard_map/ppermute | solution.py:330
  76.8 11.2 %collective-permute-start.24 = (bf16[256,512]{1,0:T(8,128)(2,1)S(1)}, bf16[256,512]{1,0:T(8,128)(2,1)S(1)}, u32[]{:S(2)}, u32[]{:S(2)}) collective-permute-start(bf16[256,512]{1,0:T(8,128)(2,1)S(1)} %shard_map.107.refs_7_), channel_id=1, source_target_pairs={{0,8},{4,28},{8,16},{12,4},{16,24},{20,12},{24,0},{28,20},{1,9},{5... | collective-permute-start | bytes 786440 | tf_op jit(solution)/shard_map/ppermute | solution.py:337
  82.4 7.4 %collective-permute-start.21 = (bf16[128,512]{1,0:T(8,128)(2,1)S(1)}, bf16[128,512]{1,0:T(8,128)(2,1)S(1)}, u32[]{:S(2)}, u32[]{:S(2)}) collective-permute-start(bf16[128,512]{1,0:T(8,128)(2,1)S(1)} %shard_map.106.refs_1_), channel_id=1, source_target_pairs={{0,8},{4,28},{8,16},{12,4},{16,24},{20,12},{24,0},{28,20},{1,9},{5... | collective-permute-start | bytes 393224 | tf_op jit(solution)/shard_map/ppermute | solution.py:337

commit v4 on v3

--- a/solution.py
+++ b/solution.py
@@ -49,18 +49,22 @@
     )(value, *earlier)
 
 
-def share_kernel(value, out):
+def share_kernel(value, out, done):
     rows = out.shape[0]
     place = lax.axis_index("rep") & 3
-    out[...] = value[pl.ds(pl.multiple_of(place * rows, rows), rows)]
+    here = pl.ds(pl.multiple_of(place * rows, rows), rows)
+    copy = pltpu.make_async_copy(value.at[here], out, done)
+    copy.start()
+    copy.wait()
 
 
 def share(value):
     return pl.pallas_call(
         share_kernel,
         out_shape=shape((value.shape[0] // 4, value.shape[1])),
-        in_specs=[vmem],
+        in_specs=[anywhere],
         out_specs=vmem,
+        scratch_shapes=[pltpu.SemaphoreType.DMA],
         compiler_params=limit(1),
         cost_estimate=cost(3 * 10**9, value.size),
     )(value)
@@ -96,7 +100,7 @@
     return hidden.astype(bf16), slope.astype(bf16)
 
 
-def forward_core(tokens, weights_in, weights_out, normed_t, slopes, total, ready=None):
+def forward_core(tokens, weights_in, weights_out, normed_t, slopes, part, base, total):
     count, width = tokens.shape
     block = weights_in[0].shape[1]
     tile = min(256, block)
@@ -104,75 +108,50 @@
     normed_t[...] = normed.T
     for side in range(2):
         for at in range(0, block, tile):
-            if ready is not None and side + at == 0:
-                ready[0].wait()
             values = matmul(normed, weights_in[side][:, at : at + tile]) * (width**-0.5)
             hidden, slopes[side][:, at : at + tile] = gelu_both(values)
-            if ready is not None and side + at == 0:
-                ready[1].wait()
             term = matmul(hidden, weights_out[side][at : at + tile])
             if side + at == 0:
                 total[...] = term
             else:
                 total[...] += term
-
-
-def forward_kernel(
-    tokens_from, in_from, mate_in, out_from, mate_out, normed_t, slope, slope_mate, out, *scratch
-):
-    total, tokens, own_in, own_out, done = scratch
-    copies = [
-        pltpu.make_async_copy(source, target, done.at[at])
-        for at, (source, target) in enumerate(
-            ((tokens_from, tokens), (in_from, own_in), (out_from, own_out))
-        )
-    ]
-    for copy in copies:
-        copy.start()
-    copies[0].wait()
-    weights = (own_in, mate_in), (own_out, mate_out)
-    forward_core(tokens, *weights, normed_t, (slope, slope_mate), total, copies[1:])
-    out[...] = total[...].astype(bf16)
-
-
-def forward_far_kernel(*refs):
-    pieces = refs[:5]
-    own_in, mate_in, own_out, mate_out, normed_t, slope, slope_mate = refs[5:12]
-    out, total, tokens = refs[12:]
-    assemble_kernel(*pieces, tokens)
-    weights = (own_in, mate_in), (own_out, mate_out)
-    forward_core(tokens, *weights, normed_t, (slope, slope_mate), total)
-    count = tokens.shape[0]
+    part[...] = total[...].astype(bf16)
     values = tokens[...].astype(f32)
     ahead = pltpu.roll(values, count - 1, 0)
     rank = lax.broadcasted_iota(jnp.int32, values.shape, 0)
-    base = total[...] + values - ahead
-    out[...] = jnp.where(rank == count - 1, 0.0, base)
-
-
-def forward(given, count, weights, far):
+    base[...] = jnp.where(rank == count - 1, 0.0, total[...] + values - ahead)
+
+
+def forward_kernel(pieces, skipped, *refs):
+    given = refs[:pieces]
+    own_in, mate_in, own_out, mate_out = refs[pieces : pieces + 4]
+    normed_t, slope, slope_mate, part, base, total, tokens = refs[pieces + 4 + skipped :]
+    if pieces > 1:
+        assemble_kernel(*given, tokens)
+    else:
+        tokens = given[0]
+    weights = (own_in, mate_in), (own_out, mate_out)
+    forward_core(tokens, *weights, normed_t, (slope, slope_mate), part, base, total)
+
+
+def forward(given, count, weights, *earlier):
     width, block = weights[0].shape
     outs = (
         shape((width, count)),
         shape((count, block)),
         shape((count, block)),
-        shape((count, width), f32 if far else bf16),
+        shape((count, width)),
+        shape((count, width), f32),
     )
-    scratch = [pltpu.VMEM((count, width), f32), pltpu.VMEM((count, width), bf16)]
-    specs = [vmem] * (len(given) + len(weights))
-    if not far:
-        specs = [anywhere, anywhere, vmem, anywhere, vmem]
-        scratch += [pltpu.VMEM(value.shape, bf16) for value in (weights[0], weights[2])]
-        scratch.append(pltpu.SemaphoreType.DMA((3,)))
-    return pl.pallas_call(
-        forward_far_kernel if far else forward_kernel,
+    return pl.pallas_call(
+        functools.partial(forward_kernel, len(given), len(earlier)),
         out_shape=outs,
-        in_specs=specs,
+        in_specs=[vmem] * (len(given) + len(weights)) + [anywhere] * len(earlier),
         out_specs=[vmem for out in outs],
-        scratch_shapes=scratch,
-        compiler_params=limit(20),
+        scratch_shapes=[pltpu.VMEM((count, width), f32), pltpu.VMEM((count, width), bf16)],
+        compiler_params=limit(12),
         cost_estimate=cost(4 * count * width * block, 8 * width * block),
-    )(*given, *weights)
+    )(*given, *weights, *earlier)
 
 
 def errors_kernel(base, sent, *refs):
@@ -188,9 +167,24 @@
         out_shape=shape(base.shape),
         in_specs=[vmem, vmem] + [anywhere] * len(earlier),
         out_specs=vmem,
-        compiler_params=limit(8),
+        compiler_params=limit(2),
         cost_estimate=cost(0, 8 * base.size),
     )(base, sent, *earlier)
+
+
+def strength_kernel(heat, out):
+    out[...] = jnp.sqrt(jnp.full(out.shape, 2.0 * drift_stride * heat[0], f32))
+
+
+def strength_of(heat, block):
+    return pl.pallas_call(
+        strength_kernel,
+        out_shape=shape((1, block), f32),
+        in_specs=[smem],
+        out_specs=vmem,
+        compiler_params=limit(1),
+        cost_estimate=cost(0, 4 * block),
+    )(heat)
 
 
 def hidden_kernel(errors, weight, slope, *refs):
@@ -215,7 +209,7 @@
     )(errors, weight, slope, *earlier)
 
 
-def update_kernel(start, heat, *refs):
+def update_kernel(start, strength, *refs):
     grads, normed = refs[:4], refs[4:8]
     params, noise = refs[8:10]
     out = refs[-1]
@@ -224,9 +218,8 @@
     for values, grad in zip(normed, grads):
         total += matmul(values[here], grad[...])
     current = params[0, here].astype(f32)
-    strength = jnp.sqrt(jnp.full((1, out.shape[1]), 2.0 * drift_stride * heat[0], f32))
     slope = total * params.shape[1] ** -0.5
-    moved = current - drift_stride * (slope + current) + strength * noise[0, here].astype(f32)
+    moved = current - drift_stride * (slope + current) + strength[...] * noise[0, here].astype(f32)
     out[...] = moved.astype(bf16)
 
 
@@ -236,7 +229,7 @@
     return pl.pallas_call(
         functools.partial(update_kernel, start),
         out_shape=shape((rows, block)),
-        in_specs=[smem] + [vmem] * 10 + [anywhere] * len(earlier),
+        in_specs=[vmem] * 11 + [anywhere] * len(earlier),
         out_specs=vmem,
         compiler_params=limit(4),
         cost_estimate=cost(4 * rows * count * block, 8 * rows * count),
@@ -254,19 +247,19 @@
     own, across, beyond = (refs[i * count : (i + 1) * count] for i in range(3))
     result, gaps, out, done = refs[-4:]
     odd, near_taken, far_taken = role(mate, swapped)
-    near_sum = far_sum = 0.0
     at = 0
-    for part in range(count):
-        mine, near, far = (pieces[part][...] for pieces in (own, across, beyond))
-        out[at : at + mine.shape[0]] = jnp.where(near_taken, near, jnp.where(far_taken, far, mine))
+    for mine, near, far in zip(own, across, beyond):
+        out[at : at + mine.shape[0]] = jnp.where(
+            near_taken, near[...], jnp.where(far_taken, far[...], mine[...])
+        )
         at += mine.shape[0]
-        mine = mine.astype(f32)
-        near = near.astype(f32) - mine
-        far = far.astype(f32) - mine
-        near_sum += jnp.sum(near * near, axis=0, keepdims=True)
-        far_sum += jnp.sum(far * far, axis=0, keepdims=True)
     copy = pltpu.make_async_copy(out, result.at[0, pl.ds(start, stop - start)], done)
     copy.start()
+    near_sum = far_sum = 0.0
+    for part in range(count):
+        mine, near, far = (pieces[part][...].astype(f32) for pieces in (own, across, beyond))
+        near_sum += jnp.sum((near - mine) * (near - mine), axis=0, keepdims=True)
+        far_sum += jnp.sum((far - mine) * (far - mine), axis=0, keepdims=True)
     if start > 0:
         so_far = refs[3 * count]
         near_sum += so_far[0, 0:1]
@@ -345,50 +338,50 @@
 
     mate_in = to_core(params)
     mate_out = to_core(output_matrix)
-    token_own = to_chip(share(residual_flow))
+    token_share = share(residual_flow)
+    token_own = to_chip(token_share)
     weights = (params, mate_in, output_matrix, mate_out)
-    normed, slope, slope_send, part = forward((residual_flow,), count, weights, False)
+    normed, slope, slope_send, part, base = forward((residual_flow,), count, weights)
     sent = to_chip(after(part, token_own))
     token_own = after(token_own, part)
     token_across, token_behind = step_one(token_own)
     token_pieces = step_two(token_own, token_across, token_behind)
     normed_mate = to_core(normed)
     slope_mate = to_core(slope_send)
-    far, far_slope, far_slope_send, base = forward(token_pieces, count, weights, True)
+    far, far_slope, far_slope_send, far_part, far_base = forward(token_pieces, count, weights)
+    far_sent = to_chip(far_part)
     far_mate = to_core(far)
     far_slope_mate = to_core(far_slope_send)
 
-    errors = errors_of(base, sent, normed_mate, slope_mate)
-    back = to_chip(errors)
+    strength = strength_of(chain_heat, block)
+    errors = errors_of(far_base, sent, normed_mate, slope_mate, strength)
     far_grads = [
         hidden_of(errors, output_matrix, far_slope),
         hidden_of(to_core(errors), output_matrix, far_slope_mate),
     ]
-    back = after(back, *far_grads, far_mate)
+    errors = errors_of(base, far_sent, *far_grads, far_mate)
     near_grads = [
-        hidden_of(back, output_matrix, slope),
-        hidden_of(to_core(back), output_matrix, slope_mate),
+        hidden_of(errors, output_matrix, slope),
+        hidden_of(to_core(errors), output_matrix, slope_mate),
     ]
     grads = near_grads + far_grads
 
     pairing = (matched_chain, swap_mask)
     width = params.shape[0]
-    sizes = [width * part // 8 for part in (1, 2, 2, 2, 1)]
+    sizes = [width * part // 8 for part in (2, 2, 2, 2)]
     starts = [sum(sizes[:chunk]) for chunk in range(len(sizes))]
     own, across, beyond = [], [], []
     for chunk, (start, rows) in enumerate(zip(starts, sizes)):
         fresh = update(
             start,
             rows,
-            chain_heat,
+            strength,
             grads,
             (normed, normed_mate, far, far_mate),
             rooted_input_matrix,
             chain_normal_draws,
             *own[-1:],
         )
-        if chunk >= 2:
-            fresh = after(fresh, across[chunk - 2])
         own.append(fresh)
         across.append(to_mate(fresh))
     done = None

time: 91.3 us -> 90 us (0.986)
  starting transfers between devices: 30.8 us -> 25.9 us
  waiting for transfers between devices: 41 us -> 45.6 us
  Pallas kernels: 15.2 us -> 14.2 us
    ppermute x7 -> x6, waiting for transfers between devices: 7.72 us -> 13.1 us  [to_mate(): return lax.ppermute(value, 'rep', [(i, i ^ 1) for i in range(replicas)])]
    ppermute x7 -> x6, starting transfers between devices: 12.8 us -> 10.2 us  [to_mate(): return lax.ppermute(value, 'rep', [(i, i ^ 1) for i in range(replicas)])]
    ppermute x5 -> x4, waiting for transfers between devices: 7.46 us -> 5.5 us  [to_next(): return lax.ppermute(value, 'rep', pairs)]
    ppermute x5 -> x4, starting transfers between devices: 7.01 us -> 5.68 us  [to_next(): return lax.ppermute(value, 'rep', pairs)]
    ppermute x8, waiting for transfers between devices: 2.13 us -> 3.09 us  [to_core(): return lax.ppermute(value, 'dp', [(i, i ^ 1) for i in range(4)])]
    pallas_call x2 -> x3, Pallas kernels: 6.55 us -> 5.85 us  [the longest x2 5.84 us: forward(): pl.pallas_call(functools.partial(forward_kernel, len(given), len(earlier)...]
    pallas_call x5 -> x4, Pallas kernels: 3.24 us -> 3.09 us  [update(): pl.pallas_call(functools.partial(update_kernel, start), out_shape=shape((...]
  transfers between devices with their start and end apart: 25 -> 23, of which waited for: 16 -> 14; matrix products, arithmetic and copies ran while one was open for 0% -> 0% of each run, Pallas kernels for 14% -> 13%
where the time goes in v4:
time: 90 us; the launch traced here: 89.8 us
  waiting for transfers between devices  45.6 us (51%)
  starting transfers between devices  25.9 us (29%)
  Pallas kernels  14.2 us (16%)
  between operations  2.82 us (3%)
  local copies, waits for them, and re-layouts  1.25 us (1%)
    ppermute x3, waiting for transfers between devices, to_chip(): return lax.ppermute(value, 'dp', [(i, i ^ 2) for i in range(4)])  19 us
    ppermute x6, waiting for transfers between devices, to_mate(): return lax.ppermute(value, 'rep', [(i, i ^ 1) for i in range(replicas)])  13.1 us
    ppermute x6, starting transfers between devices, to_mate(): return lax.ppermute(value, 'rep', [(i, i ^ 1) for i in range(replicas)])  10.2 us
    ppermute x3, starting transfers between devices, to_chip(): return lax.ppermute(value, 'dp', [(i, i ^ 2) for i in range(4)])  6.18 us
    pallas_call x2, Pallas kernels, forward(): pl.pallas_call(functools.partial(forward_kernel, len(given), len(earlier)...  5.84 us
    ppermute x4, starting transfers between devices, to_next(): return lax.ppermute(value, 'rep', pairs)  5.68 us
    ppermute x4, waiting for transfers between devices, to_next(): return lax.ppermute(value, 'rep', pairs)  5.5 us
    ppermute x2, waiting for transfers between devices, to_pair(): return lax.ppermute(value, 'rep', [(i, i ^ 2) for i in range(replicas)])  4.99 us
  transfers between devices with their start and end apart: 23, of which 14 were waited for; matrix products, arithmetic and copies ran while one was open for 0% of the time, Pallas kernels for 13%

profile of v4, /device:TPU:0, one launch (start us, length us, event | category | flops | bytes accessed | tf_op | source)
XLA Modules:
  0.0 89.8 jit_solution(12339840724538630942)
XLA Ops:
  1.2 1.2 %copy-done.3 = bf16[384,1024]{1,0:T(8,128)(2,1)S(1)} copy-done((bf16[384,1024]{1,0:T(8,128)(2,1)S(1)}, bf16[384,1024]{1,0:T(8,128)(2,1)}, u32[]{:S(2)}) %copy-start.3) | copy-done | bytes 786456
  2.7 3.0 %collective-permute-start.2 = (bf16[96,1024]{1,0:T(8,128)(2,1)S(1)}, bf16[96,1024]{1,0:T(8,128)(2,1)S(1)}, u32[]{:S(2)}, u32[]{:S(2)}) collective-permute-start(bf16[96,1024]{1,0:T(8,128)(2,1)S(1)} %shard_map.88), channel_id=1, source_target_pairs={{0,2},{1,3},{2,0},{3,1},{4,6},{5,7},{6,4},{7,5},{8,10},{9,11},{10,... | collective-permute-start | bytes 589832 | tf_op jit(solution)/shard_map/ppermute | solution.py:320
  5.7 2.9 %shard_map.87 = (bf16[1024,384]{1,0:T(8,128)(2,1)S(1)}, bf16[384,512]{1,0:T(8,128)(2,1)S(1)}, bf16[384,512]{1,0:T(8,128)(2,1)S(1)}, bf16[384,1024]{1,0:T(8,128)(2,1)S(1)}, f32[384,1024]{1,0:T(8,128)S(1)}) custom-call(bf16[384,1024]{1,0:T(8,128)(2,1)S(1)} %copy-done.4, bf16[1024,512]{1,0:T(8,128)(2,1)S(1)} %bitcast.2, ...), custom_call_target="tpu_custom_call" | custom-call | flops 1610612736 | bytes 4194304 | tf_op jit(solution)/shard_map/pallas_call | solution.py:146
  8.8 2.0 %collective-permute-done.2.refs_0_.refs_1_ = bf16[96,1024]{1,0:T(8,128)(2,1)S(1)} collective-permute-done((bf16[96,1024]{1,0:T(8,128)(2,1)S(1)}, bf16[96,1024]{1,0:T(8,128)(2,1)S(1)}, u32[]{:S(2)}, u32[]{:S(2)}) %collective-permute-start.2) | collective-permute-done | bytes 196640 | tf_op jit(solution)/shard_map/ppermute | solution.py:320
  10.8 1.7 %collective-permute-start.8 = (bf16[384,1024]{1,0:T(8,128)(2,1)S(1)}, bf16[384,1024]{1,0:T(8,128)(2,1)S(1)}, u32[]{:S(2)}, u32[]{:S(2)}) collective-permute-start(bf16[384,1024]{1,0:T(8,128)(2,1)S(1)} %shard_map.91), channel_id=1, source_target_pairs={{0,2},{1,3},{2,0},{3,1},{4,6},{5,7},{6,4},{7,5},{8,10},{9,11},{10,... | collective-permute-start | bytes 2359304 | tf_op jit(solution)/shard_map/ppermute | solution.py:320
  12.5 1.6 %collective-permute-start.4 = (bf16[96,1024]{1,0:T(8,128)(2,1)S(1)}, bf16[96,1024]{1,0:T(8,128)(2,1)S(1)}, u32[]{:S(2)}, u32[]{:S(2)}) collective-permute-start(bf16[96,1024]{1,0:T(8,128)(2,1)S(1)} %shard_map.89.refs_0_), channel_id=1, source_target_pairs={{0,8},{4,12},{8,0},{12,4},{16,24},{20,28},{24,16},{28,20},{1,9},{5... | collective-permute-start | bytes 589832 | tf_op jit(solution)/shard_map/ppermute | solution.py:326
  14.1 1.5 %collective-permute-start.3 = (bf16[96,1024]{1,0:T(8,128)(2,1)S(1)}, bf16[96,1024]{1,0:T(8,128)(2,1)S(1)}, u32[]{:S(2)}, u32[]{:S(2)}) collective-permute-start(bf16[96,1024]{1,0:T(8,128)(2,1)S(1)} %shard_map.89.refs_0_), channel_id=1, source_target_pairs={{0,4},{4,0},{8,12},{12,8},{16,20},{20,16},{24,28},{28,24},{1,5},{5... | collective-permute-start | bytes 589832 | tf_op jit(solution)/shard_map/ppermute | solution.py:323
  15.6 2.6 %collective-permute-done.4.refs_2_ = bf16[96,1024]{1,0:T(8,128)(2,1)S(1)} collective-permute-done((bf16[96,1024]{1,0:T(8,128)(2,1)S(1)}, bf16[96,1024]{1,0:T(8,128)(2,1)S(1)}, u32[]{:S(2)}, u32[]{:S(2)}) %collective-permute-start.4) | collective-permute-done | bytes 196640 | tf_op jit(solution)/shard_map/ppermute | solution.py:326
  18.3 1.6 %collective-permute-start.5 = (bf16[48,1024]{1,0:T(8,128)(2,1)S(1)}, bf16[48,1024]{1,0:T(8,128)(2,1)S(1)}, u32[]{:S(2)}, u32[]{:S(2)}) collective-permute-start(bf16[48,1024]{1,0:T(8,128)(2,1)S(1)} %slice.8), channel_id=1, source_target_pairs={{0,4},{4,0},{8,12},{12,8},{16,20},{20,16},{24,28},{28,24},{1,5},{5... | collective-permute-start | bytes 294920 | tf_op jit(solution)/shard_map/ppermute | solution.py:323
  20.6 0.9 collective-permute-start.6
  22.1 0.8 collective-permute-done.5.refs_3_
  22.9 2.3 %collective-permute-done.6.refs_4_ = bf16[48,1024]{1,0:T(8,128)(2,1)S(1)} collective-permute-done((bf16[48,1024]{1,0:T(8,128)(2,1)S(1)}, bf16[48,1024]{1,0:T(8,128)(2,1)S(1)}, u32[]{:S(2)}, u32[]{:S(2)}) %collective-permute-start.6) | collective-permute-done | bytes 98336 | tf_op jit(solution)/shard_map/ppermute | solution.py:326
  25.3 2.9 %shard_map.90 = (bf16[1024,384]{1,0:T(8,128)(2,1)S(1)}, bf16[384,512]{1,0:T(8,128)(2,1)S(1)}, bf16[384,512]{1,0:T(8,128)(2,1)S(1)}, bf16[384,1024]{1,0:T(8,128)(2,1)S(1)}, f32[384,1024]{1,0:T(8,128)S(1)}) custom-call(bf16[96,1024]{1,0:T(8,128)(2,1)S(1)} %shard_map.89.refs_0_, bf16[96,1024]{1,0:T(8,128)(2,1)S(1)} %collective-permute-done.3.refs_1_, ...), custom_call_target="tpu_custom_call" | custom-call | flops 1610612736 | bytes 4194304 | tf_op jit(solution)/shard_map/pallas_call | solution.py:146
  28.2 1.5 %collective-permute-done.8.sent = bf16[384,1024]{1,0:T(8,128)(2,1)S(1)} collective-permute-done((bf16[384,1024]{1,0:T(8,128)(2,1)S(1)}, bf16[384,1024]{1,0:T(8,128)(2,1)S(1)}, u32[]{:S(2)}, u32[]{:S(2)}) %collective-permute-start.8) | collective-permute-done | bytes 786464 | tf_op jit(solution)/shard_map/ppermute | solution.py:320
  30.5 1.4 %collective-permute-start.7 = (bf16[384,1024]{1,0:T(8,128)(2,1)S(1)}, bf16[384,1024]{1,0:T(8,128)(2,1)S(1)}, u32[]{:S(2)}, u32[]{:S(2)}) collective-permute-start(bf16[384,1024]{1,0:T(8,128)(2,1)S(1)} %get-tuple-element.16), channel_id=1, source_target_pairs={{0,2},{1,3},{2,0},{3,1},{4,6},{5,7},{6,4},{7,5},{8,10},{9,11},{10,... | collective-permute-start | bytes 2359304 | tf_op jit(solution)/shard_map/ppermute | solution.py:320
  32.5 1.4 %collective-permute-done.12.slope = bf16[384,512]{1,0:T(8,128)(2,1)S(1)} collective-permute-done((bf16[384,512]{1,0:T(8,128)(2,1)S(1)}, bf16[384,512]{1,0:T(8,128)(2,1)S(1)}, u32[]{:S(2)}, u32[]{:S(2)}) %collective-permute-start.12) | collective-permute-done | bytes 393248 | tf_op jit(solution)/shard_map/ppermute | solution.py:317
  34.5 15.4 %collective-permute-done.7.sent = bf16[384,1024]{1,0:T(8,128)(2,1)S(1)} collective-permute-done((bf16[384,1024]{1,0:T(8,128)(2,1)S(1)}, bf16[384,1024]{1,0:T(8,128)(2,1)S(1)}, u32[]{:S(2)}, u32[]{:S(2)}) %collective-permute-start.7) | collective-permute-done | bytes 786464 | tf_op jit(solution)/shard_map/ppermute | solution.py:320
  50.8 1.6 %collective-permute-done.14.errors = bf16[384,1024]{1,0:T(8,128)(2,1)S(1)} collective-permute-done((bf16[384,1024]{1,0:T(8,128)(2,1)S(1)}, bf16[384,1024]{1,0:T(8,128)(2,1)S(1)}, u32[]{:S(2)}, u32[]{:S(2)}) %collective-permute-start.14) | collective-permute-done | bytes 786464 | tf_op jit(solution)/shard_map/ppermute | solution.py:317
  53.9 1.5 %collective-permute-start.19 = (bf16[256,512]{1,0:T(8,128)(2,1)S(1)}, bf16[256,512]{1,0:T(8,128)(2,1)S(1)}, u32[]{:S(2)}, u32[]{:S(2)}) collective-permute-start(bf16[256,512]{1,0:T(8,128)(2,1)S(1)} %shard_map.98.refs_10_.refs_0_), channel_id=1, source_target_pairs={{0,4},{4,0},{8,12},{12,8},{16,20},{20,16},{24,28},{28,24},{1,5},{5... | collective-permute-start | bytes 786440 | tf_op jit(solution)/shard_map/ppermute | solution.py:323
  57.6 1.5 %collective-permute-start.20 = (bf16[256,512]{1,0:T(8,128)(2,1)S(1)}, bf16[256,512]{1,0:T(8,128)(2,1)S(1)}, u32[]{:S(2)}, u32[]{:S(2)}) collective-permute-start(bf16[256,512]{1,0:T(8,128)(2,1)S(1)} %shard_map.100.refs_10_.refs_2_), channel_id=1, source_target_pairs={{0,4},{4,0},{8,12},{12,8},{16,20},{20,16},{24,28},{28,24},{1,5},{5... | collective-permute-start | bytes 786440 | tf_op jit(solution)/shard_map/ppermute | solution.py:323
  59.0 4.0 %collective-permute-done.19.refs_3_ = bf16[256,512]{1,0:T(8,128)(2,1)S(1)} collective-permute-done((bf16[256,512]{1,0:T(8,128)(2,1)S(1)}, bf16[256,512]{1,0:T(8,128)(2,1)S(1)}, u32[]{:S(2)}, u32[]{:S(2)}) %collective-permute-start.19) | collective-permute-done | bytes 262176 | tf_op jit(solution)/shard_map/ppermute | solution.py:323
  63.1 1.5 %collective-permute-start.21 = (bf16[256,512]{1,0:T(8,128)(2,1)S(1)}, bf16[256,512]{1,0:T(8,128)(2,1)S(1)}, u32[]{:S(2)}, u32[]{:S(2)}) collective-permute-start(bf16[256,512]{1,0:T(8,128)(2,1)S(1)} %collective-permute-done.19.refs_3_), channel_id=1, source_target_pairs={{0,8},{4,28},{8,16},{12,4},{16,24},{20,12},{24,0},{28,20},{1,9},{5... | collective-permute-start | bytes 786440 | tf_op jit(solution)/shard_map/ppermute | solution.py:330
  65.3 3.6 %collective-permute-start.15 = (bf16[256,512]{1,0:T(8,128)(2,1)S(1)}, bf16[256,512]{1,0:T(8,128)(2,1)S(1)}, u32[]{:S(2)}, u32[]{:S(2)}) collective-permute-start(bf16[256,512]{1,0:T(8,128)(2,1)S(1)} %shard_map.101.refs_0_), channel_id=1, source_target_pairs={{0,4},{4,0},{8,12},{12,8},{16,20},{20,16},{24,28},{28,24},{1,5},{5... | collective-permute-start | bytes 786440 | tf_op jit(solution)/shard_map/ppermute | solution.py:323
  68.9 1.3 %collective-permute-start.17 = (bf16[256,512]{1,0:T(8,128)(2,1)S(1)}, bf16[256,512]{1,0:T(8,128)(2,1)S(1)}, u32[]{:S(2)}, u32[]{:S(2)}) collective-permute-start(bf16[256,512]{1,0:T(8,128)(2,1)S(1)} %collective-permute-done.16.refs_4_), channel_id=1, source_target_pairs={{0,8},{4,28},{8,16},{12,4},{16,24},{20,12},{24,0},{28,20},{1,9},{5... | collective-permute-start | bytes 786440 | tf_op jit(solution)/shard_map/ppermute | solution.py:330
  70.2 4.1 %collective-permute-done.20.refs_0_ = bf16[256,512]{1,0:T(8,128)(2,1)S(1)} collective-permute-done((bf16[256,512]{1,0:T(8,128)(2,1)S(1)}, bf16[256,512]{1,0:T(8,128)(2,1)S(1)}, u32[]{:S(2)}, u32[]{:S(2)}) %collective-permute-start.20) | collective-permute-done | bytes 262176 | tf_op jit(solution)/shard_map/ppermute | solution.py:323
  74.3 1.5 %collective-permute-start.22 = (bf16[256,512]{1,0:T(8,128)(2,1)S(1)}, bf16[256,512]{1,0:T(8,128)(2,1)S(1)}, u32[]{:S(2)}, u32[]{:S(2)}) collective-permute-start(bf16[256,512]{1,0:T(8,128)(2,1)S(1)} %shard_map.103.refs_5_), channel_id=1, source_target_pairs={{0,8},{4,28},{8,16},{12,4},{16,24},{20,12},{24,0},{28,20},{1,9},{5... | collective-permute-start | bytes 786440 | tf_op jit(solution)/shard_map/ppermute | solution.py:330
  75.8 3.3 %collective-permute-done.15.refs_0_ = bf16[256,512]{1,0:T(8,128)(2,1)S(1)} collective-permute-done((bf16[256,512]{1,0:T(8,128)(2,1)S(1)}, bf16[256,512]{1,0:T(8,128)(2,1)S(1)}, u32[]{:S(2)}, u32[]{:S(2)}) %collective-permute-start.15) | collective-permute-done | bytes 262176 | tf_op jit(solution)/shard_map/ppermute | solution.py:323
  79.1 1.5 %collective-permute-start.18 = (bf16[256,512]{1,0:T(8,128)(2,1)S(1)}, bf16[256,512]{1,0:T(8,128)(2,1)S(1)}, u32[]{:S(2)}, u32[]{:S(2)}) collective-permute-start(bf16[256,512]{1,0:T(8,128)(2,1)S(1)} %shard_map.102.refs_1_), channel_id=1, source_target_pairs={{0,8},{4,28},{8,16},{12,4},{16,24},{20,12},{24,0},{28,20},{1,9},{5... | collective-permute-start | bytes 786440 | tf_op jit(solution)/shard_map/ppermute | solution.py:330
  81.9 0.9 %collective-permute-done.22.refs_8_ = bf16[256,512]{1,0:T(8,128)(2,1)S(1)} collective-permute-done((bf16[256,512]{1,0:T(8,128)(2,1)S(1)}, bf16[256,512]{1,0:T(8,128)(2,1)S(1)}, u32[]{:S(2)}, u32[]{:S(2)}) %collective-permute-start.22) | collective-permute-done | bytes 262176 | tf_op jit(solution)/shard_map/ppermute | solution.py:330
  82.8 1.0 %shard_map.104 = (bf16[1,1024,512]{2,1,0:T(8,128)(2,1)}, f32[1,2,512]{2,1,0:T(2,128)S(1)}) custom-call(s32[1]{0:T(128)S(6)} %copy.20.mate, s32[1]{0:T(128)S(6)} %copy.21.swapped, bf16[256,512]{1,0:T(8,128)(2,1)S(1)} %shard_map.98.refs_10_.refs_0_, bf16[256,512]{1,0:T(8,128)(2,1)S(1)} %shard_map.99.refs_10_.refs_1_, ...), custom_call_target="tpu_custom_call" | custom-call | bytes 3145728 | tf_op jit(solution)/shard_map/pallas_call | solution.py:290
  83.9 4.6 %collective-permute-done.18.refs_2_ = bf16[256,512]{1,0:T(8,128)(2,1)S(1)} collective-permute-done((bf16[256,512]{1,0:T(8,128)(2,1)S(1)}, bf16[256,512]{1,0:T(8,128)(2,1)S(1)}, u32[]{:S(2)}, u32[]{:S(2)}) %collective-permute-start.18) | collective-permute-done | bytes 262176 | tf_op jit(solution)/shard_map/ppermute | solution.py:330
  88.5 1.4 %shard_map.105 = (bf16[1,1024,512]{2,1,0:T(8,128)(2,1)}, f32[1,2,512]{2,1,0:T(2,128)}) custom-call(s32[1]{0:T(128)S(6)} %copy.20.mate, s32[1]{0:T(128)S(6)} %copy.21.swapped, bf16[256,512]{1,0:T(8,128)(2,1)S(1)} %shard_map.101.refs_0_, bf16[256,512]{1,0:T(8,128)(2,1)S(1)} %shard_map.102.refs_1_, ...), custom_call_target="tpu_custom_call", output_to_operand_aliasing={{0}: (6, {})} | custom-call | bytes 1048576 | tf_op jit(solution)/shard_map/pallas_call | solution.py:290
  (47 shorter events, 8.9 us)
Async XLA Ops:
  0.6 5.1 %copy-start = (bf16[512,1024]{1,0:T(8,128)(2,1)S(1)}, bf16[512,1024]{1,0:T(8,128)(2,1)}, u32[]{:S(2)}) copy-start(bf16[512,1024]{1,0:T(8,128)(2,1)} %weight.7) | copy-start | bytes 3145732
  0.6 5.0 %copy-start.1 = (bf16[1,1024,512]{2,1,0:T(8,128)(2,1)S(1)}, bf16[1,1024,512]{2,1,0:T(8,128)(2,1)}, u32[]{:S(2)}) copy-start(bf16[1,1024,512]{2,1,0:T(8,128)(2,1)} %refs_8_.7) | copy-start | bytes 3145732
  0.6 5.0 %collective-permute-start = (bf16[1024,512]{1,0:T(8,128)(2,1)}, bf16[1024,512]{1,0:T(8,128)(2,1)S(1)}, u32[]{:S(2)}, u32[]{:S(2)}) collective-permute-start(bf16[1024,512]{1,0:T(8,128)(2,1)} %bitcast.1), channel_id=1, source_target_pairs={{0,1},{1,0},{2,3},{3,2},{4,5},{5,4},{6,7},{7,6},{8,9},{9,8},{10,11... | collective-permute-start | bytes 3145736 | tf_op jit(solution)/shard_map/ppermute | solution.py:317
  1.2 4.5 %collective-permute-start.1 = (bf16[512,1024]{1,0:T(8,128)(2,1)}, bf16[512,1024]{1,0:T(8,128)(2,1)S(1)}, u32[]{:S(2)}, u32[]{:S(2)}) collective-permute-start(bf16[512,1024]{1,0:T(8,128)(2,1)} %weight.7), channel_id=1, source_target_pairs={{0,1},{1,0},{2,3},{3,2},{4,5},{5,4},{6,7},{7,6},{8,9},{9,8},{10,11... | collective-permute-start | bytes 3145736 | tf_op jit(solution)/shard_map/ppermute | solution.py:317
  1.2 1.2 %copy-start.3 = (bf16[384,1024]{1,0:T(8,128)(2,1)S(1)}, bf16[384,1024]{1,0:T(8,128)(2,1)}, u32[]{:S(2)}) copy-start(bf16[384,1024]{1,0:T(8,128)(2,1)} %value.1) | copy-start | bytes 2359300
  2.4 3.3 %copy-start.4 = (bf16[384,1024]{1,0:T(8,128)(2,1)S(1)}, bf16[384,1024]{1,0:T(8,128)(2,1)}, u32[]{:S(2)}) copy-start(bf16[384,1024]{1,0:T(8,128)(2,1)} %value.1) | copy-start | bytes 2359300
  2.7 8.1 %collective-permute-start.2 = (bf16[96,1024]{1,0:T(8,128)(2,1)S(1)}, bf16[96,1024]{1,0:T(8,128)(2,1)S(1)}, u32[]{:S(2)}, u32[]{:S(2)}) collective-permute-start(bf16[96,1024]{1,0:T(8,128)(2,1)S(1)} %shard_map.88), channel_id=1, source_target_pairs={{0,2},{1,3},{2,0},{3,1},{4,6},{5,7},{6,4},{7,5},{8,10},{9,11},{10,... | collective-permute-start | bytes 589832 | tf_op jit(solution)/shard_map/ppermute | solution.py:320
  8.7 19.5 %collective-permute-start.9 = (bf16[1024,384]{1,0:T(8,128)(2,1)S(1)}, bf16[1024,384]{1,0:T(8,128)(2,1)S(1)}, u32[]{:S(2)}, u32[]{:S(2)}) collective-permute-start(bf16[1024,384]{1,0:T(8,128)(2,1)S(1)} %get-tuple-element.18.refs_4_), channel_id=1, source_target_pairs={{0,1},{1,0},{2,3},{3,2},{4,5},{5,4},{6,7},{7,6},{8,9},{9,8},{10,11... | collective-permute-start | bytes 2359304 | tf_op jit(solution)/shard_map/ppermute | solution.py:317
  10.8 19.0 %collective-permute-start.8 = (bf16[384,1024]{1,0:T(8,128)(2,1)S(1)}, bf16[384,1024]{1,0:T(8,128)(2,1)S(1)}, u32[]{:S(2)}, u32[]{:S(2)}) collective-permute-start(bf16[384,1024]{1,0:T(8,128)(2,1)S(1)} %shard_map.91), channel_id=1, source_target_pairs={{0,2},{1,3},{2,0},{3,1},{4,6},{5,7},{6,4},{7,5},{8,10},{9,11},{10,... | collective-permute-start | bytes 2359304 | tf_op jit(solution)/shard_map/ppermute | solution.py:320
  12.5 5.7 %collective-permute-start.4 = (bf16[96,1024]{1,0:T(8,128)(2,1)S(1)}, bf16[96,1024]{1,0:T(8,128)(2,1)S(1)}, u32[]{:S(2)}, u32[]{:S(2)}) collective-permute-start(bf16[96,1024]{1,0:T(8,128)(2,1)S(1)} %shard_map.89.refs_0_), channel_id=1, source_target_pairs={{0,8},{4,12},{8,0},{12,4},{16,24},{20,28},{24,16},{28,20},{1,9},{5... | collective-permute-start | bytes 589832 | tf_op jit(solution)/shard_map/ppermute | solution.py:326
  14.1 6.5 %collective-permute-start.3 = (bf16[96,1024]{1,0:T(8,128)(2,1)S(1)}, bf16[96,1024]{1,0:T(8,128)(2,1)S(1)}, u32[]{:S(2)}, u32[]{:S(2)}) collective-permute-start(bf16[96,1024]{1,0:T(8,128)(2,1)S(1)} %shard_map.89.refs_0_), channel_id=1, source_target_pairs={{0,4},{4,0},{8,12},{12,8},{16,20},{20,16},{24,28},{28,24},{1,5},{5... | collective-permute-start | bytes 589832 | tf_op jit(solution)/shard_map/ppermute | solution.py:323
  15.6 12.6 %collective-permute-start.10 = (bf16[384,512]{1,0:T(8,128)(2,1)S(1)}, bf16[384,512]{1,0:T(8,128)(2,1)S(1)}, u32[]{:S(2)}, u32[]{:S(2)}) collective-permute-start(bf16[384,512]{1,0:T(8,128)(2,1)S(1)} %get-tuple-element.19), channel_id=1, source_target_pairs={{0,1},{1,0},{2,3},{3,2},{4,5},{5,4},{6,7},{7,6},{8,9},{9,8},{10,11... | collective-permute-start | bytes 1179656 | tf_op jit(solution)/shard_map/ppermute | solution.py:317
  18.3 4.7 %collective-permute-start.5 = (bf16[48,1024]{1,0:T(8,128)(2,1)S(1)}, bf16[48,1024]{1,0:T(8,128)(2,1)S(1)}, u32[]{:S(2)}, u32[]{:S(2)}) collective-permute-start(bf16[48,1024]{1,0:T(8,128)(2,1)S(1)} %slice.8), channel_id=1, source_target_pairs={{0,4},{4,0},{8,12},{12,8},{16,20},{20,16},{24,28},{28,24},{1,5},{5... | collective-permute-start | bytes 294920 | tf_op jit(solution)/shard_map/ppermute | solution.py:323
  20.6 4.7 %collective-permute-start.6 = (bf16[48,1024]{1,0:T(8,128)(2,1)S(1)}, bf16[48,1024]{1,0:T(8,128)(2,1)S(1)}, u32[]{:S(2)}, u32[]{:S(2)}) collective-permute-start(bf16[48,1024]{1,0:T(8,128)(2,1)S(1)} %slice.9), channel_id=1, source_target_pairs={{0,8},{4,12},{8,0},{12,4},{16,24},{20,28},{24,16},{28,20},{1,9},{5... | collective-permute-start | bytes 294920 | tf_op jit(solution)/shard_map/ppermute | solution.py:326
  29.9 4.0 %collective-permute-start.11 = (bf16[384,1024]{1,0:T(8,128)(2,1)S(1)}, bf16[384,1024]{1,0:T(8,128)(2,1)S(1)}, u32[]{:S(2)}, u32[]{:S(2)}) collective-permute-start(bf16[384,1024]{1,0:T(8,128)(2,1)S(1)} %shard_map.92.errors), channel_id=1, source_target_pairs={{0,1},{1,0},{2,3},{3,2},{4,5},{5,4},{6,7},{7,6},{8,9},{9,8},{10,11... | collective-permute-start | bytes 2359304 | tf_op jit(solution)/shard_map/ppermute | solution.py:317
  30.0 4.6 %collective-permute-start.13 = (bf16[1024,384]{1,0:T(8,128)(2,1)S(1)}, bf16[1024,384]{1,0:T(8,128)(2,1)S(1)}, u32[]{:S(2)}, u32[]{:S(2)}) collective-permute-start(bf16[1024,384]{1,0:T(8,128)(2,1)S(1)} %get-tuple-element.22.refs_6_), channel_id=1, source_target_pairs={{0,1},{1,0},{2,3},{3,2},{4,5},{5,4},{6,7},{7,6},{8,9},{9,8},{10,11... | collective-permute-start | bytes 2359304 | tf_op jit(solution)/shard_map/ppermute | solution.py:317
  30.5 19.5 %collective-permute-start.7 = (bf16[384,1024]{1,0:T(8,128)(2,1)S(1)}, bf16[384,1024]{1,0:T(8,128)(2,1)S(1)}, u32[]{:S(2)}, u32[]{:S(2)}) collective-permute-start(bf16[384,1024]{1,0:T(8,128)(2,1)S(1)} %get-tuple-element.16), channel_id=1, source_target_pairs={{0,2},{1,3},{2,0},{3,1},{4,6},{5,7},{6,4},{7,5},{8,10},{9,11},{10,... | collective-permute-start | bytes 2359304 | tf_op jit(solution)/shard_map/ppermute | solution.py:320
  31.9 2.0 %collective-permute-start.12 = (bf16[384,512]{1,0:T(8,128)(2,1)S(1)}, bf16[384,512]{1,0:T(8,128)(2,1)S(1)}, u32[]{:S(2)}, u32[]{:S(2)}) collective-permute-start(bf16[384,512]{1,0:T(8,128)(2,1)S(1)} %get-tuple-element.21), channel_id=1, source_target_pairs={{0,1},{1,0},{2,3},{3,2},{4,5},{5,4},{6,7},{7,6},{8,9},{9,8},{10,11... | collective-permute-start | bytes 1179656 | tf_op jit(solution)/shard_map/ppermute | solution.py:317
  50.1 2.4 %collective-permute-start.14 = (bf16[384,1024]{1,0:T(8,128)(2,1)S(1)}, bf16[384,1024]{1,0:T(8,128)(2,1)S(1)}, u32[]{:S(2)}, u32[]{:S(2)}) collective-permute-start(bf16[384,1024]{1,0:T(8,128)(2,1)S(1)} %shard_map.95.errors), channel_id=1, source_target_pairs={{0,1},{1,0},{2,3},{3,2},{4,5},{5,4},{6,7},{7,6},{8,9},{9,8},{10,11... | collective-permute-start | bytes 2359304 | tf_op jit(solution)/shard_map/ppermute | solution.py:317
  50.8 2.3 %copy-start.2 = (bf16[1,1024,512]{2,1,0:T(8,128)(2,1)S(1)}, bf16[1,1024,512]{2,1,0:T(8,128)(2,1)}, u32[]{:S(2)}) copy-start(bf16[1,1024,512]{2,1,0:T(8,128)(2,1)} %refs_9_.7) | copy-start | bytes 3145732
  53.9 9.2 %collective-permute-start.19 = (bf16[256,512]{1,0:T(8,128)(2,1)S(1)}, bf16[256,512]{1,0:T(8,128)(2,1)S(1)}, u32[]{:S(2)}, u32[]{:S(2)}) collective-permute-start(bf16[256,512]{1,0:T(8,128)(2,1)S(1)} %shard_map.98.refs_10_.refs_0_), channel_id=1, source_target_pairs={{0,4},{4,0},{8,12},{12,8},{16,20},{20,16},{24,28},{28,24},{1,5},{5... | collective-permute-start | bytes 786440 | tf_op jit(solution)/shard_map/ppermute | solution.py:323
  56.1 12.8 %collective-permute-start.16 = (bf16[256,512]{1,0:T(8,128)(2,1)S(1)}, bf16[256,512]{1,0:T(8,128)(2,1)S(1)}, u32[]{:S(2)}, u32[]{:S(2)}) collective-permute-start(bf16[256,512]{1,0:T(8,128)(2,1)S(1)} %shard_map.99.refs_10_.refs_1_), channel_id=1, source_target_pairs={{0,4},{4,0},{8,12},{12,8},{16,20},{20,16},{24,28},{28,24},{1,5},{5... | collective-permute-start | bytes 786440 | tf_op jit(solution)/shard_map/ppermute | solution.py:323
  57.6 16.7 %collective-permute-start.20 = (bf16[256,512]{1,0:T(8,128)(2,1)S(1)}, bf16[256,512]{1,0:T(8,128)(2,1)S(1)}, u32[]{:S(2)}, u32[]{:S(2)}) collective-permute-start(bf16[256,512]{1,0:T(8,128)(2,1)S(1)} %shard_map.100.refs_10_.refs_2_), channel_id=1, source_target_pairs={{0,4},{4,0},{8,12},{12,8},{16,20},{20,16},{24,28},{28,24},{1,5},{5... | collective-permute-start | bytes 786440 | tf_op jit(solution)/shard_map/ppermute | solution.py:323
  63.1 11.2 %collective-permute-start.21 = (bf16[256,512]{1,0:T(8,128)(2,1)S(1)}, bf16[256,512]{1,0:T(8,128)(2,1)S(1)}, u32[]{:S(2)}, u32[]{:S(2)}) collective-permute-start(bf16[256,512]{1,0:T(8,128)(2,1)S(1)} %collective-permute-done.19.refs_3_), channel_id=1, source_target_pairs={{0,8},{4,28},{8,16},{12,4},{16,24},{20,12},{24,0},{28,20},{1,9},{5... | collective-permute-start | bytes 786440 | tf_op jit(solution)/shard_map/ppermute | solution.py:330
  65.3 13.8 %collective-permute-start.15 = (bf16[256,512]{1,0:T(8,128)(2,1)S(1)}, bf16[256,512]{1,0:T(8,128)(2,1)S(1)}, u32[]{:S(2)}, u32[]{:S(2)}) collective-permute-start(bf16[256,512]{1,0:T(8,128)(2,1)S(1)} %shard_map.101.refs_0_), channel_id=1, source_target_pairs={{0,4},{4,0},{8,12},{12,8},{16,20},{20,16},{24,28},{28,24},{1,5},{5... | collective-permute-start | bytes 786440 | tf_op jit(solution)/shard_map/ppermute | solution.py:323
  68.9 10.2 %collective-permute-start.17 = (bf16[256,512]{1,0:T(8,128)(2,1)S(1)}, bf16[256,512]{1,0:T(8,128)(2,1)S(1)}, u32[]{:S(2)}, u32[]{:S(2)}) collective-permute-start(bf16[256,512]{1,0:T(8,128)(2,1)S(1)} %collective-permute-done.16.refs_4_), channel_id=1, source_target_pairs={{0,8},{4,28},{8,16},{12,4},{16,24},{20,12},{24,0},{28,20},{1,9},{5... | collective-permute-start | bytes 786440 | tf_op jit(solution)/shard_map/ppermute | solution.py:330
  74.3 8.5 %collective-permute-start.22 = (bf16[256,512]{1,0:T(8,128)(2,1)S(1)}, bf16[256,512]{1,0:T(8,128)(2,1)S(1)}, u32[]{:S(2)}, u32[]{:S(2)}) collective-permute-start(bf16[256,512]{1,0:T(8,128)(2,1)S(1)} %shard_map.103.refs_5_), channel_id=1, source_target_pairs={{0,8},{4,28},{8,16},{12,4},{16,24},{20,12},{24,0},{28,20},{1,9},{5... | collective-permute-start | bytes 786440 | tf_op jit(solution)/shard_map/ppermute | solution.py:330
  79.1 9.3 %collective-permute-start.18 = (bf16[256,512]{1,0:T(8,128)(2,1)S(1)}, bf16[256,512]{1,0:T(8,128)(2,1)S(1)}, u32[]{:S(2)}, u32[]{:S(2)}) collective-permute-start(bf16[256,512]{1,0:T(8,128)(2,1)S(1)} %shard_map.102.refs_1_), channel_id=1, source_target_pairs={{0,8},{4,28},{8,16},{12,4},{16,24},{20,12},{24,0},{28,20},{1,9},{5... | collective-permute-start | bytes 786440 | tf_op jit(solution)/shard_map/ppermute | solution.py:330

commit v5 on v4

--- a/solution.py
+++ b/solution.py
@@ -150,7 +150,7 @@
         out_specs=[vmem for out in outs],
         scratch_shapes=[pltpu.VMEM((count, width), f32), pltpu.VMEM((count, width), bf16)],
         compiler_params=limit(12),
-        cost_estimate=cost(4 * count * width * block, 8 * width * block),
+        cost_estimate=cost(0, 1000),
     )(*given, *weights, *earlier)
 
 
@@ -209,31 +209,50 @@
     )(errors, weight, slope, *earlier)
 
 
-def update_kernel(start, strength, *refs):
-    grads, normed = refs[:4], refs[4:8]
-    params, noise = refs[8:10]
-    out = refs[-1]
-    here = slice(start, start + out.shape[0])
-    total = 0.0
-    for values, grad in zip(normed, grads):
-        total += matmul(values[here], grad[...])
-    current = params[0, here].astype(f32)
-    slope = total * params.shape[1] ** -0.5
-    moved = current - drift_stride * (slope + current) + strength[...] * noise[0, here].astype(f32)
-    out[...] = moved.astype(bf16)
-
-
-def update(start, rows, heat, grads, normed, params, noise, *earlier):
+def begin_kernel(strength, first, second, normed, normed_mate, params, noise, out):
+    width = params.shape[1]
+    rows = width // 4
+    for start in range(0, width, rows):
+        here = slice(start, start + rows)
+        slope = matmul(normed[here], first[...]) + matmul(normed_mate[here], second[...])
+        out[here] = (
+            (1.0 - drift_stride) * params[0, here].astype(f32)
+            + strength[...] * noise[0, here].astype(f32)
+            - (drift_stride * width**-0.5) * slope
+        )
+
+
+def begin(strength, grads, normed, params, noise):
     width, count = normed[0].shape
     block = grads[0].shape[1]
     return pl.pallas_call(
+        begin_kernel,
+        out_shape=shape((width, block), f32),
+        in_specs=[vmem] * 7,
+        out_specs=vmem,
+        compiler_params=limit(4),
+        cost_estimate=cost(2 * width * count * block, 8 * width * count),
+    )(strength, *grads, *normed, params, noise)
+
+
+def update_kernel(start, begun, first, second, normed, normed_mate, *rest):
+    out = rest[-1]
+    here = slice(start, start + out.shape[0])
+    slope = matmul(normed[here], first[...]) + matmul(normed_mate[here], second[...])
+    out[...] = (begun[here] - (drift_stride * normed.shape[0] ** -0.5) * slope).astype(bf16)
+
+
+def update(start, rows, begun, grads, normed, *earlier):
+    count = normed[0].shape[1]
+    block = grads[0].shape[1]
+    return pl.pallas_call(
         functools.partial(update_kernel, start),
         out_shape=shape((rows, block)),
-        in_specs=[vmem] * 11 + [anywhere] * len(earlier),
+        in_specs=[vmem] * 5 + [anywhere] * len(earlier),
         out_specs=vmem,
         compiler_params=limit(4),
-        cost_estimate=cost(4 * rows * count * block, 8 * rows * count),
-    )(heat, *grads, *normed, params, noise, *earlier)
+        cost_estimate=cost(2 * rows * count * block, 8 * rows * count),
+    )(begun, *grads, *normed, *earlier)
 
 
 def role(mate, swapped):
@@ -347,24 +366,24 @@
     token_across, token_behind = step_one(token_own)
     token_pieces = step_two(token_own, token_across, token_behind)
     normed_mate = to_core(normed)
-    slope_mate = to_core(slope_send)
     far, far_slope, far_slope_send, far_part, far_base = forward(token_pieces, count, weights)
     far_sent = to_chip(far_part)
     far_mate = to_core(far)
-    far_slope_mate = to_core(far_slope_send)
 
     strength = strength_of(chain_heat, block)
-    errors = errors_of(far_base, sent, normed_mate, slope_mate, strength)
+    errors = errors_of(far_base, sent, normed_mate, strength)
     far_grads = [
         hidden_of(errors, output_matrix, far_slope),
-        hidden_of(to_core(errors), output_matrix, far_slope_mate),
+        to_core(hidden_of(errors, mate_out, far_slope_send)),
     ]
-    errors = errors_of(base, far_sent, *far_grads, far_mate)
-    near_grads = [
+    begun = begin(
+        strength, far_grads, (far, far_mate), rooted_input_matrix, chain_normal_draws
+    )
+    errors = errors_of(base, far_sent, begun)
+    grads = [
         hidden_of(errors, output_matrix, slope),
-        hidden_of(to_core(errors), output_matrix, slope_mate),
+        to_core(hidden_of(errors, mate_out, slope_send)),
     ]
-    grads = near_grads + far_grads
 
     pairing = (matched_chain, swap_mask)
     width = params.shape[0]
@@ -372,16 +391,7 @@
     starts = [sum(sizes[:chunk]) for chunk in range(len(sizes))]
     own, across, beyond = [], [], []
     for chunk, (start, rows) in enumerate(zip(starts, sizes)):
-        fresh = update(
-            start,
-            rows,
-            strength,
-            grads,
-            (normed, normed_mate, far, far_mate),
-            rooted_input_matrix,
-            chain_normal_draws,
-            *own[-1:],
-        )
+        fresh = update(start, rows, begun, grads, (normed, normed_mate), *own[-1:])
         own.append(fresh)
         across.append(to_mate(fresh))
     done = None

time: 90 us -> 87.3 us (0.970)
  starting transfers between devices: 25.9 us -> 20.9 us
  waiting for transfers between devices: 45.6 us -> 48 us
    ppermute x6, waiting for transfers between devices: 13.1 us -> 17.4 us  [to_mate(): return lax.ppermute(value, 'rep', [(i, i ^ 1) for i in range(replicas)])]
    ppermute x4, starting transfers between devices: 5.68 us -> 3.16 us  [to_next(): return lax.ppermute(value, 'rep', pairs)]
    ppermute x3, waiting for transfers between devices: 19 us -> 17.4 us  [to_chip(): return lax.ppermute(value, 'dp', [(i, i ^ 2) for i in range(4)])]
    pallas_call x4, Pallas kernels: 3.09 us -> 1.72 us  [update(): pl.pallas_call(functools.partial(update_kernel, start), out_shape=shape((...]
    ppermute x3, starting transfers between devices: 6.18 us -> 4.89 us  [to_chip(): return lax.ppermute(value, 'dp', [(i, i ^ 2) for i in range(4)])]
    pallas_call x0 -> x1, Pallas kernels: none -> 1.25 us  [begin(): pl.pallas_call(begin_kernel, out_shape=shape((width, block), f32), in_spe...]
    ppermute x8 -> x6, waiting for transfers between devices: 3.09 us -> 2.19 us  [to_core(): return lax.ppermute(value, 'dp', [(i, i ^ 1) for i in range(4)])]
  transfers between devices with their start and end apart: 23 -> 21, of which waited for: 14 -> 15; matrix products, arithmetic and copies ran while one was open for 0% -> 0% of each run, Pallas kernels for 13% -> 13%
where the time goes in v5:
time: 87.3 us; the launch traced here: 87.2 us
  waiting for transfers between devices  48 us (55%)
  starting transfers between devices  20.9 us (24%)
  Pallas kernels  14.2 us (16%)
  between operations  2.82 us (3%)
  local copies, waits for them, and re-layouts  1.25 us (1%)
    ppermute x6, waiting for transfers between devices, to_mate(): return lax.ppermute(value, 'rep', [(i, i ^ 1) for i in range(replicas)])  17.4 us
    ppermute x3, waiting for transfers between devices, to_chip(): return lax.ppermute(value, 'dp', [(i, i ^ 2) for i in range(4)])  17.4 us
    ppermute x6, starting transfers between devices, to_mate(): return lax.ppermute(value, 'rep', [(i, i ^ 1) for i in range(replicas)])  9.52 us
    ppermute x4, waiting for transfers between devices, to_next(): return lax.ppermute(value, 'rep', pairs)  6.13 us
    pallas_call x2, Pallas kernels, forward(): pl.pallas_call(functools.partial(forward_kernel, len(given), len(earlier)...  5.84 us
    ppermute x2, waiting for transfers between devices, to_pair(): return lax.ppermute(value, 'rep', [(i, i ^ 2) for i in range(replicas)])  4.99 us
    ppermute x3, starting transfers between devices, to_chip(): return lax.ppermute(value, 'dp', [(i, i ^ 2) for i in range(4)])  4.89 us
    ppermute x4, starting transfers between devices, to_next(): return lax.ppermute(value, 'rep', pairs)  3.16 us
  transfers between devices with their start and end apart: 21, of which 15 were waited for; matrix products, arithmetic and copies ran while one was open for 0% of the time, Pallas kernels for 13%

profile of v5, /device:TPU:0, one launch (start us, length us, event | category | flops | bytes accessed | tf_op | source)
XLA Modules:
  0.0 87.2 jit_solution(12260504562989303044)
XLA Ops:
  1.2 1.2 %copy-done.3 = bf16[384,1024]{1,0:T(8,128)(2,1)S(1)} copy-done((bf16[384,1024]{1,0:T(8,128)(2,1)S(1)}, bf16[384,1024]{1,0:T(8,128)(2,1)}, u32[]{:S(2)}) %copy-start.3) | copy-done | bytes 786456
  2.7 3.0 %collective-permute-start = (bf16[96,1024]{1,0:T(8,128)(2,1)S(1)}, bf16[96,1024]{1,0:T(8,128)(2,1)S(1)}, u32[]{:S(2)}, u32[]{:S(2)}) collective-permute-start(bf16[96,1024]{1,0:T(8,128)(2,1)S(1)} %shard_map.87), channel_id=1, source_target_pairs={{0,2},{1,3},{2,0},{3,1},{4,6},{5,7},{6,4},{7,5},{8,10},{9,11},{10,... | collective-permute-start | bytes 589832 | tf_op jit(solution)/shard_map/ppermute | solution.py:339
  5.7 2.9 %shard_map.88 = (bf16[1024,384]{1,0:T(8,128)(2,1)S(1)}, bf16[384,512]{1,0:T(8,128)(2,1)S(1)}, bf16[384,512]{1,0:T(8,128)(2,1)S(1)}, bf16[384,1024]{1,0:T(8,128)(2,1)S(1)}, f32[384,1024]{1,0:T(8,128)S(1)}) custom-call(bf16[384,1024]{1,0:T(8,128)(2,1)S(1)} %copy-done.4, bf16[1024,512]{1,0:T(8,128)(2,1)S(1)} %bitcast.2, ...), custom_call_target="tpu_custom_call" | custom-call | bytes 1000 | tf_op jit(solution)/shard_map/pallas_call | solution.py:146
  8.8 2.0 %collective-permute-done.refs_0_.refs_1_ = bf16[96,1024]{1,0:T(8,128)(2,1)S(1)} collective-permute-done((bf16[96,1024]{1,0:T(8,128)(2,1)S(1)}, bf16[96,1024]{1,0:T(8,128)(2,1)S(1)}, u32[]{:S(2)}, u32[]{:S(2)}) %collective-permute-start) | collective-permute-done | bytes 196640 | tf_op jit(solution)/shard_map/ppermute | solution.py:339
  10.8 1.7 %collective-permute-start.7 = (bf16[384,1024]{1,0:T(8,128)(2,1)S(1)}, bf16[384,1024]{1,0:T(8,128)(2,1)S(1)}, u32[]{:S(2)}, u32[]{:S(2)}) collective-permute-start(bf16[384,1024]{1,0:T(8,128)(2,1)S(1)} %shard_map.91), channel_id=1, source_target_pairs={{0,2},{1,3},{2,0},{3,1},{4,6},{5,7},{6,4},{7,5},{8,10},{9,11},{10,... | collective-permute-start | bytes 2359304 | tf_op jit(solution)/shard_map/ppermute | solution.py:339
  12.5 1.6 %collective-permute-start.4 = (bf16[96,1024]{1,0:T(8,128)(2,1)S(1)}, bf16[96,1024]{1,0:T(8,128)(2,1)S(1)}, u32[]{:S(2)}, u32[]{:S(2)}) collective-permute-start(bf16[96,1024]{1,0:T(8,128)(2,1)S(1)} %shard_map.89.refs_0_), channel_id=1, source_target_pairs={{0,8},{4,12},{8,0},{12,4},{16,24},{20,28},{24,16},{28,20},{1,9},{5... | collective-permute-start | bytes 589832 | tf_op jit(solution)/shard_map/ppermute | solution.py:345
  14.1 1.5 %collective-permute-start.3 = (bf16[96,1024]{1,0:T(8,128)(2,1)S(1)}, bf16[96,1024]{1,0:T(8,128)(2,1)S(1)}, u32[]{:S(2)}, u32[]{:S(2)}) collective-permute-start(bf16[96,1024]{1,0:T(8,128)(2,1)S(1)} %shard_map.89.refs_0_), channel_id=1, source_target_pairs={{0,4},{4,0},{8,12},{12,8},{16,20},{20,16},{24,28},{28,24},{1,5},{5... | collective-permute-start | bytes 589832 | tf_op jit(solution)/shard_map/ppermute | solution.py:342
  15.6 2.7 %collective-permute-done.4.refs_2_ = bf16[96,1024]{1,0:T(8,128)(2,1)S(1)} collective-permute-done((bf16[96,1024]{1,0:T(8,128)(2,1)S(1)}, bf16[96,1024]{1,0:T(8,128)(2,1)S(1)}, u32[]{:S(2)}, u32[]{:S(2)}) %collective-permute-start.4) | collective-permute-done | bytes 196640 | tf_op jit(solution)/shard_map/ppermute | solution.py:345
  18.3 1.6 %collective-permute-start.5 = (bf16[48,1024]{1,0:T(8,128)(2,1)S(1)}, bf16[48,1024]{1,0:T(8,128)(2,1)S(1)}, u32[]{:S(2)}, u32[]{:S(2)}) collective-permute-start(bf16[48,1024]{1,0:T(8,128)(2,1)S(1)} %slice.8), channel_id=1, source_target_pairs={{0,4},{4,0},{8,12},{12,8},{16,20},{20,16},{24,28},{28,24},{1,5},{5... | collective-permute-start | bytes 294920 | tf_op jit(solution)/shard_map/ppermute | solution.py:342
  20.6 0.9 %collective-permute-start.6 = (bf16[48,1024]{1,0:T(8,128)(2,1)S(1)}, bf16[48,1024]{1,0:T(8,128)(2,1)S(1)}, u32[]{:S(2)}, u32[]{:S(2)}) collective-permute-start(bf16[48,1024]{1,0:T(8,128)(2,1)S(1)} %slice.9), channel_id=1, source_target_pairs={{0,8},{4,12},{8,0},{12,4},{16,24},{20,28},{24,16},{28,20},{1,9},{5... | collective-permute-start | bytes 294920 | tf_op jit(solution)/shard_map/ppermute | solution.py:345
  21.5 1.5 %collective-permute-done.5.refs_3_ = bf16[48,1024]{1,0:T(8,128)(2,1)S(1)} collective-permute-done((bf16[48,1024]{1,0:T(8,128)(2,1)S(1)}, bf16[48,1024]{1,0:T(8,128)(2,1)S(1)}, u32[]{:S(2)}, u32[]{:S(2)}) %collective-permute-start.5) | collective-permute-done | bytes 98336 | tf_op jit(solution)/shard_map/ppermute | solution.py:342
  22.9 2.3 %collective-permute-done.6.refs_4_ = bf16[48,1024]{1,0:T(8,128)(2,1)S(1)} collective-permute-done((bf16[48,1024]{1,0:T(8,128)(2,1)S(1)}, bf16[48,1024]{1,0:T(8,128)(2,1)S(1)}, u32[]{:S(2)}, u32[]{:S(2)}) %collective-permute-start.6) | collective-permute-done | bytes 98336 | tf_op jit(solution)/shard_map/ppermute | solution.py:345
  25.3 2.9 %shard_map.90 = (bf16[1024,384]{1,0:T(8,128)(2,1)S(1)}, bf16[384,512]{1,0:T(8,128)(2,1)S(1)}, bf16[384,512]{1,0:T(8,128)(2,1)S(1)}, bf16[384,1024]{1,0:T(8,128)(2,1)S(1)}, f32[384,1024]{1,0:T(8,128)S(1)}) custom-call(bf16[96,1024]{1,0:T(8,128)(2,1)S(1)} %shard_map.89.refs_0_, bf16[96,1024]{1,0:T(8,128)(2,1)S(1)} %collective-permute-done.3.refs_1_, ...), custom_call_target="tpu_custom_call" | custom-call | bytes 1000 | tf_op jit(solution)/shard_map/pallas_call | solution.py:146
  31.2 1.1 %collective-permute-done.9.second = bf16[384,512]{1,0:T(8,128)(2,1)S(1)} collective-permute-done((bf16[384,512]{1,0:T(8,128)(2,1)S(1)}, bf16[384,512]{1,0:T(8,128)(2,1)S(1)}, u32[]{:S(2)}, u32[]{:S(2)}) %collective-permute-start.9) | collective-permute-done | bytes 393248 | tf_op jit(solution)/shard_map/ppermute | solution.py:336
  32.3 1.3 %shard_map.95.refs_0_.begun = f32[1024,512]{1,0:T(8,128)S(1)} custom-call(f32[1,512]{1,0:T(1,128)S(1)} %shard_map.86.refs_1_.strength, bf16[384,512]{1,0:T(8,128)(2,1)S(1)} %shard_map.93.first, bf16[384,512]{1,0:T(8,128)(2,1)S(1)} %collective-permute-done.9.second, bf16[1024,384]{1,0:T(8,128)(2,1)S(1)} %get-tuple-element.19.normed, ...), custom_call_target="tpu_custom_call" | custom-call | flops 805306368 | bytes 3145728 | tf_op jit(solution)/shard_map/pallas_call | solution.py:228
  33.6 14.7 %collective-permute-done.11.sent = bf16[384,1024]{1,0:T(8,128)(2,1)S(1)} collective-permute-done((bf16[384,1024]{1,0:T(8,128)(2,1)S(1)}, bf16[384,1024]{1,0:T(8,128)(2,1)S(1)}, u32[]{:S(2)}, u32[]{:S(2)}) %collective-permute-start.11) | collective-permute-done | bytes 786464 | tf_op jit(solution)/shard_map/ppermute | solution.py:339
  49.7 1.1 %collective-permute-done.12.second = bf16[384,512]{1,0:T(8,128)(2,1)S(1)} collective-permute-done((bf16[384,512]{1,0:T(8,128)(2,1)S(1)}, bf16[384,512]{1,0:T(8,128)(2,1)S(1)}, u32[]{:S(2)}, u32[]{:S(2)}) %collective-permute-start.12) | collective-permute-done | bytes 393248 | tf_op jit(solution)/shard_map/ppermute | solution.py:336
  51.2 1.5 %collective-permute-start.17 = (bf16[256,512]{1,0:T(8,128)(2,1)S(1)}, bf16[256,512]{1,0:T(8,128)(2,1)S(1)}, u32[]{:S(2)}, u32[]{:S(2)}) collective-permute-start(bf16[256,512]{1,0:T(8,128)(2,1)S(1)} %shard_map.99.rest_0_.refs_0_), channel_id=1, source_target_pairs={{0,4},{4,0},{8,12},{12,8},{16,20},{20,16},{24,28},{28,24},{1,5},{5... | collective-permute-start | bytes 786440 | tf_op jit(solution)/shard_map/ppermute | solution.py:342
  54.3 1.5 %collective-permute-start.18 = (bf16[256,512]{1,0:T(8,128)(2,1)S(1)}, bf16[256,512]{1,0:T(8,128)(2,1)S(1)}, u32[]{:S(2)}, u32[]{:S(2)}) collective-permute-start(bf16[256,512]{1,0:T(8,128)(2,1)S(1)} %shard_map.101.rest_0_.refs_2_), channel_id=1, source_target_pairs={{0,4},{4,0},{8,12},{12,8},{16,20},{20,16},{24,28},{28,24},{1,5},{5... | collective-permute-start | bytes 786440 | tf_op jit(solution)/shard_map/ppermute | solution.py:342
  55.8 4.7 %collective-permute-done.17.refs_3_ = bf16[256,512]{1,0:T(8,128)(2,1)S(1)} collective-permute-done((bf16[256,512]{1,0:T(8,128)(2,1)S(1)}, bf16[256,512]{1,0:T(8,128)(2,1)S(1)}, u32[]{:S(2)}, u32[]{:S(2)}) %collective-permute-start.17) | collective-permute-done | bytes 262176 | tf_op jit(solution)/shard_map/ppermute | solution.py:342
  60.5 0.8 collective-permute-start.19
  61.7 2.8 %collective-permute-start.13 = (bf16[256,512]{1,0:T(8,128)(2,1)S(1)}, bf16[256,512]{1,0:T(8,128)(2,1)S(1)}, u32[]{:S(2)}, u32[]{:S(2)}) collective-permute-start(bf16[256,512]{1,0:T(8,128)(2,1)S(1)} %shard_map.102.refs_0_), channel_id=1, source_target_pairs={{0,4},{4,0},{8,12},{12,8},{16,20},{20,16},{24,28},{28,24},{1,5},{5... | collective-permute-start | bytes 786440 | tf_op jit(solution)/shard_map/ppermute | solution.py:342
  64.4 1.6 %collective-permute-done.14.refs_4_ = bf16[256,512]{1,0:T(8,128)(2,1)S(1)} collective-permute-done((bf16[256,512]{1,0:T(8,128)(2,1)S(1)}, bf16[256,512]{1,0:T(8,128)(2,1)S(1)}, u32[]{:S(2)}, u32[]{:S(2)}) %collective-permute-start.14) | collective-permute-done | bytes 262176 | tf_op jit(solution)/shard_map/ppermute | solution.py:342
  66.1 0.8 collective-permute-start.15
  66.9 4.8 %collective-permute-done.18.refs_0_ = bf16[256,512]{1,0:T(8,128)(2,1)S(1)} collective-permute-done((bf16[256,512]{1,0:T(8,128)(2,1)S(1)}, bf16[256,512]{1,0:T(8,128)(2,1)S(1)}, u32[]{:S(2)}, u32[]{:S(2)}) %collective-permute-start.18) | collective-permute-done | bytes 262176 | tf_op jit(solution)/shard_map/ppermute | solution.py:342
  71.7 0.8 collective-permute-start.20
  72.5 4.0 %collective-permute-done.13.refs_0_ = bf16[256,512]{1,0:T(8,128)(2,1)S(1)} collective-permute-done((bf16[256,512]{1,0:T(8,128)(2,1)S(1)}, bf16[256,512]{1,0:T(8,128)(2,1)S(1)}, u32[]{:S(2)}, u32[]{:S(2)}) %collective-permute-start.13) | collective-permute-done | bytes 262176 | tf_op jit(solution)/shard_map/ppermute | solution.py:342
  76.5 0.8 collective-permute-start.16
  78.6 1.6 %collective-permute-done.20.refs_8_ = bf16[256,512]{1,0:T(8,128)(2,1)S(1)} collective-permute-done((bf16[256,512]{1,0:T(8,128)(2,1)S(1)}, bf16[256,512]{1,0:T(8,128)(2,1)S(1)}, u32[]{:S(2)}, u32[]{:S(2)}) %collective-permute-start.20) | collective-permute-done | bytes 262176 | tf_op jit(solution)/shard_map/ppermute | solution.py:349
  80.2 1.1 %shard_map.105 = (bf16[1,1024,512]{2,1,0:T(8,128)(2,1)}, f32[1,2,512]{2,1,0:T(2,128)S(1)}) custom-call(s32[1]{0:T(128)S(6)} %copy.20.mate, s32[1]{0:T(128)S(6)} %copy.21.swapped, bf16[256,512]{1,0:T(8,128)(2,1)S(1)} %shard_map.99.rest_0_.refs_0_, bf16[256,512]{1,0:T(8,128)(2,1)S(1)} %shard_map.100.rest_0_.refs_1_, ...), custom_call_target="tpu_custom_call" | custom-call | bytes 3145728 | tf_op jit(solution)/shard_map/pallas_call | solution.py:309
  81.2 4.5 %collective-permute-done.16.refs_2_ = bf16[256,512]{1,0:T(8,128)(2,1)S(1)} collective-permute-done((bf16[256,512]{1,0:T(8,128)(2,1)S(1)}, bf16[256,512]{1,0:T(8,128)(2,1)S(1)}, u32[]{:S(2)}, u32[]{:S(2)}) %collective-permute-start.16) | collective-permute-done | bytes 262176 | tf_op jit(solution)/shard_map/ppermute | solution.py:349
  85.8 1.4 %shard_map.106 = (bf16[1,1024,512]{2,1,0:T(8,128)(2,1)}, f32[1,2,512]{2,1,0:T(2,128)}) custom-call(s32[1]{0:T(128)S(6)} %copy.20.mate, s32[1]{0:T(128)S(6)} %copy.21.swapped, bf16[256,512]{1,0:T(8,128)(2,1)S(1)} %shard_map.102.refs_0_, bf16[256,512]{1,0:T(8,128)(2,1)S(1)} %shard_map.103.refs_1_, ...), custom_call_target="tpu_custom_call", output_to_operand_aliasing={{0}: (6, {})} | custom-call | bytes 1048576 | tf_op jit(solution)/shard_map/pallas_call | solution.py:309
  (44 shorter events, 7.8 us)
Async XLA Ops:
  0.6 5.1 %copy-start = (bf16[512,1024]{1,0:T(8,128)(2,1)S(1)}, bf16[512,1024]{1,0:T(8,128)(2,1)}, u32[]{:S(2)}) copy-start(bf16[512,1024]{1,0:T(8,128)(2,1)} %weight.3) | copy-start | bytes 3145732
  0.6 5.0 %copy-start.1 = (bf16[1,1024,512]{2,1,0:T(8,128)(2,1)S(1)}, bf16[1,1024,512]{2,1,0:T(8,128)(2,1)}, u32[]{:S(2)}) copy-start(bf16[1,1024,512]{2,1,0:T(8,128)(2,1)} %params.1) | copy-start | bytes 3145732
  0.6 5.0 %collective-permute-start.1 = (bf16[1024,512]{1,0:T(8,128)(2,1)}, bf16[1024,512]{1,0:T(8,128)(2,1)S(1)}, u32[]{:S(2)}, u32[]{:S(2)}) collective-permute-start(bf16[1024,512]{1,0:T(8,128)(2,1)} %bitcast.1), channel_id=1, source_target_pairs={{0,1},{1,0},{2,3},{3,2},{4,5},{5,4},{6,7},{7,6},{8,9},{9,8},{10,11... | collective-permute-start | bytes 3145736 | tf_op jit(solution)/shard_map/ppermute | solution.py:336
  1.2 4.5 %collective-permute-start.2 = (bf16[512,1024]{1,0:T(8,128)(2,1)}, bf16[512,1024]{1,0:T(8,128)(2,1)S(1)}, u32[]{:S(2)}, u32[]{:S(2)}) collective-permute-start(bf16[512,1024]{1,0:T(8,128)(2,1)} %weight.3), channel_id=1, source_target_pairs={{0,1},{1,0},{2,3},{3,2},{4,5},{5,4},{6,7},{7,6},{8,9},{9,8},{10,11... | collective-permute-start | bytes 3145736 | tf_op jit(solution)/shard_map/ppermute | solution.py:336
  1.2 1.2 %copy-start.3 = (bf16[384,1024]{1,0:T(8,128)(2,1)S(1)}, bf16[384,1024]{1,0:T(8,128)(2,1)}, u32[]{:S(2)}) copy-start(bf16[384,1024]{1,0:T(8,128)(2,1)} %refs_0_.1) | copy-start | bytes 2359300
  2.4 3.3 %copy-start.4 = (bf16[384,1024]{1,0:T(8,128)(2,1)S(1)}, bf16[384,1024]{1,0:T(8,128)(2,1)}, u32[]{:S(2)}) copy-start(bf16[384,1024]{1,0:T(8,128)(2,1)} %refs_0_.1) | copy-start | bytes 2359300
  2.7 8.1 %collective-permute-start = (bf16[96,1024]{1,0:T(8,128)(2,1)S(1)}, bf16[96,1024]{1,0:T(8,128)(2,1)S(1)}, u32[]{:S(2)}, u32[]{:S(2)}) collective-permute-start(bf16[96,1024]{1,0:T(8,128)(2,1)S(1)} %shard_map.87), channel_id=1, source_target_pairs={{0,2},{1,3},{2,0},{3,1},{4,6},{5,7},{6,4},{7,5},{8,10},{9,11},{10,... | collective-permute-start | bytes 589832 | tf_op jit(solution)/shard_map/ppermute | solution.py:339
  8.7 20.4 %collective-permute-start.8 = (bf16[1024,384]{1,0:T(8,128)(2,1)S(1)}, bf16[1024,384]{1,0:T(8,128)(2,1)S(1)}, u32[]{:S(2)}, u32[]{:S(2)}) collective-permute-start(bf16[1024,384]{1,0:T(8,128)(2,1)S(1)} %get-tuple-element.16.normed), channel_id=1, source_target_pairs={{0,1},{1,0},{2,3},{3,2},{4,5},{5,4},{6,7},{7,6},{8,9},{9,8},{10,11... | collective-permute-start | bytes 2359304 | tf_op jit(solution)/shard_map/ppermute | solution.py:336
  10.8 19.0 %collective-permute-start.7 = (bf16[384,1024]{1,0:T(8,128)(2,1)S(1)}, bf16[384,1024]{1,0:T(8,128)(2,1)S(1)}, u32[]{:S(2)}, u32[]{:S(2)}) collective-permute-start(bf16[384,1024]{1,0:T(8,128)(2,1)S(1)} %shard_map.91), channel_id=1, source_target_pairs={{0,2},{1,3},{2,0},{3,1},{4,6},{5,7},{6,4},{7,5},{8,10},{9,11},{10,... | collective-permute-start | bytes 2359304 | tf_op jit(solution)/shard_map/ppermute | solution.py:339
  12.5 5.7 %collective-permute-start.4 = (bf16[96,1024]{1,0:T(8,128)(2,1)S(1)}, bf16[96,1024]{1,0:T(8,128)(2,1)S(1)}, u32[]{:S(2)}, u32[]{:S(2)}) collective-permute-start(bf16[96,1024]{1,0:T(8,128)(2,1)S(1)} %shard_map.89.refs_0_), channel_id=1, source_target_pairs={{0,8},{4,12},{8,0},{12,4},{16,24},{20,28},{24,16},{28,20},{1,9},{5... | collective-permute-start | bytes 589832 | tf_op jit(solution)/shard_map/ppermute | solution.py:345
  14.1 6.5 %collective-permute-start.3 = (bf16[96,1024]{1,0:T(8,128)(2,1)S(1)}, bf16[96,1024]{1,0:T(8,128)(2,1)S(1)}, u32[]{:S(2)}, u32[]{:S(2)}) collective-permute-start(bf16[96,1024]{1,0:T(8,128)(2,1)S(1)} %shard_map.89.refs_0_), channel_id=1, source_target_pairs={{0,4},{4,0},{8,12},{12,8},{16,20},{20,16},{24,28},{28,24},{1,5},{5... | collective-permute-start | bytes 589832 | tf_op jit(solution)/shard_map/ppermute | solution.py:342
  18.3 4.7 %collective-permute-start.5 = (bf16[48,1024]{1,0:T(8,128)(2,1)S(1)}, bf16[48,1024]{1,0:T(8,128)(2,1)S(1)}, u32[]{:S(2)}, u32[]{:S(2)}) collective-permute-start(bf16[48,1024]{1,0:T(8,128)(2,1)S(1)} %slice.8), channel_id=1, source_target_pairs={{0,4},{4,0},{8,12},{12,8},{16,20},{20,16},{24,28},{28,24},{1,5},{5... | collective-permute-start | bytes 294920 | tf_op jit(solution)/shard_map/ppermute | solution.py:342
  20.6 4.7 %collective-permute-start.6 = (bf16[48,1024]{1,0:T(8,128)(2,1)S(1)}, bf16[48,1024]{1,0:T(8,128)(2,1)S(1)}, u32[]{:S(2)}, u32[]{:S(2)}) collective-permute-start(bf16[48,1024]{1,0:T(8,128)(2,1)S(1)} %slice.9), channel_id=1, source_target_pairs={{0,8},{4,12},{8,0},{12,4},{16,24},{20,28},{24,16},{28,20},{1,9},{5... | collective-permute-start | bytes 294920 | tf_op jit(solution)/shard_map/ppermute | solution.py:345
  28.2 3.0 %collective-permute-start.10 = (bf16[1024,384]{1,0:T(8,128)(2,1)S(1)}, bf16[1024,384]{1,0:T(8,128)(2,1)S(1)}, u32[]{:S(2)}, u32[]{:S(2)}) collective-permute-start(bf16[1024,384]{1,0:T(8,128)(2,1)S(1)} %get-tuple-element.19.normed), channel_id=1, source_target_pairs={{0,1},{1,0},{2,3},{3,2},{4,5},{5,4},{6,7},{7,6},{8,9},{9,8},{10,11... | collective-permute-start | bytes 2359304 | tf_op jit(solution)/shard_map/ppermute | solution.py:336
  28.3 20.0 %collective-permute-start.11 = (bf16[384,1024]{1,0:T(8,128)(2,1)S(1)}, bf16[384,1024]{1,0:T(8,128)(2,1)S(1)}, u32[]{:S(2)}, u32[]{:S(2)}) collective-permute-start(bf16[384,1024]{1,0:T(8,128)(2,1)S(1)} %get-tuple-element.21), channel_id=1, source_target_pairs={{0,2},{1,3},{2,0},{3,1},{4,6},{5,7},{6,4},{7,5},{8,10},{9,11},{10,... | collective-permute-start | bytes 2359304 | tf_op jit(solution)/shard_map/ppermute | solution.py:339
  30.5 1.8 %copy-start.2 = (bf16[1,1024,512]{2,1,0:T(8,128)(2,1)S(1)}, bf16[1,1024,512]{2,1,0:T(8,128)(2,1)}, u32[]{:S(2)}) copy-start(bf16[1,1024,512]{2,1,0:T(8,128)(2,1)} %noise.1) | copy-start | bytes 3145732
  30.5 1.8 %collective-permute-start.9 = (bf16[384,512]{1,0:T(8,128)(2,1)S(1)}, bf16[384,512]{1,0:T(8,128)(2,1)S(1)}, u32[]{:S(2)}, u32[]{:S(2)}) collective-permute-start(bf16[384,512]{1,0:T(8,128)(2,1)S(1)} %shard_map.94), channel_id=1, source_target_pairs={{0,1},{1,0},{2,3},{3,2},{4,5},{5,4},{6,7},{7,6},{8,9},{9,8},{10,11... | collective-permute-start | bytes 1179656 | tf_op jit(solution)/shard_map/ppermute | solution.py:336
  49.0 1.8 %collective-permute-start.12 = (bf16[384,512]{1,0:T(8,128)(2,1)S(1)}, bf16[384,512]{1,0:T(8,128)(2,1)S(1)}, u32[]{:S(2)}, u32[]{:S(2)}) collective-permute-start(bf16[384,512]{1,0:T(8,128)(2,1)S(1)} %shard_map.98), channel_id=1, source_target_pairs={{0,1},{1,0},{2,3},{3,2},{4,5},{5,4},{6,7},{7,6},{8,9},{9,8},{10,11... | collective-permute-start | bytes 1179656 | tf_op jit(solution)/shard_map/ppermute | solution.py:336
  51.2 9.2 %collective-permute-start.17 = (bf16[256,512]{1,0:T(8,128)(2,1)S(1)}, bf16[256,512]{1,0:T(8,128)(2,1)S(1)}, u32[]{:S(2)}, u32[]{:S(2)}) collective-permute-start(bf16[256,512]{1,0:T(8,128)(2,1)S(1)} %shard_map.99.rest_0_.refs_0_), channel_id=1, source_target_pairs={{0,4},{4,0},{8,12},{12,8},{16,20},{20,16},{24,28},{28,24},{1,5},{5... | collective-permute-start | bytes 786440 | tf_op jit(solution)/shard_map/ppermute | solution.py:342
  53.2 12.9 %collective-permute-start.14 = (bf16[256,512]{1,0:T(8,128)(2,1)S(1)}, bf16[256,512]{1,0:T(8,128)(2,1)S(1)}, u32[]{:S(2)}, u32[]{:S(2)}) collective-permute-start(bf16[256,512]{1,0:T(8,128)(2,1)S(1)} %shard_map.100.rest_0_.refs_1_), channel_id=1, source_target_pairs={{0,4},{4,0},{8,12},{12,8},{16,20},{20,16},{24,28},{28,24},{1,5},{5... | collective-permute-start | bytes 786440 | tf_op jit(solution)/shard_map/ppermute | solution.py:342
  54.3 17.4 %collective-permute-start.18 = (bf16[256,512]{1,0:T(8,128)(2,1)S(1)}, bf16[256,512]{1,0:T(8,128)(2,1)S(1)}, u32[]{:S(2)}, u32[]{:S(2)}) collective-permute-start(bf16[256,512]{1,0:T(8,128)(2,1)S(1)} %shard_map.101.rest_0_.refs_2_), channel_id=1, source_target_pairs={{0,4},{4,0},{8,12},{12,8},{16,20},{20,16},{24,28},{28,24},{1,5},{5... | collective-permute-start | bytes 786440 | tf_op jit(solution)/shard_map/ppermute | solution.py:342
  60.5 11.2 %collective-permute-start.19 = (bf16[256,512]{1,0:T(8,128)(2,1)S(1)}, bf16[256,512]{1,0:T(8,128)(2,1)S(1)}, u32[]{:S(2)}, u32[]{:S(2)}) collective-permute-start(bf16[256,512]{1,0:T(8,128)(2,1)S(1)} %collective-permute-done.17.refs_3_), channel_id=1, source_target_pairs={{0,8},{4,28},{8,16},{12,4},{16,24},{20,12},{24,0},{28,20},{1,9},{5... | collective-permute-start | bytes 786440 | tf_op jit(solution)/shard_map/ppermute | solution.py:349
  61.7 14.8 %collective-permute-start.13 = (bf16[256,512]{1,0:T(8,128)(2,1)S(1)}, bf16[256,512]{1,0:T(8,128)(2,1)S(1)}, u32[]{:S(2)}, u32[]{:S(2)}) collective-permute-start(bf16[256,512]{1,0:T(8,128)(2,1)S(1)} %shard_map.102.refs_0_), channel_id=1, source_target_pairs={{0,4},{4,0},{8,12},{12,8},{16,20},{20,16},{24,28},{28,24},{1,5},{5... | collective-permute-start | bytes 786440 | tf_op jit(solution)/shard_map/ppermute | solution.py:342
  66.1 10.4 %collective-permute-start.15 = (bf16[256,512]{1,0:T(8,128)(2,1)S(1)}, bf16[256,512]{1,0:T(8,128)(2,1)S(1)}, u32[]{:S(2)}, u32[]{:S(2)}) collective-permute-start(bf16[256,512]{1,0:T(8,128)(2,1)S(1)} %collective-permute-done.14.refs_4_), channel_id=1, source_target_pairs={{0,8},{4,28},{8,16},{12,4},{16,24},{20,12},{24,0},{28,20},{1,9},{5... | collective-permute-start | bytes 786440 | tf_op jit(solution)/shard_map/ppermute | solution.py:349
  71.7 8.5 %collective-permute-start.20 = (bf16[256,512]{1,0:T(8,128)(2,1)S(1)}, bf16[256,512]{1,0:T(8,128)(2,1)S(1)}, u32[]{:S(2)}, u32[]{:S(2)}) collective-permute-start(bf16[256,512]{1,0:T(8,128)(2,1)S(1)} %shard_map.104.refs_5_), channel_id=1, source_target_pairs={{0,8},{4,28},{8,16},{12,4},{16,24},{20,12},{24,0},{28,20},{1,9},{5... | collective-permute-start | bytes 786440 | tf_op jit(solution)/shard_map/ppermute | solution.py:349
  76.5 9.3 %collective-permute-start.16 = (bf16[256,512]{1,0:T(8,128)(2,1)S(1)}, bf16[256,512]{1,0:T(8,128)(2,1)S(1)}, u32[]{:S(2)}, u32[]{:S(2)}) collective-permute-start(bf16[256,512]{1,0:T(8,128)(2,1)S(1)} %shard_map.103.refs_1_), channel_id=1, source_target_pairs={{0,8},{4,28},{8,16},{12,4},{16,24},{20,12},{24,0},{28,20},{1,9},{5... | collective-permute-start | bytes 786440 | tf_op jit(solution)/shard_map/ppermute | solution.py:349

commit v6 on v5

--- a/solution.py
+++ b/solution.py
@@ -70,18 +70,14 @@
     )(value)
 
 
-def assemble_kernel(own, across, behind, upper, lower, out):
-    rows = own.shape[0]
-    half = rows // 2
+def assemble_kernel(pieces, out):
+    rows = pieces[0].shape[0]
     for place in range(4):
 
         @pl.when((lax.axis_index("rep") & 3) == place)
         def _():
-            out[place * rows : (place + 1) * rows] = own[...]
-            out[(place ^ 1) * rows : ((place ^ 1) + 1) * rows] = across[...]
-            out[(place ^ 2) * rows : ((place ^ 2) + 1) * rows] = behind[...]
-            out[(place ^ 3) * rows : (place ^ 3) * rows + half] = upper[...]
-            out[(place ^ 3) * rows + half : ((place ^ 3) + 1) * rows] = lower[...]
+            for at, piece in enumerate(pieces):
+                out[(place ^ at) * rows : ((place ^ at) + 1) * rows] = piece[...]
 
 
 def normalized(tokens):
@@ -127,7 +123,7 @@
     own_in, mate_in, own_out, mate_out = refs[pieces : pieces + 4]
     normed_t, slope, slope_mate, part, base, total, tokens = refs[pieces + 4 + skipped :]
     if pieces > 1:
-        assemble_kernel(*given, tokens)
+        assemble_kernel(given, tokens)
     else:
         tokens = given[0]
     weights = (own_in, mate_in), (own_out, mate_out)
@@ -348,12 +344,8 @@
         pairs = [(i, (i + (2 if i % 2 == 0 else -2)) % replicas) for i in range(replicas)]
         return lax.ppermute(value, "rep", pairs)
 
-    def step_one(own):
-        return to_mate(own), to_pair(own)
-
-    def step_two(own, across, behind):
-        half = own.shape[0] // 2
-        return own, across, behind, to_mate(behind[:half]), to_pair(across[half:])
+    def to_diagonal(value):
+        return lax.ppermute(value, "rep", [(i, i ^ 3) for i in range(replicas)])
 
     mate_in = to_core(params)
     mate_out = to_core(output_matrix)
@@ -363,8 +355,7 @@
     normed, slope, slope_send, part, base = forward((residual_flow,), count, weights)
     sent = to_chip(after(part, token_own))
     token_own = after(token_own, part)
-    token_across, token_behind = step_one(token_own)
-    token_pieces = step_two(token_own, token_across, token_behind)
+    token_pieces = (token_own, to_mate(token_own), to_pair(token_own), to_diagonal(token_own))
     normed_mate = to_core(normed)
     far, far_slope, far_slope_send, far_part, far_base = forward(token_pieces, count, weights)
     far_sent = to_chip(far_part)
@@ -387,20 +378,21 @@
 
     pairing = (matched_chain, swap_mask)
     width = params.shape[0]
-    sizes = [width * part // 8 for part in (2, 2, 2, 2)]
+    sizes = [width * part // 64 for part in (13, 13, 13, 13, 12)]
     starts = [sum(sizes[:chunk]) for chunk in range(len(sizes))]
     own, across, beyond = [], [], []
     for chunk, (start, rows) in enumerate(zip(starts, sizes)):
         fresh = update(start, rows, begun, grads, (normed, normed_mate), *own[-1:])
+        if chunk >= 3:
+            fresh = after(fresh, across[chunk - 3])
         own.append(fresh)
         across.append(to_mate(fresh))
+    for chunk in range(len(sizes)):
+        if chunk >= 2:
+            across[chunk] = after(across[chunk], beyond[chunk - 2])
+        beyond.append(to_next(across[chunk]))
     done = None
-    cut = len(sizes) - 1
-    for first, stop in ((0, cut), (cut, cut + 1)):
-        for chunk in range(first, stop):
-            if chunk >= 2:
-                across[chunk] = after(across[chunk], beyond[chunk - 2])
-            beyond.append(to_next(across[chunk]))
+    for first, stop in ((0, 4), (4, 5)):
         given = (pieces[first:stop] for pieces in (own, across, beyond))
         done = finish(width, starts[first], pairing, *given, done)
     return done

time: 87.3 us -> 85.7 us (0.982)
  waiting for transfers between devices: 48 us -> 42.6 us
  starting transfers between devices: 20.9 us -> 24.6 us
    ppermute x6, waiting for transfers between devices: 17.4 us -> 13.2 us  [to_mate(): return lax.ppermute(value, 'rep', [(i, i ^ 1) for i in range(replicas)])]
    ppermute x6, starting transfers between devices: 9.52 us -> 12.2 us  [to_mate(): return lax.ppermute(value, 'rep', [(i, i ^ 1) for i in range(replicas)])]
    ppermute x2 -> x1, waiting for transfers between devices: 4.99 us -> 2.41 us  [to_pair(): return lax.ppermute(value, 'rep', [(i, i ^ 2) for i in range(replicas)])]
    ppermute x0 -> x1, waiting for transfers between devices: none -> 2.2 us  [to_diagonal(): return lax.ppermute(value, 'rep', [(i, i ^ 3) for i in range(replicas)])]
    ppermute x4 -> x5, starting transfers between devices: 3.16 us -> 4.21 us  [to_next(): return lax.ppermute(value, 'rep', pairs)]
    ppermute x2 -> x1, starting transfers between devices: 2.45 us -> 1.58 us  [to_pair(): return lax.ppermute(value, 'rep', [(i, i ^ 2) for i in range(replicas)])]
    ppermute x4 -> x5, waiting for transfers between devices: 6.13 us -> 5.67 us  [to_next(): return lax.ppermute(value, 'rep', pairs)]
    pallas_call x4 -> x5, Pallas kernels: 1.72 us -> 1.89 us  [update(): pl.pallas_call(functools.partial(update_kernel, start), out_shape=shape((...]
  transfers between devices with their start and end apart: 21 -> 22, of which waited for: 15 -> 14; matrix products, arithmetic and copies ran while one was open for 0% -> 0% of each run, Pallas kernels for 13% -> 14%
where the time goes in v6:
time: 85.7 us; the launch traced here: 85.6 us
  waiting for transfers between devices  42.6 us (50%)
  starting transfers between devices  24.6 us (29%)
  Pallas kernels  14.3 us (17%)
  between operations  2.83 us (3%)
  local copies, waits for them, and re-layouts  1.24 us (1%)
    ppermute x3, waiting for transfers between devices, to_chip(): return lax.ppermute(value, 'dp', [(i, i ^ 2) for i in range(4)])  16.9 us
    ppermute x6, waiting for transfers between devices, to_mate(): return lax.ppermute(value, 'rep', [(i, i ^ 1) for i in range(replicas)])  13.2 us
    ppermute x6, starting transfers between devices, to_mate(): return lax.ppermute(value, 'rep', [(i, i ^ 1) for i in range(replicas)])  12.2 us
    pallas_call x2, Pallas kernels, forward(): pl.pallas_call(functools.partial(forward_kernel, len(given), len(earlier)...  5.84 us
    ppermute x5, waiting for transfers between devices, to_next(): return lax.ppermute(value, 'rep', pairs)  5.67 us
    ppermute x3, starting transfers between devices, to_chip(): return lax.ppermute(value, 'dp', [(i, i ^ 2) for i in range(4)])  5.31 us
    ppermute x5, starting transfers between devices, to_next(): return lax.ppermute(value, 'rep', pairs)  4.21 us
    pallas_call x4, Pallas kernels, hidden_of(): pl.pallas_call(hidden_kernel, out_shape=shape((count, block)), in_specs=[...  2.42 us
  transfers between devices with their start and end apart: 22, of which 14 were waited for; matrix products, arithmetic and copies ran while one was open for 0% of the time, Pallas kernels for 14%

profile of v6, /device:TPU:0, one launch (start us, length us, event | category | flops | bytes accessed | tf_op | source)
XLA Modules:
  0.0 85.6 jit_solution(6266726774153207563)
XLA Ops:
  1.2 1.2 %copy-done.3 = bf16[384,1024]{1,0:T(8,128)(2,1)S(1)} copy-done((bf16[384,1024]{1,0:T(8,128)(2,1)S(1)}, bf16[384,1024]{1,0:T(8,128)(2,1)}, u32[]{:S(2)}) %copy-start.3) | copy-done | bytes 786456
  2.7 3.0 %collective-permute-start = (bf16[96,1024]{1,0:T(8,128)(2,1)S(1)}, bf16[96,1024]{1,0:T(8,128)(2,1)S(1)}, u32[]{:S(2)}, u32[]{:S(2)}) collective-permute-start(bf16[96,1024]{1,0:T(8,128)(2,1)S(1)} %shard_map.87), channel_id=1, source_target_pairs={{0,2},{1,3},{2,0},{3,1},{4,6},{5,7},{6,4},{7,5},{8,10},{9,11},{10,... | collective-permute-start | bytes 589832 | tf_op jit(solution)/shard_map/ppermute | solution.py:335
  5.7 2.9 %shard_map.88 = (bf16[1024,384]{1,0:T(8,128)(2,1)S(1)}, bf16[384,512]{1,0:T(8,128)(2,1)S(1)}, bf16[384,512]{1,0:T(8,128)(2,1)S(1)}, bf16[384,1024]{1,0:T(8,128)(2,1)S(1)}, f32[384,1024]{1,0:T(8,128)S(1)}) custom-call(bf16[384,1024]{1,0:T(8,128)(2,1)S(1)} %copy-done.4, bf16[1024,512]{1,0:T(8,128)(2,1)S(1)} %bitcast.2, ...), custom_call_target="tpu_custom_call" | custom-call | bytes 1000 | tf_op jit(solution)/shard_map/pallas_call | solution.py:142
  8.8 2.0 %collective-permute-done.refs_0_.refs_1_ = bf16[96,1024]{1,0:T(8,128)(2,1)S(1)} collective-permute-done((bf16[96,1024]{1,0:T(8,128)(2,1)S(1)}, bf16[96,1024]{1,0:T(8,128)(2,1)S(1)}, u32[]{:S(2)}, u32[]{:S(2)}) %collective-permute-start) | collective-permute-done | bytes 196640 | tf_op jit(solution)/shard_map/ppermute | solution.py:335
  10.8 1.7 %collective-permute-start.6 = (bf16[384,1024]{1,0:T(8,128)(2,1)S(1)}, bf16[384,1024]{1,0:T(8,128)(2,1)S(1)}, u32[]{:S(2)}, u32[]{:S(2)}) collective-permute-start(bf16[384,1024]{1,0:T(8,128)(2,1)S(1)} %shard_map.91), channel_id=1, source_target_pairs={{0,2},{1,3},{2,0},{3,1},{4,6},{5,7},{6,4},{7,5},{8,10},{9,11},{10,... | collective-permute-start | bytes 2359304 | tf_op jit(solution)/shard_map/ppermute | solution.py:335
  12.5 1.5 %collective-permute-start.3 = (bf16[96,1024]{1,0:T(8,128)(2,1)S(1)}, bf16[96,1024]{1,0:T(8,128)(2,1)S(1)}, u32[]{:S(2)}, u32[]{:S(2)}) collective-permute-start(bf16[96,1024]{1,0:T(8,128)(2,1)S(1)} %shard_map.89.refs_0_), channel_id=1, source_target_pairs={{0,4},{4,0},{8,12},{12,8},{16,20},{20,16},{24,28},{28,24},{1,5},{5... | collective-permute-start | bytes 589832 | tf_op jit(solution)/shard_map/ppermute | solution.py:338
  14.0 1.6 %collective-permute-start.4 = (bf16[96,1024]{1,0:T(8,128)(2,1)S(1)}, bf16[96,1024]{1,0:T(8,128)(2,1)S(1)}, u32[]{:S(2)}, u32[]{:S(2)}) collective-permute-start(bf16[96,1024]{1,0:T(8,128)(2,1)S(1)} %shard_map.89.refs_0_), channel_id=1, source_target_pairs={{0,8},{4,12},{8,0},{12,4},{16,24},{20,28},{24,16},{28,20},{1,9},{5... | collective-permute-start | bytes 589832 | tf_op jit(solution)/shard_map/ppermute | solution.py:341
  16.0 3.1 %collective-permute-done.3.refs_1_ = bf16[96,1024]{1,0:T(8,128)(2,1)S(1)} collective-permute-done((bf16[96,1024]{1,0:T(8,128)(2,1)S(1)}, bf16[96,1024]{1,0:T(8,128)(2,1)S(1)}, u32[]{:S(2)}, u32[]{:S(2)}) %collective-permute-start.3) | collective-permute-done | bytes 196640 | tf_op jit(solution)/shard_map/ppermute | solution.py:338
  19.2 2.4 %collective-permute-done.4.refs_2_ = bf16[96,1024]{1,0:T(8,128)(2,1)S(1)} collective-permute-done((bf16[96,1024]{1,0:T(8,128)(2,1)S(1)}, bf16[96,1024]{1,0:T(8,128)(2,1)S(1)}, u32[]{:S(2)}, u32[]{:S(2)}) %collective-permute-start.4) | collective-permute-done | bytes 196640 | tf_op jit(solution)/shard_map/ppermute | solution.py:341
  21.6 2.2 %collective-permute-done.5.refs_3_ = bf16[96,1024]{1,0:T(8,128)(2,1)S(1)} collective-permute-done((bf16[96,1024]{1,0:T(8,128)(2,1)S(1)}, bf16[96,1024]{1,0:T(8,128)(2,1)S(1)}, u32[]{:S(2)}, u32[]{:S(2)}) %collective-permute-start.5) | collective-permute-done | bytes 196640 | tf_op jit(solution)/shard_map/ppermute | solution.py:348
  23.8 2.9 %shard_map.90 = (bf16[1024,384]{1,0:T(8,128)(2,1)S(1)}, bf16[384,512]{1,0:T(8,128)(2,1)S(1)}, bf16[384,512]{1,0:T(8,128)(2,1)S(1)}, bf16[384,1024]{1,0:T(8,128)(2,1)S(1)}, f32[384,1024]{1,0:T(8,128)S(1)}) custom-call(bf16[96,1024]{1,0:T(8,128)(2,1)S(1)} %shard_map.89.refs_0_, bf16[96,1024]{1,0:T(8,128)(2,1)S(1)} %collective-permute-done.3.refs_1_, ...), custom_call_target="tpu_custom_call" | custom-call | bytes 1000 | tf_op jit(solution)/shard_map/pallas_call | solution.py:142
  28.0 1.7 %collective-permute-done.6.sent = bf16[384,1024]{1,0:T(8,128)(2,1)S(1)} collective-permute-done((bf16[384,1024]{1,0:T(8,128)(2,1)S(1)}, bf16[384,1024]{1,0:T(8,128)(2,1)S(1)}, u32[]{:S(2)}, u32[]{:S(2)}) %collective-permute-start.6) | collective-permute-done | bytes 786464 | tf_op jit(solution)/shard_map/ppermute | solution.py:335
  30.6 0.6 shard_map.93.first
  31.2 1.1 %collective-permute-done.8.second = bf16[384,512]{1,0:T(8,128)(2,1)S(1)} collective-permute-done((bf16[384,512]{1,0:T(8,128)(2,1)S(1)}, bf16[384,512]{1,0:T(8,128)(2,1)S(1)}, u32[]{:S(2)}, u32[]{:S(2)}) %collective-permute-start.8) | collective-permute-done | bytes 393248 | tf_op jit(solution)/shard_map/ppermute | solution.py:332
  32.3 1.3 %shard_map.95.refs_0_.begun = f32[1024,512]{1,0:T(8,128)S(1)} custom-call(f32[1,512]{1,0:T(1,128)S(1)} %shard_map.86.refs_1_.strength, bf16[384,512]{1,0:T(8,128)(2,1)S(1)} %shard_map.93.first, bf16[384,512]{1,0:T(8,128)(2,1)S(1)} %collective-permute-done.8.second, bf16[1024,384]{1,0:T(8,128)(2,1)S(1)} %get-tuple-element.19.normed, ...), custom_call_target="tpu_custom_call" | custom-call | flops 805306368 | bytes 3145728 | tf_op jit(solution)/shard_map/pallas_call | solution.py:224
  33.6 13.2 %collective-permute-done.10.sent = bf16[384,1024]{1,0:T(8,128)(2,1)S(1)} collective-permute-done((bf16[384,1024]{1,0:T(8,128)(2,1)S(1)}, bf16[384,1024]{1,0:T(8,128)(2,1)S(1)}, u32[]{:S(2)}, u32[]{:S(2)}) %collective-permute-start.10) | collective-permute-done | bytes 786464 | tf_op jit(solution)/shard_map/ppermute | solution.py:335
  47.6 0.6 shard_map.97.first
  48.2 1.1 %collective-permute-done.11.second = bf16[384,512]{1,0:T(8,128)(2,1)S(1)} collective-permute-done((bf16[384,512]{1,0:T(8,128)(2,1)S(1)}, bf16[384,512]{1,0:T(8,128)(2,1)S(1)}, u32[]{:S(2)}, u32[]{:S(2)}) %collective-permute-start.11) | collective-permute-done | bytes 393248 | tf_op jit(solution)/shard_map/ppermute | solution.py:332
  49.7 1.4 %collective-permute-start.12 = (bf16[208,512]{1,0:T(8,128)(2,1)S(1)}, bf16[208,512]{1,0:T(8,128)(2,1)S(1)}, u32[]{:S(2)}, u32[]{:S(2)}) collective-permute-start(bf16[208,512]{1,0:T(8,128)(2,1)S(1)} %shard_map.99.rest_0_.refs_0_), channel_id=1, source_target_pairs={{0,4},{4,0},{8,12},{12,8},{16,20},{20,16},{24,28},{28,24},{1,5},{5... | collective-permute-start | bytes 638984 | tf_op jit(solution)/shard_map/ppermute | solution.py:338
  51.5 0.7 collective-permute-start.13
  52.6 1.4 %collective-permute-start.15 = (bf16[208,512]{1,0:T(8,128)(2,1)S(1)}, bf16[208,512]{1,0:T(8,128)(2,1)S(1)}, u32[]{:S(2)}, u32[]{:S(2)}) collective-permute-start(bf16[208,512]{1,0:T(8,128)(2,1)S(1)} %shard_map.101.rest_0_.refs_2_), channel_id=1, source_target_pairs={{0,4},{4,0},{8,12},{12,8},{16,20},{20,16},{24,28},{28,24},{1,5},{5... | collective-permute-start | bytes 638984 | tf_op jit(solution)/shard_map/ppermute | solution.py:338
  54.0 3.8 %collective-permute-done.12.refs_1_.refs_4_ = bf16[208,512]{1,0:T(8,128)(2,1)S(1)} collective-permute-done((bf16[208,512]{1,0:T(8,128)(2,1)S(1)}, bf16[208,512]{1,0:T(8,128)(2,1)S(1)}, u32[]{:S(2)}, u32[]{:S(2)}) %collective-permute-start.12) | collective-permute-done | bytes 213024 | tf_op jit(solution)/shard_map/ppermute | solution.py:338
  57.8 1.5 %collective-permute-start.16 = (bf16[208,512]{1,0:T(8,128)(2,1)S(1)}, bf16[208,512]{1,0:T(8,128)(2,1)S(1)}, u32[]{:S(2)}, u32[]{:S(2)}) collective-permute-start(bf16[208,512]{1,0:T(8,128)(2,1)S(1)} %collective-permute-done.12.refs_1_.refs_4_), channel_id=1, source_target_pairs={{0,8},{4,28},{8,16},{12,4},{16,24},{20,12},{24,0},{28,20},{1,9},{5... | collective-permute-start | bytes 638984 | tf_op jit(solution)/shard_map/ppermute | solution.py:345
  59.7 3.6 %collective-permute-start.19 = (bf16[208,512]{1,0:T(8,128)(2,1)S(1)}, bf16[208,512]{1,0:T(8,128)(2,1)S(1)}, u32[]{:S(2)}, u32[]{:S(2)}) collective-permute-start(bf16[208,512]{1,0:T(8,128)(2,1)S(1)} %shard_map.103.rest_0_.refs_3_), channel_id=1, source_target_pairs={{0,4},{4,0},{8,12},{12,8},{16,20},{20,16},{24,28},{28,24},{1,5},{5... | collective-permute-start | bytes 638984 | tf_op jit(solution)/shard_map/ppermute | solution.py:338
  63.8 3.1 %collective-permute-done.15.refs_0_ = bf16[208,512]{1,0:T(8,128)(2,1)S(1)} collective-permute-done((bf16[208,512]{1,0:T(8,128)(2,1)S(1)}, bf16[208,512]{1,0:T(8,128)(2,1)S(1)}, u32[]{:S(2)}, u32[]{:S(2)}) %collective-permute-start.15) | collective-permute-done | bytes 213024 | tf_op jit(solution)/shard_map/ppermute | solution.py:338
  67.0 1.5 %collective-permute-start.17 = (bf16[208,512]{1,0:T(8,128)(2,1)S(1)}, bf16[208,512]{1,0:T(8,128)(2,1)S(1)}, u32[]{:S(2)}, u32[]{:S(2)}) collective-permute-start(bf16[208,512]{1,0:T(8,128)(2,1)S(1)} %shard_map.106.refs_6_), channel_id=1, source_target_pairs={{0,8},{4,28},{8,16},{12,4},{16,24},{20,12},{24,0},{28,20},{1,9},{5... | collective-permute-start | bytes 638984 | tf_op jit(solution)/shard_map/ppermute | solution.py:345
  68.8 3.6 %collective-permute-start.14 = (bf16[192,512]{1,0:T(8,128)(2,1)S(1)}, bf16[192,512]{1,0:T(8,128)(2,1)S(1)}, u32[]{:S(2)}, u32[]{:S(2)}) collective-permute-start(bf16[192,512]{1,0:T(8,128)(2,1)S(1)} %shard_map.105.refs_0_), channel_id=1, source_target_pairs={{0,4},{4,0},{8,12},{12,8},{16,20},{20,16},{24,28},{28,24},{1,5},{5... | collective-permute-start | bytes 589832 | tf_op jit(solution)/shard_map/ppermute | solution.py:338
  72.9 3.1 %collective-permute-done.14.refs_0_ = bf16[192,512]{1,0:T(8,128)(2,1)S(1)} collective-permute-done((bf16[192,512]{1,0:T(8,128)(2,1)S(1)}, bf16[192,512]{1,0:T(8,128)(2,1)S(1)}, u32[]{:S(2)}, u32[]{:S(2)}) %collective-permute-start.14) | collective-permute-done | bytes 196640 | tf_op jit(solution)/shard_map/ppermute | solution.py:338
  77.7 3.9 %collective-permute-done.21.refs_11_ = bf16[208,512]{1,0:T(8,128)(2,1)S(1)} collective-permute-done((bf16[208,512]{1,0:T(8,128)(2,1)S(1)}, bf16[208,512]{1,0:T(8,128)(2,1)S(1)}, u32[]{:S(2)}, u32[]{:S(2)}) %collective-permute-start.21) | collective-permute-done | bytes 213024 | tf_op jit(solution)/shard_map/ppermute | solution.py:345
  81.5 1.1 %shard_map.109 = (bf16[1,1024,512]{2,1,0:T(8,128)(2,1)}, f32[1,2,512]{2,1,0:T(2,128)S(1)}) custom-call(s32[1]{0:T(128)S(6)} %copy.26.mate, s32[1]{0:T(128)S(6)} %copy.27.swapped, bf16[208,512]{1,0:T(8,128)(2,1)S(1)} %shard_map.99.rest_0_.refs_0_, bf16[208,512]{1,0:T(8,128)(2,1)S(1)} %shard_map.100.rest_0_.refs_1_, ...), custom_call_target="tpu_custom_call" | custom-call | bytes 3407872 | tf_op jit(solution)/shard_map/pallas_call | solution.py:305
  82.6 1.7 %collective-permute-done.18.refs_2_ = bf16[192,512]{1,0:T(8,128)(2,1)S(1)} collective-permute-done((bf16[192,512]{1,0:T(8,128)(2,1)S(1)}, bf16[192,512]{1,0:T(8,128)(2,1)S(1)}, u32[]{:S(2)}, u32[]{:S(2)}) %collective-permute-start.18) | collective-permute-done | bytes 196640 | tf_op jit(solution)/shard_map/ppermute | solution.py:345
  84.2 1.3 %shard_map.110 = (bf16[1,1024,512]{2,1,0:T(8,128)(2,1)}, f32[1,2,512]{2,1,0:T(2,128)}) custom-call(s32[1]{0:T(128)S(6)} %copy.26.mate, s32[1]{0:T(128)S(6)} %copy.27.swapped, bf16[192,512]{1,0:T(8,128)(2,1)S(1)} %shard_map.105.refs_0_, bf16[192,512]{1,0:T(8,128)(2,1)S(1)} %shard_map.107.refs_1_, ...), custom_call_target="tpu_custom_call", output_to_operand_aliasing={{0}: (6, {})} | custom-call | bytes 786432 | tf_op jit(solution)/shard_map/pallas_call | solution.py:305
  (48 shorter events, 7.0 us)
Async XLA Ops:
  0.6 5.1 %copy-start = (bf16[512,1024]{1,0:T(8,128)(2,1)S(1)}, bf16[512,1024]{1,0:T(8,128)(2,1)}, u32[]{:S(2)}) copy-start(bf16[512,1024]{1,0:T(8,128)(2,1)} %weight.3) | copy-start | bytes 3145732
  0.6 5.0 %copy-start.1 = (bf16[1,1024,512]{2,1,0:T(8,128)(2,1)S(1)}, bf16[1,1024,512]{2,1,0:T(8,128)(2,1)}, u32[]{:S(2)}) copy-start(bf16[1,1024,512]{2,1,0:T(8,128)(2,1)} %params.1) | copy-start | bytes 3145732
  0.6 5.0 %collective-permute-start.1 = (bf16[1024,512]{1,0:T(8,128)(2,1)}, bf16[1024,512]{1,0:T(8,128)(2,1)S(1)}, u32[]{:S(2)}, u32[]{:S(2)}) collective-permute-start(bf16[1024,512]{1,0:T(8,128)(2,1)} %bitcast.1), channel_id=1, source_target_pairs={{0,1},{1,0},{2,3},{3,2},{4,5},{5,4},{6,7},{7,6},{8,9},{9,8},{10,11... | collective-permute-start | bytes 3145736 | tf_op jit(solution)/shard_map/ppermute | solution.py:332
  1.2 4.5 %collective-permute-start.2 = (bf16[512,1024]{1,0:T(8,128)(2,1)}, bf16[512,1024]{1,0:T(8,128)(2,1)S(1)}, u32[]{:S(2)}, u32[]{:S(2)}) collective-permute-start(bf16[512,1024]{1,0:T(8,128)(2,1)} %weight.3), channel_id=1, source_target_pairs={{0,1},{1,0},{2,3},{3,2},{4,5},{5,4},{6,7},{7,6},{8,9},{9,8},{10,11... | collective-permute-start | bytes 3145736 | tf_op jit(solution)/shard_map/ppermute | solution.py:332
  1.2 1.2 %copy-start.3 = (bf16[384,1024]{1,0:T(8,128)(2,1)S(1)}, bf16[384,1024]{1,0:T(8,128)(2,1)}, u32[]{:S(2)}) copy-start(bf16[384,1024]{1,0:T(8,128)(2,1)} %refs_0_.1) | copy-start | bytes 2359300
  2.4 3.3 %copy-start.4 = (bf16[384,1024]{1,0:T(8,128)(2,1)S(1)}, bf16[384,1024]{1,0:T(8,128)(2,1)}, u32[]{:S(2)}) copy-start(bf16[384,1024]{1,0:T(8,128)(2,1)} %refs_0_.1) | copy-start | bytes 2359300
  2.7 8.1 %collective-permute-start = (bf16[96,1024]{1,0:T(8,128)(2,1)S(1)}, bf16[96,1024]{1,0:T(8,128)(2,1)S(1)}, u32[]{:S(2)}, u32[]{:S(2)}) collective-permute-start(bf16[96,1024]{1,0:T(8,128)(2,1)S(1)} %shard_map.87), channel_id=1, source_target_pairs={{0,2},{1,3},{2,0},{3,1},{4,6},{5,7},{6,4},{7,5},{8,10},{9,11},{10,... | collective-permute-start | bytes 589832 | tf_op jit(solution)/shard_map/ppermute | solution.py:335
  8.7 19.3 %collective-permute-start.7 = (bf16[1024,384]{1,0:T(8,128)(2,1)S(1)}, bf16[1024,384]{1,0:T(8,128)(2,1)S(1)}, u32[]{:S(2)}, u32[]{:S(2)}) collective-permute-start(bf16[1024,384]{1,0:T(8,128)(2,1)S(1)} %get-tuple-element.16.normed), channel_id=1, source_target_pairs={{0,1},{1,0},{2,3},{3,2},{4,5},{5,4},{6,7},{7,6},{8,9},{9,8},{10,11... | collective-permute-start | bytes 2359304 | tf_op jit(solution)/shard_map/ppermute | solution.py:332
  10.8 19.0 %collective-permute-start.6 = (bf16[384,1024]{1,0:T(8,128)(2,1)S(1)}, bf16[384,1024]{1,0:T(8,128)(2,1)S(1)}, u32[]{:S(2)}, u32[]{:S(2)}) collective-permute-start(bf16[384,1024]{1,0:T(8,128)(2,1)S(1)} %shard_map.91), channel_id=1, source_target_pairs={{0,2},{1,3},{2,0},{3,1},{4,6},{5,7},{6,4},{7,5},{8,10},{9,11},{10,... | collective-permute-start | bytes 2359304 | tf_op jit(solution)/shard_map/ppermute | solution.py:335
  12.5 6.6 %collective-permute-start.3 = (bf16[96,1024]{1,0:T(8,128)(2,1)S(1)}, bf16[96,1024]{1,0:T(8,128)(2,1)S(1)}, u32[]{:S(2)}, u32[]{:S(2)}) collective-permute-start(bf16[96,1024]{1,0:T(8,128)(2,1)S(1)} %shard_map.89.refs_0_), channel_id=1, source_target_pairs={{0,4},{4,0},{8,12},{12,8},{16,20},{20,16},{24,28},{28,24},{1,5},{5... | collective-permute-start | bytes 589832 | tf_op jit(solution)/shard_map/ppermute | solution.py:338
  14.0 7.5 %collective-permute-start.4 = (bf16[96,1024]{1,0:T(8,128)(2,1)S(1)}, bf16[96,1024]{1,0:T(8,128)(2,1)S(1)}, u32[]{:S(2)}, u32[]{:S(2)}) collective-permute-start(bf16[96,1024]{1,0:T(8,128)(2,1)S(1)} %shard_map.89.refs_0_), channel_id=1, source_target_pairs={{0,8},{4,12},{8,0},{12,4},{16,24},{20,28},{24,16},{28,20},{1,9},{5... | collective-permute-start | bytes 589832 | tf_op jit(solution)/shard_map/ppermute | solution.py:341
  15.6 8.2 %collective-permute-start.5 = (bf16[96,1024]{1,0:T(8,128)(2,1)S(1)}, bf16[96,1024]{1,0:T(8,128)(2,1)S(1)}, u32[]{:S(2)}, u32[]{:S(2)}) collective-permute-start(bf16[96,1024]{1,0:T(8,128)(2,1)S(1)} %shard_map.89.refs_0_), channel_id=1, source_target_pairs={{0,12},{4,8},{8,4},{12,0},{16,28},{20,24},{24,20},{28,16},{1,13},{... | collective-permute-start | bytes 589832 | tf_op jit(solution)/shard_map/ppermute | solution.py:348
  26.7 4.5 %collective-permute-start.9 = (bf16[1024,384]{1,0:T(8,128)(2,1)S(1)}, bf16[1024,384]{1,0:T(8,128)(2,1)S(1)}, u32[]{:S(2)}, u32[]{:S(2)}) collective-permute-start(bf16[1024,384]{1,0:T(8,128)(2,1)S(1)} %get-tuple-element.19.normed), channel_id=1, source_target_pairs={{0,1},{1,0},{2,3},{3,2},{4,5},{5,4},{6,7},{7,6},{8,9},{9,8},{10,11... | collective-permute-start | bytes 2359304 | tf_op jit(solution)/shard_map/ppermute | solution.py:332
  26.8 20.0 %collective-permute-start.10 = (bf16[384,1024]{1,0:T(8,128)(2,1)S(1)}, bf16[384,1024]{1,0:T(8,128)(2,1)S(1)}, u32[]{:S(2)}, u32[]{:S(2)}) collective-permute-start(bf16[384,1024]{1,0:T(8,128)(2,1)S(1)} %get-tuple-element.21), channel_id=1, source_target_pairs={{0,2},{1,3},{2,0},{3,1},{4,6},{5,7},{6,4},{7,5},{8,10},{9,11},{10,... | collective-permute-start | bytes 2359304 | tf_op jit(solution)/shard_map/ppermute | solution.py:335
  30.5 1.8 %copy-start.2 = (bf16[1,1024,512]{2,1,0:T(8,128)(2,1)S(1)}, bf16[1,1024,512]{2,1,0:T(8,128)(2,1)}, u32[]{:S(2)}) copy-start(bf16[1,1024,512]{2,1,0:T(8,128)(2,1)} %noise.1) | copy-start | bytes 3145732
  30.5 1.8 %collective-permute-start.8 = (bf16[384,512]{1,0:T(8,128)(2,1)S(1)}, bf16[384,512]{1,0:T(8,128)(2,1)S(1)}, u32[]{:S(2)}, u32[]{:S(2)}) collective-permute-start(bf16[384,512]{1,0:T(8,128)(2,1)S(1)} %shard_map.94), channel_id=1, source_target_pairs={{0,1},{1,0},{2,3},{3,2},{4,5},{5,4},{6,7},{7,6},{8,9},{9,8},{10,11... | collective-permute-start | bytes 1179656 | tf_op jit(solution)/shard_map/ppermute | solution.py:332
  47.5 1.8 %collective-permute-start.11 = (bf16[384,512]{1,0:T(8,128)(2,1)S(1)}, bf16[384,512]{1,0:T(8,128)(2,1)S(1)}, u32[]{:S(2)}, u32[]{:S(2)}) collective-permute-start(bf16[384,512]{1,0:T(8,128)(2,1)S(1)} %shard_map.98), channel_id=1, source_target_pairs={{0,1},{1,0},{2,3},{3,2},{4,5},{5,4},{6,7},{7,6},{8,9},{9,8},{10,11... | collective-permute-start | bytes 1179656 | tf_op jit(solution)/shard_map/ppermute | solution.py:332
  49.7 8.2 %collective-permute-start.12 = (bf16[208,512]{1,0:T(8,128)(2,1)S(1)}, bf16[208,512]{1,0:T(8,128)(2,1)S(1)}, u32[]{:S(2)}, u32[]{:S(2)}) collective-permute-start(bf16[208,512]{1,0:T(8,128)(2,1)S(1)} %shard_map.99.rest_0_.refs_0_), channel_id=1, source_target_pairs={{0,4},{4,0},{8,12},{12,8},{16,20},{20,16},{24,28},{28,24},{1,5},{5... | collective-permute-start | bytes 638984 | tf_op jit(solution)/shard_map/ppermute | solution.py:338
  51.5 11.8 %collective-permute-start.13 = (bf16[208,512]{1,0:T(8,128)(2,1)S(1)}, bf16[208,512]{1,0:T(8,128)(2,1)S(1)}, u32[]{:S(2)}, u32[]{:S(2)}) collective-permute-start(bf16[208,512]{1,0:T(8,128)(2,1)S(1)} %shard_map.100.rest_0_.refs_1_), channel_id=1, source_target_pairs={{0,4},{4,0},{8,12},{12,8},{16,20},{20,16},{24,28},{28,24},{1,5},{5... | collective-permute-start | bytes 638984 | tf_op jit(solution)/shard_map/ppermute | solution.py:338
  52.6 14.4 %collective-permute-start.15 = (bf16[208,512]{1,0:T(8,128)(2,1)S(1)}, bf16[208,512]{1,0:T(8,128)(2,1)S(1)}, u32[]{:S(2)}, u32[]{:S(2)}) collective-permute-start(bf16[208,512]{1,0:T(8,128)(2,1)S(1)} %shard_map.101.rest_0_.refs_2_), channel_id=1, source_target_pairs={{0,4},{4,0},{8,12},{12,8},{16,20},{20,16},{24,28},{28,24},{1,5},{5... | collective-permute-start | bytes 638984 | tf_op jit(solution)/shard_map/ppermute | solution.py:338
  57.8 9.1 %collective-permute-start.16 = (bf16[208,512]{1,0:T(8,128)(2,1)S(1)}, bf16[208,512]{1,0:T(8,128)(2,1)S(1)}, u32[]{:S(2)}, u32[]{:S(2)}) collective-permute-start(bf16[208,512]{1,0:T(8,128)(2,1)S(1)} %collective-permute-done.12.refs_1_.refs_4_), channel_id=1, source_target_pairs={{0,8},{4,28},{8,16},{12,4},{16,24},{20,12},{24,0},{28,20},{1,9},{5... | collective-permute-start | bytes 638984 | tf_op jit(solution)/shard_map/ppermute | solution.py:345
  59.7 12.7 %collective-permute-start.19 = (bf16[208,512]{1,0:T(8,128)(2,1)S(1)}, bf16[208,512]{1,0:T(8,128)(2,1)S(1)}, u32[]{:S(2)}, u32[]{:S(2)}) collective-permute-start(bf16[208,512]{1,0:T(8,128)(2,1)S(1)} %shard_map.103.rest_0_.refs_3_), channel_id=1, source_target_pairs={{0,4},{4,0},{8,12},{12,8},{16,20},{20,16},{24,28},{28,24},{1,5},{5... | collective-permute-start | bytes 638984 | tf_op jit(solution)/shard_map/ppermute | solution.py:338
  63.3 9.1 %collective-permute-start.20 = (bf16[208,512]{1,0:T(8,128)(2,1)S(1)}, bf16[208,512]{1,0:T(8,128)(2,1)S(1)}, u32[]{:S(2)}, u32[]{:S(2)}) collective-permute-start(bf16[208,512]{1,0:T(8,128)(2,1)S(1)} %collective-permute-done.13.refs_1_.refs_5_), channel_id=1, source_target_pairs={{0,8},{4,28},{8,16},{12,4},{16,24},{20,12},{24,0},{28,20},{1,9},{5... | collective-permute-start | bytes 638984 | tf_op jit(solution)/shard_map/ppermute | solution.py:345
  67.0 9.2 %collective-permute-start.17 = (bf16[208,512]{1,0:T(8,128)(2,1)S(1)}, bf16[208,512]{1,0:T(8,128)(2,1)S(1)}, u32[]{:S(2)}, u32[]{:S(2)}) collective-permute-start(bf16[208,512]{1,0:T(8,128)(2,1)S(1)} %shard_map.106.refs_6_), channel_id=1, source_target_pairs={{0,8},{4,28},{8,16},{12,4},{16,24},{20,12},{24,0},{28,20},{1,9},{5... | collective-permute-start | bytes 638984 | tf_op jit(solution)/shard_map/ppermute | solution.py:345
  68.8 7.2 %collective-permute-start.14 = (bf16[192,512]{1,0:T(8,128)(2,1)S(1)}, bf16[192,512]{1,0:T(8,128)(2,1)S(1)}, u32[]{:S(2)}, u32[]{:S(2)}) collective-permute-start(bf16[192,512]{1,0:T(8,128)(2,1)S(1)} %shard_map.105.refs_0_), channel_id=1, source_target_pairs={{0,4},{4,0},{8,12},{12,8},{16,20},{20,16},{24,28},{28,24},{1,5},{5... | collective-permute-start | bytes 589832 | tf_op jit(solution)/shard_map/ppermute | solution.py:338
  72.4 9.1 %collective-permute-start.21 = (bf16[208,512]{1,0:T(8,128)(2,1)S(1)}, bf16[208,512]{1,0:T(8,128)(2,1)S(1)}, u32[]{:S(2)}, u32[]{:S(2)}) collective-permute-start(bf16[208,512]{1,0:T(8,128)(2,1)S(1)} %shard_map.108.refs_7_), channel_id=1, source_target_pairs={{0,8},{4,28},{8,16},{12,4},{16,24},{20,12},{24,0},{28,20},{1,9},{5... | collective-permute-start | bytes 638984 | tf_op jit(solution)/shard_map/ppermute | solution.py:345
  76.2 8.1 %collective-permute-start.18 = (bf16[192,512]{1,0:T(8,128)(2,1)S(1)}, bf16[192,512]{1,0:T(8,128)(2,1)S(1)}, u32[]{:S(2)}, u32[]{:S(2)}) collective-permute-start(bf16[192,512]{1,0:T(8,128)(2,1)S(1)} %shard_map.107.refs_1_), channel_id=1, source_target_pairs={{0,8},{4,28},{8,16},{12,4},{16,24},{20,12},{24,0},{28,20},{1,9},{5... | collective-permute-start | bytes 589832 | tf_op jit(solution)/shard_map/ppermute | solution.py:345

commit v7 on v6

--- a/solution.py
+++ b/solution.py
@@ -380,13 +380,16 @@
     width = params.shape[0]
     sizes = [width * part // 64 for part in (13, 13, 13, 13, 12)]
     starts = [sum(sizes[:chunk]) for chunk in range(len(sizes))]
+    fresh = []
+    for start, rows in zip(starts, sizes):
+        fresh.append(update(start, rows, begun, grads, (normed, normed_mate), *fresh[-1:]))
     own, across, beyond = [], [], []
-    for chunk, (start, rows) in enumerate(zip(starts, sizes)):
-        fresh = update(start, rows, begun, grads, (normed, normed_mate), *own[-1:])
-        if chunk >= 3:
-            fresh = after(fresh, across[chunk - 3])
-        own.append(fresh)
-        across.append(to_mate(fresh))
+    for chunk, piece in enumerate(fresh):
+        earlier = across[chunk - 3 : chunk - 3 + 1] if chunk >= 3 else []
+        if chunk == 1:
+            earlier = [*earlier, fresh[-1]]
+        own.append(after(piece, *earlier) if earlier else piece)
+        across.append(to_mate(own[-1]))
     for chunk in range(len(sizes)):
         if chunk >= 2:
             across[chunk] = after(across[chunk], beyond[chunk - 2])

time: 85.7 us -> 85.3 us (level)
  waiting for transfers between devices: 42.6 us -> 40.8 us
  starting transfers between devices: 24.6 us -> 26 us
    ppermute x5, starting transfers between devices: 4.21 us -> 5.77 us  [to_next(): return lax.ppermute(value, 'rep', pairs)]
    ppermute x6, waiting for transfers between devices: 13.2 us -> 12 us  [to_mate(): return lax.ppermute(value, 'rep', [(i, i ^ 1) for i in range(replicas)])]
  transfers between devices with their start and end apart: 22 -> 22, of which waited for: 14 -> 13; matrix products, arithmetic and copies ran while one was open for 0% -> 0% of each run, Pallas kernels for 14% -> 14%
where the time goes in v7:
time: 85.3 us; the launch traced here: 85.1 us
  waiting for transfers between devices  40.8 us (48%)
  starting transfers between devices  26 us (30%)
  Pallas kernels  14.3 us (17%)
  between operations  2.83 us (3%)
  local copies, waits for them, and re-layouts  1.24 us (1%)
    ppermute x3, waiting for transfers between devices, to_chip(): return lax.ppermute(value, 'dp', [(i, i ^ 2) for i in range(4)])  16.9 us
    ppermute x6, starting transfers between devices, to_mate(): return lax.ppermute(value, 'rep', [(i, i ^ 1) for i in range(replicas)])  12.1 us
    ppermute x6, waiting for transfers between devices, to_mate(): return lax.ppermute(value, 'rep', [(i, i ^ 1) for i in range(replicas)])  12 us
    pallas_call x2, Pallas kernels, forward(): pl.pallas_call(functools.partial(forward_kernel, len(given), len(earlier)...  5.84 us
    ppermute x5, starting transfers between devices, to_next(): return lax.ppermute(value, 'rep', pairs)  5.77 us
    ppermute x3, starting transfers between devices, to_chip(): return lax.ppermute(value, 'dp', [(i, i ^ 2) for i in range(4)])  5.31 us
    ppermute x5, waiting for transfers between devices, to_next(): return lax.ppermute(value, 'rep', pairs)  5.1 us
    pallas_call x4, Pallas kernels, hidden_of(): pl.pallas_call(hidden_kernel, out_shape=shape((count, block)), in_specs=[...  2.42 us
  transfers between devices with their start and end apart: 22, of which 13 were waited for; matrix products, arithmetic and copies ran while one was open for 0% of the time, Pallas kernels for 14%

profile of v7, /device:TPU:0, one launch (start us, length us, event | category | flops | bytes accessed | tf_op | source)
XLA Modules:
  0.0 85.1 jit_solution(3032385857475452296)
XLA Ops:
  1.2 1.2 %copy-done.3 = bf16[384,1024]{1,0:T(8,128)(2,1)S(1)} copy-done((bf16[384,1024]{1,0:T(8,128)(2,1)S(1)}, bf16[384,1024]{1,0:T(8,128)(2,1)}, u32[]{:S(2)}) %copy-start.3) | copy-done | bytes 786456
  2.7 3.0 %collective-permute-start = (bf16[96,1024]{1,0:T(8,128)(2,1)S(1)}, bf16[96,1024]{1,0:T(8,128)(2,1)S(1)}, u32[]{:S(2)}, u32[]{:S(2)}) collective-permute-start(bf16[96,1024]{1,0:T(8,128)(2,1)S(1)} %shard_map.87), channel_id=1, source_target_pairs={{0,2},{1,3},{2,0},{3,1},{4,6},{5,7},{6,4},{7,5},{8,10},{9,11},{10,... | collective-permute-start | bytes 589832 | tf_op jit(solution)/shard_map/ppermute | solution.py:335
  5.7 2.9 %shard_map.88 = (bf16[1024,384]{1,0:T(8,128)(2,1)S(1)}, bf16[384,512]{1,0:T(8,128)(2,1)S(1)}, bf16[384,512]{1,0:T(8,128)(2,1)S(1)}, bf16[384,1024]{1,0:T(8,128)(2,1)S(1)}, f32[384,1024]{1,0:T(8,128)S(1)}) custom-call(bf16[384,1024]{1,0:T(8,128)(2,1)S(1)} %copy-done.4, bf16[1024,512]{1,0:T(8,128)(2,1)S(1)} %bitcast.2, ...), custom_call_target="tpu_custom_call" | custom-call | bytes 1000 | tf_op jit(solution)/shard_map/pallas_call | solution.py:142
  8.8 2.0 %collective-permute-done.refs_0_.refs_1_ = bf16[96,1024]{1,0:T(8,128)(2,1)S(1)} collective-permute-done((bf16[96,1024]{1,0:T(8,128)(2,1)S(1)}, bf16[96,1024]{1,0:T(8,128)(2,1)S(1)}, u32[]{:S(2)}, u32[]{:S(2)}) %collective-permute-start) | collective-permute-done | bytes 196640 | tf_op jit(solution)/shard_map/ppermute | solution.py:335
  10.8 1.7 %collective-permute-start.6 = (bf16[384,1024]{1,0:T(8,128)(2,1)S(1)}, bf16[384,1024]{1,0:T(8,128)(2,1)S(1)}, u32[]{:S(2)}, u32[]{:S(2)}) collective-permute-start(bf16[384,1024]{1,0:T(8,128)(2,1)S(1)} %shard_map.91), channel_id=1, source_target_pairs={{0,2},{1,3},{2,0},{3,1},{4,6},{5,7},{6,4},{7,5},{8,10},{9,11},{10,... | collective-permute-start | bytes 2359304 | tf_op jit(solution)/shard_map/ppermute | solution.py:335
  12.5 1.5 %collective-permute-start.3 = (bf16[96,1024]{1,0:T(8,128)(2,1)S(1)}, bf16[96,1024]{1,0:T(8,128)(2,1)S(1)}, u32[]{:S(2)}, u32[]{:S(2)}) collective-permute-start(bf16[96,1024]{1,0:T(8,128)(2,1)S(1)} %shard_map.89.refs_0_), channel_id=1, source_target_pairs={{0,4},{4,0},{8,12},{12,8},{16,20},{20,16},{24,28},{28,24},{1,5},{5... | collective-permute-start | bytes 589832 | tf_op jit(solution)/shard_map/ppermute | solution.py:338
  14.0 1.6 %collective-permute-start.4 = (bf16[96,1024]{1,0:T(8,128)(2,1)S(1)}, bf16[96,1024]{1,0:T(8,128)(2,1)S(1)}, u32[]{:S(2)}, u32[]{:S(2)}) collective-permute-start(bf16[96,1024]{1,0:T(8,128)(2,1)S(1)} %shard_map.89.refs_0_), channel_id=1, source_target_pairs={{0,8},{4,12},{8,0},{12,4},{16,24},{20,28},{24,16},{28,20},{1,9},{5... | collective-permute-start | bytes 589832 | tf_op jit(solution)/shard_map/ppermute | solution.py:341
  16.0 3.1 %collective-permute-done.3.refs_1_ = bf16[96,1024]{1,0:T(8,128)(2,1)S(1)} collective-permute-done((bf16[96,1024]{1,0:T(8,128)(2,1)S(1)}, bf16[96,1024]{1,0:T(8,128)(2,1)S(1)}, u32[]{:S(2)}, u32[]{:S(2)}) %collective-permute-start.3) | collective-permute-done | bytes 196640 | tf_op jit(solution)/shard_map/ppermute | solution.py:338
  19.2 2.4 %collective-permute-done.4.refs_2_ = bf16[96,1024]{1,0:T(8,128)(2,1)S(1)} collective-permute-done((bf16[96,1024]{1,0:T(8,128)(2,1)S(1)}, bf16[96,1024]{1,0:T(8,128)(2,1)S(1)}, u32[]{:S(2)}, u32[]{:S(2)}) %collective-permute-start.4) | collective-permute-done | bytes 196640 | tf_op jit(solution)/shard_map/ppermute | solution.py:341
  21.6 2.2 %collective-permute-done.5.refs_3_ = bf16[96,1024]{1,0:T(8,128)(2,1)S(1)} collective-permute-done((bf16[96,1024]{1,0:T(8,128)(2,1)S(1)}, bf16[96,1024]{1,0:T(8,128)(2,1)S(1)}, u32[]{:S(2)}, u32[]{:S(2)}) %collective-permute-start.5) | collective-permute-done | bytes 196640 | tf_op jit(solution)/shard_map/ppermute | solution.py:348
  23.8 2.9 %shard_map.90 = (bf16[1024,384]{1,0:T(8,128)(2,1)S(1)}, bf16[384,512]{1,0:T(8,128)(2,1)S(1)}, bf16[384,512]{1,0:T(8,128)(2,1)S(1)}, bf16[384,1024]{1,0:T(8,128)(2,1)S(1)}, f32[384,1024]{1,0:T(8,128)S(1)}) custom-call(bf16[96,1024]{1,0:T(8,128)(2,1)S(1)} %shard_map.89.refs_0_, bf16[96,1024]{1,0:T(8,128)(2,1)S(1)} %collective-permute-done.3.refs_1_, ...), custom_call_target="tpu_custom_call" | custom-call | bytes 1000 | tf_op jit(solution)/shard_map/pallas_call | solution.py:142
  28.0 1.7 %collective-permute-done.6.sent = bf16[384,1024]{1,0:T(8,128)(2,1)S(1)} collective-permute-done((bf16[384,1024]{1,0:T(8,128)(2,1)S(1)}, bf16[384,1024]{1,0:T(8,128)(2,1)S(1)}, u32[]{:S(2)}, u32[]{:S(2)}) %collective-permute-start.6) | collective-permute-done | bytes 786464 | tf_op jit(solution)/shard_map/ppermute | solution.py:335
  31.2 1.1 %collective-permute-done.8.second = bf16[384,512]{1,0:T(8,128)(2,1)S(1)} collective-permute-done((bf16[384,512]{1,0:T(8,128)(2,1)S(1)}, bf16[384,512]{1,0:T(8,128)(2,1)S(1)}, u32[]{:S(2)}, u32[]{:S(2)}) %collective-permute-start.8) | collective-permute-done | bytes 393248 | tf_op jit(solution)/shard_map/ppermute | solution.py:332
  32.3 1.3 %shard_map.95.refs_0_.begun = f32[1024,512]{1,0:T(8,128)S(1)} custom-call(f32[1,512]{1,0:T(1,128)S(1)} %shard_map.86.refs_1_.strength, bf16[384,512]{1,0:T(8,128)(2,1)S(1)} %shard_map.93.first, bf16[384,512]{1,0:T(8,128)(2,1)S(1)} %collective-permute-done.8.second, bf16[1024,384]{1,0:T(8,128)(2,1)S(1)} %get-tuple-element.19.normed, ...), custom_call_target="tpu_custom_call" | custom-call | flops 805306368 | bytes 3145728 | tf_op jit(solution)/shard_map/pallas_call | solution.py:224
  33.6 13.2 %collective-permute-done.10.sent = bf16[384,1024]{1,0:T(8,128)(2,1)S(1)} collective-permute-done((bf16[384,1024]{1,0:T(8,128)(2,1)S(1)}, bf16[384,1024]{1,0:T(8,128)(2,1)S(1)}, u32[]{:S(2)}, u32[]{:S(2)}) %collective-permute-start.10) | collective-permute-done | bytes 786464 | tf_op jit(solution)/shard_map/ppermute | solution.py:335
  48.2 1.1 %collective-permute-done.11.second = bf16[384,512]{1,0:T(8,128)(2,1)S(1)} collective-permute-done((bf16[384,512]{1,0:T(8,128)(2,1)S(1)}, bf16[384,512]{1,0:T(8,128)(2,1)S(1)}, u32[]{:S(2)}, u32[]{:S(2)}) %collective-permute-start.11) | collective-permute-done | bytes 393248 | tf_op jit(solution)/shard_map/ppermute | solution.py:332
  49.7 1.4 %collective-permute-start.15 = (bf16[208,512]{1,0:T(8,128)(2,1)S(1)}, bf16[208,512]{1,0:T(8,128)(2,1)S(1)}, u32[]{:S(2)}, u32[]{:S(2)}) collective-permute-start(bf16[208,512]{1,0:T(8,128)(2,1)S(1)} %shard_map.99.rest_0_.refs_0_), channel_id=1, source_target_pairs={{0,4},{4,0},{8,12},{12,8},{16,20},{20,16},{24,28},{28,24},{1,5},{5... | collective-permute-start | bytes 638984 | tf_op jit(solution)/shard_map/ppermute | solution.py:338
  53.4 1.4 %collective-permute-start.14 = (bf16[208,512]{1,0:T(8,128)(2,1)S(1)}, bf16[208,512]{1,0:T(8,128)(2,1)S(1)}, u32[]{:S(2)}, u32[]{:S(2)}) collective-permute-start(bf16[208,512]{1,0:T(8,128)(2,1)S(1)} %shard_map.101.rest_0_.refs_2_), channel_id=1, source_target_pairs={{0,4},{4,0},{8,12},{12,8},{16,20},{20,16},{24,28},{28,24},{1,5},{5... | collective-permute-start | bytes 638984 | tf_op jit(solution)/shard_map/ppermute | solution.py:338
  54.7 3.1 %collective-permute-done.15.refs_1_.refs_4_ = bf16[208,512]{1,0:T(8,128)(2,1)S(1)} collective-permute-done((bf16[208,512]{1,0:T(8,128)(2,1)S(1)}, bf16[208,512]{1,0:T(8,128)(2,1)S(1)}, u32[]{:S(2)}, u32[]{:S(2)}) %collective-permute-start.15) | collective-permute-done | bytes 213024 | tf_op jit(solution)/shard_map/ppermute | solution.py:338
  57.8 1.5 %collective-permute-start.16 = (bf16[208,512]{1,0:T(8,128)(2,1)S(1)}, bf16[208,512]{1,0:T(8,128)(2,1)S(1)}, u32[]{:S(2)}, u32[]{:S(2)}) collective-permute-start(bf16[208,512]{1,0:T(8,128)(2,1)S(1)} %collective-permute-done.15.refs_1_.refs_4_), channel_id=1, source_target_pairs={{0,8},{4,28},{8,16},{12,4},{16,24},{20,12},{24,0},{28,20},{1,9},{5... | collective-permute-start | bytes 638984 | tf_op jit(solution)/shard_map/ppermute | solution.py:345
  59.3 3.5 %collective-permute-start.19 = (bf16[208,512]{1,0:T(8,128)(2,1)S(1)}, bf16[208,512]{1,0:T(8,128)(2,1)S(1)}, u32[]{:S(2)}, u32[]{:S(2)}) collective-permute-start(bf16[208,512]{1,0:T(8,128)(2,1)S(1)} %shard_map.108.refs_3_), channel_id=1, source_target_pairs={{0,4},{4,0},{8,12},{12,8},{16,20},{20,16},{24,28},{28,24},{1,5},{5... | collective-permute-start | bytes 638984 | tf_op jit(solution)/shard_map/ppermute | solution.py:338
  62.8 1.0 %collective-permute-start.20 = (bf16[208,512]{1,0:T(8,128)(2,1)S(1)}, bf16[208,512]{1,0:T(8,128)(2,1)S(1)}, u32[]{:S(2)}, u32[]{:S(2)}) collective-permute-start(bf16[208,512]{1,0:T(8,128)(2,1)S(1)} %collective-permute-done.12.refs_1_.refs_5_), channel_id=1, source_target_pairs={{0,8},{4,28},{8,16},{12,4},{16,24},{20,12},{24,0},{28,20},{1,9},{5... | collective-permute-start | bytes 638984 | tf_op jit(solution)/shard_map/ppermute | solution.py:345
  63.8 3.1 %collective-permute-done.14.refs_0_ = bf16[208,512]{1,0:T(8,128)(2,1)S(1)} collective-permute-done((bf16[208,512]{1,0:T(8,128)(2,1)S(1)}, bf16[208,512]{1,0:T(8,128)(2,1)S(1)}, u32[]{:S(2)}, u32[]{:S(2)}) %collective-permute-start.14) | collective-permute-done | bytes 213024 | tf_op jit(solution)/shard_map/ppermute | solution.py:338
  67.0 1.5 %collective-permute-start.17 = (bf16[208,512]{1,0:T(8,128)(2,1)S(1)}, bf16[208,512]{1,0:T(8,128)(2,1)S(1)}, u32[]{:S(2)}, u32[]{:S(2)}) collective-permute-start(bf16[208,512]{1,0:T(8,128)(2,1)S(1)} %shard_map.106.refs_6_), channel_id=1, source_target_pairs={{0,8},{4,28},{8,16},{12,4},{16,24},{20,12},{24,0},{28,20},{1,9},{5... | collective-permute-start | bytes 638984 | tf_op jit(solution)/shard_map/ppermute | solution.py:345
  68.4 3.5 %collective-permute-start.13 = (bf16[192,512]{1,0:T(8,128)(2,1)S(1)}, bf16[192,512]{1,0:T(8,128)(2,1)S(1)}, u32[]{:S(2)}, u32[]{:S(2)}) collective-permute-start(bf16[192,512]{1,0:T(8,128)(2,1)S(1)} %shard_map.105.refs_0_), channel_id=1, source_target_pairs={{0,4},{4,0},{8,12},{12,8},{16,20},{20,16},{24,28},{28,24},{1,5},{5... | collective-permute-start | bytes 589832 | tf_op jit(solution)/shard_map/ppermute | solution.py:338
  71.9 1.0 %collective-permute-start.21 = (bf16[208,512]{1,0:T(8,128)(2,1)S(1)}, bf16[208,512]{1,0:T(8,128)(2,1)S(1)}, u32[]{:S(2)}, u32[]{:S(2)}) collective-permute-start(bf16[208,512]{1,0:T(8,128)(2,1)S(1)} %shard_map.109.refs_7_), channel_id=1, source_target_pairs={{0,8},{4,28},{8,16},{12,4},{16,24},{20,12},{24,0},{28,20},{1,9},{5... | collective-permute-start | bytes 638984 | tf_op jit(solution)/shard_map/ppermute | solution.py:345
  73.0 2.6 %collective-permute-done.13.refs_0_ = bf16[192,512]{1,0:T(8,128)(2,1)S(1)} collective-permute-done((bf16[192,512]{1,0:T(8,128)(2,1)S(1)}, bf16[192,512]{1,0:T(8,128)(2,1)S(1)}, u32[]{:S(2)}, u32[]{:S(2)}) %collective-permute-start.13) | collective-permute-done | bytes 196640 | tf_op jit(solution)/shard_map/ppermute | solution.py:338
  75.6 0.8 collective-permute-start.18
  77.7 2.9 %collective-permute-done.21.refs_11_ = bf16[208,512]{1,0:T(8,128)(2,1)S(1)} collective-permute-done((bf16[208,512]{1,0:T(8,128)(2,1)S(1)}, bf16[208,512]{1,0:T(8,128)(2,1)S(1)}, u32[]{:S(2)}, u32[]{:S(2)}) %collective-permute-start.21) | collective-permute-done | bytes 213024 | tf_op jit(solution)/shard_map/ppermute | solution.py:345
  80.6 1.0 %shard_map.110 = (bf16[1,1024,512]{2,1,0:T(8,128)(2,1)}, f32[1,2,512]{2,1,0:T(2,128)S(1)}) custom-call(s32[1]{0:T(128)S(6)} %copy.28.mate, s32[1]{0:T(128)S(6)} %copy.29.swapped, bf16[208,512]{1,0:T(8,128)(2,1)S(1)} %shard_map.99.rest_0_.refs_0_, bf16[208,512]{1,0:T(8,128)(2,1)S(1)} %shard_map.104.refs_1_, bf16[208,512]{1,0:T(8,128)(2,1)S(1)} %shard_map.101.rest_0_.refs_2_, ...), custom_call_target="tpu_custom_call" | custom-call | bytes 3407872 | tf_op jit(solution)/shard_map/pallas_call | solution.py:305
  81.6 2.2 %collective-permute-done.18.refs_2_ = bf16[192,512]{1,0:T(8,128)(2,1)S(1)} collective-permute-done((bf16[192,512]{1,0:T(8,128)(2,1)S(1)}, bf16[192,512]{1,0:T(8,128)(2,1)S(1)}, u32[]{:S(2)}, u32[]{:S(2)}) %collective-permute-start.18) | collective-permute-done | bytes 196640 | tf_op jit(solution)/shard_map/ppermute | solution.py:345
  83.8 1.3 %shard_map.111 = (bf16[1,1024,512]{2,1,0:T(8,128)(2,1)}, f32[1,2,512]{2,1,0:T(2,128)}) custom-call(s32[1]{0:T(128)S(6)} %copy.28.mate, s32[1]{0:T(128)S(6)} %copy.29.swapped, bf16[192,512]{1,0:T(8,128)(2,1)S(1)} %shard_map.105.refs_0_, bf16[192,512]{1,0:T(8,128)(2,1)S(1)} %shard_map.107.refs_1_, ...), custom_call_target="tpu_custom_call", output_to_operand_aliasing={{0}: (6, {})} | custom-call | bytes 786432 | tf_op jit(solution)/shard_map/pallas_call | solution.py:305
  (49 shorter events, 7.5 us)
Async XLA Ops:
  0.6 5.1 %copy-start = (bf16[512,1024]{1,0:T(8,128)(2,1)S(1)}, bf16[512,1024]{1,0:T(8,128)(2,1)}, u32[]{:S(2)}) copy-start(bf16[512,1024]{1,0:T(8,128)(2,1)} %weight.3) | copy-start | bytes 3145732
  0.6 5.0 %copy-start.1 = (bf16[1,1024,512]{2,1,0:T(8,128)(2,1)S(1)}, bf16[1,1024,512]{2,1,0:T(8,128)(2,1)}, u32[]{:S(2)}) copy-start(bf16[1,1024,512]{2,1,0:T(8,128)(2,1)} %params.1) | copy-start | bytes 3145732
  0.6 5.0 %collective-permute-start.1 = (bf16[1024,512]{1,0:T(8,128)(2,1)}, bf16[1024,512]{1,0:T(8,128)(2,1)S(1)}, u32[]{:S(2)}, u32[]{:S(2)}) collective-permute-start(bf16[1024,512]{1,0:T(8,128)(2,1)} %bitcast.1), channel_id=1, source_target_pairs={{0,1},{1,0},{2,3},{3,2},{4,5},{5,4},{6,7},{7,6},{8,9},{9,8},{10,11... | collective-permute-start | bytes 3145736 | tf_op jit(solution)/shard_map/ppermute | solution.py:332
  1.2 4.5 %collective-permute-start.2 = (bf16[512,1024]{1,0:T(8,128)(2,1)}, bf16[512,1024]{1,0:T(8,128)(2,1)S(1)}, u32[]{:S(2)}, u32[]{:S(2)}) collective-permute-start(bf16[512,1024]{1,0:T(8,128)(2,1)} %weight.3), channel_id=1, source_target_pairs={{0,1},{1,0},{2,3},{3,2},{4,5},{5,4},{6,7},{7,6},{8,9},{9,8},{10,11... | collective-permute-start | bytes 3145736 | tf_op jit(solution)/shard_map/ppermute | solution.py:332
  1.2 1.2 %copy-start.3 = (bf16[384,1024]{1,0:T(8,128)(2,1)S(1)}, bf16[384,1024]{1,0:T(8,128)(2,1)}, u32[]{:S(2)}) copy-start(bf16[384,1024]{1,0:T(8,128)(2,1)} %refs_0_.1) | copy-start | bytes 2359300
  2.4 3.3 %copy-start.4 = (bf16[384,1024]{1,0:T(8,128)(2,1)S(1)}, bf16[384,1024]{1,0:T(8,128)(2,1)}, u32[]{:S(2)}) copy-start(bf16[384,1024]{1,0:T(8,128)(2,1)} %refs_0_.1) | copy-start | bytes 2359300
  2.7 8.1 %collective-permute-start = (bf16[96,1024]{1,0:T(8,128)(2,1)S(1)}, bf16[96,1024]{1,0:T(8,128)(2,1)S(1)}, u32[]{:S(2)}, u32[]{:S(2)}) collective-permute-start(bf16[96,1024]{1,0:T(8,128)(2,1)S(1)} %shard_map.87), channel_id=1, source_target_pairs={{0,2},{1,3},{2,0},{3,1},{4,6},{5,7},{6,4},{7,5},{8,10},{9,11},{10,... | collective-permute-start | bytes 589832 | tf_op jit(solution)/shard_map/ppermute | solution.py:335
  8.7 19.3 %collective-permute-start.7 = (bf16[1024,384]{1,0:T(8,128)(2,1)S(1)}, bf16[1024,384]{1,0:T(8,128)(2,1)S(1)}, u32[]{:S(2)}, u32[]{:S(2)}) collective-permute-start(bf16[1024,384]{1,0:T(8,128)(2,1)S(1)} %get-tuple-element.16.normed), channel_id=1, source_target_pairs={{0,1},{1,0},{2,3},{3,2},{4,5},{5,4},{6,7},{7,6},{8,9},{9,8},{10,11... | collective-permute-start | bytes 2359304 | tf_op jit(solution)/shard_map/ppermute | solution.py:332
  10.8 19.0 %collective-permute-start.6 = (bf16[384,1024]{1,0:T(8,128)(2,1)S(1)}, bf16[384,1024]{1,0:T(8,128)(2,1)S(1)}, u32[]{:S(2)}, u32[]{:S(2)}) collective-permute-start(bf16[384,1024]{1,0:T(8,128)(2,1)S(1)} %shard_map.91), channel_id=1, source_target_pairs={{0,2},{1,3},{2,0},{3,1},{4,6},{5,7},{6,4},{7,5},{8,10},{9,11},{10,... | collective-permute-start | bytes 2359304 | tf_op jit(solution)/shard_map/ppermute | solution.py:335
  12.5 6.6 %collective-permute-start.3 = (bf16[96,1024]{1,0:T(8,128)(2,1)S(1)}, bf16[96,1024]{1,0:T(8,128)(2,1)S(1)}, u32[]{:S(2)}, u32[]{:S(2)}) collective-permute-start(bf16[96,1024]{1,0:T(8,128)(2,1)S(1)} %shard_map.89.refs_0_), channel_id=1, source_target_pairs={{0,4},{4,0},{8,12},{12,8},{16,20},{20,16},{24,28},{28,24},{1,5},{5... | collective-permute-start | bytes 589832 | tf_op jit(solution)/shard_map/ppermute | solution.py:338
  14.0 7.5 %collective-permute-start.4 = (bf16[96,1024]{1,0:T(8,128)(2,1)S(1)}, bf16[96,1024]{1,0:T(8,128)(2,1)S(1)}, u32[]{:S(2)}, u32[]{:S(2)}) collective-permute-start(bf16[96,1024]{1,0:T(8,128)(2,1)S(1)} %shard_map.89.refs_0_), channel_id=1, source_target_pairs={{0,8},{4,12},{8,0},{12,4},{16,24},{20,28},{24,16},{28,20},{1,9},{5... | collective-permute-start | bytes 589832 | tf_op jit(solution)/shard_map/ppermute | solution.py:341
  15.6 8.2 %collective-permute-start.5 = (bf16[96,1024]{1,0:T(8,128)(2,1)S(1)}, bf16[96,1024]{1,0:T(8,128)(2,1)S(1)}, u32[]{:S(2)}, u32[]{:S(2)}) collective-permute-start(bf16[96,1024]{1,0:T(8,128)(2,1)S(1)} %shard_map.89.refs_0_), channel_id=1, source_target_pairs={{0,12},{4,8},{8,4},{12,0},{16,28},{20,24},{24,20},{28,16},{1,13},{... | collective-permute-start | bytes 589832 | tf_op jit(solution)/shard_map/ppermute | solution.py:348
  26.7 4.5 %collective-permute-start.9 = (bf16[1024,384]{1,0:T(8,128)(2,1)S(1)}, bf16[1024,384]{1,0:T(8,128)(2,1)S(1)}, u32[]{:S(2)}, u32[]{:S(2)}) collective-permute-start(bf16[1024,384]{1,0:T(8,128)(2,1)S(1)} %get-tuple-element.19.normed), channel_id=1, source_target_pairs={{0,1},{1,0},{2,3},{3,2},{4,5},{5,4},{6,7},{7,6},{8,9},{9,8},{10,11... | collective-permute-start | bytes 2359304 | tf_op jit(solution)/shard_map/ppermute | solution.py:332
  26.8 20.0 %collective-permute-start.10 = (bf16[384,1024]{1,0:T(8,128)(2,1)S(1)}, bf16[384,1024]{1,0:T(8,128)(2,1)S(1)}, u32[]{:S(2)}, u32[]{:S(2)}) collective-permute-start(bf16[384,1024]{1,0:T(8,128)(2,1)S(1)} %get-tuple-element.21), channel_id=1, source_target_pairs={{0,2},{1,3},{2,0},{3,1},{4,6},{5,7},{6,4},{7,5},{8,10},{9,11},{10,... | collective-permute-start | bytes 2359304 | tf_op jit(solution)/shard_map/ppermute | solution.py:335
  30.5 1.8 %copy-start.2 = (bf16[1,1024,512]{2,1,0:T(8,128)(2,1)S(1)}, bf16[1,1024,512]{2,1,0:T(8,128)(2,1)}, u32[]{:S(2)}) copy-start(bf16[1,1024,512]{2,1,0:T(8,128)(2,1)} %noise.1) | copy-start | bytes 3145732
  30.5 1.8 %collective-permute-start.8 = (bf16[384,512]{1,0:T(8,128)(2,1)S(1)}, bf16[384,512]{1,0:T(8,128)(2,1)S(1)}, u32[]{:S(2)}, u32[]{:S(2)}) collective-permute-start(bf16[384,512]{1,0:T(8,128)(2,1)S(1)} %shard_map.94), channel_id=1, source_target_pairs={{0,1},{1,0},{2,3},{3,2},{4,5},{5,4},{6,7},{7,6},{8,9},{9,8},{10,11... | collective-permute-start | bytes 1179656 | tf_op jit(solution)/shard_map/ppermute | solution.py:332
  47.5 1.8 %collective-permute-start.11 = (bf16[384,512]{1,0:T(8,128)(2,1)S(1)}, bf16[384,512]{1,0:T(8,128)(2,1)S(1)}, u32[]{:S(2)}, u32[]{:S(2)}) collective-permute-start(bf16[384,512]{1,0:T(8,128)(2,1)S(1)} %shard_map.98), channel_id=1, source_target_pairs={{0,1},{1,0},{2,3},{3,2},{4,5},{5,4},{6,7},{7,6},{8,9},{9,8},{10,11... | collective-permute-start | bytes 1179656 | tf_op jit(solution)/shard_map/ppermute | solution.py:332
  49.7 8.2 %collective-permute-start.15 = (bf16[208,512]{1,0:T(8,128)(2,1)S(1)}, bf16[208,512]{1,0:T(8,128)(2,1)S(1)}, u32[]{:S(2)}, u32[]{:S(2)}) collective-permute-start(bf16[208,512]{1,0:T(8,128)(2,1)S(1)} %shard_map.99.rest_0_.refs_0_), channel_id=1, source_target_pairs={{0,4},{4,0},{8,12},{12,8},{16,20},{20,16},{24,28},{28,24},{1,5},{5... | collective-permute-start | bytes 638984 | tf_op jit(solution)/shard_map/ppermute | solution.py:338
  52.6 10.2 %collective-permute-start.12 = (bf16[208,512]{1,0:T(8,128)(2,1)S(1)}, bf16[208,512]{1,0:T(8,128)(2,1)S(1)}, u32[]{:S(2)}, u32[]{:S(2)}) collective-permute-start(bf16[208,512]{1,0:T(8,128)(2,1)S(1)} %shard_map.104.refs_1_), channel_id=1, source_target_pairs={{0,4},{4,0},{8,12},{12,8},{16,20},{20,16},{24,28},{28,24},{1,5},{5... | collective-permute-start | bytes 638984 | tf_op jit(solution)/shard_map/ppermute | solution.py:338
  53.4 13.6 %collective-permute-start.14 = (bf16[208,512]{1,0:T(8,128)(2,1)S(1)}, bf16[208,512]{1,0:T(8,128)(2,1)S(1)}, u32[]{:S(2)}, u32[]{:S(2)}) collective-permute-start(bf16[208,512]{1,0:T(8,128)(2,1)S(1)} %shard_map.101.rest_0_.refs_2_), channel_id=1, source_target_pairs={{0,4},{4,0},{8,12},{12,8},{16,20},{20,16},{24,28},{28,24},{1,5},{5... | collective-permute-start | bytes 638984 | tf_op jit(solution)/shard_map/ppermute | solution.py:338
  57.8 9.1 %collective-permute-start.16 = (bf16[208,512]{1,0:T(8,128)(2,1)S(1)}, bf16[208,512]{1,0:T(8,128)(2,1)S(1)}, u32[]{:S(2)}, u32[]{:S(2)}) collective-permute-start(bf16[208,512]{1,0:T(8,128)(2,1)S(1)} %collective-permute-done.15.refs_1_.refs_4_), channel_id=1, source_target_pairs={{0,8},{4,28},{8,16},{12,4},{16,24},{20,12},{24,0},{28,20},{1,9},{5... | collective-permute-start | bytes 638984 | tf_op jit(solution)/shard_map/ppermute | solution.py:345
  59.3 12.7 %collective-permute-start.19 = (bf16[208,512]{1,0:T(8,128)(2,1)S(1)}, bf16[208,512]{1,0:T(8,128)(2,1)S(1)}, u32[]{:S(2)}, u32[]{:S(2)}) collective-permute-start(bf16[208,512]{1,0:T(8,128)(2,1)S(1)} %shard_map.108.refs_3_), channel_id=1, source_target_pairs={{0,4},{4,0},{8,12},{12,8},{16,20},{20,16},{24,28},{28,24},{1,5},{5... | collective-permute-start | bytes 638984 | tf_op jit(solution)/shard_map/ppermute | solution.py:338
  62.8 9.1 %collective-permute-start.20 = (bf16[208,512]{1,0:T(8,128)(2,1)S(1)}, bf16[208,512]{1,0:T(8,128)(2,1)S(1)}, u32[]{:S(2)}, u32[]{:S(2)}) collective-permute-start(bf16[208,512]{1,0:T(8,128)(2,1)S(1)} %collective-permute-done.12.refs_1_.refs_5_), channel_id=1, source_target_pairs={{0,8},{4,28},{8,16},{12,4},{16,24},{20,12},{24,0},{28,20},{1,9},{5... | collective-permute-start | bytes 638984 | tf_op jit(solution)/shard_map/ppermute | solution.py:345
  67.0 8.6 %collective-permute-start.17 = (bf16[208,512]{1,0:T(8,128)(2,1)S(1)}, bf16[208,512]{1,0:T(8,128)(2,1)S(1)}, u32[]{:S(2)}, u32[]{:S(2)}) collective-permute-start(bf16[208,512]{1,0:T(8,128)(2,1)S(1)} %shard_map.106.refs_6_), channel_id=1, source_target_pairs={{0,8},{4,28},{8,16},{12,4},{16,24},{20,12},{24,0},{28,20},{1,9},{5... | collective-permute-start | bytes 638984 | tf_op jit(solution)/shard_map/ppermute | solution.py:345
  68.4 7.2 %collective-permute-start.13 = (bf16[192,512]{1,0:T(8,128)(2,1)S(1)}, bf16[192,512]{1,0:T(8,128)(2,1)S(1)}, u32[]{:S(2)}, u32[]{:S(2)}) collective-permute-start(bf16[192,512]{1,0:T(8,128)(2,1)S(1)} %shard_map.105.refs_0_), channel_id=1, source_target_pairs={{0,4},{4,0},{8,12},{12,8},{16,20},{20,16},{24,28},{28,24},{1,5},{5... | collective-permute-start | bytes 589832 | tf_op jit(solution)/shard_map/ppermute | solution.py:338
  71.9 8.6 %collective-permute-start.21 = (bf16[208,512]{1,0:T(8,128)(2,1)S(1)}, bf16[208,512]{1,0:T(8,128)(2,1)S(1)}, u32[]{:S(2)}, u32[]{:S(2)}) collective-permute-start(bf16[208,512]{1,0:T(8,128)(2,1)S(1)} %shard_map.109.refs_7_), channel_id=1, source_target_pairs={{0,8},{4,28},{8,16},{12,4},{16,24},{20,12},{24,0},{28,20},{1,9},{5... | collective-permute-start | bytes 638984 | tf_op jit(solution)/shard_map/ppermute | solution.py:345
  75.6 8.2 %collective-permute-start.18 = (bf16[192,512]{1,0:T(8,128)(2,1)S(1)}, bf16[192,512]{1,0:T(8,128)(2,1)S(1)}, u32[]{:S(2)}, u32[]{:S(2)}) collective-permute-start(bf16[192,512]{1,0:T(8,128)(2,1)S(1)} %shard_map.107.refs_1_), channel_id=1, source_target_pairs={{0,8},{4,28},{8,16},{12,4},{16,24},{20,12},{24,0},{28,20},{1,9},{5... | collective-permute-start | bytes 589832 | tf_op jit(solution)/shard_map/ppermute | solution.py:345

commit v8 on v7

--- a/solution.py
+++ b/solution.py
@@ -205,6 +205,45 @@
     )(errors, weight, slope, *earlier)
 
 
+def send_kernel(base, sent, weight, slope, order, errors, grad):
+    errors_kernel(base, sent, errors)
+    hidden_kernel(errors, weight, slope, grad)
+
+
+def send_of(base, sent, weight, slope, order):
+    count, block = slope.shape
+    return pl.pallas_call(
+        send_kernel,
+        out_shape=(shape(base.shape), shape((count, block))),
+        in_specs=[vmem] * 4 + [anywhere],
+        out_specs=(vmem, vmem),
+        compiler_params=limit(8),
+        cost_estimate=cost(base.size * block, 8 * base.size),
+    )(base, sent, weight, slope, order)
+
+
+def carry_kernel(begun, errors, weight, slope, normed, out, grad):
+    hidden_kernel(errors, weight, slope, grad)
+    width = normed.shape[0]
+    rows = width // 4
+    scale = drift_stride * width**-0.5
+    for start in range(0, width, rows):
+        here = slice(start, start + rows)
+        out[here] = begun[here] - scale * matmul(normed[here], grad[...])
+
+
+def carry(begun, errors, weight, slope, normed):
+    return pl.pallas_call(
+        carry_kernel,
+        out_shape=shape(begun.shape, f32),
+        in_specs=[vmem] * 5,
+        out_specs=vmem,
+        scratch_shapes=[pltpu.VMEM(slope.shape, bf16)],
+        compiler_params=limit(8),
+        cost_estimate=cost(2 * errors.size * slope.shape[1], 8 * begun.size),
+    )(begun, errors, weight, slope, normed)
+
+
 def begin_kernel(strength, first, second, normed, normed_mate, params, noise, out):
     width = params.shape[1]
     rows = width // 4
@@ -231,24 +270,23 @@
     )(strength, *grads, *normed, params, noise)
 
 
-def update_kernel(start, begun, first, second, normed, normed_mate, *rest):
+def update_kernel(start, begun, grad, normed, *rest):
     out = rest[-1]
     here = slice(start, start + out.shape[0])
-    slope = matmul(normed[here], first[...]) + matmul(normed_mate[here], second[...])
+    slope = matmul(normed[here], grad[...])
     out[...] = (begun[here] - (drift_stride * normed.shape[0] ** -0.5) * slope).astype(bf16)
 
 
-def update(start, rows, begun, grads, normed, *earlier):
-    count = normed[0].shape[1]
-    block = grads[0].shape[1]
+def update(start, rows, begun, grad, normed, *earlier):
+    count, block = grad.shape
     return pl.pallas_call(
         functools.partial(update_kernel, start),
         out_shape=shape((rows, block)),
-        in_specs=[vmem] * 5 + [anywhere] * len(earlier),
+        in_specs=[vmem] * 3 + [anywhere] * len(earlier),
         out_specs=vmem,
         compiler_params=limit(4),
-        cost_estimate=cost(2 * rows * count * block, 8 * rows * count),
-    )(begun, *grads, *normed, *earlier)
+        cost_estimate=cost(rows * count * block, 8 * rows * count),
+    )(begun, grad, normed, *earlier)
 
 
 def role(mate, swapped):
@@ -370,11 +408,9 @@
     begun = begin(
         strength, far_grads, (far, far_mate), rooted_input_matrix, chain_normal_draws
     )
-    errors = errors_of(base, far_sent, begun)
-    grads = [
-        hidden_of(errors, output_matrix, slope),
-        to_core(hidden_of(errors, mate_out, slope_send)),
-    ]
+    errors, grad = send_of(base, far_sent, mate_out, slope_send, begun)
+    begun = carry(begun, errors, output_matrix, slope, normed)
+    grad = to_core(grad)
 
     pairing = (matched_chain, swap_mask)
     width = params.shape[0]
@@ -382,7 +418,7 @@
     starts = [sum(sizes[:chunk]) for chunk in range(len(sizes))]
     fresh = []
     for start, rows in zip(starts, sizes):
-        fresh.append(update(start, rows, begun, grads, (normed, normed_mate), *fresh[-1:]))
+        fresh.append(update(start, rows, begun, grad, normed_mate, *fresh[-1:]))
     own, across, beyond = [], [], []
     for chunk, piece in enumerate(fresh):
         earlier = across[chunk - 3 : chunk - 3 + 1] if chunk >= 3 else []

time: 85.3 us -> 85.1 us (level)
    pallas_call x0 -> x2, Pallas kernels: none -> 1.88 us  [the longest x1 1.25 us: carry(): pl.pallas_call(carry_kernel, out_shape=shape(begun.shape, f32), in_specs=...]
    pallas_call x4 -> x2, Pallas kernels: 2.42 us -> 1.21 us  [hidden_of(): pl.pallas_call(hidden_kernel, out_shape=shape((count, block)), in_specs=[...]
where the time goes in v8:
time: 85.1 us; the launch traced here: 84.9 us
  waiting for transfers between devices  40.6 us (48%)
  starting transfers between devices  26 us (31%)
  Pallas kernels  14.3 us (17%)
  between operations  2.82 us (3%)
  local copies, waits for them, and re-layouts  1.24 us (1%)
    ppermute x3, waiting for transfers between devices, to_chip(): return lax.ppermute(value, 'dp', [(i, i ^ 2) for i in range(4)])  16.9 us
    ppermute x6, waiting for transfers between devices, to_mate(): return lax.ppermute(value, 'rep', [(i, i ^ 1) for i in range(replicas)])  12.4 us
    ppermute x6, starting transfers between devices, to_mate(): return lax.ppermute(value, 'rep', [(i, i ^ 1) for i in range(replicas)])  12 us
    pallas_call x2, Pallas kernels, forward(): pl.pallas_call(functools.partial(forward_kernel, len(given), len(earlier)...  5.84 us
    ppermute x5, starting transfers between devices, to_next(): return lax.ppermute(value, 'rep', pairs)  5.77 us
    ppermute x3, starting transfers between devices, to_chip(): return lax.ppermute(value, 'dp', [(i, i ^ 2) for i in range(4)])  5.31 us
    ppermute x5, waiting for transfers between devices, to_next(): return lax.ppermute(value, 'rep', pairs)  5.09 us
    ppermute x1, waiting for transfers between devices, to_pair(): return lax.ppermute(value, 'rep', [(i, i ^ 2) for i in range(replicas)])  2.41 us
  transfers between devices with their start and end apart: 22, of which 13 were waited for; matrix products, arithmetic and copies ran while one was open for 0% of the time, Pallas kernels for 14%

profile of v8, /device:TPU:0, one launch (start us, length us, event | category | flops | bytes accessed | tf_op | source)
XLA Modules:
  0.0 84.9 jit_solution(14611952710908687692)
XLA Ops:
  1.2 1.2 %copy-done.3 = bf16[384,1024]{1,0:T(8,128)(2,1)S(1)} copy-done((bf16[384,1024]{1,0:T(8,128)(2,1)S(1)}, bf16[384,1024]{1,0:T(8,128)(2,1)}, u32[]{:S(2)}) %copy-start.3) | copy-done | bytes 786456
  2.7 3.0 %collective-permute-start = (bf16[96,1024]{1,0:T(8,128)(2,1)S(1)}, bf16[96,1024]{1,0:T(8,128)(2,1)S(1)}, u32[]{:S(2)}, u32[]{:S(2)}) collective-permute-start(bf16[96,1024]{1,0:T(8,128)(2,1)S(1)} %shard_map.87), channel_id=1, source_target_pairs={{0,2},{1,3},{2,0},{3,1},{4,6},{5,7},{6,4},{7,5},{8,10},{9,11},{10,... | collective-permute-start | bytes 589832 | tf_op jit(solution)/shard_map/ppermute | solution.py:373
  5.7 2.9 %shard_map.88 = (bf16[1024,384]{1,0:T(8,128)(2,1)S(1)}, bf16[384,512]{1,0:T(8,128)(2,1)S(1)}, bf16[384,512]{1,0:T(8,128)(2,1)S(1)}, bf16[384,1024]{1,0:T(8,128)(2,1)S(1)}, f32[384,1024]{1,0:T(8,128)S(1)}) custom-call(bf16[384,1024]{1,0:T(8,128)(2,1)S(1)} %copy-done.4, bf16[1024,512]{1,0:T(8,128)(2,1)S(1)} %bitcast.2, ...), custom_call_target="tpu_custom_call" | custom-call | bytes 1000 | tf_op jit(solution)/shard_map/pallas_call | solution.py:142
  8.8 2.0 %collective-permute-done.refs_0_.refs_1_ = bf16[96,1024]{1,0:T(8,128)(2,1)S(1)} collective-permute-done((bf16[96,1024]{1,0:T(8,128)(2,1)S(1)}, bf16[96,1024]{1,0:T(8,128)(2,1)S(1)}, u32[]{:S(2)}, u32[]{:S(2)}) %collective-permute-start) | collective-permute-done | bytes 196640 | tf_op jit(solution)/shard_map/ppermute | solution.py:373
  10.8 1.7 %collective-permute-start.6 = (bf16[384,1024]{1,0:T(8,128)(2,1)S(1)}, bf16[384,1024]{1,0:T(8,128)(2,1)S(1)}, u32[]{:S(2)}, u32[]{:S(2)}) collective-permute-start(bf16[384,1024]{1,0:T(8,128)(2,1)S(1)} %shard_map.91), channel_id=1, source_target_pairs={{0,2},{1,3},{2,0},{3,1},{4,6},{5,7},{6,4},{7,5},{8,10},{9,11},{10,... | collective-permute-start | bytes 2359304 | tf_op jit(solution)/shard_map/ppermute | solution.py:373
  12.5 1.5 %collective-permute-start.3 = (bf16[96,1024]{1,0:T(8,128)(2,1)S(1)}, bf16[96,1024]{1,0:T(8,128)(2,1)S(1)}, u32[]{:S(2)}, u32[]{:S(2)}) collective-permute-start(bf16[96,1024]{1,0:T(8,128)(2,1)S(1)} %shard_map.89.refs_0_), channel_id=1, source_target_pairs={{0,4},{4,0},{8,12},{12,8},{16,20},{20,16},{24,28},{28,24},{1,5},{5... | collective-permute-start | bytes 589832 | tf_op jit(solution)/shard_map/ppermute | solution.py:376
  14.0 1.6 %collective-permute-start.4 = (bf16[96,1024]{1,0:T(8,128)(2,1)S(1)}, bf16[96,1024]{1,0:T(8,128)(2,1)S(1)}, u32[]{:S(2)}, u32[]{:S(2)}) collective-permute-start(bf16[96,1024]{1,0:T(8,128)(2,1)S(1)} %shard_map.89.refs_0_), channel_id=1, source_target_pairs={{0,8},{4,12},{8,0},{12,4},{16,24},{20,28},{24,16},{28,20},{1,9},{5... | collective-permute-start | bytes 589832 | tf_op jit(solution)/shard_map/ppermute | solution.py:379
  16.0 3.1 %collective-permute-done.3.refs_1_ = bf16[96,1024]{1,0:T(8,128)(2,1)S(1)} collective-permute-done((bf16[96,1024]{1,0:T(8,128)(2,1)S(1)}, bf16[96,1024]{1,0:T(8,128)(2,1)S(1)}, u32[]{:S(2)}, u32[]{:S(2)}) %collective-permute-start.3) | collective-permute-done | bytes 196640 | tf_op jit(solution)/shard_map/ppermute | solution.py:376
  19.2 2.4 %collective-permute-done.4.refs_2_ = bf16[96,1024]{1,0:T(8,128)(2,1)S(1)} collective-permute-done((bf16[96,1024]{1,0:T(8,128)(2,1)S(1)}, bf16[96,1024]{1,0:T(8,128)(2,1)S(1)}, u32[]{:S(2)}, u32[]{:S(2)}) %collective-permute-start.4) | collective-permute-done | bytes 196640 | tf_op jit(solution)/shard_map/ppermute | solution.py:379
  21.6 2.2 %collective-permute-done.5.refs_3_ = bf16[96,1024]{1,0:T(8,128)(2,1)S(1)} collective-permute-done((bf16[96,1024]{1,0:T(8,128)(2,1)S(1)}, bf16[96,1024]{1,0:T(8,128)(2,1)S(1)}, u32[]{:S(2)}, u32[]{:S(2)}) %collective-permute-start.5) | collective-permute-done | bytes 196640 | tf_op jit(solution)/shard_map/ppermute | solution.py:386
  23.8 2.9 %shard_map.90 = (bf16[1024,384]{1,0:T(8,128)(2,1)S(1)}, bf16[384,512]{1,0:T(8,128)(2,1)S(1)}, bf16[384,512]{1,0:T(8,128)(2,1)S(1)}, bf16[384,1024]{1,0:T(8,128)(2,1)S(1)}, f32[384,1024]{1,0:T(8,128)S(1)}) custom-call(bf16[96,1024]{1,0:T(8,128)(2,1)S(1)} %shard_map.89.refs_0_, bf16[96,1024]{1,0:T(8,128)(2,1)S(1)} %collective-permute-done.3.refs_1_, ...), custom_call_target="tpu_custom_call" | custom-call | bytes 1000 | tf_op jit(solution)/shard_map/pallas_call | solution.py:142
  28.0 1.7 %collective-permute-done.6.sent = bf16[384,1024]{1,0:T(8,128)(2,1)S(1)} collective-permute-done((bf16[384,1024]{1,0:T(8,128)(2,1)S(1)}, bf16[384,1024]{1,0:T(8,128)(2,1)S(1)}, u32[]{:S(2)}, u32[]{:S(2)}) %collective-permute-start.6) | collective-permute-done | bytes 786464 | tf_op jit(solution)/shard_map/ppermute | solution.py:373
  31.2 1.1 %collective-permute-done.8.second = bf16[384,512]{1,0:T(8,128)(2,1)S(1)} collective-permute-done((bf16[384,512]{1,0:T(8,128)(2,1)S(1)}, bf16[384,512]{1,0:T(8,128)(2,1)S(1)}, u32[]{:S(2)}, u32[]{:S(2)}) %collective-permute-start.8) | collective-permute-done | bytes 393248 | tf_op jit(solution)/shard_map/ppermute | solution.py:370
  32.3 1.3 %shard_map.95.order.begun = f32[1024,512]{1,0:T(8,128)S(1)} custom-call(f32[1,512]{1,0:T(1,128)S(1)} %shard_map.86.refs_1_.strength, bf16[384,512]{1,0:T(8,128)(2,1)S(1)} %shard_map.93.first, bf16[384,512]{1,0:T(8,128)(2,1)S(1)} %collective-permute-done.8.second, bf16[1024,384]{1,0:T(8,128)(2,1)S(1)} %get-tuple-element.21.normed, ...), custom_call_target="tpu_custom_call" | custom-call | flops 805306368 | bytes 3145728 | tf_op jit(solution)/shard_map/pallas_call | solution.py:263
  33.6 13.2 %collective-permute-done.10.sent = bf16[384,1024]{1,0:T(8,128)(2,1)S(1)} collective-permute-done((bf16[384,1024]{1,0:T(8,128)(2,1)S(1)}, bf16[384,1024]{1,0:T(8,128)(2,1)S(1)}, u32[]{:S(2)}, u32[]{:S(2)}) %collective-permute-start.10) | collective-permute-done | bytes 786464 | tf_op jit(solution)/shard_map/ppermute | solution.py:373
  47.4 1.3 %shard_map.97.begun = f32[1024,512]{1,0:T(8,128)S(1)} custom-call(f32[1024,512]{1,0:T(8,128)S(1)} %shard_map.95.order.begun, bf16[384,1024]{1,0:T(8,128)(2,1)S(1)} %get-tuple-element.25.errors, bf16[512,1024]{1,0:T(8,128)(2,1)S(1)} %copy-done, bf16[384,512]{1,0:T(8,128)(2,1)S(1)} %get-tuple-element.26.slope, bf16[1024,384]{1,0:T(8,128)(2,1)S(1)} %get-tuple-element.18.normed), custom_call_target="tpu_custom_call" | custom-call | flops 805306368 | bytes 4194304 | tf_op jit(solution)/shard_map/pallas_call | solution.py:236
  49.4 1.4 %collective-permute-start.15 = (bf16[208,512]{1,0:T(8,128)(2,1)S(1)}, bf16[208,512]{1,0:T(8,128)(2,1)S(1)}, u32[]{:S(2)}, u32[]{:S(2)}) collective-permute-start(bf16[208,512]{1,0:T(8,128)(2,1)S(1)} %shard_map.98.rest_0_.refs_0_), channel_id=1, source_target_pairs={{0,4},{4,0},{8,12},{12,8},{16,20},{20,16},{24,28},{28,24},{1,5},{5... | collective-permute-start | bytes 638984 | tf_op jit(solution)/shard_map/ppermute | solution.py:376
  52.7 1.4 %collective-permute-start.14 = (bf16[208,512]{1,0:T(8,128)(2,1)S(1)}, bf16[208,512]{1,0:T(8,128)(2,1)S(1)}, u32[]{:S(2)}, u32[]{:S(2)}) collective-permute-start(bf16[208,512]{1,0:T(8,128)(2,1)S(1)} %shard_map.100.rest_0_.refs_2_), channel_id=1, source_target_pairs={{0,4},{4,0},{8,12},{12,8},{16,20},{20,16},{24,28},{28,24},{1,5},{5... | collective-permute-start | bytes 638984 | tf_op jit(solution)/shard_map/ppermute | solution.py:376
  54.1 3.5 %collective-permute-done.15.refs_1_.refs_4_ = bf16[208,512]{1,0:T(8,128)(2,1)S(1)} collective-permute-done((bf16[208,512]{1,0:T(8,128)(2,1)S(1)}, bf16[208,512]{1,0:T(8,128)(2,1)S(1)}, u32[]{:S(2)}, u32[]{:S(2)}) %collective-permute-start.15) | collective-permute-done | bytes 213024 | tf_op jit(solution)/shard_map/ppermute | solution.py:376
  57.6 1.4 %collective-permute-start.16 = (bf16[208,512]{1,0:T(8,128)(2,1)S(1)}, bf16[208,512]{1,0:T(8,128)(2,1)S(1)}, u32[]{:S(2)}, u32[]{:S(2)}) collective-permute-start(bf16[208,512]{1,0:T(8,128)(2,1)S(1)} %collective-permute-done.15.refs_1_.refs_4_), channel_id=1, source_target_pairs={{0,8},{4,28},{8,16},{12,4},{16,24},{20,12},{24,0},{28,20},{1,9},{5... | collective-permute-start | bytes 638984 | tf_op jit(solution)/shard_map/ppermute | solution.py:383
  59.0 3.5 %collective-permute-start.19 = (bf16[208,512]{1,0:T(8,128)(2,1)S(1)}, bf16[208,512]{1,0:T(8,128)(2,1)S(1)}, u32[]{:S(2)}, u32[]{:S(2)}) collective-permute-start(bf16[208,512]{1,0:T(8,128)(2,1)S(1)} %shard_map.107.refs_3_), channel_id=1, source_target_pairs={{0,4},{4,0},{8,12},{12,8},{16,20},{20,16},{24,28},{28,24},{1,5},{5... | collective-permute-start | bytes 638984 | tf_op jit(solution)/shard_map/ppermute | solution.py:376
  62.6 1.0 %collective-permute-start.20 = (bf16[208,512]{1,0:T(8,128)(2,1)S(1)}, bf16[208,512]{1,0:T(8,128)(2,1)S(1)}, u32[]{:S(2)}, u32[]{:S(2)}) collective-permute-start(bf16[208,512]{1,0:T(8,128)(2,1)S(1)} %collective-permute-done.12.refs_1_.refs_5_), channel_id=1, source_target_pairs={{0,8},{4,28},{8,16},{12,4},{16,24},{20,12},{24,0},{28,20},{1,9},{5... | collective-permute-start | bytes 638984 | tf_op jit(solution)/shard_map/ppermute | solution.py:383
  63.6 3.1 %collective-permute-done.14.refs_0_ = bf16[208,512]{1,0:T(8,128)(2,1)S(1)} collective-permute-done((bf16[208,512]{1,0:T(8,128)(2,1)S(1)}, bf16[208,512]{1,0:T(8,128)(2,1)S(1)}, u32[]{:S(2)}, u32[]{:S(2)}) %collective-permute-start.14) | collective-permute-done | bytes 213024 | tf_op jit(solution)/shard_map/ppermute | solution.py:376
  66.7 1.4 %collective-permute-start.17 = (bf16[208,512]{1,0:T(8,128)(2,1)S(1)}, bf16[208,512]{1,0:T(8,128)(2,1)S(1)}, u32[]{:S(2)}, u32[]{:S(2)}) collective-permute-start(bf16[208,512]{1,0:T(8,128)(2,1)S(1)} %shard_map.105.refs_6_), channel_id=1, source_target_pairs={{0,8},{4,28},{8,16},{12,4},{16,24},{20,12},{24,0},{28,20},{1,9},{5... | collective-permute-start | bytes 638984 | tf_op jit(solution)/shard_map/ppermute | solution.py:383
  68.2 3.5 %collective-permute-start.13 = (bf16[192,512]{1,0:T(8,128)(2,1)S(1)}, bf16[192,512]{1,0:T(8,128)(2,1)S(1)}, u32[]{:S(2)}, u32[]{:S(2)}) collective-permute-start(bf16[192,512]{1,0:T(8,128)(2,1)S(1)} %shard_map.104.refs_0_), channel_id=1, source_target_pairs={{0,4},{4,0},{8,12},{12,8},{16,20},{20,16},{24,28},{28,24},{1,5},{5... | collective-permute-start | bytes 589832 | tf_op jit(solution)/shard_map/ppermute | solution.py:376
  71.7 1.0 %collective-permute-start.21 = (bf16[208,512]{1,0:T(8,128)(2,1)S(1)}, bf16[208,512]{1,0:T(8,128)(2,1)S(1)}, u32[]{:S(2)}, u32[]{:S(2)}) collective-permute-start(bf16[208,512]{1,0:T(8,128)(2,1)S(1)} %shard_map.108.refs_7_), channel_id=1, source_target_pairs={{0,8},{4,28},{8,16},{12,4},{16,24},{20,12},{24,0},{28,20},{1,9},{5... | collective-permute-start | bytes 638984 | tf_op jit(solution)/shard_map/ppermute | solution.py:383
  72.7 2.6 %collective-permute-done.13.refs_0_ = bf16[192,512]{1,0:T(8,128)(2,1)S(1)} collective-permute-done((bf16[192,512]{1,0:T(8,128)(2,1)S(1)}, bf16[192,512]{1,0:T(8,128)(2,1)S(1)}, u32[]{:S(2)}, u32[]{:S(2)}) %collective-permute-start.13) | collective-permute-done | bytes 196640 | tf_op jit(solution)/shard_map/ppermute | solution.py:376
  75.4 0.8 collective-permute-start.18
  77.5 2.9 %collective-permute-done.21.refs_11_ = bf16[208,512]{1,0:T(8,128)(2,1)S(1)} collective-permute-done((bf16[208,512]{1,0:T(8,128)(2,1)S(1)}, bf16[208,512]{1,0:T(8,128)(2,1)S(1)}, u32[]{:S(2)}, u32[]{:S(2)}) %collective-permute-start.21) | collective-permute-done | bytes 213024 | tf_op jit(solution)/shard_map/ppermute | solution.py:383
  80.3 1.0 %shard_map.109 = (bf16[1,1024,512]{2,1,0:T(8,128)(2,1)}, f32[1,2,512]{2,1,0:T(2,128)S(1)}) custom-call(s32[1]{0:T(128)S(6)} %copy.28.mate, s32[1]{0:T(128)S(6)} %copy.29.swapped, bf16[208,512]{1,0:T(8,128)(2,1)S(1)} %shard_map.98.rest_0_.refs_0_, bf16[208,512]{1,0:T(8,128)(2,1)S(1)} %shard_map.103.refs_1_, bf16[208,512]{1,0:T(8,128)(2,1)S(1)} %shard_map.100.rest_0_.refs_2_, ...), custom_call_target="tpu_custom_call" | custom-call | bytes 3407872 | tf_op jit(solution)/shard_map/pallas_call | solution.py:343
  81.4 2.2 %collective-permute-done.18.refs_2_ = bf16[192,512]{1,0:T(8,128)(2,1)S(1)} collective-permute-done((bf16[192,512]{1,0:T(8,128)(2,1)S(1)}, bf16[192,512]{1,0:T(8,128)(2,1)S(1)}, u32[]{:S(2)}, u32[]{:S(2)}) %collective-permute-start.18) | collective-permute-done | bytes 196640 | tf_op jit(solution)/shard_map/ppermute | solution.py:383
  83.6 1.3 %shard_map.110 = (bf16[1,1024,512]{2,1,0:T(8,128)(2,1)}, f32[1,2,512]{2,1,0:T(2,128)}) custom-call(s32[1]{0:T(128)S(6)} %copy.28.mate, s32[1]{0:T(128)S(6)} %copy.29.swapped, bf16[192,512]{1,0:T(8,128)(2,1)S(1)} %shard_map.104.refs_0_, bf16[192,512]{1,0:T(8,128)(2,1)S(1)} %shard_map.106.refs_1_, ...), custom_call_target="tpu_custom_call", output_to_operand_aliasing={{0}: (6, {})} | custom-call | bytes 786432 | tf_op jit(solution)/shard_map/pallas_call | solution.py:343
  (48 shorter events, 6.7 us)
Async XLA Ops:
  0.6 5.1 %copy-start = (bf16[512,1024]{1,0:T(8,128)(2,1)S(1)}, bf16[512,1024]{1,0:T(8,128)(2,1)}, u32[]{:S(2)}) copy-start(bf16[512,1024]{1,0:T(8,128)(2,1)} %weight.3) | copy-start | bytes 3145732
  0.6 5.0 %copy-start.1 = (bf16[1,1024,512]{2,1,0:T(8,128)(2,1)S(1)}, bf16[1,1024,512]{2,1,0:T(8,128)(2,1)}, u32[]{:S(2)}) copy-start(bf16[1,1024,512]{2,1,0:T(8,128)(2,1)} %params.1) | copy-start | bytes 3145732
  0.6 5.0 %collective-permute-start.1 = (bf16[1024,512]{1,0:T(8,128)(2,1)}, bf16[1024,512]{1,0:T(8,128)(2,1)S(1)}, u32[]{:S(2)}, u32[]{:S(2)}) collective-permute-start(bf16[1024,512]{1,0:T(8,128)(2,1)} %bitcast.1), channel_id=1, source_target_pairs={{0,1},{1,0},{2,3},{3,2},{4,5},{5,4},{6,7},{7,6},{8,9},{9,8},{10,11... | collective-permute-start | bytes 3145736 | tf_op jit(solution)/shard_map/ppermute | solution.py:370
  1.2 4.5 %collective-permute-start.2 = (bf16[512,1024]{1,0:T(8,128)(2,1)}, bf16[512,1024]{1,0:T(8,128)(2,1)S(1)}, u32[]{:S(2)}, u32[]{:S(2)}) collective-permute-start(bf16[512,1024]{1,0:T(8,128)(2,1)} %weight.3), channel_id=1, source_target_pairs={{0,1},{1,0},{2,3},{3,2},{4,5},{5,4},{6,7},{7,6},{8,9},{9,8},{10,11... | collective-permute-start | bytes 3145736 | tf_op jit(solution)/shard_map/ppermute | solution.py:370
  1.2 1.2 %copy-start.3 = (bf16[384,1024]{1,0:T(8,128)(2,1)S(1)}, bf16[384,1024]{1,0:T(8,128)(2,1)}, u32[]{:S(2)}) copy-start(bf16[384,1024]{1,0:T(8,128)(2,1)} %refs_0_.1) | copy-start | bytes 2359300
  2.4 3.3 %copy-start.4 = (bf16[384,1024]{1,0:T(8,128)(2,1)S(1)}, bf16[384,1024]{1,0:T(8,128)(2,1)}, u32[]{:S(2)}) copy-start(bf16[384,1024]{1,0:T(8,128)(2,1)} %refs_0_.1) | copy-start | bytes 2359300
  2.7 8.1 %collective-permute-start = (bf16[96,1024]{1,0:T(8,128)(2,1)S(1)}, bf16[96,1024]{1,0:T(8,128)(2,1)S(1)}, u32[]{:S(2)}, u32[]{:S(2)}) collective-permute-start(bf16[96,1024]{1,0:T(8,128)(2,1)S(1)} %shard_map.87), channel_id=1, source_target_pairs={{0,2},{1,3},{2,0},{3,1},{4,6},{5,7},{6,4},{7,5},{8,10},{9,11},{10,... | collective-permute-start | bytes 589832 | tf_op jit(solution)/shard_map/ppermute | solution.py:373
  8.7 19.3 %collective-permute-start.7 = (bf16[1024,384]{1,0:T(8,128)(2,1)S(1)}, bf16[1024,384]{1,0:T(8,128)(2,1)S(1)}, u32[]{:S(2)}, u32[]{:S(2)}) collective-permute-start(bf16[1024,384]{1,0:T(8,128)(2,1)S(1)} %get-tuple-element.18.normed), channel_id=1, source_target_pairs={{0,1},{1,0},{2,3},{3,2},{4,5},{5,4},{6,7},{7,6},{8,9},{9,8},{10,11... | collective-permute-start | bytes 2359304 | tf_op jit(solution)/shard_map/ppermute | solution.py:370
  10.8 19.0 %collective-permute-start.6 = (bf16[384,1024]{1,0:T(8,128)(2,1)S(1)}, bf16[384,1024]{1,0:T(8,128)(2,1)S(1)}, u32[]{:S(2)}, u32[]{:S(2)}) collective-permute-start(bf16[384,1024]{1,0:T(8,128)(2,1)S(1)} %shard_map.91), channel_id=1, source_target_pairs={{0,2},{1,3},{2,0},{3,1},{4,6},{5,7},{6,4},{7,5},{8,10},{9,11},{10,... | collective-permute-start | bytes 2359304 | tf_op jit(solution)/shard_map/ppermute | solution.py:373
  12.5 6.6 %collective-permute-start.3 = (bf16[96,1024]{1,0:T(8,128)(2,1)S(1)}, bf16[96,1024]{1,0:T(8,128)(2,1)S(1)}, u32[]{:S(2)}, u32[]{:S(2)}) collective-permute-start(bf16[96,1024]{1,0:T(8,128)(2,1)S(1)} %shard_map.89.refs_0_), channel_id=1, source_target_pairs={{0,4},{4,0},{8,12},{12,8},{16,20},{20,16},{24,28},{28,24},{1,5},{5... | collective-permute-start | bytes 589832 | tf_op jit(solution)/shard_map/ppermute | solution.py:376
  14.0 7.5 %collective-permute-start.4 = (bf16[96,1024]{1,0:T(8,128)(2,1)S(1)}, bf16[96,1024]{1,0:T(8,128)(2,1)S(1)}, u32[]{:S(2)}, u32[]{:S(2)}) collective-permute-start(bf16[96,1024]{1,0:T(8,128)(2,1)S(1)} %shard_map.89.refs_0_), channel_id=1, source_target_pairs={{0,8},{4,12},{8,0},{12,4},{16,24},{20,28},{24,16},{28,20},{1,9},{5... | collective-permute-start | bytes 589832 | tf_op jit(solution)/shard_map/ppermute | solution.py:379
  15.6 8.2 %collective-permute-start.5 = (bf16[96,1024]{1,0:T(8,128)(2,1)S(1)}, bf16[96,1024]{1,0:T(8,128)(2,1)S(1)}, u32[]{:S(2)}, u32[]{:S(2)}) collective-permute-start(bf16[96,1024]{1,0:T(8,128)(2,1)S(1)} %shard_map.89.refs_0_), channel_id=1, source_target_pairs={{0,12},{4,8},{8,4},{12,0},{16,28},{20,24},{24,20},{28,16},{1,13},{... | collective-permute-start | bytes 589832 | tf_op jit(solution)/shard_map/ppermute | solution.py:386
  26.7 4.5 %collective-permute-start.9 = (bf16[1024,384]{1,0:T(8,128)(2,1)S(1)}, bf16[1024,384]{1,0:T(8,128)(2,1)S(1)}, u32[]{:S(2)}, u32[]{:S(2)}) collective-permute-start(bf16[1024,384]{1,0:T(8,128)(2,1)S(1)} %get-tuple-element.21.normed), channel_id=1, source_target_pairs={{0,1},{1,0},{2,3},{3,2},{4,5},{5,4},{6,7},{7,6},{8,9},{9,8},{10,11... | collective-permute-start | bytes 2359304 | tf_op jit(solution)/shard_map/ppermute | solution.py:370
  26.8 20.0 %collective-permute-start.10 = (bf16[384,1024]{1,0:T(8,128)(2,1)S(1)}, bf16[384,1024]{1,0:T(8,128)(2,1)S(1)}, u32[]{:S(2)}, u32[]{:S(2)}) collective-permute-start(bf16[384,1024]{1,0:T(8,128)(2,1)S(1)} %get-tuple-element.23), channel_id=1, source_target_pairs={{0,2},{1,3},{2,0},{3,1},{4,6},{5,7},{6,4},{7,5},{8,10},{9,11},{10,... | collective-permute-start | bytes 2359304 | tf_op jit(solution)/shard_map/ppermute | solution.py:373
  29.9 2.4 %copy-start.2 = (bf16[1,1024,512]{2,1,0:T(8,128)(2,1)S(1)}, bf16[1,1024,512]{2,1,0:T(8,128)(2,1)}, u32[]{:S(2)}) copy-start(bf16[1,1024,512]{2,1,0:T(8,128)(2,1)} %noise.1) | copy-start | bytes 3145732
  30.5 1.8 %collective-permute-start.8 = (bf16[384,512]{1,0:T(8,128)(2,1)S(1)}, bf16[384,512]{1,0:T(8,128)(2,1)S(1)}, u32[]{:S(2)}, u32[]{:S(2)}) collective-permute-start(bf16[384,512]{1,0:T(8,128)(2,1)S(1)} %shard_map.94), channel_id=1, source_target_pairs={{0,1},{1,0},{2,3},{3,2},{4,5},{5,4},{6,7},{7,6},{8,9},{9,8},{10,11... | collective-permute-start | bytes 1179656 | tf_op jit(solution)/shard_map/ppermute | solution.py:370
  47.4 1.8 %collective-permute-start.11 = (bf16[384,512]{1,0:T(8,128)(2,1)S(1)}, bf16[384,512]{1,0:T(8,128)(2,1)S(1)}, u32[]{:S(2)}, u32[]{:S(2)}) collective-permute-start(bf16[384,512]{1,0:T(8,128)(2,1)S(1)} %get-tuple-element.27), channel_id=1, source_target_pairs={{0,1},{1,0},{2,3},{3,2},{4,5},{5,4},{6,7},{7,6},{8,9},{9,8},{10,11... | collective-permute-start | bytes 1179656 | tf_op jit(solution)/shard_map/ppermute | solution.py:370
  49.4 8.2 %collective-permute-start.15 = (bf16[208,512]{1,0:T(8,128)(2,1)S(1)}, bf16[208,512]{1,0:T(8,128)(2,1)S(1)}, u32[]{:S(2)}, u32[]{:S(2)}) collective-permute-start(bf16[208,512]{1,0:T(8,128)(2,1)S(1)} %shard_map.98.rest_0_.refs_0_), channel_id=1, source_target_pairs={{0,4},{4,0},{8,12},{12,8},{16,20},{20,16},{24,28},{28,24},{1,5},{5... | collective-permute-start | bytes 638984 | tf_op jit(solution)/shard_map/ppermute | solution.py:376
  52.0 10.6 %collective-permute-start.12 = (bf16[208,512]{1,0:T(8,128)(2,1)S(1)}, bf16[208,512]{1,0:T(8,128)(2,1)S(1)}, u32[]{:S(2)}, u32[]{:S(2)}) collective-permute-start(bf16[208,512]{1,0:T(8,128)(2,1)S(1)} %shard_map.103.refs_1_), channel_id=1, source_target_pairs={{0,4},{4,0},{8,12},{12,8},{16,20},{20,16},{24,28},{28,24},{1,5},{5... | collective-permute-start | bytes 638984 | tf_op jit(solution)/shard_map/ppermute | solution.py:376
  52.7 14.0 %collective-permute-start.14 = (bf16[208,512]{1,0:T(8,128)(2,1)S(1)}, bf16[208,512]{1,0:T(8,128)(2,1)S(1)}, u32[]{:S(2)}, u32[]{:S(2)}) collective-permute-start(bf16[208,512]{1,0:T(8,128)(2,1)S(1)} %shard_map.100.rest_0_.refs_2_), channel_id=1, source_target_pairs={{0,4},{4,0},{8,12},{12,8},{16,20},{20,16},{24,28},{28,24},{1,5},{5... | collective-permute-start | bytes 638984 | tf_op jit(solution)/shard_map/ppermute | solution.py:376
  57.6 9.1 %collective-permute-start.16 = (bf16[208,512]{1,0:T(8,128)(2,1)S(1)}, bf16[208,512]{1,0:T(8,128)(2,1)S(1)}, u32[]{:S(2)}, u32[]{:S(2)}) collective-permute-start(bf16[208,512]{1,0:T(8,128)(2,1)S(1)} %collective-permute-done.15.refs_1_.refs_4_), channel_id=1, source_target_pairs={{0,8},{4,28},{8,16},{12,4},{16,24},{20,12},{24,0},{28,20},{1,9},{5... | collective-permute-start | bytes 638984 | tf_op jit(solution)/shard_map/ppermute | solution.py:383
  59.0 12.7 %collective-permute-start.19 = (bf16[208,512]{1,0:T(8,128)(2,1)S(1)}, bf16[208,512]{1,0:T(8,128)(2,1)S(1)}, u32[]{:S(2)}, u32[]{:S(2)}) collective-permute-start(bf16[208,512]{1,0:T(8,128)(2,1)S(1)} %shard_map.107.refs_3_), channel_id=1, source_target_pairs={{0,4},{4,0},{8,12},{12,8},{16,20},{20,16},{24,28},{28,24},{1,5},{5... | collective-permute-start | bytes 638984 | tf_op jit(solution)/shard_map/ppermute | solution.py:376
  62.6 9.1 %collective-permute-start.20 = (bf16[208,512]{1,0:T(8,128)(2,1)S(1)}, bf16[208,512]{1,0:T(8,128)(2,1)S(1)}, u32[]{:S(2)}, u32[]{:S(2)}) collective-permute-start(bf16[208,512]{1,0:T(8,128)(2,1)S(1)} %collective-permute-done.12.refs_1_.refs_5_), channel_id=1, source_target_pairs={{0,8},{4,28},{8,16},{12,4},{16,24},{20,12},{24,0},{28,20},{1,9},{5... | collective-permute-start | bytes 638984 | tf_op jit(solution)/shard_map/ppermute | solution.py:383
  66.7 8.6 %collective-permute-start.17 = (bf16[208,512]{1,0:T(8,128)(2,1)S(1)}, bf16[208,512]{1,0:T(8,128)(2,1)S(1)}, u32[]{:S(2)}, u32[]{:S(2)}) collective-permute-start(bf16[208,512]{1,0:T(8,128)(2,1)S(1)} %shard_map.105.refs_6_), channel_id=1, source_target_pairs={{0,8},{4,28},{8,16},{12,4},{16,24},{20,12},{24,0},{28,20},{1,9},{5... | collective-permute-start | bytes 638984 | tf_op jit(solution)/shard_map/ppermute | solution.py:383
  68.2 7.2 %collective-permute-start.13 = (bf16[192,512]{1,0:T(8,128)(2,1)S(1)}, bf16[192,512]{1,0:T(8,128)(2,1)S(1)}, u32[]{:S(2)}, u32[]{:S(2)}) collective-permute-start(bf16[192,512]{1,0:T(8,128)(2,1)S(1)} %shard_map.104.refs_0_), channel_id=1, source_target_pairs={{0,4},{4,0},{8,12},{12,8},{16,20},{20,16},{24,28},{28,24},{1,5},{5... | collective-permute-start | bytes 589832 | tf_op jit(solution)/shard_map/ppermute | solution.py:376
  71.7 8.6 %collective-permute-start.21 = (bf16[208,512]{1,0:T(8,128)(2,1)S(1)}, bf16[208,512]{1,0:T(8,128)(2,1)S(1)}, u32[]{:S(2)}, u32[]{:S(2)}) collective-permute-start(bf16[208,512]{1,0:T(8,128)(2,1)S(1)} %shard_map.108.refs_7_), channel_id=1, source_target_pairs={{0,8},{4,28},{8,16},{12,4},{16,24},{20,12},{24,0},{28,20},{1,9},{5... | collective-permute-start | bytes 638984 | tf_op jit(solution)/shard_map/ppermute | solution.py:383
  75.4 8.2 %collective-permute-start.18 = (bf16[192,512]{1,0:T(8,128)(2,1)S(1)}, bf16[192,512]{1,0:T(8,128)(2,1)S(1)}, u32[]{:S(2)}, u32[]{:S(2)}) collective-permute-start(bf16[192,512]{1,0:T(8,128)(2,1)S(1)} %shard_map.106.refs_1_), channel_id=1, source_target_pairs={{0,8},{4,28},{8,16},{12,4},{16,24},{20,12},{24,0},{28,20},{1,9},{5... | collective-permute-start | bytes 589832 | tf_op jit(solution)/shard_map/ppermute | solution.py:383

commit v9 on v8

--- a/solution.py
+++ b/solution.py
@@ -414,7 +414,7 @@
 
     pairing = (matched_chain, swap_mask)
     width = params.shape[0]
-    sizes = [width * part // 64 for part in (13, 13, 13, 13, 12)]
+    sizes = [width * part // 64 for part in (11, 14, 14, 14, 11)]
     starts = [sum(sizes[:chunk]) for chunk in range(len(sizes))]
     fresh = []
     for start, rows in zip(starts, sizes):

time: 85.1 us -> 84.9 us (level)
  waiting for transfers between devices: 40.6 us -> 39.5 us
  starting transfers between devices: 26 us -> 26.9 us
    ppermute x6, waiting for transfers between devices: 12.4 us -> 11.5 us  [to_mate(): return lax.ppermute(value, 'rep', [(i, i ^ 1) for i in range(replicas)])]
    ppermute x5, starting transfers between devices: 5.77 us -> 6.65 us  [to_next(): return lax.ppermute(value, 'rep', pairs)]
where the time goes in v9:
time: 84.9 us; the launch traced here: 84.7 us
  waiting for transfers between devices  39.5 us (47%)
  starting transfers between devices  26.9 us (32%)
  Pallas kernels  14.3 us (17%)
  between operations  2.82 us (3%)
  local copies, waits for them, and re-layouts  1.24 us (1%)
    ppermute x3, waiting for transfers between devices, to_chip(): return lax.ppermute(value, 'dp', [(i, i ^ 2) for i in range(4)])  16.9 us
    ppermute x6, starting transfers between devices, to_mate(): return lax.ppermute(value, 'rep', [(i, i ^ 1) for i in range(replicas)])  12 us
    ppermute x6, waiting for transfers between devices, to_mate(): return lax.ppermute(value, 'rep', [(i, i ^ 1) for i in range(replicas)])  11.5 us
    ppermute x5, starting transfers between devices, to_next(): return lax.ppermute(value, 'rep', pairs)  6.65 us
    pallas_call x2, Pallas kernels, forward(): pl.pallas_call(functools.partial(forward_kernel, len(given), len(earlier)...  5.84 us
    ppermute x3, starting transfers between devices, to_chip(): return lax.ppermute(value, 'dp', [(i, i ^ 2) for i in range(4)])  5.31 us
    ppermute x5, waiting for transfers between devices, to_next(): return lax.ppermute(value, 'rep', pairs)  4.91 us
    ppermute x1, waiting for transfers between devices, to_pair(): return lax.ppermute(value, 'rep', [(i, i ^ 2) for i in range(replicas)])  2.41 us
  transfers between devices with their start and end apart: 22, of which 13 were waited for; matrix products, arithmetic and copies ran while one was open for 0% of the time, Pallas kernels for 14%

profile of v9, /device:TPU:0, one launch (start us, length us, event | category | flops | bytes accessed | tf_op | source)
XLA Modules:
  0.0 84.7 jit_solution(2717481088581970276)
XLA Ops:
  1.2 1.2 %copy-done.3 = bf16[384,1024]{1,0:T(8,128)(2,1)S(1)} copy-done((bf16[384,1024]{1,0:T(8,128)(2,1)S(1)}, bf16[384,1024]{1,0:T(8,128)(2,1)}, u32[]{:S(2)}) %copy-start.3) | copy-done | bytes 786456
  2.7 3.0 %collective-permute-start = (bf16[96,1024]{1,0:T(8,128)(2,1)S(1)}, bf16[96,1024]{1,0:T(8,128)(2,1)S(1)}, u32[]{:S(2)}, u32[]{:S(2)}) collective-permute-start(bf16[96,1024]{1,0:T(8,128)(2,1)S(1)} %shard_map.87), channel_id=1, source_target_pairs={{0,2},{1,3},{2,0},{3,1},{4,6},{5,7},{6,4},{7,5},{8,10},{9,11},{10,... | collective-permute-start | bytes 589832 | tf_op jit(solution)/shard_map/ppermute | solution.py:373
  5.7 2.9 %shard_map.88 = (bf16[1024,384]{1,0:T(8,128)(2,1)S(1)}, bf16[384,512]{1,0:T(8,128)(2,1)S(1)}, bf16[384,512]{1,0:T(8,128)(2,1)S(1)}, bf16[384,1024]{1,0:T(8,128)(2,1)S(1)}, f32[384,1024]{1,0:T(8,128)S(1)}) custom-call(bf16[384,1024]{1,0:T(8,128)(2,1)S(1)} %copy-done.4, bf16[1024,512]{1,0:T(8,128)(2,1)S(1)} %bitcast.2, ...), custom_call_target="tpu_custom_call" | custom-call | bytes 1000 | tf_op jit(solution)/shard_map/pallas_call | solution.py:142
  8.8 2.0 %collective-permute-done.refs_0_.refs_1_ = bf16[96,1024]{1,0:T(8,128)(2,1)S(1)} collective-permute-done((bf16[96,1024]{1,0:T(8,128)(2,1)S(1)}, bf16[96,1024]{1,0:T(8,128)(2,1)S(1)}, u32[]{:S(2)}, u32[]{:S(2)}) %collective-permute-start) | collective-permute-done | bytes 196640 | tf_op jit(solution)/shard_map/ppermute | solution.py:373
  10.8 1.7 %collective-permute-start.6 = (bf16[384,1024]{1,0:T(8,128)(2,1)S(1)}, bf16[384,1024]{1,0:T(8,128)(2,1)S(1)}, u32[]{:S(2)}, u32[]{:S(2)}) collective-permute-start(bf16[384,1024]{1,0:T(8,128)(2,1)S(1)} %shard_map.91), channel_id=1, source_target_pairs={{0,2},{1,3},{2,0},{3,1},{4,6},{5,7},{6,4},{7,5},{8,10},{9,11},{10,... | collective-permute-start | bytes 2359304 | tf_op jit(solution)/shard_map/ppermute | solution.py:373
  12.5 1.5 %collective-permute-start.3 = (bf16[96,1024]{1,0:T(8,128)(2,1)S(1)}, bf16[96,1024]{1,0:T(8,128)(2,1)S(1)}, u32[]{:S(2)}, u32[]{:S(2)}) collective-permute-start(bf16[96,1024]{1,0:T(8,128)(2,1)S(1)} %shard_map.89.refs_0_), channel_id=1, source_target_pairs={{0,4},{4,0},{8,12},{12,8},{16,20},{20,16},{24,28},{28,24},{1,5},{5... | collective-permute-start | bytes 589832 | tf_op jit(solution)/shard_map/ppermute | solution.py:376
  14.0 1.6 %collective-permute-start.4 = (bf16[96,1024]{1,0:T(8,128)(2,1)S(1)}, bf16[96,1024]{1,0:T(8,128)(2,1)S(1)}, u32[]{:S(2)}, u32[]{:S(2)}) collective-permute-start(bf16[96,1024]{1,0:T(8,128)(2,1)S(1)} %shard_map.89.refs_0_), channel_id=1, source_target_pairs={{0,8},{4,12},{8,0},{12,4},{16,24},{20,28},{24,16},{28,20},{1,9},{5... | collective-permute-start | bytes 589832 | tf_op jit(solution)/shard_map/ppermute | solution.py:379
  16.0 3.1 %collective-permute-done.3.refs_1_ = bf16[96,1024]{1,0:T(8,128)(2,1)S(1)} collective-permute-done((bf16[96,1024]{1,0:T(8,128)(2,1)S(1)}, bf16[96,1024]{1,0:T(8,128)(2,1)S(1)}, u32[]{:S(2)}, u32[]{:S(2)}) %collective-permute-start.3) | collective-permute-done | bytes 196640 | tf_op jit(solution)/shard_map/ppermute | solution.py:376
  19.2 2.4 %collective-permute-done.4.refs_2_ = bf16[96,1024]{1,0:T(8,128)(2,1)S(1)} collective-permute-done((bf16[96,1024]{1,0:T(8,128)(2,1)S(1)}, bf16[96,1024]{1,0:T(8,128)(2,1)S(1)}, u32[]{:S(2)}, u32[]{:S(2)}) %collective-permute-start.4) | collective-permute-done | bytes 196640 | tf_op jit(solution)/shard_map/ppermute | solution.py:379
  21.6 2.2 %collective-permute-done.5.refs_3_ = bf16[96,1024]{1,0:T(8,128)(2,1)S(1)} collective-permute-done((bf16[96,1024]{1,0:T(8,128)(2,1)S(1)}, bf16[96,1024]{1,0:T(8,128)(2,1)S(1)}, u32[]{:S(2)}, u32[]{:S(2)}) %collective-permute-start.5) | collective-permute-done | bytes 196640 | tf_op jit(solution)/shard_map/ppermute | solution.py:386
  23.8 2.9 %shard_map.90 = (bf16[1024,384]{1,0:T(8,128)(2,1)S(1)}, bf16[384,512]{1,0:T(8,128)(2,1)S(1)}, bf16[384,512]{1,0:T(8,128)(2,1)S(1)}, bf16[384,1024]{1,0:T(8,128)(2,1)S(1)}, f32[384,1024]{1,0:T(8,128)S(1)}) custom-call(bf16[96,1024]{1,0:T(8,128)(2,1)S(1)} %shard_map.89.refs_0_, bf16[96,1024]{1,0:T(8,128)(2,1)S(1)} %collective-permute-done.3.refs_1_, ...), custom_call_target="tpu_custom_call" | custom-call | bytes 1000 | tf_op jit(solution)/shard_map/pallas_call | solution.py:142
  28.0 1.7 %collective-permute-done.6.sent = bf16[384,1024]{1,0:T(8,128)(2,1)S(1)} collective-permute-done((bf16[384,1024]{1,0:T(8,128)(2,1)S(1)}, bf16[384,1024]{1,0:T(8,128)(2,1)S(1)}, u32[]{:S(2)}, u32[]{:S(2)}) %collective-permute-start.6) | collective-permute-done | bytes 786464 | tf_op jit(solution)/shard_map/ppermute | solution.py:373
  31.2 1.1 %collective-permute-done.8.second = bf16[384,512]{1,0:T(8,128)(2,1)S(1)} collective-permute-done((bf16[384,512]{1,0:T(8,128)(2,1)S(1)}, bf16[384,512]{1,0:T(8,128)(2,1)S(1)}, u32[]{:S(2)}, u32[]{:S(2)}) %collective-permute-start.8) | collective-permute-done | bytes 393248 | tf_op jit(solution)/shard_map/ppermute | solution.py:370
  32.3 1.3 %shard_map.95.order.begun = f32[1024,512]{1,0:T(8,128)S(1)} custom-call(f32[1,512]{1,0:T(1,128)S(1)} %shard_map.86.refs_1_.strength, bf16[384,512]{1,0:T(8,128)(2,1)S(1)} %shard_map.93.first, bf16[384,512]{1,0:T(8,128)(2,1)S(1)} %collective-permute-done.8.second, bf16[1024,384]{1,0:T(8,128)(2,1)S(1)} %get-tuple-element.21.normed, ...), custom_call_target="tpu_custom_call" | custom-call | flops 805306368 | bytes 3145728 | tf_op jit(solution)/shard_map/pallas_call | solution.py:263
  33.6 13.2 %collective-permute-done.10.sent = bf16[384,1024]{1,0:T(8,128)(2,1)S(1)} collective-permute-done((bf16[384,1024]{1,0:T(8,128)(2,1)S(1)}, bf16[384,1024]{1,0:T(8,128)(2,1)S(1)}, u32[]{:S(2)}, u32[]{:S(2)}) %collective-permute-start.10) | collective-permute-done | bytes 786464 | tf_op jit(solution)/shard_map/ppermute | solution.py:373
  47.4 1.3 %shard_map.97.begun = f32[1024,512]{1,0:T(8,128)S(1)} custom-call(f32[1024,512]{1,0:T(8,128)S(1)} %shard_map.95.order.begun, bf16[384,1024]{1,0:T(8,128)(2,1)S(1)} %get-tuple-element.25.errors, bf16[512,1024]{1,0:T(8,128)(2,1)S(1)} %copy-done, bf16[384,512]{1,0:T(8,128)(2,1)S(1)} %get-tuple-element.26.slope, bf16[1024,384]{1,0:T(8,128)(2,1)S(1)} %get-tuple-element.18.normed), custom_call_target="tpu_custom_call" | custom-call | flops 805306368 | bytes 4194304 | tf_op jit(solution)/shard_map/pallas_call | solution.py:236
  49.4 1.4 %collective-permute-start.15 = (bf16[176,512]{1,0:T(8,128)(2,1)S(1)}, bf16[176,512]{1,0:T(8,128)(2,1)S(1)}, u32[]{:S(2)}, u32[]{:S(2)}) collective-permute-start(bf16[176,512]{1,0:T(8,128)(2,1)S(1)} %shard_map.98.rest_0_.refs_0_), channel_id=1, source_target_pairs={{0,4},{4,0},{8,12},{12,8},{16,20},{20,16},{24,28},{28,24},{1,5},{5... | collective-permute-start | bytes 540680 | tf_op jit(solution)/shard_map/ppermute | solution.py:376
  52.7 1.4 %collective-permute-start.14 = (bf16[224,512]{1,0:T(8,128)(2,1)S(1)}, bf16[224,512]{1,0:T(8,128)(2,1)S(1)}, u32[]{:S(2)}, u32[]{:S(2)}) collective-permute-start(bf16[224,512]{1,0:T(8,128)(2,1)S(1)} %shard_map.100.rest_0_.refs_2_), channel_id=1, source_target_pairs={{0,4},{4,0},{8,12},{12,8},{16,20},{20,16},{24,28},{28,24},{1,5},{5... | collective-permute-start | bytes 688136 | tf_op jit(solution)/shard_map/ppermute | solution.py:376
  54.1 2.8 %collective-permute-done.15.refs_1_.refs_4_ = bf16[176,512]{1,0:T(8,128)(2,1)S(1)} collective-permute-done((bf16[176,512]{1,0:T(8,128)(2,1)S(1)}, bf16[176,512]{1,0:T(8,128)(2,1)S(1)}, u32[]{:S(2)}, u32[]{:S(2)}) %collective-permute-start.15) | collective-permute-done | bytes 180256 | tf_op jit(solution)/shard_map/ppermute | solution.py:376
  56.9 1.4 %collective-permute-start.16 = (bf16[176,512]{1,0:T(8,128)(2,1)S(1)}, bf16[176,512]{1,0:T(8,128)(2,1)S(1)}, u32[]{:S(2)}, u32[]{:S(2)}) collective-permute-start(bf16[176,512]{1,0:T(8,128)(2,1)S(1)} %collective-permute-done.15.refs_1_.refs_4_), channel_id=1, source_target_pairs={{0,8},{4,28},{8,16},{12,4},{16,24},{20,12},{24,0},{28,20},{1,9},{5... | collective-permute-start | bytes 540680 | tf_op jit(solution)/shard_map/ppermute | solution.py:383
  58.3 3.5 %collective-permute-start.19 = (bf16[224,512]{1,0:T(8,128)(2,1)S(1)}, bf16[224,512]{1,0:T(8,128)(2,1)S(1)}, u32[]{:S(2)}, u32[]{:S(2)}) collective-permute-start(bf16[224,512]{1,0:T(8,128)(2,1)S(1)} %shard_map.107.refs_3_), channel_id=1, source_target_pairs={{0,4},{4,0},{8,12},{12,8},{16,20},{20,16},{24,28},{28,24},{1,5},{5... | collective-permute-start | bytes 688136 | tf_op jit(solution)/shard_map/ppermute | solution.py:376
  61.9 1.4 %collective-permute-start.20 = (bf16[224,512]{1,0:T(8,128)(2,1)S(1)}, bf16[224,512]{1,0:T(8,128)(2,1)S(1)}, u32[]{:S(2)}, u32[]{:S(2)}) collective-permute-start(bf16[224,512]{1,0:T(8,128)(2,1)S(1)} %collective-permute-done.12.refs_1_.refs_5_), channel_id=1, source_target_pairs={{0,8},{4,28},{8,16},{12,4},{16,24},{20,12},{24,0},{28,20},{1,9},{5... | collective-permute-start | bytes 688136 | tf_op jit(solution)/shard_map/ppermute | solution.py:383
  63.2 3.5 %collective-permute-done.14.refs_0_ = bf16[224,512]{1,0:T(8,128)(2,1)S(1)} collective-permute-done((bf16[224,512]{1,0:T(8,128)(2,1)S(1)}, bf16[224,512]{1,0:T(8,128)(2,1)S(1)}, u32[]{:S(2)}, u32[]{:S(2)}) %collective-permute-start.14) | collective-permute-done | bytes 229408 | tf_op jit(solution)/shard_map/ppermute | solution.py:376
  66.7 1.4 %collective-permute-start.17 = (bf16[224,512]{1,0:T(8,128)(2,1)S(1)}, bf16[224,512]{1,0:T(8,128)(2,1)S(1)}, u32[]{:S(2)}, u32[]{:S(2)}) collective-permute-start(bf16[224,512]{1,0:T(8,128)(2,1)S(1)} %shard_map.105.refs_6_), channel_id=1, source_target_pairs={{0,8},{4,28},{8,16},{12,4},{16,24},{20,12},{24,0},{28,20},{1,9},{5... | collective-permute-start | bytes 688136 | tf_op jit(solution)/shard_map/ppermute | solution.py:383
  68.2 3.5 %collective-permute-start.13 = (bf16[176,512]{1,0:T(8,128)(2,1)S(1)}, bf16[176,512]{1,0:T(8,128)(2,1)S(1)}, u32[]{:S(2)}, u32[]{:S(2)}) collective-permute-start(bf16[176,512]{1,0:T(8,128)(2,1)S(1)} %shard_map.104.refs_0_), channel_id=1, source_target_pairs={{0,4},{4,0},{8,12},{12,8},{16,20},{20,16},{24,28},{28,24},{1,5},{5... | collective-permute-start | bytes 540680 | tf_op jit(solution)/shard_map/ppermute | solution.py:376
  71.7 1.4 %collective-permute-start.21 = (bf16[224,512]{1,0:T(8,128)(2,1)S(1)}, bf16[224,512]{1,0:T(8,128)(2,1)S(1)}, u32[]{:S(2)}, u32[]{:S(2)}) collective-permute-start(bf16[224,512]{1,0:T(8,128)(2,1)S(1)} %shard_map.108.refs_7_), channel_id=1, source_target_pairs={{0,8},{4,28},{8,16},{12,4},{16,24},{20,12},{24,0},{28,20},{1,9},{5... | collective-permute-start | bytes 688136 | tf_op jit(solution)/shard_map/ppermute | solution.py:383
  73.1 2.1 %collective-permute-done.13.refs_0_ = bf16[176,512]{1,0:T(8,128)(2,1)S(1)} collective-permute-done((bf16[176,512]{1,0:T(8,128)(2,1)S(1)}, bf16[176,512]{1,0:T(8,128)(2,1)S(1)}, u32[]{:S(2)}, u32[]{:S(2)}) %collective-permute-start.13) | collective-permute-done | bytes 180256 | tf_op jit(solution)/shard_map/ppermute | solution.py:376
  75.2 1.0 %collective-permute-start.18 = (bf16[176,512]{1,0:T(8,128)(2,1)S(1)}, bf16[176,512]{1,0:T(8,128)(2,1)S(1)}, u32[]{:S(2)}, u32[]{:S(2)}) collective-permute-start(bf16[176,512]{1,0:T(8,128)(2,1)S(1)} %shard_map.106.refs_1_), channel_id=1, source_target_pairs={{0,8},{4,28},{8,16},{12,4},{16,24},{20,12},{24,0},{28,20},{1,9},{5... | collective-permute-start | bytes 540680 | tf_op jit(solution)/shard_map/ppermute | solution.py:383
  77.4 3.2 %collective-permute-done.21.refs_11_ = bf16[224,512]{1,0:T(8,128)(2,1)S(1)} collective-permute-done((bf16[224,512]{1,0:T(8,128)(2,1)S(1)}, bf16[224,512]{1,0:T(8,128)(2,1)S(1)}, u32[]{:S(2)}, u32[]{:S(2)}) %collective-permute-start.21) | collective-permute-done | bytes 229408 | tf_op jit(solution)/shard_map/ppermute | solution.py:383
  80.7 1.0 %shard_map.109 = (bf16[1,1024,512]{2,1,0:T(8,128)(2,1)}, f32[1,2,512]{2,1,0:T(2,128)S(1)}) custom-call(s32[1]{0:T(128)S(6)} %copy.28.mate, s32[1]{0:T(128)S(6)} %copy.29.swapped, bf16[176,512]{1,0:T(8,128)(2,1)S(1)} %shard_map.98.rest_0_.refs_0_, bf16[224,512]{1,0:T(8,128)(2,1)S(1)} %shard_map.103.refs_1_, bf16[224,512]{1,0:T(8,128)(2,1)S(1)} %shard_map.100.rest_0_.refs_2_, ...), custom_call_target="tpu_custom_call" | custom-call | bytes 3473408 | tf_op jit(solution)/shard_map/pallas_call | solution.py:343
  81.7 1.7 %collective-permute-done.18.refs_2_ = bf16[176,512]{1,0:T(8,128)(2,1)S(1)} collective-permute-done((bf16[176,512]{1,0:T(8,128)(2,1)S(1)}, bf16[176,512]{1,0:T(8,128)(2,1)S(1)}, u32[]{:S(2)}, u32[]{:S(2)}) %collective-permute-start.18) | collective-permute-done | bytes 180256 | tf_op jit(solution)/shard_map/ppermute | solution.py:383
  83.4 1.3 %shard_map.110 = (bf16[1,1024,512]{2,1,0:T(8,128)(2,1)}, f32[1,2,512]{2,1,0:T(2,128)}) custom-call(s32[1]{0:T(128)S(6)} %copy.28.mate, s32[1]{0:T(128)S(6)} %copy.29.swapped, bf16[176,512]{1,0:T(8,128)(2,1)S(1)} %shard_map.104.refs_0_, bf16[176,512]{1,0:T(8,128)(2,1)S(1)} %shard_map.106.refs_1_, ...), custom_call_target="tpu_custom_call", output_to_operand_aliasing={{0}: (6, {})} | custom-call | bytes 720896 | tf_op jit(solution)/shard_map/pallas_call | solution.py:343
  (48 shorter events, 6.7 us)
Async XLA Ops:
  0.6 5.1 %copy-start = (bf16[512,1024]{1,0:T(8,128)(2,1)S(1)}, bf16[512,1024]{1,0:T(8,128)(2,1)}, u32[]{:S(2)}) copy-start(bf16[512,1024]{1,0:T(8,128)(2,1)} %weight.3) | copy-start | bytes 3145732
  0.6 5.0 %copy-start.1 = (bf16[1,1024,512]{2,1,0:T(8,128)(2,1)S(1)}, bf16[1,1024,512]{2,1,0:T(8,128)(2,1)}, u32[]{:S(2)}) copy-start(bf16[1,1024,512]{2,1,0:T(8,128)(2,1)} %params.1) | copy-start | bytes 3145732
  0.6 5.0 %collective-permute-start.1 = (bf16[1024,512]{1,0:T(8,128)(2,1)}, bf16[1024,512]{1,0:T(8,128)(2,1)S(1)}, u32[]{:S(2)}, u32[]{:S(2)}) collective-permute-start(bf16[1024,512]{1,0:T(8,128)(2,1)} %bitcast.1), channel_id=1, source_target_pairs={{0,1},{1,0},{2,3},{3,2},{4,5},{5,4},{6,7},{7,6},{8,9},{9,8},{10,11... | collective-permute-start | bytes 3145736 | tf_op jit(solution)/shard_map/ppermute | solution.py:370
  1.2 4.5 %collective-permute-start.2 = (bf16[512,1024]{1,0:T(8,128)(2,1)}, bf16[512,1024]{1,0:T(8,128)(2,1)S(1)}, u32[]{:S(2)}, u32[]{:S(2)}) collective-permute-start(bf16[512,1024]{1,0:T(8,128)(2,1)} %weight.3), channel_id=1, source_target_pairs={{0,1},{1,0},{2,3},{3,2},{4,5},{5,4},{6,7},{7,6},{8,9},{9,8},{10,11... | collective-permute-start | bytes 3145736 | tf_op jit(solution)/shard_map/ppermute | solution.py:370
  1.2 1.2 %copy-start.3 = (bf16[384,1024]{1,0:T(8,128)(2,1)S(1)}, bf16[384,1024]{1,0:T(8,128)(2,1)}, u32[]{:S(2)}) copy-start(bf16[384,1024]{1,0:T(8,128)(2,1)} %refs_0_.1) | copy-start | bytes 2359300
  2.4 3.3 %copy-start.4 = (bf16[384,1024]{1,0:T(8,128)(2,1)S(1)}, bf16[384,1024]{1,0:T(8,128)(2,1)}, u32[]{:S(2)}) copy-start(bf16[384,1024]{1,0:T(8,128)(2,1)} %refs_0_.1) | copy-start | bytes 2359300
  2.7 8.1 %collective-permute-start = (bf16[96,1024]{1,0:T(8,128)(2,1)S(1)}, bf16[96,1024]{1,0:T(8,128)(2,1)S(1)}, u32[]{:S(2)}, u32[]{:S(2)}) collective-permute-start(bf16[96,1024]{1,0:T(8,128)(2,1)S(1)} %shard_map.87), channel_id=1, source_target_pairs={{0,2},{1,3},{2,0},{3,1},{4,6},{5,7},{6,4},{7,5},{8,10},{9,11},{10,... | collective-permute-start | bytes 589832 | tf_op jit(solution)/shard_map/ppermute | solution.py:373
  8.7 19.3 %collective-permute-start.7 = (bf16[1024,384]{1,0:T(8,128)(2,1)S(1)}, bf16[1024,384]{1,0:T(8,128)(2,1)S(1)}, u32[]{:S(2)}, u32[]{:S(2)}) collective-permute-start(bf16[1024,384]{1,0:T(8,128)(2,1)S(1)} %get-tuple-element.18.normed), channel_id=1, source_target_pairs={{0,1},{1,0},{2,3},{3,2},{4,5},{5,4},{6,7},{7,6},{8,9},{9,8},{10,11... | collective-permute-start | bytes 2359304 | tf_op jit(solution)/shard_map/ppermute | solution.py:370
  10.8 19.0 %collective-permute-start.6 = (bf16[384,1024]{1,0:T(8,128)(2,1)S(1)}, bf16[384,1024]{1,0:T(8,128)(2,1)S(1)}, u32[]{:S(2)}, u32[]{:S(2)}) collective-permute-start(bf16[384,1024]{1,0:T(8,128)(2,1)S(1)} %shard_map.91), channel_id=1, source_target_pairs={{0,2},{1,3},{2,0},{3,1},{4,6},{5,7},{6,4},{7,5},{8,10},{9,11},{10,... | collective-permute-start | bytes 2359304 | tf_op jit(solution)/shard_map/ppermute | solution.py:373
  12.5 6.6 %collective-permute-start.3 = (bf16[96,1024]{1,0:T(8,128)(2,1)S(1)}, bf16[96,1024]{1,0:T(8,128)(2,1)S(1)}, u32[]{:S(2)}, u32[]{:S(2)}) collective-permute-start(bf16[96,1024]{1,0:T(8,128)(2,1)S(1)} %shard_map.89.refs_0_), channel_id=1, source_target_pairs={{0,4},{4,0},{8,12},{12,8},{16,20},{20,16},{24,28},{28,24},{1,5},{5... | collective-permute-start | bytes 589832 | tf_op jit(solution)/shard_map/ppermute | solution.py:376
  14.0 7.5 %collective-permute-start.4 = (bf16[96,1024]{1,0:T(8,128)(2,1)S(1)}, bf16[96,1024]{1,0:T(8,128)(2,1)S(1)}, u32[]{:S(2)}, u32[]{:S(2)}) collective-permute-start(bf16[96,1024]{1,0:T(8,128)(2,1)S(1)} %shard_map.89.refs_0_), channel_id=1, source_target_pairs={{0,8},{4,12},{8,0},{12,4},{16,24},{20,28},{24,16},{28,20},{1,9},{5... | collective-permute-start | bytes 589832 | tf_op jit(solution)/shard_map/ppermute | solution.py:379
  15.6 8.2 %collective-permute-start.5 = (bf16[96,1024]{1,0:T(8,128)(2,1)S(1)}, bf16[96,1024]{1,0:T(8,128)(2,1)S(1)}, u32[]{:S(2)}, u32[]{:S(2)}) collective-permute-start(bf16[96,1024]{1,0:T(8,128)(2,1)S(1)} %shard_map.89.refs_0_), channel_id=1, source_target_pairs={{0,12},{4,8},{8,4},{12,0},{16,28},{20,24},{24,20},{28,16},{1,13},{... | collective-permute-start | bytes 589832 | tf_op jit(solution)/shard_map/ppermute | solution.py:386
  26.7 4.5 %collective-permute-start.9 = (bf16[1024,384]{1,0:T(8,128)(2,1)S(1)}, bf16[1024,384]{1,0:T(8,128)(2,1)S(1)}, u32[]{:S(2)}, u32[]{:S(2)}) collective-permute-start(bf16[1024,384]{1,0:T(8,128)(2,1)S(1)} %get-tuple-element.21.normed), channel_id=1, source_target_pairs={{0,1},{1,0},{2,3},{3,2},{4,5},{5,4},{6,7},{7,6},{8,9},{9,8},{10,11... | collective-permute-start | bytes 2359304 | tf_op jit(solution)/shard_map/ppermute | solution.py:370
  26.8 20.0 %collective-permute-start.10 = (bf16[384,1024]{1,0:T(8,128)(2,1)S(1)}, bf16[384,1024]{1,0:T(8,128)(2,1)S(1)}, u32[]{:S(2)}, u32[]{:S(2)}) collective-permute-start(bf16[384,1024]{1,0:T(8,128)(2,1)S(1)} %get-tuple-element.23), channel_id=1, source_target_pairs={{0,2},{1,3},{2,0},{3,1},{4,6},{5,7},{6,4},{7,5},{8,10},{9,11},{10,... | collective-permute-start | bytes 2359304 | tf_op jit(solution)/shard_map/ppermute | solution.py:373
  29.9 2.4 %copy-start.2 = (bf16[1,1024,512]{2,1,0:T(8,128)(2,1)S(1)}, bf16[1,1024,512]{2,1,0:T(8,128)(2,1)}, u32[]{:S(2)}) copy-start(bf16[1,1024,512]{2,1,0:T(8,128)(2,1)} %noise.1) | copy-start | bytes 3145732
  30.5 1.8 %collective-permute-start.8 = (bf16[384,512]{1,0:T(8,128)(2,1)S(1)}, bf16[384,512]{1,0:T(8,128)(2,1)S(1)}, u32[]{:S(2)}, u32[]{:S(2)}) collective-permute-start(bf16[384,512]{1,0:T(8,128)(2,1)S(1)} %shard_map.94), channel_id=1, source_target_pairs={{0,1},{1,0},{2,3},{3,2},{4,5},{5,4},{6,7},{7,6},{8,9},{9,8},{10,11... | collective-permute-start | bytes 1179656 | tf_op jit(solution)/shard_map/ppermute | solution.py:370
  47.4 1.8 %collective-permute-start.11 = (bf16[384,512]{1,0:T(8,128)(2,1)S(1)}, bf16[384,512]{1,0:T(8,128)(2,1)S(1)}, u32[]{:S(2)}, u32[]{:S(2)}) collective-permute-start(bf16[384,512]{1,0:T(8,128)(2,1)S(1)} %get-tuple-element.27), channel_id=1, source_target_pairs={{0,1},{1,0},{2,3},{3,2},{4,5},{5,4},{6,7},{7,6},{8,9},{9,8},{10,11... | collective-permute-start | bytes 1179656 | tf_op jit(solution)/shard_map/ppermute | solution.py:370
  49.4 7.5 %collective-permute-start.15 = (bf16[176,512]{1,0:T(8,128)(2,1)S(1)}, bf16[176,512]{1,0:T(8,128)(2,1)S(1)}, u32[]{:S(2)}, u32[]{:S(2)}) collective-permute-start(bf16[176,512]{1,0:T(8,128)(2,1)S(1)} %shard_map.98.rest_0_.refs_0_), channel_id=1, source_target_pairs={{0,4},{4,0},{8,12},{12,8},{16,20},{20,16},{24,28},{28,24},{1,5},{5... | collective-permute-start | bytes 540680 | tf_op jit(solution)/shard_map/ppermute | solution.py:376
  52.0 9.9 %collective-permute-start.12 = (bf16[224,512]{1,0:T(8,128)(2,1)S(1)}, bf16[224,512]{1,0:T(8,128)(2,1)S(1)}, u32[]{:S(2)}, u32[]{:S(2)}) collective-permute-start(bf16[224,512]{1,0:T(8,128)(2,1)S(1)} %shard_map.103.refs_1_), channel_id=1, source_target_pairs={{0,4},{4,0},{8,12},{12,8},{16,20},{20,16},{24,28},{28,24},{1,5},{5... | collective-permute-start | bytes 688136 | tf_op jit(solution)/shard_map/ppermute | solution.py:376
  52.7 14.0 %collective-permute-start.14 = (bf16[224,512]{1,0:T(8,128)(2,1)S(1)}, bf16[224,512]{1,0:T(8,128)(2,1)S(1)}, u32[]{:S(2)}, u32[]{:S(2)}) collective-permute-start(bf16[224,512]{1,0:T(8,128)(2,1)S(1)} %shard_map.100.rest_0_.refs_2_), channel_id=1, source_target_pairs={{0,4},{4,0},{8,12},{12,8},{16,20},{20,16},{24,28},{28,24},{1,5},{5... | collective-permute-start | bytes 688136 | tf_op jit(solution)/shard_map/ppermute | solution.py:376
  56.9 9.8 %collective-permute-start.16 = (bf16[176,512]{1,0:T(8,128)(2,1)S(1)}, bf16[176,512]{1,0:T(8,128)(2,1)S(1)}, u32[]{:S(2)}, u32[]{:S(2)}) collective-permute-start(bf16[176,512]{1,0:T(8,128)(2,1)S(1)} %collective-permute-done.15.refs_1_.refs_4_), channel_id=1, source_target_pairs={{0,8},{4,28},{8,16},{12,4},{16,24},{20,12},{24,0},{28,20},{1,9},{5... | collective-permute-start | bytes 540680 | tf_op jit(solution)/shard_map/ppermute | solution.py:383
  58.3 13.4 %collective-permute-start.19 = (bf16[224,512]{1,0:T(8,128)(2,1)S(1)}, bf16[224,512]{1,0:T(8,128)(2,1)S(1)}, u32[]{:S(2)}, u32[]{:S(2)}) collective-permute-start(bf16[224,512]{1,0:T(8,128)(2,1)S(1)} %shard_map.107.refs_3_), channel_id=1, source_target_pairs={{0,4},{4,0},{8,12},{12,8},{16,20},{20,16},{24,28},{28,24},{1,5},{5... | collective-permute-start | bytes 688136 | tf_op jit(solution)/shard_map/ppermute | solution.py:376
  61.9 9.8 %collective-permute-start.20 = (bf16[224,512]{1,0:T(8,128)(2,1)S(1)}, bf16[224,512]{1,0:T(8,128)(2,1)S(1)}, u32[]{:S(2)}, u32[]{:S(2)}) collective-permute-start(bf16[224,512]{1,0:T(8,128)(2,1)S(1)} %collective-permute-done.12.refs_1_.refs_5_), channel_id=1, source_target_pairs={{0,8},{4,28},{8,16},{12,4},{16,24},{20,12},{24,0},{28,20},{1,9},{5... | collective-permute-start | bytes 688136 | tf_op jit(solution)/shard_map/ppermute | solution.py:383
  66.7 8.4 %collective-permute-start.17 = (bf16[224,512]{1,0:T(8,128)(2,1)S(1)}, bf16[224,512]{1,0:T(8,128)(2,1)S(1)}, u32[]{:S(2)}, u32[]{:S(2)}) collective-permute-start(bf16[224,512]{1,0:T(8,128)(2,1)S(1)} %shard_map.105.refs_6_), channel_id=1, source_target_pairs={{0,8},{4,28},{8,16},{12,4},{16,24},{20,12},{24,0},{28,20},{1,9},{5... | collective-permute-start | bytes 688136 | tf_op jit(solution)/shard_map/ppermute | solution.py:383
  68.2 7.0 %collective-permute-start.13 = (bf16[176,512]{1,0:T(8,128)(2,1)S(1)}, bf16[176,512]{1,0:T(8,128)(2,1)S(1)}, u32[]{:S(2)}, u32[]{:S(2)}) collective-permute-start(bf16[176,512]{1,0:T(8,128)(2,1)S(1)} %shard_map.104.refs_0_), channel_id=1, source_target_pairs={{0,4},{4,0},{8,12},{12,8},{16,20},{20,16},{24,28},{28,24},{1,5},{5... | collective-permute-start | bytes 540680 | tf_op jit(solution)/shard_map/ppermute | solution.py:376
  71.7 9.0 %collective-permute-start.21 = (bf16[224,512]{1,0:T(8,128)(2,1)S(1)}, bf16[224,512]{1,0:T(8,128)(2,1)S(1)}, u32[]{:S(2)}, u32[]{:S(2)}) collective-permute-start(bf16[224,512]{1,0:T(8,128)(2,1)S(1)} %shard_map.108.refs_7_), channel_id=1, source_target_pairs={{0,8},{4,28},{8,16},{12,4},{16,24},{20,12},{24,0},{28,20},{1,9},{5... | collective-permute-start | bytes 688136 | tf_op jit(solution)/shard_map/ppermute | solution.py:383
  75.2 8.2 %collective-permute-start.18 = (bf16[176,512]{1,0:T(8,128)(2,1)S(1)}, bf16[176,512]{1,0:T(8,128)(2,1)S(1)}, u32[]{:S(2)}, u32[]{:S(2)}) collective-permute-start(bf16[176,512]{1,0:T(8,128)(2,1)S(1)} %shard_map.106.refs_1_), channel_id=1, source_target_pairs={{0,8},{4,28},{8,16},{12,4},{16,24},{20,12},{24,0},{28,20},{1,9},{5... | collective-permute-start | bytes 540680 | tf_op jit(solution)/shard_map/ppermute | solution.py:383

commit v10 on v9

--- a/solution.py
+++ b/solution.py
@@ -431,7 +431,7 @@
             across[chunk] = after(across[chunk], beyond[chunk - 2])
         beyond.append(to_next(across[chunk]))
     done = None
-    for first, stop in ((0, 4), (4, 5)):
+    for first, stop in ((0, 3), (3, 4), (4, 5)):
         given = (pieces[first:stop] for pieces in (own, across, beyond))
         done = finish(width, starts[first], pairing, *given, done)
     return done

time: 84.9 us -> 84.9 us (level)
    pallas_call x2 -> x3, Pallas kernels: 2.35 us -> 2.99 us  [finish(): pl.pallas_call(functools.partial(finish_kernel, start, stop, count), out_...]
  transfers between devices with their start and end apart: 22 -> 22, of which waited for: 13 -> 13; matrix products, arithmetic and copies ran while one was open for 0% -> 0% of each run, Pallas kernels for 14% -> 15%
where the time goes in v10:
time: 84.9 us; the launch traced here: 84.7 us
  waiting for transfers between devices  38.8 us (46%)
  starting transfers between devices  26.9 us (32%)
  Pallas kernels  14.9 us (18%)
  between operations  2.83 us (3%)
  local copies, waits for them, and re-layouts  1.24 us (1%)
    ppermute x3, waiting for transfers between devices, to_chip(): return lax.ppermute(value, 'dp', [(i, i ^ 2) for i in range(4)])  16.9 us
    ppermute x6, starting transfers between devices, to_mate(): return lax.ppermute(value, 'rep', [(i, i ^ 1) for i in range(replicas)])  12 us
    ppermute x6, waiting for transfers between devices, to_mate(): return lax.ppermute(value, 'rep', [(i, i ^ 1) for i in range(replicas)])  11.5 us
    ppermute x5, starting transfers between devices, to_next(): return lax.ppermute(value, 'rep', pairs)  6.65 us
    pallas_call x2, Pallas kernels, forward(): pl.pallas_call(functools.partial(forward_kernel, len(given), len(earlier)...  5.84 us
    ppermute x3, starting transfers between devices, to_chip(): return lax.ppermute(value, 'dp', [(i, i ^ 2) for i in range(4)])  5.31 us
    ppermute x5, waiting for transfers between devices, to_next(): return lax.ppermute(value, 'rep', pairs)  4.25 us
    pallas_call x3, Pallas kernels, finish(): pl.pallas_call(functools.partial(finish_kernel, start, stop, count), out_...  2.99 us
  transfers between devices with their start and end apart: 22, of which 13 were waited for; matrix products, arithmetic and copies ran while one was open for 0% of the time, Pallas kernels for 15%

profile of v10, /device:TPU:0, one launch (start us, length us, event | category | flops | bytes accessed | tf_op | source)
XLA Modules:
  0.0 84.7 jit_solution(4489539937804256270)
XLA Ops:
  1.2 1.2 %copy-done.3 = bf16[384,1024]{1,0:T(8,128)(2,1)S(1)} copy-done((bf16[384,1024]{1,0:T(8,128)(2,1)S(1)}, bf16[384,1024]{1,0:T(8,128)(2,1)}, u32[]{:S(2)}) %copy-start.3) | copy-done | bytes 786456
  2.7 3.0 %collective-permute-start = (bf16[96,1024]{1,0:T(8,128)(2,1)S(1)}, bf16[96,1024]{1,0:T(8,128)(2,1)S(1)}, u32[]{:S(2)}, u32[]{:S(2)}) collective-permute-start(bf16[96,1024]{1,0:T(8,128)(2,1)S(1)} %shard_map.87), channel_id=1, source_target_pairs={{0,2},{1,3},{2,0},{3,1},{4,6},{5,7},{6,4},{7,5},{8,10},{9,11},{10,... | collective-permute-start | bytes 589832 | tf_op jit(solution)/shard_map/ppermute | solution.py:373
  5.7 2.9 %shard_map.88 = (bf16[1024,384]{1,0:T(8,128)(2,1)S(1)}, bf16[384,512]{1,0:T(8,128)(2,1)S(1)}, bf16[384,512]{1,0:T(8,128)(2,1)S(1)}, bf16[384,1024]{1,0:T(8,128)(2,1)S(1)}, f32[384,1024]{1,0:T(8,128)S(1)}) custom-call(bf16[384,1024]{1,0:T(8,128)(2,1)S(1)} %copy-done.4, bf16[1024,512]{1,0:T(8,128)(2,1)S(1)} %bitcast.2, ...), custom_call_target="tpu_custom_call" | custom-call | bytes 1000 | tf_op jit(solution)/shard_map/pallas_call | solution.py:142
  8.8 2.0 %collective-permute-done.refs_0_.refs_1_ = bf16[96,1024]{1,0:T(8,128)(2,1)S(1)} collective-permute-done((bf16[96,1024]{1,0:T(8,128)(2,1)S(1)}, bf16[96,1024]{1,0:T(8,128)(2,1)S(1)}, u32[]{:S(2)}, u32[]{:S(2)}) %collective-permute-start) | collective-permute-done | bytes 196640 | tf_op jit(solution)/shard_map/ppermute | solution.py:373
  10.8 1.7 %collective-permute-start.6 = (bf16[384,1024]{1,0:T(8,128)(2,1)S(1)}, bf16[384,1024]{1,0:T(8,128)(2,1)S(1)}, u32[]{:S(2)}, u32[]{:S(2)}) collective-permute-start(bf16[384,1024]{1,0:T(8,128)(2,1)S(1)} %shard_map.91), channel_id=1, source_target_pairs={{0,2},{1,3},{2,0},{3,1},{4,6},{5,7},{6,4},{7,5},{8,10},{9,11},{10,... | collective-permute-start | bytes 2359304 | tf_op jit(solution)/shard_map/ppermute | solution.py:373
  12.5 1.5 %collective-permute-start.3 = (bf16[96,1024]{1,0:T(8,128)(2,1)S(1)}, bf16[96,1024]{1,0:T(8,128)(2,1)S(1)}, u32[]{:S(2)}, u32[]{:S(2)}) collective-permute-start(bf16[96,1024]{1,0:T(8,128)(2,1)S(1)} %shard_map.89.refs_0_), channel_id=1, source_target_pairs={{0,4},{4,0},{8,12},{12,8},{16,20},{20,16},{24,28},{28,24},{1,5},{5... | collective-permute-start | bytes 589832 | tf_op jit(solution)/shard_map/ppermute | solution.py:376
  14.0 1.6 %collective-permute-start.4 = (bf16[96,1024]{1,0:T(8,128)(2,1)S(1)}, bf16[96,1024]{1,0:T(8,128)(2,1)S(1)}, u32[]{:S(2)}, u32[]{:S(2)}) collective-permute-start(bf16[96,1024]{1,0:T(8,128)(2,1)S(1)} %shard_map.89.refs_0_), channel_id=1, source_target_pairs={{0,8},{4,12},{8,0},{12,4},{16,24},{20,28},{24,16},{28,20},{1,9},{5... | collective-permute-start | bytes 589832 | tf_op jit(solution)/shard_map/ppermute | solution.py:379
  16.0 3.1 %collective-permute-done.3.refs_1_ = bf16[96,1024]{1,0:T(8,128)(2,1)S(1)} collective-permute-done((bf16[96,1024]{1,0:T(8,128)(2,1)S(1)}, bf16[96,1024]{1,0:T(8,128)(2,1)S(1)}, u32[]{:S(2)}, u32[]{:S(2)}) %collective-permute-start.3) | collective-permute-done | bytes 196640 | tf_op jit(solution)/shard_map/ppermute | solution.py:376
  19.2 2.4 %collective-permute-done.4.refs_2_ = bf16[96,1024]{1,0:T(8,128)(2,1)S(1)} collective-permute-done((bf16[96,1024]{1,0:T(8,128)(2,1)S(1)}, bf16[96,1024]{1,0:T(8,128)(2,1)S(1)}, u32[]{:S(2)}, u32[]{:S(2)}) %collective-permute-start.4) | collective-permute-done | bytes 196640 | tf_op jit(solution)/shard_map/ppermute | solution.py:379
  21.6 2.2 %collective-permute-done.5.refs_3_ = bf16[96,1024]{1,0:T(8,128)(2,1)S(1)} collective-permute-done((bf16[96,1024]{1,0:T(8,128)(2,1)S(1)}, bf16[96,1024]{1,0:T(8,128)(2,1)S(1)}, u32[]{:S(2)}, u32[]{:S(2)}) %collective-permute-start.5) | collective-permute-done | bytes 196640 | tf_op jit(solution)/shard_map/ppermute | solution.py:386
  23.8 2.9 %shard_map.90 = (bf16[1024,384]{1,0:T(8,128)(2,1)S(1)}, bf16[384,512]{1,0:T(8,128)(2,1)S(1)}, bf16[384,512]{1,0:T(8,128)(2,1)S(1)}, bf16[384,1024]{1,0:T(8,128)(2,1)S(1)}, f32[384,1024]{1,0:T(8,128)S(1)}) custom-call(bf16[96,1024]{1,0:T(8,128)(2,1)S(1)} %shard_map.89.refs_0_, bf16[96,1024]{1,0:T(8,128)(2,1)S(1)} %collective-permute-done.3.refs_1_, ...), custom_call_target="tpu_custom_call" | custom-call | bytes 1000 | tf_op jit(solution)/shard_map/pallas_call | solution.py:142
  28.0 1.7 %collective-permute-done.6.sent = bf16[384,1024]{1,0:T(8,128)(2,1)S(1)} collective-permute-done((bf16[384,1024]{1,0:T(8,128)(2,1)S(1)}, bf16[384,1024]{1,0:T(8,128)(2,1)S(1)}, u32[]{:S(2)}, u32[]{:S(2)}) %collective-permute-start.6) | collective-permute-done | bytes 786464 | tf_op jit(solution)/shard_map/ppermute | solution.py:373
  31.2 1.1 %collective-permute-done.8.second = bf16[384,512]{1,0:T(8,128)(2,1)S(1)} collective-permute-done((bf16[384,512]{1,0:T(8,128)(2,1)S(1)}, bf16[384,512]{1,0:T(8,128)(2,1)S(1)}, u32[]{:S(2)}, u32[]{:S(2)}) %collective-permute-start.8) | collective-permute-done | bytes 393248 | tf_op jit(solution)/shard_map/ppermute | solution.py:370
  32.3 1.3 %shard_map.95.order.begun = f32[1024,512]{1,0:T(8,128)S(1)} custom-call(f32[1,512]{1,0:T(1,128)S(1)} %shard_map.86.refs_1_.strength, bf16[384,512]{1,0:T(8,128)(2,1)S(1)} %shard_map.93.first, bf16[384,512]{1,0:T(8,128)(2,1)S(1)} %collective-permute-done.8.second, bf16[1024,384]{1,0:T(8,128)(2,1)S(1)} %get-tuple-element.23.normed, ...), custom_call_target="tpu_custom_call" | custom-call | flops 805306368 | bytes 3145728 | tf_op jit(solution)/shard_map/pallas_call | solution.py:263
  33.6 13.2 %collective-permute-done.10.sent = bf16[384,1024]{1,0:T(8,128)(2,1)S(1)} collective-permute-done((bf16[384,1024]{1,0:T(8,128)(2,1)S(1)}, bf16[384,1024]{1,0:T(8,128)(2,1)S(1)}, u32[]{:S(2)}, u32[]{:S(2)}) %collective-permute-start.10) | collective-permute-done | bytes 786464 | tf_op jit(solution)/shard_map/ppermute | solution.py:373
  47.4 1.3 %shard_map.97.begun = f32[1024,512]{1,0:T(8,128)S(1)} custom-call(f32[1024,512]{1,0:T(8,128)S(1)} %shard_map.95.order.begun, bf16[384,1024]{1,0:T(8,128)(2,1)S(1)} %get-tuple-element.27.errors, bf16[512,1024]{1,0:T(8,128)(2,1)S(1)} %copy-done, bf16[384,512]{1,0:T(8,128)(2,1)S(1)} %get-tuple-element.28.slope, bf16[1024,384]{1,0:T(8,128)(2,1)S(1)} %get-tuple-element.20.normed), custom_call_target="tpu_custom_call" | custom-call | flops 805306368 | bytes 4194304 | tf_op jit(solution)/shard_map/pallas_call | solution.py:236
  49.4 1.4 %collective-permute-start.15 = (bf16[176,512]{1,0:T(8,128)(2,1)S(1)}, bf16[176,512]{1,0:T(8,128)(2,1)S(1)}, u32[]{:S(2)}, u32[]{:S(2)}) collective-permute-start(bf16[176,512]{1,0:T(8,128)(2,1)S(1)} %shard_map.98.rest_0_.refs_0_), channel_id=1, source_target_pairs={{0,4},{4,0},{8,12},{12,8},{16,20},{20,16},{24,28},{28,24},{1,5},{5... | collective-permute-start | bytes 540680 | tf_op jit(solution)/shard_map/ppermute | solution.py:376
  52.7 1.4 %collective-permute-start.14 = (bf16[224,512]{1,0:T(8,128)(2,1)S(1)}, bf16[224,512]{1,0:T(8,128)(2,1)S(1)}, u32[]{:S(2)}, u32[]{:S(2)}) collective-permute-start(bf16[224,512]{1,0:T(8,128)(2,1)S(1)} %shard_map.100.rest_0_.refs_2_), channel_id=1, source_target_pairs={{0,4},{4,0},{8,12},{12,8},{16,20},{20,16},{24,28},{28,24},{1,5},{5... | collective-permute-start | bytes 688136 | tf_op jit(solution)/shard_map/ppermute | solution.py:376
  54.1 2.8 %collective-permute-done.15.refs_1_.refs_3_ = bf16[176,512]{1,0:T(8,128)(2,1)S(1)} collective-permute-done((bf16[176,512]{1,0:T(8,128)(2,1)S(1)}, bf16[176,512]{1,0:T(8,128)(2,1)S(1)}, u32[]{:S(2)}, u32[]{:S(2)}) %collective-permute-start.15) | collective-permute-done | bytes 180256 | tf_op jit(solution)/shard_map/ppermute | solution.py:376
  56.9 1.4 %collective-permute-start.16 = (bf16[176,512]{1,0:T(8,128)(2,1)S(1)}, bf16[176,512]{1,0:T(8,128)(2,1)S(1)}, u32[]{:S(2)}, u32[]{:S(2)}) collective-permute-start(bf16[176,512]{1,0:T(8,128)(2,1)S(1)} %collective-permute-done.15.refs_1_.refs_3_), channel_id=1, source_target_pairs={{0,8},{4,28},{8,16},{12,4},{16,24},{20,12},{24,0},{28,20},{1,9},{5... | collective-permute-start | bytes 540680 | tf_op jit(solution)/shard_map/ppermute | solution.py:383
  58.3 3.5 %collective-permute-start.19 = (bf16[224,512]{1,0:T(8,128)(2,1)S(1)}, bf16[224,512]{1,0:T(8,128)(2,1)S(1)}, u32[]{:S(2)}, u32[]{:S(2)}) collective-permute-start(bf16[224,512]{1,0:T(8,128)(2,1)S(1)} %shard_map.107.refs_0_), channel_id=1, source_target_pairs={{0,4},{4,0},{8,12},{12,8},{16,20},{20,16},{24,28},{28,24},{1,5},{5... | collective-permute-start | bytes 688136 | tf_op jit(solution)/shard_map/ppermute | solution.py:376
  61.9 1.4 %collective-permute-start.20 = (bf16[224,512]{1,0:T(8,128)(2,1)S(1)}, bf16[224,512]{1,0:T(8,128)(2,1)S(1)}, u32[]{:S(2)}, u32[]{:S(2)}) collective-permute-start(bf16[224,512]{1,0:T(8,128)(2,1)S(1)} %collective-permute-done.12.refs_1_.refs_4_), channel_id=1, source_target_pairs={{0,8},{4,28},{8,16},{12,4},{16,24},{20,12},{24,0},{28,20},{1,9},{5... | collective-permute-start | bytes 688136 | tf_op jit(solution)/shard_map/ppermute | solution.py:383
  63.2 3.5 %collective-permute-done.14.refs_0_ = bf16[224,512]{1,0:T(8,128)(2,1)S(1)} collective-permute-done((bf16[224,512]{1,0:T(8,128)(2,1)S(1)}, bf16[224,512]{1,0:T(8,128)(2,1)S(1)}, u32[]{:S(2)}, u32[]{:S(2)}) %collective-permute-start.14) | collective-permute-done | bytes 229408 | tf_op jit(solution)/shard_map/ppermute | solution.py:376
  66.7 1.4 %collective-permute-start.17 = (bf16[224,512]{1,0:T(8,128)(2,1)S(1)}, bf16[224,512]{1,0:T(8,128)(2,1)S(1)}, u32[]{:S(2)}, u32[]{:S(2)}) collective-permute-start(bf16[224,512]{1,0:T(8,128)(2,1)S(1)} %shard_map.105.refs_5_), channel_id=1, source_target_pairs={{0,8},{4,28},{8,16},{12,4},{16,24},{20,12},{24,0},{28,20},{1,9},{5... | collective-permute-start | bytes 688136 | tf_op jit(solution)/shard_map/ppermute | solution.py:383
  68.2 3.5 %collective-permute-start.13 = (bf16[176,512]{1,0:T(8,128)(2,1)S(1)}, bf16[176,512]{1,0:T(8,128)(2,1)S(1)}, u32[]{:S(2)}, u32[]{:S(2)}) collective-permute-start(bf16[176,512]{1,0:T(8,128)(2,1)S(1)} %shard_map.104.refs_0_), channel_id=1, source_target_pairs={{0,4},{4,0},{8,12},{12,8},{16,20},{20,16},{24,28},{28,24},{1,5},{5... | collective-permute-start | bytes 540680 | tf_op jit(solution)/shard_map/ppermute | solution.py:376
  71.7 1.4 %collective-permute-start.21 = (bf16[224,512]{1,0:T(8,128)(2,1)S(1)}, bf16[224,512]{1,0:T(8,128)(2,1)S(1)}, u32[]{:S(2)}, u32[]{:S(2)}) collective-permute-start(bf16[224,512]{1,0:T(8,128)(2,1)S(1)} %shard_map.108.refs_1_), channel_id=1, source_target_pairs={{0,8},{4,28},{8,16},{12,4},{16,24},{20,12},{24,0},{28,20},{1,9},{5... | collective-permute-start | bytes 688136 | tf_op jit(solution)/shard_map/ppermute | solution.py:383
  73.1 2.1 %collective-permute-done.13.refs_0_ = bf16[176,512]{1,0:T(8,128)(2,1)S(1)} collective-permute-done((bf16[176,512]{1,0:T(8,128)(2,1)S(1)}, bf16[176,512]{1,0:T(8,128)(2,1)S(1)}, u32[]{:S(2)}, u32[]{:S(2)}) %collective-permute-start.13) | collective-permute-done | bytes 180256 | tf_op jit(solution)/shard_map/ppermute | solution.py:376
  75.2 1.0 %collective-permute-start.18 = (bf16[176,512]{1,0:T(8,128)(2,1)S(1)}, bf16[176,512]{1,0:T(8,128)(2,1)S(1)}, u32[]{:S(2)}, u32[]{:S(2)}) collective-permute-start(bf16[176,512]{1,0:T(8,128)(2,1)S(1)} %shard_map.106.refs_1_), channel_id=1, source_target_pairs={{0,8},{4,28},{8,16},{12,4},{16,24},{20,12},{24,0},{28,20},{1,9},{5... | collective-permute-start | bytes 540680 | tf_op jit(solution)/shard_map/ppermute | solution.py:383
  77.4 0.9 %shard_map.109 = (bf16[1,1024,512]{2,1,0:T(8,128)(2,1)}, f32[1,2,512]{2,1,0:T(2,128)S(1)}) custom-call(s32[1]{0:T(128)S(6)} %copy.30.mate, s32[1]{0:T(128)S(6)} %copy.31.swapped, bf16[176,512]{1,0:T(8,128)(2,1)S(1)} %shard_map.98.rest_0_.refs_0_, bf16[224,512]{1,0:T(8,128)(2,1)S(1)} %shard_map.103.refs_1_, bf16[224,512]{1,0:T(8,128)(2,1)S(1)} %shard_map.100.rest_0_.refs_2_, ...), custom_call_target="tpu_custom_call" | custom-call | bytes 2555904 | tf_op jit(solution)/shard_map/pallas_call | solution.py:343
  78.4 2.3 %collective-permute-done.21.refs_2_ = bf16[224,512]{1,0:T(8,128)(2,1)S(1)} collective-permute-done((bf16[224,512]{1,0:T(8,128)(2,1)S(1)}, bf16[224,512]{1,0:T(8,128)(2,1)S(1)}, u32[]{:S(2)}, u32[]{:S(2)}) %collective-permute-start.21) | collective-permute-done | bytes 229408 | tf_op jit(solution)/shard_map/ppermute | solution.py:383
  81.4 1.9 %collective-permute-done.18.refs_2_ = bf16[176,512]{1,0:T(8,128)(2,1)S(1)} collective-permute-done((bf16[176,512]{1,0:T(8,128)(2,1)S(1)}, bf16[176,512]{1,0:T(8,128)(2,1)S(1)}, u32[]{:S(2)}, u32[]{:S(2)}) %collective-permute-start.18) | collective-permute-done | bytes 180256 | tf_op jit(solution)/shard_map/ppermute | solution.py:383
  83.4 1.3 %shard_map.111 = (bf16[1,1024,512]{2,1,0:T(8,128)(2,1)}, f32[1,2,512]{2,1,0:T(2,128)}) custom-call(s32[1]{0:T(128)S(6)} %copy.30.mate, s32[1]{0:T(128)S(6)} %copy.31.swapped, bf16[176,512]{1,0:T(8,128)(2,1)S(1)} %shard_map.104.refs_0_, bf16[176,512]{1,0:T(8,128)(2,1)S(1)} %shard_map.106.refs_1_, ...), custom_call_target="tpu_custom_call", output_to_operand_aliasing={{0}: (6, {})} | custom-call | bytes 720896 | tf_op jit(solution)/shard_map/pallas_call | solution.py:343
  (49 shorter events, 7.4 us)
Async XLA Ops:
  0.6 5.1 %copy-start = (bf16[512,1024]{1,0:T(8,128)(2,1)S(1)}, bf16[512,1024]{1,0:T(8,128)(2,1)}, u32[]{:S(2)}) copy-start(bf16[512,1024]{1,0:T(8,128)(2,1)} %weight.3) | copy-start | bytes 3145732
  0.6 5.0 %copy-start.1 = (bf16[1,1024,512]{2,1,0:T(8,128)(2,1)S(1)}, bf16[1,1024,512]{2,1,0:T(8,128)(2,1)}, u32[]{:S(2)}) copy-start(bf16[1,1024,512]{2,1,0:T(8,128)(2,1)} %params.1) | copy-start | bytes 3145732
  0.6 5.0 %collective-permute-start.1 = (bf16[1024,512]{1,0:T(8,128)(2,1)}, bf16[1024,512]{1,0:T(8,128)(2,1)S(1)}, u32[]{:S(2)}, u32[]{:S(2)}) collective-permute-start(bf16[1024,512]{1,0:T(8,128)(2,1)} %bitcast.1), channel_id=1, source_target_pairs={{0,1},{1,0},{2,3},{3,2},{4,5},{5,4},{6,7},{7,6},{8,9},{9,8},{10,11... | collective-permute-start | bytes 3145736 | tf_op jit(solution)/shard_map/ppermute | solution.py:370
  1.2 4.5 %collective-permute-start.2 = (bf16[512,1024]{1,0:T(8,128)(2,1)}, bf16[512,1024]{1,0:T(8,128)(2,1)S(1)}, u32[]{:S(2)}, u32[]{:S(2)}) collective-permute-start(bf16[512,1024]{1,0:T(8,128)(2,1)} %weight.3), channel_id=1, source_target_pairs={{0,1},{1,0},{2,3},{3,2},{4,5},{5,4},{6,7},{7,6},{8,9},{9,8},{10,11... | collective-permute-start | bytes 3145736 | tf_op jit(solution)/shard_map/ppermute | solution.py:370
  1.2 1.2 %copy-start.3 = (bf16[384,1024]{1,0:T(8,128)(2,1)S(1)}, bf16[384,1024]{1,0:T(8,128)(2,1)}, u32[]{:S(2)}) copy-start(bf16[384,1024]{1,0:T(8,128)(2,1)} %refs_0_.1) | copy-start | bytes 2359300
  2.4 3.3 %copy-start.4 = (bf16[384,1024]{1,0:T(8,128)(2,1)S(1)}, bf16[384,1024]{1,0:T(8,128)(2,1)}, u32[]{:S(2)}) copy-start(bf16[384,1024]{1,0:T(8,128)(2,1)} %refs_0_.1) | copy-start | bytes 2359300
  2.7 8.1 %collective-permute-start = (bf16[96,1024]{1,0:T(8,128)(2,1)S(1)}, bf16[96,1024]{1,0:T(8,128)(2,1)S(1)}, u32[]{:S(2)}, u32[]{:S(2)}) collective-permute-start(bf16[96,1024]{1,0:T(8,128)(2,1)S(1)} %shard_map.87), channel_id=1, source_target_pairs={{0,2},{1,3},{2,0},{3,1},{4,6},{5,7},{6,4},{7,5},{8,10},{9,11},{10,... | collective-permute-start | bytes 589832 | tf_op jit(solution)/shard_map/ppermute | solution.py:373
  8.7 19.3 %collective-permute-start.7 = (bf16[1024,384]{1,0:T(8,128)(2,1)S(1)}, bf16[1024,384]{1,0:T(8,128)(2,1)S(1)}, u32[]{:S(2)}, u32[]{:S(2)}) collective-permute-start(bf16[1024,384]{1,0:T(8,128)(2,1)S(1)} %get-tuple-element.20.normed), channel_id=1, source_target_pairs={{0,1},{1,0},{2,3},{3,2},{4,5},{5,4},{6,7},{7,6},{8,9},{9,8},{10,11... | collective-permute-start | bytes 2359304 | tf_op jit(solution)/shard_map/ppermute | solution.py:370
  10.8 19.0 %collective-permute-start.6 = (bf16[384,1024]{1,0:T(8,128)(2,1)S(1)}, bf16[384,1024]{1,0:T(8,128)(2,1)S(1)}, u32[]{:S(2)}, u32[]{:S(2)}) collective-permute-start(bf16[384,1024]{1,0:T(8,128)(2,1)S(1)} %shard_map.91), channel_id=1, source_target_pairs={{0,2},{1,3},{2,0},{3,1},{4,6},{5,7},{6,4},{7,5},{8,10},{9,11},{10,... | collective-permute-start | bytes 2359304 | tf_op jit(solution)/shard_map/ppermute | solution.py:373
  12.5 6.6 %collective-permute-start.3 = (bf16[96,1024]{1,0:T(8,128)(2,1)S(1)}, bf16[96,1024]{1,0:T(8,128)(2,1)S(1)}, u32[]{:S(2)}, u32[]{:S(2)}) collective-permute-start(bf16[96,1024]{1,0:T(8,128)(2,1)S(1)} %shard_map.89.refs_0_), channel_id=1, source_target_pairs={{0,4},{4,0},{8,12},{12,8},{16,20},{20,16},{24,28},{28,24},{1,5},{5... | collective-permute-start | bytes 589832 | tf_op jit(solution)/shard_map/ppermute | solution.py:376
  14.0 7.5 %collective-permute-start.4 = (bf16[96,1024]{1,0:T(8,128)(2,1)S(1)}, bf16[96,1024]{1,0:T(8,128)(2,1)S(1)}, u32[]{:S(2)}, u32[]{:S(2)}) collective-permute-start(bf16[96,1024]{1,0:T(8,128)(2,1)S(1)} %shard_map.89.refs_0_), channel_id=1, source_target_pairs={{0,8},{4,12},{8,0},{12,4},{16,24},{20,28},{24,16},{28,20},{1,9},{5... | collective-permute-start | bytes 589832 | tf_op jit(solution)/shard_map/ppermute | solution.py:379
  15.6 8.2 %collective-permute-start.5 = (bf16[96,1024]{1,0:T(8,128)(2,1)S(1)}, bf16[96,1024]{1,0:T(8,128)(2,1)S(1)}, u32[]{:S(2)}, u32[]{:S(2)}) collective-permute-start(bf16[96,1024]{1,0:T(8,128)(2,1)S(1)} %shard_map.89.refs_0_), channel_id=1, source_target_pairs={{0,12},{4,8},{8,4},{12,0},{16,28},{20,24},{24,20},{28,16},{1,13},{... | collective-permute-start | bytes 589832 | tf_op jit(solution)/shard_map/ppermute | solution.py:386
  26.7 4.5 %collective-permute-start.9 = (bf16[1024,384]{1,0:T(8,128)(2,1)S(1)}, bf16[1024,384]{1,0:T(8,128)(2,1)S(1)}, u32[]{:S(2)}, u32[]{:S(2)}) collective-permute-start(bf16[1024,384]{1,0:T(8,128)(2,1)S(1)} %get-tuple-element.23.normed), channel_id=1, source_target_pairs={{0,1},{1,0},{2,3},{3,2},{4,5},{5,4},{6,7},{7,6},{8,9},{9,8},{10,11... | collective-permute-start | bytes 2359304 | tf_op jit(solution)/shard_map/ppermute | solution.py:370
  26.8 20.0 %collective-permute-start.10 = (bf16[384,1024]{1,0:T(8,128)(2,1)S(1)}, bf16[384,1024]{1,0:T(8,128)(2,1)S(1)}, u32[]{:S(2)}, u32[]{:S(2)}) collective-permute-start(bf16[384,1024]{1,0:T(8,128)(2,1)S(1)} %get-tuple-element.25), channel_id=1, source_target_pairs={{0,2},{1,3},{2,0},{3,1},{4,6},{5,7},{6,4},{7,5},{8,10},{9,11},{10,... | collective-permute-start | bytes 2359304 | tf_op jit(solution)/shard_map/ppermute | solution.py:373
  29.9 2.4 %copy-start.2 = (bf16[1,1024,512]{2,1,0:T(8,128)(2,1)S(1)}, bf16[1,1024,512]{2,1,0:T(8,128)(2,1)}, u32[]{:S(2)}) copy-start(bf16[1,1024,512]{2,1,0:T(8,128)(2,1)} %noise.1) | copy-start | bytes 3145732
  30.5 1.8 %collective-permute-start.8 = (bf16[384,512]{1,0:T(8,128)(2,1)S(1)}, bf16[384,512]{1,0:T(8,128)(2,1)S(1)}, u32[]{:S(2)}, u32[]{:S(2)}) collective-permute-start(bf16[384,512]{1,0:T(8,128)(2,1)S(1)} %shard_map.94), channel_id=1, source_target_pairs={{0,1},{1,0},{2,3},{3,2},{4,5},{5,4},{6,7},{7,6},{8,9},{9,8},{10,11... | collective-permute-start | bytes 1179656 | tf_op jit(solution)/shard_map/ppermute | solution.py:370
  47.4 1.8 %collective-permute-start.11 = (bf16[384,512]{1,0:T(8,128)(2,1)S(1)}, bf16[384,512]{1,0:T(8,128)(2,1)S(1)}, u32[]{:S(2)}, u32[]{:S(2)}) collective-permute-start(bf16[384,512]{1,0:T(8,128)(2,1)S(1)} %get-tuple-element.29), channel_id=1, source_target_pairs={{0,1},{1,0},{2,3},{3,2},{4,5},{5,4},{6,7},{7,6},{8,9},{9,8},{10,11... | collective-permute-start | bytes 1179656 | tf_op jit(solution)/shard_map/ppermute | solution.py:370
  49.4 7.5 %collective-permute-start.15 = (bf16[176,512]{1,0:T(8,128)(2,1)S(1)}, bf16[176,512]{1,0:T(8,128)(2,1)S(1)}, u32[]{:S(2)}, u32[]{:S(2)}) collective-permute-start(bf16[176,512]{1,0:T(8,128)(2,1)S(1)} %shard_map.98.rest_0_.refs_0_), channel_id=1, source_target_pairs={{0,4},{4,0},{8,12},{12,8},{16,20},{20,16},{24,28},{28,24},{1,5},{5... | collective-permute-start | bytes 540680 | tf_op jit(solution)/shard_map/ppermute | solution.py:376
  52.0 9.9 %collective-permute-start.12 = (bf16[224,512]{1,0:T(8,128)(2,1)S(1)}, bf16[224,512]{1,0:T(8,128)(2,1)S(1)}, u32[]{:S(2)}, u32[]{:S(2)}) collective-permute-start(bf16[224,512]{1,0:T(8,128)(2,1)S(1)} %shard_map.103.refs_1_), channel_id=1, source_target_pairs={{0,4},{4,0},{8,12},{12,8},{16,20},{20,16},{24,28},{28,24},{1,5},{5... | collective-permute-start | bytes 688136 | tf_op jit(solution)/shard_map/ppermute | solution.py:376
  52.7 14.0 %collective-permute-start.14 = (bf16[224,512]{1,0:T(8,128)(2,1)S(1)}, bf16[224,512]{1,0:T(8,128)(2,1)S(1)}, u32[]{:S(2)}, u32[]{:S(2)}) collective-permute-start(bf16[224,512]{1,0:T(8,128)(2,1)S(1)} %shard_map.100.rest_0_.refs_2_), channel_id=1, source_target_pairs={{0,4},{4,0},{8,12},{12,8},{16,20},{20,16},{24,28},{28,24},{1,5},{5... | collective-permute-start | bytes 688136 | tf_op jit(solution)/shard_map/ppermute | solution.py:376
  56.9 9.8 %collective-permute-start.16 = (bf16[176,512]{1,0:T(8,128)(2,1)S(1)}, bf16[176,512]{1,0:T(8,128)(2,1)S(1)}, u32[]{:S(2)}, u32[]{:S(2)}) collective-permute-start(bf16[176,512]{1,0:T(8,128)(2,1)S(1)} %collective-permute-done.15.refs_1_.refs_3_), channel_id=1, source_target_pairs={{0,8},{4,28},{8,16},{12,4},{16,24},{20,12},{24,0},{28,20},{1,9},{5... | collective-permute-start | bytes 540680 | tf_op jit(solution)/shard_map/ppermute | solution.py:383
  58.3 13.4 %collective-permute-start.19 = (bf16[224,512]{1,0:T(8,128)(2,1)S(1)}, bf16[224,512]{1,0:T(8,128)(2,1)S(1)}, u32[]{:S(2)}, u32[]{:S(2)}) collective-permute-start(bf16[224,512]{1,0:T(8,128)(2,1)S(1)} %shard_map.107.refs_0_), channel_id=1, source_target_pairs={{0,4},{4,0},{8,12},{12,8},{16,20},{20,16},{24,28},{28,24},{1,5},{5... | collective-permute-start | bytes 688136 | tf_op jit(solution)/shard_map/ppermute | solution.py:376
  61.9 9.8 %collective-permute-start.20 = (bf16[224,512]{1,0:T(8,128)(2,1)S(1)}, bf16[224,512]{1,0:T(8,128)(2,1)S(1)}, u32[]{:S(2)}, u32[]{:S(2)}) collective-permute-start(bf16[224,512]{1,0:T(8,128)(2,1)S(1)} %collective-permute-done.12.refs_1_.refs_4_), channel_id=1, source_target_pairs={{0,8},{4,28},{8,16},{12,4},{16,24},{20,12},{24,0},{28,20},{1,9},{5... | collective-permute-start | bytes 688136 | tf_op jit(solution)/shard_map/ppermute | solution.py:383
  66.7 8.4 %collective-permute-start.17 = (bf16[224,512]{1,0:T(8,128)(2,1)S(1)}, bf16[224,512]{1,0:T(8,128)(2,1)S(1)}, u32[]{:S(2)}, u32[]{:S(2)}) collective-permute-start(bf16[224,512]{1,0:T(8,128)(2,1)S(1)} %shard_map.105.refs_5_), channel_id=1, source_target_pairs={{0,8},{4,28},{8,16},{12,4},{16,24},{20,12},{24,0},{28,20},{1,9},{5... | collective-permute-start | bytes 688136 | tf_op jit(solution)/shard_map/ppermute | solution.py:383
  68.2 7.0 %collective-permute-start.13 = (bf16[176,512]{1,0:T(8,128)(2,1)S(1)}, bf16[176,512]{1,0:T(8,128)(2,1)S(1)}, u32[]{:S(2)}, u32[]{:S(2)}) collective-permute-start(bf16[176,512]{1,0:T(8,128)(2,1)S(1)} %shard_map.104.refs_0_), channel_id=1, source_target_pairs={{0,4},{4,0},{8,12},{12,8},{16,20},{20,16},{24,28},{28,24},{1,5},{5... | collective-permute-start | bytes 540680 | tf_op jit(solution)/shard_map/ppermute | solution.py:376
  71.7 9.0 %collective-permute-start.21 = (bf16[224,512]{1,0:T(8,128)(2,1)S(1)}, bf16[224,512]{1,0:T(8,128)(2,1)S(1)}, u32[]{:S(2)}, u32[]{:S(2)}) collective-permute-start(bf16[224,512]{1,0:T(8,128)(2,1)S(1)} %shard_map.108.refs_1_), channel_id=1, source_target_pairs={{0,8},{4,28},{8,16},{12,4},{16,24},{20,12},{24,0},{28,20},{1,9},{5... | collective-permute-start | bytes 688136 | tf_op jit(solution)/shard_map/ppermute | solution.py:383
  75.2 8.2 %collective-permute-start.18 = (bf16[176,512]{1,0:T(8,128)(2,1)S(1)}, bf16[176,512]{1,0:T(8,128)(2,1)S(1)}, u32[]{:S(2)}, u32[]{:S(2)}) collective-permute-start(bf16[176,512]{1,0:T(8,128)(2,1)S(1)} %shard_map.106.refs_1_), channel_id=1, source_target_pairs={{0,8},{4,28},{8,16},{12,4},{16,24},{20,12},{24,0},{28,20},{1,9},{5... | collective-permute-start | bytes 540680 | tf_op jit(solution)/shard_map/ppermute | solution.py:383
